TPU v7x, 32 devices: a whole 2x2x4 slice. The times are simulated.
32 devices in a mesh: groups: 2 (over y), bay: 4 (over z), sec: 4 (over x, core).
Axes of the slice: x: 2, y: 2, z: 4, core: 2. Of those that a mesh axis runs over, the one named last changes fastest.
Arguments:
- edge_load: bfloat16 [8, 4, 8, 3072], P(('groups', 'bay'), None, None, 'sec'), parts along dimension 0, may hold values from -6 to 6
- interior_load: bfloat16 [8, 4, 8, 3072], P(('groups', 'bay'), None, None, 'sec'), parts along dimension 0, may hold values from -6 to 6
- coupling: bfloat16 [8, 3072, 3072], P(('groups', 'bay'), 'sec'), parts along dimension 0, may hold values from -0.109375 to 0.109375
- block_cols: int32 [8, 24, 8], P(('groups', 'bay'), 'sec'), parts along dimension 0, may hold values from 0 to 23, as said below
- transfer: bfloat16 [8, 24, 8, 4, 128, 128], P(('groups', 'bay'), 'sec'), parts along dimension 0, may hold values from -0.21875 to 0.21875
- local_inverse: bfloat16 [8, 24, 4, 128, 128], P(('groups', 'bay'), 'sec'), parts along dimension 0
Outputs:
- edge_response: bfloat16 [8, 4, 8, 3072], P(('groups', 'bay'), None, None, 'sec'), parts along dimension 0
There are 2 independent parts, one for each index of `groups`. A program takes and returns all parts, laid end to end along the dimension named above; each array names one. Nothing has to cross between parts.
Inputs may be any that keep to these rules, and one draw needn't show every extreme that they name: `block_cols`: the first entry of block row r is r itself; the 8 entries of a block row are distinct.
All inputs are finite; a program needn't handle non-finite values.
Results may differ from a plain program's by a relative error of at most 0.0074.
Values may be sent and summed in bfloat16 or wider, within the bound.
No kernel may reach another device: no remote copies, remote signals or barrier semaphores. Data moves between devices by JAX's collectives and lax.ppermute only.
A program may use at most 64 MiB of HBM per device.

v0:
```python
import jax
import jax.numpy as jnp
from jax import lax
from jax.sharding import PartitionSpec as P


def passed_along(block, axis, distance):
    devices = range(lax.axis_size(axis))
    route = [((i - distance) % len(devices), i) for i in devices]
    return lax.ppermute(block, axis, route)


def solve_all(inverse, load):
    freqs, cases, width = load.shape
    row_blocks = inverse.shape[0]
    block = inverse.shape[-1]
    pieces = load.reshape(freqs, cases, row_blocks, block)
    result = jnp.einsum("rfij,fcrj->fcri", inverse, pieces, preferred_element_type=jnp.float32)
    return result.reshape(freqs, cases, width)


def couple_all(transfer_rows, block_ids, state):
    freqs, cases, width = state.shape
    row_blocks, nonzero = block_ids.shape
    block = transfer_rows.shape[-1]
    pieces = state.reshape(freqs, cases, width // block, block)
    picked = jnp.take(pieces, block_ids.reshape(-1), axis=2).reshape(
        freqs, cases, row_blocks, nonzero, block
    )
    result = jnp.einsum(
        "rkfij,fcrkj->fcri", transfer_rows, picked, preferred_element_type=jnp.float32
    )
    return result.reshape(freqs, cases, row_blocks * block)


def receive(full_piece):
    return passed_along(full_piece, "bay", 1)


def widen(updated):
    return lax.all_gather(updated, "sec", axis=2, tiled=True)


def per_device(edge_load, interior_load, coupling, block_cols, transfer, local_inverse):
    edge_rows = edge_load[0]
    interior_rows = interior_load[0]
    coupling_rows = coupling[0]
    block_ids = block_cols[0]
    transfer_rows = transfer[0]
    inverse_rows = local_inverse[0]
    freqs, cases, rows = edge_rows.shape
    inner = interior_rows.shape[2]
    width = coupling_rows.shape[1]
    partial_value = jnp.dot(
        interior_rows.reshape(freqs * cases, inner),
        coupling_rows,
        preferred_element_type=jnp.float32,
    )
    partial_value = partial_value.reshape(freqs, cases, width)
    load_term = edge_rows.astype(jnp.float32) - lax.psum_scatter(
        partial_value, "sec", scatter_dimension=2, tiled=True
    )
    initial = solve_all(inverse_rows, load_term.astype(jnp.bfloat16)).astype(jnp.bfloat16)
    position = lax.axis_index("bay")
    bay_count = lax.axis_size("bay")
    initial_full = lax.all_gather(initial, "sec", axis=2, tiled=True)

    def advance(step, state_pair):
        own_rows, full_state = state_pair
        incoming = receive(full_state)
        summed = (load_term + couple_all(transfer_rows, block_ids, incoming)).astype(jnp.bfloat16)
        updated = solve_all(inverse_rows, summed).astype(jnp.bfloat16)
        active = position == step
        new_rows = jnp.where(active, updated, own_rows)
        new_full = jnp.where(active, widen(updated), full_state)
        return (new_rows, new_full)

    own_rows, _ = lax.fori_loop(0, bay_count, advance, (initial, initial_full))
    return own_rows[None]


def solution(mesh):
    in_specs = (
        P(("groups", "bay"), None, None, "sec"),
        P(("groups", "bay"), None, None, "sec"),
        P(("groups", "bay"), "sec", None),
        P(("groups", "bay"), "sec", None),
        P(("groups", "bay"), "sec", None, None, None, None),
        P(("groups", "bay"), "sec", None, None, None),
    )
    out_specs = P(("groups", "bay"), None, None, "sec")
    return jax.shard_map(
        per_device, mesh=mesh, in_specs=in_specs, out_specs=out_specs, check_vma=False
    )
```

profile of v0, /device:TPU:0, one launch (start us, length us, event | category | flops | bytes accessed | tf_op | source)
XLA Modules:
  0.0 130.8 jit_solution(17279884645777835035)
XLA Ops:
  6.5 0.0 copy-start
  6.5 0.0 copy-start.4
  6.5 0.0 copy-start.1
  6.5 0.0 copy-start.3
  6.5 0.0 reduce-scatter.2.cloned.1.call-start
  6.6 0.7 copy-done
  7.3 4.0 %fusion.18 = f32[4,8,3072]{2,1,0:T(8,128)} fusion(bf16[1,768,3072]{2,1,0:T(8,128)(2,1)} %param.10, bf16[1,4,8,768]{3,2,1,0:T(8,128)(2,1)S(1)} %copy-done), kind=kOutput, calls=%fused_computation.18 | convolution fusion | flops 150994944 | bytes 5160960 | tf_op jit(solution)/shard_map/dot_general | solution.py:54
  11.3 0.0 reduce-scatter.2.cloned.1.call-update
  11.3 0.0 copy-done.4
  11.3 0.1 reshape_squeeze.8
  11.4 0.0 copy-done.1
  11.4 0.1 copy.33
  11.5 23.5 %reduce-scatter.2.cloned.1.call-done = f32[4,8,768]{2,1,0:T(8,128)} async-done(((f32[4,8,3072]{2,1,0:T(8,128)}), f32[4,8,768]{2,1,0:T(8,128)}) %reduce-scatter.2.cloned.1.call-update) | async-done | bytes 98320 | tf_op jit(solution)/shard_map/reduce_scatter | solution.py:60
  35.0 0.0 copy-done.3
  35.0 0.9 convert_subtract_fusion
  35.9 0.5 fusion.20
  36.4 5.6 %all_gather.10 = bf16[4,8,3072]{2,1,0:T(8,128)(2,1)S(1)} all-gather(bf16[4,8,768]{2,1,0:T(8,128)(2,1)S(1)} %fusion.20), channel_id=1, replica_groups=mesh['groups'=2,'bay'=4,'sec'=4] {'sec'}, dimensions={2}, use_global_device_ids=true | all-gather | bytes 245760 | tf_op jit(solution)/shard_map/all_gather | solution.py:66
  42.0 81.3 %while.16 = (s32[]{:T(128)}, bf16[4,8,768]{2,1,0:T(8,128)(2,1)S(1)}, bf16[4,8,3072]{2,1,0:T(8,128)(2,1)S(1)}, s32[]{:T(128)}, f32[4,8,768]{2,1,0:T(8,128)S(1)}, ...) while((s32[]{:T(128)}, ...), condition=%wide.wide.region_2.0_spmd, body=%wide.wide.region_1.2_spmd.sunk | while | flops 57017776 | bytes 10130616 | solution.py:78
  42.0 1.5 %collective-permute-start = (bf16[4,8,3072]{2,1,0:T(8,128)(2,1)S(1)}, bf16[4,8,3072]{2,1,0:T(8,128)(2,1)S(1)}, u32[]{:S(2)}, u32[]{:S(2)}) collective-permute-start(bf16[4,8,3072]{2,1,0:T(8,128)(2,1)S(1)} %get-tuple-element.284), channel_id=1, source_target_pairs={{12,0},{0,4},{4,8},{8,12},{13,1},{1,5},{5,9},{9,13},{14,2},{2,6},{... | collective-permute-start | bytes 589832 | tf_op jit(solution)/shard_map/while/body/eval_jaxpr/ppermute | solution.py:10
  43.5 7.4 %collective-permute-done = bf16[4,8,3072]{2,1,0:T(8,128)(2,1)S(1)} collective-permute-done((bf16[4,8,3072]{2,1,0:T(8,128)(2,1)S(1)}, bf16[4,8,3072]{2,1,0:T(8,128)(2,1)S(1)}, u32[]{:S(2)}, u32[]{:S(2)}) %collective-permute-start) | collective-permute-done | bytes 196640 | tf_op jit(solution)/shard_map/while/body/eval_jaxpr/ppermute | solution.py:10
  51.0 0.7 gather_fusion
  51.7 5.0 %broadcast_select_fusion.13 = (bf16[4,8,768]{2,1,0:T(8,128)(2,1)S(1)}, bf16[4,8,768]{2,1,0:T(8,128)(2,1)S(1)}) fusion(bf16[4,8,768]{2,1,0:T(8,128)(2,1)S(1)} %get-tuple-element.283, pred[]{:T(512)S(6)} %eq.9, bf16[6,4,128,128]{3,2,0,1:T(8,128)(2,1)S(1)} %get-tuple-element.299, bf16[6,8,4,128,128]{4,3,2,1,0:T(8,128)(2,1)} %get-tuple-element.298, ...), kind=kOutput, calls=%fused_computation.12.clone.clone.1 | convolution fusion | flops 56918016 | bytes 7716913 | tf_op jit(solution)/shard_map/while/body/eval_jaxpr/rfij,fcrj->fcri/dot_general | solution.py:18
  56.6 5.6 %all_gather.13 = bf16[4,8,3072]{2,1,0:T(8,128)(2,1)S(1)} all-gather(bf16[4,8,768]{2,1,0:T(8,128)(2,1)S(1)} %get-tuple-element.271), channel_id=1, replica_groups=mesh['groups'=2,'bay'=4,'sec'=4] {'sec'}, dimensions={2}, use_global_device_ids=true | all-gather | bytes 245760 | tf_op jit(solution)/shard_map/while/body/eval_jaxpr/all_gather | solution.py:41
  62.2 0.1 broadcast_select_fusion.14
  62.3 0.1 collective-permute-start
  62.4 8.9 %collective-permute-done = bf16[4,8,3072]{2,1,0:T(8,128)(2,1)S(1)} collective-permute-done((bf16[4,8,3072]{2,1,0:T(8,128)(2,1)S(1)}, bf16[4,8,3072]{2,1,0:T(8,128)(2,1)S(1)}, u32[]{:S(2)}, u32[]{:S(2)}) %collective-permute-start) | collective-permute-done | bytes 196640 | tf_op jit(solution)/shard_map/while/body/eval_jaxpr/ppermute | solution.py:10
  71.3 0.7 gather_fusion
  72.0 5.0 %broadcast_select_fusion.13 = (bf16[4,8,768]{2,1,0:T(8,128)(2,1)S(1)}, bf16[4,8,768]{2,1,0:T(8,128)(2,1)S(1)}) fusion(bf16[4,8,768]{2,1,0:T(8,128)(2,1)S(1)} %get-tuple-element.283, pred[]{:T(512)S(6)} %eq.9, bf16[6,4,128,128]{3,2,0,1:T(8,128)(2,1)S(1)} %get-tuple-element.299, bf16[6,8,4,128,128]{4,3,2,1,0:T(8,128)(2,1)} %get-tuple-element.298, ...), kind=kOutput, calls=%fused_computation.12.clone.clone.1 | convolution fusion | flops 56918016 | bytes 7716913 | tf_op jit(solution)/shard_map/while/body/eval_jaxpr/rfij,fcrj->fcri/dot_general | solution.py:18
  77.0 5.6 %all_gather.13 = bf16[4,8,3072]{2,1,0:T(8,128)(2,1)S(1)} all-gather(bf16[4,8,768]{2,1,0:T(8,128)(2,1)S(1)} %get-tuple-element.271), channel_id=1, replica_groups=mesh['groups'=2,'bay'=4,'sec'=4] {'sec'}, dimensions={2}, use_global_device_ids=true | all-gather | bytes 245760 | tf_op jit(solution)/shard_map/while/body/eval_jaxpr/all_gather | solution.py:41
  82.6 0.1 broadcast_select_fusion.14
  82.7 0.1 collective-permute-start
  82.8 8.9 %collective-permute-done = bf16[4,8,3072]{2,1,0:T(8,128)(2,1)S(1)} collective-permute-done((bf16[4,8,3072]{2,1,0:T(8,128)(2,1)S(1)}, bf16[4,8,3072]{2,1,0:T(8,128)(2,1)S(1)}, u32[]{:S(2)}, u32[]{:S(2)}) %collective-permute-start) | collective-permute-done | bytes 196640 | tf_op jit(solution)/shard_map/while/body/eval_jaxpr/ppermute | solution.py:10
  91.7 0.7 gather_fusion
  92.4 5.0 %broadcast_select_fusion.13 = (bf16[4,8,768]{2,1,0:T(8,128)(2,1)S(1)}, bf16[4,8,768]{2,1,0:T(8,128)(2,1)S(1)}) fusion(bf16[4,8,768]{2,1,0:T(8,128)(2,1)S(1)} %get-tuple-element.283, pred[]{:T(512)S(6)} %eq.9, bf16[6,4,128,128]{3,2,0,1:T(8,128)(2,1)S(1)} %get-tuple-element.299, bf16[6,8,4,128,128]{4,3,2,1,0:T(8,128)(2,1)} %get-tuple-element.298, ...), kind=kOutput, calls=%fused_computation.12.clone.clone.1 | convolution fusion | flops 56918016 | bytes 7716913 | tf_op jit(solution)/shard_map/while/body/eval_jaxpr/rfij,fcrj->fcri/dot_general | solution.py:18
  97.3 5.6 %all_gather.13 = bf16[4,8,3072]{2,1,0:T(8,128)(2,1)S(1)} all-gather(bf16[4,8,768]{2,1,0:T(8,128)(2,1)S(1)} %get-tuple-element.271), channel_id=1, replica_groups=mesh['groups'=2,'bay'=4,'sec'=4] {'sec'}, dimensions={2}, use_global_device_ids=true | all-gather | bytes 245760 | tf_op jit(solution)/shard_map/while/body/eval_jaxpr/all_gather | solution.py:41
  102.9 0.1 broadcast_select_fusion.14
  103.0 0.1 collective-permute-start
  103.1 8.9 %collective-permute-done = bf16[4,8,3072]{2,1,0:T(8,128)(2,1)S(1)} collective-permute-done((bf16[4,8,3072]{2,1,0:T(8,128)(2,1)S(1)}, bf16[4,8,3072]{2,1,0:T(8,128)(2,1)S(1)}, u32[]{:S(2)}, u32[]{:S(2)}) %collective-permute-start) | collective-permute-done | bytes 196640 | tf_op jit(solution)/shard_map/while/body/eval_jaxpr/ppermute | solution.py:10
  112.0 0.7 gather_fusion
  112.7 5.0 %broadcast_select_fusion.13 = (bf16[4,8,768]{2,1,0:T(8,128)(2,1)S(1)}, bf16[4,8,768]{2,1,0:T(8,128)(2,1)S(1)}) fusion(bf16[4,8,768]{2,1,0:T(8,128)(2,1)S(1)} %get-tuple-element.283, pred[]{:T(512)S(6)} %eq.9, bf16[6,4,128,128]{3,2,0,1:T(8,128)(2,1)S(1)} %get-tuple-element.299, bf16[6,8,4,128,128]{4,3,2,1,0:T(8,128)(2,1)} %get-tuple-element.298, ...), kind=kOutput, calls=%fused_computation.12.clone.clone.1 | convolution fusion | flops 56918016 | bytes 7716913 | tf_op jit(solution)/shard_map/while/body/eval_jaxpr/rfij,fcrj->fcri/dot_general | solution.py:18
  117.7 5.6 %all_gather.13 = bf16[4,8,3072]{2,1,0:T(8,128)(2,1)S(1)} all-gather(bf16[4,8,768]{2,1,0:T(8,128)(2,1)S(1)} %get-tuple-element.271), channel_id=1, replica_groups=mesh['groups'=2,'bay'=4,'sec'=4] {'sec'}, dimensions={2}, use_global_device_ids=true | all-gather | bytes 245760 | tf_op jit(solution)/shard_map/while/body/eval_jaxpr/all_gather | solution.py:41
  123.3 0.1 broadcast_select_fusion.14
  123.3 0.0 copy-start.2
  123.4 0.6 copy-done.2
  (13 shorter events, 0.1 us)
Async XLA Ops:
  6.5 0.8 copy-start
  6.5 4.8 %copy-start.4 = (s32[1,6,8]{2,0,1:T(1,128)S(1)}, s32[1,6,8]{2,0,1:T(1,128)}, u32[]{:S(2)}) copy-start(s32[1,6,8]{2,0,1:T(1,128)} %param.11) | copy-start | bytes 580
  6.5 4.9 %copy-start.1 = (bf16[1,6,4,128,128]{4,3,2,1,0:T(8,128)(2,1)S(1)}, bf16[1,6,4,128,128]{4,3,2,1,0:T(8,128)(2,1)}, u32[]{:S(2)}) copy-start(bf16[1,6,4,128,128]{4,3,2,1,0:T(8,128)(2,1)} %param.13) | copy-start | bytes 2359300
  6.5 28.5 %copy-start.3 = (bf16[1,4,8,768]{3,2,1,0:T(8,128)(2,1)S(1)}, bf16[1,4,8,768]{3,2,1,0:T(8,128)(2,1)}, u32[]{:S(2)}) copy-start(bf16[1,4,8,768]{3,2,1,0:T(8,128)(2,1)} %param.8) | copy-start | bytes 147460
  6.5 28.5 %reduce-scatter.2.cloned.1.call-start = ((), (), s32[]{:S(2)}) async-start(), calls=%async_computation.1 | async-start | bytes 491520 | tf_op jit(solution)/shard_map/reduce_scatter | solution.py:60
  42.0 8.9 %collective-permute-start = (bf16[4,8,3072]{2,1,0:T(8,128)(2,1)S(1)}, bf16[4,8,3072]{2,1,0:T(8,128)(2,1)S(1)}, u32[]{:S(2)}, u32[]{:S(2)}) collective-permute-start(bf16[4,8,3072]{2,1,0:T(8,128)(2,1)S(1)} %get-tuple-element.284), channel_id=1, source_target_pairs={{12,0},{0,4},{4,8},{8,12},{13,1},{1,5},{5,9},{9,13},{14,2},{2,6},{... | collective-permute-start | bytes 589832 | tf_op jit(solution)/shard_map/while/body/eval_jaxpr/ppermute | solution.py:10
  62.3 9.0 %collective-permute-start = (bf16[4,8,3072]{2,1,0:T(8,128)(2,1)S(1)}, bf16[4,8,3072]{2,1,0:T(8,128)(2,1)S(1)}, u32[]{:S(2)}, u32[]{:S(2)}) collective-permute-start(bf16[4,8,3072]{2,1,0:T(8,128)(2,1)S(1)} %get-tuple-element.284), channel_id=1, source_target_pairs={{12,0},{0,4},{4,8},{8,12},{13,1},{1,5},{5,9},{9,13},{14,2},{2,6},{... | collective-permute-start | bytes 589832 | tf_op jit(solution)/shard_map/while/body/eval_jaxpr/ppermute | solution.py:10
  82.7 9.0 %collective-permute-start = (bf16[4,8,3072]{2,1,0:T(8,128)(2,1)S(1)}, bf16[4,8,3072]{2,1,0:T(8,128)(2,1)S(1)}, u32[]{:S(2)}, u32[]{:S(2)}) collective-permute-start(bf16[4,8,3072]{2,1,0:T(8,128)(2,1)S(1)} %get-tuple-element.284), channel_id=1, source_target_pairs={{12,0},{0,4},{4,8},{8,12},{13,1},{1,5},{5,9},{9,13},{14,2},{2,6},{... | collective-permute-start | bytes 589832 | tf_op jit(solution)/shard_map/while/body/eval_jaxpr/ppermute | solution.py:10
  103.0 9.0 %collective-permute-start = (bf16[4,8,3072]{2,1,0:T(8,128)(2,1)S(1)}, bf16[4,8,3072]{2,1,0:T(8,128)(2,1)S(1)}, u32[]{:S(2)}, u32[]{:S(2)}) collective-permute-start(bf16[4,8,3072]{2,1,0:T(8,128)(2,1)S(1)} %get-tuple-element.284), channel_id=1, source_target_pairs={{12,0},{0,4},{4,8},{8,12},{13,1},{1,5},{5,9},{9,13},{14,2},{2,6},{... | collective-permute-start | bytes 589832 | tf_op jit(solution)/shard_map/while/body/eval_jaxpr/ppermute | solution.py:10
  123.3 0.6 copy-start.2
Sparse Core Ops, SparseCore 0:
  11.4 23.5 reduce-scatter.1
where the time goes:
time: 131 us
  waiting for transfers between devices  57.6 us (44%)
  blocking collectives  28 us (21%)
  matrix products  24.3 us (19%)
  between operations  13.5 us (10%)
  local copies, waits for them, and re-layouts  4.29 us (3%)
  starting transfers between devices  1.69 us (1%)
    ppermute x4, waiting for transfers between devices, passed_along(): return lax.ppermute(block, axis, route)  34.1 us
    reduce_scatter x1, waiting for transfers between devices, per_device(): lax.psum_scatter(partial_value, 'sec', scatter_dimension=2, tiled=True)  23.5 us
    all_gather x4, blocking collectives, widen(): return lax.all_gather(updated, 'sec', axis=2, tiled=True)  22.4 us
    dot_general x5, matrix products, solve_all(): jnp.einsum('rfij,fcrj->fcri', inverse, pieces, preferred_element_type=jnp...  20.3 us
    all_gather x1, blocking collectives, per_device(): initial_full = lax.all_gather(initial, 'sec', axis=2, tiled=True)  5.61 us
    dot_general x1, matrix products, per_device(): jnp.dot(interior_rows.reshape(freqs * cases, inner), coupling_rows, prefe...  3.96 us
    gather x4, local copies, waits for them, and re-layouts, couple_all(): jnp.take(pieces, block_ids.reshape(-1), axis=2)  2.78 us
  transfers between devices with their start and end apart: 5, of which 5 were waited for; matrix products, arithmetic and copies ran while one was open for 0% of the time, Pallas kernels for 0%

commit v1 on v0

v1 whole, which is shorter than its diff:
```python
import functools

import jax
import jax.numpy as jnp
from jax import lax
from jax.experimental import pallas as pl
from jax.experimental.pallas import tpu as pltpu
from jax.sharding import PartitionSpec as P

VMEM = pl.BlockSpec(memory_space=pltpu.VMEM)
SMEM = pl.BlockSpec(memory_space=pltpu.SMEM)
ANY = pl.BlockSpec(memory_space=pl.ANY)
MIB = 1 << 20


def nt_dot(left, right):
    return lax.dot_general(left, right, (((1,), (1,)), ((), ())), preferred_element_type=jnp.float32)


def diagonal(product, freqs):
    rows, cols = product.shape[0] // freqs, product.shape[1] // freqs
    return jnp.concatenate(
        [product[f * rows:(f + 1) * rows, f * cols:(f + 1) * cols] for f in range(freqs)], axis=0
    )


def by_parity(odd, rows):
    half = rows.shape[0] // 2
    return jnp.where(odd, rows[half:], rows[:half]), jnp.where(odd, rows[:half], rows[half:])


def columns_of(coupling, owner, width):
    return coupling.at[:, pl.ds(pl.multiple_of(owner * width, width), width)]


def far_kernel(sec_ref, interior, coupling, piece2, piece3, held, sems):
    sec = sec_ref[0]
    width = held.shape[-1]
    copies = [
        pltpu.make_async_copy(columns_of(coupling, sec ^ d, width), held.at[n], sems.at[n])
        for n, d in enumerate((2, 3))
    ]
    for copy in copies:
        copy.start()
    pieces = {2: piece2, 3: piece3}
    for n, d in enumerate((2, 3)):
        copies[n].wait()
        part = -jnp.dot(interior[...], held[n], preferred_element_type=jnp.float32)
        first, second = by_parity(((sec ^ d) & 1) == 1, part)
        pieces[d][:, :width] = first.astype(jnp.bfloat16)
        pieces[d ^ 1][:, width:] = second.astype(jnp.bfloat16)


def near_kernel(
    sec_ref, interior, edge, coupling, transfer, inverse,
    piece1, own, transfer_own, transfer_out, inverse_own, inverse_out, held, sems,
):
    sec = sec_ref[0]
    width = held.shape[-1]
    odd = (sec & 1) == 1
    half = transfer.shape[2] // 2
    mine = (sec & 1) * half
    other = half - mine
    copies = [
        pltpu.make_async_copy(columns_of(coupling, sec ^ d, width), held.at[n], sems.at[n])
        for n, d in enumerate((1, 0))
    ]
    moves = [
        pltpu.make_async_copy(inverse.at[:, pl.ds(other, half)], inverse_out, sems.at[2]),
        pltpu.make_async_copy(transfer.at[:, :, pl.ds(other, half)], transfer_out, sems.at[3]),
        pltpu.make_async_copy(inverse.at[:, pl.ds(mine, half)], inverse_own, sems.at[4]),
        pltpu.make_async_copy(transfer.at[:, :, pl.ds(mine, half)], transfer_own, sems.at[5]),
    ]
    for copy in copies + moves:
        copy.start()
    copies[0].wait()
    part = -jnp.dot(interior[...], held[0], preferred_element_type=jnp.float32)
    first, second = by_parity(jnp.logical_not(odd), part)
    piece1[:, :width] = first.astype(jnp.bfloat16)
    own[:, width:] = second
    copies[1].wait()
    part = edge[...].astype(jnp.float32) - jnp.dot(
        interior[...], held[1], preferred_element_type=jnp.float32
    )
    first, second = by_parity(odd, part)
    own[:, :width] = first
    piece1[:, width:] = second.astype(jnp.bfloat16)
    for move in moves:
        move.wait()


def initial_kernel(own, got1, got2, got3, inverse_own, inverse_got, load, initial):
    rows, freqs, block, _ = inverse_own.shape
    for r in range(2 * rows):
        cols = slice(r * block, (r + 1) * block)
        inverse = inverse_own if r < rows else inverse_got
        total = own[:, cols] + got1[:, cols].astype(jnp.float32)
        total += got2[:, cols].astype(jnp.float32) + got3[:, cols].astype(jnp.float32)
        load[:, cols] = total
        solved = nt_dot(
            total.astype(jnp.bfloat16), inverse[r % rows].reshape(freqs * block, block)
        )
        initial[:, cols] = diagonal(solved, freqs).astype(jnp.bfloat16)


def step_kernel(
    active, place, near, far, previous, load, transfer_own, transfer_got, inverse_own, inverse_got,
    out, state,
):
    rows, nonzero, freqs, block, _ = transfer_own.shape

    @pl.when(active[0] == 1)
    def _():
        for r in range(2 * rows):
            state[r] = near[:, r * block:(r + 1) * block]
            state[2 * rows + r] = far[:, r * block:(r + 1) * block]
        for r in range(2 * rows):
            cols = slice(r * block, (r + 1) * block)
            transfer, inverse = (
                (transfer_own, inverse_own) if r < rows else (transfer_got, inverse_got)
            )
            picked = jnp.concatenate([state[place[r * nonzero + k]] for k in range(nonzero)], axis=1)
            matrix = jnp.concatenate(
                [transfer[r % rows, k].reshape(freqs * block, block) for k in range(nonzero)], axis=1
            )
            summed = (load[:, cols] + diagonal(nt_dot(picked, matrix), freqs)).astype(jnp.bfloat16)
            solved = nt_dot(summed, inverse[r % rows].reshape(freqs * block, block))
            out[:, cols] = diagonal(solved, freqs).astype(jnp.bfloat16)

    @pl.when(active[0] != 1)
    def _():
        out[...] = previous[...]


def moved(value, distance, offset):
    bays, secs = lax.axis_size("bay"), lax.axis_size("sec")
    route = [
        (b * secs + s, (b + distance) % bays * secs + (s ^ offset))
        for b in range(bays)
        for s in range(secs)
    ]
    return lax.ppermute(value, ("bay", "sec"), route)


def hop(value, source, offset):
    bays, secs = lax.axis_size("bay"), lax.axis_size("sec")
    route = [
        (source * secs + s, (source + 1) % bays * secs + (s ^ offset)) for s in range(secs)
    ]
    return lax.ppermute(value, ("bay", "sec"), route)


def per_device(edge_load, interior_load, coupling, block_cols, transfer, local_inverse):
    _, freqs, cases, width = edge_load.shape
    _, rows, nonzero, _, block, _ = transfer.shape
    inner = interior_load.shape[-1]
    half = freqs // 2
    lines = half * cases
    sec = lax.axis_index("sec")
    position = lax.axis_index("bay")
    bays = lax.axis_size("bay")
    edge = edge_load.reshape(freqs * cases, width)
    interior = interior_load.reshape(freqs * cases, inner)
    sec_word = sec.astype(jnp.int32).reshape(1)
    params = pltpu.CompilerParams(vmem_limit_bytes=24 * MIB)
    bf16, f32 = jnp.bfloat16, jnp.float32
    wide = (lines, 2 * width)

    piece2, piece3 = pl.pallas_call(
        far_kernel,
        out_shape=[jax.ShapeDtypeStruct(wide, bf16)] * 2,
        in_specs=[SMEM, VMEM, ANY],
        out_specs=[VMEM] * 2,
        scratch_shapes=[pltpu.VMEM((2, inner, width), bf16), pltpu.SemaphoreType.DMA((2,))],
        compiler_params=params,
        name="far",
    )(sec_word, interior, coupling[0])
    got2, got3 = moved(piece2, 0, 2), moved(piece3, 0, 3)

    matrices = (rows, nonzero, half, block, block)
    inverses = (rows, half, block, block)
    piece1, own, transfer_own, transfer_out, inverse_own, inverse_out = pl.pallas_call(
        near_kernel,
        out_shape=[
            jax.ShapeDtypeStruct(wide, bf16),
            jax.ShapeDtypeStruct(wide, f32),
            pltpu.VMEM(matrices, bf16),
            pltpu.VMEM(matrices, bf16),
            pltpu.VMEM(inverses, bf16),
            pltpu.VMEM(inverses, bf16),
        ],
        in_specs=[SMEM, VMEM, VMEM, ANY, ANY, ANY],
        out_specs=[VMEM] * 6,
        scratch_shapes=[pltpu.VMEM((2, inner, width), bf16), pltpu.SemaphoreType.DMA((6,))],
        compiler_params=params,
        name="near",
    )(sec_word, interior, edge, coupling[0], transfer[0], local_inverse[0])
    got1 = moved(piece1, 0, 1)
    inverse_got = moved(inverse_out, 0, 1)
    transfer_got = moved(transfer_out, 0, 1)

    cols = block_cols[0]
    cols = jnp.concatenate([cols, moved(cols, 0, 1)], axis=0)
    place = ((cols // rows) ^ sec) * rows + cols % rows
    place = place.reshape(-1).astype(jnp.int32)

    load, state = pl.pallas_call(
        initial_kernel,
        out_shape=[jax.ShapeDtypeStruct(wide, f32), jax.ShapeDtypeStruct(wide, bf16)],
        in_specs=[VMEM] * 6,
        out_specs=[VMEM] * 2,
        compiler_params=params,
        name="initial",
    )(own, got1, got2, got3, inverse_own, inverse_got)

    for step in range(bays):
        source = (step - 1) % bays
        near, far = hop(state, source, 0), hop(state, source, 2)
        active = (position == step).astype(jnp.int32).reshape(1)
        state = pl.pallas_call(
            step_kernel,
            out_shape=jax.ShapeDtypeStruct(wide, bf16),
            in_specs=[SMEM, SMEM] + [VMEM] * 8,
            out_specs=VMEM,
            scratch_shapes=[pltpu.VMEM((4 * rows, lines, block), bf16)],
            compiler_params=params,
            name="step",
        )(active, place, near, far, state, load, transfer_own, transfer_got, inverse_own, inverse_got)

    kept, sent = state[:, :width], state[:, width:]
    got = moved(sent, 0, 1)
    odd = (sec & 1) == 1
    low, high = jnp.where(odd, got, kept), jnp.where(odd, kept, got)
    return jnp.concatenate([low, high], axis=0).reshape(1, freqs, cases, width)


def solution(mesh):
    in_specs = (
        P(("groups", "bay"), None, None, "sec"),
        P(("groups", "bay"), None, None, "sec"),
        P(("groups", "bay"), "sec", None),
        P(("groups", "bay"), "sec", None),
        P(("groups", "bay"), "sec", None, None, None, None),
        P(("groups", "bay"), "sec", None, None, None),
    )
    out_specs = P(("groups", "bay"), None, None, "sec")
    return jax.shard_map(
        per_device, mesh=mesh, in_specs=in_specs, out_specs=out_specs, check_vma=False
    )
```

time: 131 us -> 82.8 us (0.63)
  the two profiles are of different devices: /device:TPU:0 before, /device:TPU:29 now
where the time goes in v1:
time: 82.8 us; the launch traced here: 82.1 us
  waiting for transfers between devices  25.9 us (31%)
  Pallas kernels  19.6 us (24%)
  starting transfers between devices  18.4 us (22%)
  local copies, waits for them, and re-layouts  14.8 us (18%)
  other arithmetic  3.17 us (4%)
    ppermute x8, waiting for transfers between devices, hop(): return lax.ppermute(value, ('bay', 'sec'), route)  23.7 us
    pallas_call x4, Pallas kernels, per_device(): pl.pallas_call(step_kernel, out_shape=jax.ShapeDtypeStruct(wide, bf16), i...  13.1 us
    unnamed x31, local copies, waits for them, and re-layouts  12.7 us
    ppermute x8, starting transfers between devices, hop(): return lax.ppermute(value, ('bay', 'sec'), route)  11 us
    ppermute x7, starting transfers between devices, moved(): return lax.ppermute(value, ('bay', 'sec'), route)  7.48 us
    pallas_call x1, Pallas kernels, per_device(): pl.pallas_call(near_kernel, out_shape=[jax.ShapeDtypeStruct(wide, bf16),...  3.5 us
    ppermute x7, waiting for transfers between devices, moved(): return lax.ppermute(value, ('bay', 'sec'), route)  2.23 us
  transfers between devices with their start and end apart: 15, of which 5 were waited for; matrix products, arithmetic and copies ran while one was open for 5% of the time, Pallas kernels for 4%

profile of v1, /device:TPU:29, one launch (start us, length us, event | category | flops | bytes accessed | tf_op | source)
XLA Modules:
  0.0 82.1 jit_solution(9393627626327063828)
XLA Ops:
  0.0 2.3 %copy-done = bf16[1,768,3072]{2,1,0:T(8,128)(2,1)S(1)} copy-done((bf16[1,768,3072]{2,1,0:T(8,128)(2,1)S(1)}, bf16[1,768,3072]{2,1,0:T(8,128)(2,1)}, u32[]{:S(2)}) %copy-start) | copy-done | bytes 4718616
  2.3 2.8 %copy-done.2 = bf16[1,6,8,4,128,128]{5,4,3,2,1,0:T(8,128)(2,1)S(1)} copy-done((bf16[1,6,8,4,128,128]{5,4,3,2,1,0:T(8,128)(2,1)S(1)}, bf16[1,6,8,4,128,128]{5,4,3,2,1,0:T(8,128)(2,1)}, u32[]{:S(2)}) %copy-start.2) | copy-done | bytes 6291480
  5.1 1.1 %copy-done.7 = bf16[1,6,4,128,128]{4,3,2,1,0:T(8,128)(2,1)S(1)} copy-done((bf16[1,6,4,128,128]{4,3,2,1,0:T(8,128)(2,1)S(1)}, bf16[1,6,4,128,128]{4,3,2,1,0:T(8,128)(2,1)}, u32[]{:S(2)}) %copy-start.7) | copy-done | bytes 786456
  6.3 0.8 copy-done.8
  7.1 0.8 copy-done.12
  7.9 3.5 %near.1 = (bf16[16,1536]{1,0:T(8,128)(2,1)}, f32[16,1536]{1,0:T(8,128)S(1)}, bf16[6,8,2,128,128]{4,3,2,1,0:T(8,128)(2,1)S(1)}, bf16[6,8,2,128,128]{4,3,2,1,0:T(8...) custom-call(s32[1]{0:T(128)} %bitcast.4.sec_ref, bf16[32,768]{1,0:T(8,128)(2,1)S(1)} %bitcast.19, ...), custom_call_target="tpu_custom_call" | custom-call | tf_op jit(solution)/shard_map/near/pallas_call | solution.py:182
  11.4 0.0 copy-start.10
  11.4 0.0 copy-start.14
  11.4 0.7 collective-permute-start.7
  12.1 0.1 collective-permute-start.4
  12.2 0.4 collective-permute-start.1
  12.6 0.0 copy-done.1
  12.6 1.6 %far.1 = (bf16[16,1536]{1,0:T(8,128)(2,1)}, bf16[16,1536]{1,0:T(8,128)(2,1)S(1)}) custom-call(s32[1]{0:T(128)} %bitcast.4.sec_ref, bf16[32,768]{1,0:T(8,128)(2,1)S(1)} %bitcast.20, bf16[768,3072]{1,0:T(8,128)(2,1)S(1)} %bitcast.16), custom_call_target="tpu_custom_call" | custom-call | tf_op jit(solution)/shard_map/far/pallas_call | solution.py:169
  14.3 0.0 copy-done.10
  14.3 0.0 copy-start.13
  14.3 0.6 copy-done.13
  14.9 1.2 %collective-permute-start.2 = (bf16[16,1536]{1,0:T(8,128)(2,1)}, bf16[16,1536]{1,0:T(8,128)(2,1)}, u32[]{:S(2)}, u32[]{:S(2)}) collective-permute-start(bf16[16,1536]{1,0:T(8,128)(2,1)} %get-tuple-element.17), channel_id=1, source_target_pairs={{0,2},{1,3},{2,0},{3,1},{4,6},{5,7},{6,4},{7,5},{8,10},{9,11},{10,... | collective-permute-start | bytes 147464 | tf_op jit(solution)/shard_map/ppermute | solution.py:142
  16.1 0.0 copy-done.14
  16.1 0.3 collective-permute-start
  16.5 1.4 %collective-permute-done = s32[6,8]{1,0:T(8,128)S(1)} collective-permute-done((s32[6,8]{1,0:T(8,128)S(1)}, s32[6,8]{1,0:T(8,128)S(1)}, u32[]{:S(2)}, u32[]{:S(2)}) %collective-permute-start) | collective-permute-done | bytes 224 | tf_op jit(solution)/shard_map/ppermute | solution.py:142
  17.9 1.0 %collective-permute-start.3 = (bf16[16,1536]{1,0:T(8,128)(2,1)}, bf16[16,1536]{1,0:T(8,128)(2,1)}, u32[]{:S(2)}, u32[]{:S(2)}) collective-permute-start(bf16[16,1536]{1,0:T(8,128)(2,1)} %copy-done.13), channel_id=1, source_target_pairs={{0,3},{1,2},{2,1},{3,0},{4,7},{5,6},{6,5},{7,4},{8,11},{9,10},{10,... | collective-permute-start | bytes 147464 | tf_op jit(solution)/shard_map/ppermute | solution.py:142
  18.9 0.6 fusion
  19.5 0.6 sign_compare_fusion
  20.1 0.8 div.11
  20.9 0.6 rem.21
  21.5 0.8 ne.31
  22.2 0.0 collective-permute-done.1.got1
  22.2 0.0 collective-permute-done.2.got2
  22.2 0.0 collective-permute-done.3.got3
  22.3 0.0 collective-permute-done.4.inverse_got
  22.3 0.0 copy-start.11
  22.3 0.9 %copy-done.11 = f32[16,1536]{1,0:T(8,128)S(1)} copy-done((f32[16,1536]{1,0:T(8,128)S(1)}, f32[16,1536]{1,0:T(8,128)}, u32[]{:S(2)}) %copy-start.11) | copy-done | bytes 98328
  23.2 1.4 %initial.1 = (f32[16,1536]{1,0:T(8,128)S(1)}, bf16[16,1536]{1,0:T(8,128)(2,1)S(1)}) custom-call(f32[16,1536]{1,0:T(8,128)S(1)} %copy-done.11, bf16[16,1536]{1,0:T(8,128)(2,1)} %collective-permute-done.1.got1, bf16[16,1536]{1,0:T(8,128)(2,1)} %collective-permute-done.2.got2, bf16[16,1536]{1,0:T(8,128)(2,1)} %collective-permute-done.3.got3, ...), custom_call_target="tpu_custom_call" | custom-call | tf_op jit(solution)/shard_map/initial/pallas_call | solution.py:207
  24.6 1.9 %collective-permute-start.5 = (bf16[16,1536]{1,0:T(8,128)(2,1)S(1)}, bf16[16,1536]{1,0:T(8,128)(2,1)S(1)}, u32[]{:S(2)}, u32[]{:S(2)}) collective-permute-start(bf16[16,1536]{1,0:T(8,128)(2,1)S(1)} %get-tuple-element.21.previous), channel_id=1, source_target_pairs={{12,0},{13,1},{14,2},{15,3},{28,16},{29,17},{30,18},{31,19}} | collective-permute-start | bytes 147464 | tf_op jit(solution)/shard_map/ppermute | solution.py:150
  26.4 1.5 %collective-permute-start.6 = (bf16[16,1536]{1,0:T(8,128)(2,1)S(1)}, bf16[16,1536]{1,0:T(8,128)(2,1)S(1)}, u32[]{:S(2)}, u32[]{:S(2)}) collective-permute-start(bf16[16,1536]{1,0:T(8,128)(2,1)S(1)} %get-tuple-element.21.previous), channel_id=1, source_target_pairs={{12,2},{13,3},{14,0},{15,1},{28,18},{29,19},{30,16},{31,17}} | collective-permute-start | bytes 147464 | tf_op jit(solution)/shard_map/ppermute | solution.py:150
  27.9 0.6 fusion.2.place
  28.5 0.0 collective-permute-done.5.near
  28.5 0.6 collective-permute-done.6.far
  29.1 0.0 collective-permute-done.7.transfer_got
  29.1 2.6 %step.4.previous = bf16[16,1536]{1,0:T(8,128)(2,1)} custom-call(s32[1]{0:T(128)} %bitcast.3.active, s32[96]{0:T(128)S(1)} %fusion.2.place, bf16[16,1536]{1,0:T(8,128)(2,1)S(1)} %collective-permute-done.5.near, bf16[16,1536]{1,0:T(8,128)(2,1)S(1)} %collective-permute-done.6.far, bf16[16,1536]{1,0:T(8,128)(2,1)S(1)} %get-tuple-element.21.previous, ...), custom_call_target="tpu_custom_call" | custom-call | tf_op jit(solution)/shard_map/step/pallas_call | solution.py:220
  31.6 0.0 copy-done.3
  31.6 1.3 %collective-permute-start.8 = (bf16[16,1536]{1,0:T(8,128)(2,1)}, bf16[16,1536]{1,0:T(8,128)(2,1)}, u32[]{:S(2)}, u32[]{:S(2)}) collective-permute-start(bf16[16,1536]{1,0:T(8,128)(2,1)} %step.4.previous), channel_id=1, source_target_pairs={{0,4},{1,5},{2,6},{3,7},{16,20},{17,21},{18,22},{19,23}} | collective-permute-start | bytes 147464 | tf_op jit(solution)/shard_map/ppermute | solution.py:150
  32.9 1.3 %collective-permute-start.9 = (bf16[16,1536]{1,0:T(8,128)(2,1)}, bf16[16,1536]{1,0:T(8,128)(2,1)}, u32[]{:S(2)}, u32[]{:S(2)}) collective-permute-start(bf16[16,1536]{1,0:T(8,128)(2,1)} %step.4.previous), channel_id=1, source_target_pairs={{0,6},{1,7},{2,4},{3,5},{16,22},{17,23},{18,20},{19,21}} | collective-permute-start | bytes 147464 | tf_op jit(solution)/shard_map/ppermute | solution.py:150
  34.2 0.0 collective-permute-done.8.near
  34.2 0.0 collective-permute-done.9.far
  34.2 0.9 %copy-done.4 = f32[16,1536]{1,0:T(8,128)S(1)} copy-done((f32[16,1536]{1,0:T(8,128)S(1)}, f32[16,1536]{1,0:T(8,128)}, u32[]{:S(2)}) %copy-start.4) | copy-done | bytes 98328
  35.1 2.6 %step.5.previous = bf16[16,1536]{1,0:T(8,128)(2,1)} custom-call(s32[1]{0:T(128)} %bitcast.2.active, s32[96]{0:T(128)S(1)} %fusion.2.place, bf16[16,1536]{1,0:T(8,128)(2,1)} %collective-permute-done.8.near, bf16[16,1536]{1,0:T(8,128)(2,1)} %collective-permute-done.9.far, bf16[16,1536]{1,0:T(8,128)(2,1)} %step.4.previous, f32[16,1536]{1,0:T(8,128)S(1)} %copy-done.4, ...), custom_call_target="tpu_custom_call" | custom-call | tf_op jit(solution)/shard_map/step/pallas_call | solution.py:220
  37.7 1.3 %collective-permute-start.10 = (bf16[16,1536]{1,0:T(8,128)(2,1)}, bf16[16,1536]{1,0:T(8,128)(2,1)}, u32[]{:S(2)}, u32[]{:S(2)}) collective-permute-start(bf16[16,1536]{1,0:T(8,128)(2,1)} %step.5.previous), channel_id=1, source_target_pairs={{4,8},{5,9},{6,10},{7,11},{20,24},{21,25},{22,26},{23,27}} | collective-permute-start | bytes 147464 | tf_op jit(solution)/shard_map/ppermute | solution.py:150
  39.0 1.3 %collective-permute-start.11 = (bf16[16,1536]{1,0:T(8,128)(2,1)}, bf16[16,1536]{1,0:T(8,128)(2,1)}, u32[]{:S(2)}, u32[]{:S(2)}) collective-permute-start(bf16[16,1536]{1,0:T(8,128)(2,1)} %step.5.previous), channel_id=1, source_target_pairs={{4,10},{5,11},{6,8},{7,9},{20,26},{21,27},{22,24},{23,25}} | collective-permute-start | bytes 147464 | tf_op jit(solution)/shard_map/ppermute | solution.py:150
  40.3 0.0 collective-permute-done.10.near
  40.3 0.0 collective-permute-done.11.far
  40.3 0.9 %copy-done.5 = f32[16,1536]{1,0:T(8,128)S(1)} copy-done((f32[16,1536]{1,0:T(8,128)S(1)}, f32[16,1536]{1,0:T(8,128)}, u32[]{:S(2)}) %copy-start.5) | copy-done | bytes 98328
  41.2 2.6 %step.6.previous = bf16[16,1536]{1,0:T(8,128)(2,1)} custom-call(s32[1]{0:T(128)} %bitcast.1.active, s32[96]{0:T(128)S(1)} %fusion.2.place, bf16[16,1536]{1,0:T(8,128)(2,1)} %collective-permute-done.10.near, bf16[16,1536]{1,0:T(8,128)(2,1)} %collective-permute-done.11.far, bf16[16,1536]{1,0:T(8,128)(2,1)} %step.5.previous, f32[16,1536]{1,0:T(8,128)S(1)} %copy-done.5, ...), custom_call_target="tpu_custom_call" | custom-call | tf_op jit(solution)/shard_map/step/pallas_call | solution.py:220
  43.8 1.3 %collective-permute-start.12 = (bf16[16,1536]{1,0:T(8,128)(2,1)}, bf16[16,1536]{1,0:T(8,128)(2,1)}, u32[]{:S(2)}, u32[]{:S(2)}) collective-permute-start(bf16[16,1536]{1,0:T(8,128)(2,1)} %step.6.previous), channel_id=1, source_target_pairs={{8,12},{9,13},{10,14},{11,15},{24,28},{25,29},{26,30},{27,31}} | collective-permute-start | bytes 147464 | tf_op jit(solution)/shard_map/ppermute | solution.py:150
  45.1 1.3 %collective-permute-start.13 = (bf16[16,1536]{1,0:T(8,128)(2,1)}, bf16[16,1536]{1,0:T(8,128)(2,1)}, u32[]{:S(2)}, u32[]{:S(2)}) collective-permute-start(bf16[16,1536]{1,0:T(8,128)(2,1)} %step.6.previous), channel_id=1, source_target_pairs={{8,14},{9,15},{10,12},{11,13},{24,30},{25,31},{26,28},{27,29}} | collective-permute-start | bytes 147464 | tf_op jit(solution)/shard_map/ppermute | solution.py:150
  46.4 20.8 %collective-permute-done.12.near = bf16[16,1536]{1,0:T(8,128)(2,1)} collective-permute-done((bf16[16,1536]{1,0:T(8,128)(2,1)}, bf16[16,1536]{1,0:T(8,128)(2,1)}, u32[]{:S(2)}, u32[]{:S(2)}) %collective-permute-start.12) | collective-permute-done | bytes 49184 | tf_op jit(solution)/shard_map/ppermute | solution.py:150
  67.2 2.3 %collective-permute-done.13.far = bf16[16,1536]{1,0:T(8,128)(2,1)} collective-permute-done((bf16[16,1536]{1,0:T(8,128)(2,1)}, bf16[16,1536]{1,0:T(8,128)(2,1)}, u32[]{:S(2)}, u32[]{:S(2)}) %collective-permute-start.13) | collective-permute-done | bytes 49184 | tf_op jit(solution)/shard_map/ppermute | solution.py:150
  69.5 0.9 %copy-done.6 = f32[16,1536]{1,0:T(8,128)S(1)} copy-done((f32[16,1536]{1,0:T(8,128)S(1)}, f32[16,1536]{1,0:T(8,128)}, u32[]{:S(2)}) %copy-start.6) | copy-done | bytes 98328
  70.4 5.2 %step.7 = bf16[16,1536]{1,0:T(8,128)(2,1)S(1)} custom-call(s32[1]{0:T(128)} %bitcast.active, s32[96]{0:T(128)S(1)} %fusion.2.place, bf16[16,1536]{1,0:T(8,128)(2,1)} %collective-permute-done.12.near, bf16[16,1536]{1,0:T(8,128)(2,1)} %collective-permute-done.13.far, bf16[16,1536]{1,0:T(8,128)(2,1)} %step.6.previous, f32[16,1536]{1,0:T(8,128)S(1)} %copy-done.6, ...), custom_call_target="tpu_custom_call" | custom-call | tf_op jit(solution)/shard_map/step/pallas_call | solution.py:220
  75.6 0.6 copy-done.9
  76.2 3.6 %collective-permute-start.14 = (bf16[16,768]{1,0:T(8,128)(2,1)S(1)}, bf16[16,768]{1,0:T(8,128)(2,1)S(1)}, u32[]{:S(2)}, u32[]{:S(2)}) collective-permute-start(bf16[16,768]{1,0:T(8,128)(2,1)S(1)} %slice.8), channel_id=1, source_target_pairs={{0,1},{1,0},{2,3},{3,2},{4,5},{5,4},{6,7},{7,6},{8,9},{9,8},{10,11... | collective-permute-start | bytes 73736 | tf_op jit(solution)/shard_map/ppermute | solution.py:142
  79.8 0.8 %collective-permute-done.14 = bf16[16,768]{1,0:T(8,128)(2,1)S(1)} collective-permute-done((bf16[16,768]{1,0:T(8,128)(2,1)S(1)}, bf16[16,768]{1,0:T(8,128)(2,1)S(1)}, u32[]{:S(2)}, u32[]{:S(2)}) %collective-permute-start.14) | collective-permute-done | bytes 24608 | tf_op jit(solution)/shard_map/ppermute | solution.py:142
  80.7 0.7 broadcast_select_fusion.1
  81.4 0.6 maximum_bitcast_fusion
  (13 shorter events, 0.0 us)
Async XLA Ops:
  0.0 2.3 %copy-start = (bf16[1,768,3072]{2,1,0:T(8,128)(2,1)S(1)}, bf16[1,768,3072]{2,1,0:T(8,128)(2,1)}, u32[]{:S(2)}) copy-start(bf16[1,768,3072]{2,1,0:T(8,128)(2,1)} %param.8) | copy-start | bytes 14155780
  2.3 2.8 %copy-start.2 = (bf16[1,6,8,4,128,128]{5,4,3,2,1,0:T(8,128)(2,1)S(1)}, bf16[1,6,8,4,128,128]{5,4,3,2,1,0:T(8,128)(2,1)}, u32[]{:S(2)}) copy-start(bf16[1,6,8,4,128,128]{5,4,3,2,1,0:T(8,128)(2,1)} %param.10) | copy-start | bytes 18874372
  5.1 1.1 %copy-start.7 = (bf16[1,6,4,128,128]{4,3,2,1,0:T(8,128)(2,1)S(1)}, bf16[1,6,4,128,128]{4,3,2,1,0:T(8,128)(2,1)}, u32[]{:S(2)}) copy-start(bf16[1,6,4,128,128]{4,3,2,1,0:T(8,128)(2,1)} %param.11) | copy-start | bytes 2359300
  6.3 0.8 copy-start.8
  7.1 0.8 copy-start.12
  7.9 4.8 %copy-start.1 = (bf16[1,768,3072]{2,1,0:T(8,128)(2,1)S(1)}, bf16[1,768,3072]{2,1,0:T(8,128)(2,1)}, u32[]{:S(2)}) copy-start(bf16[1,768,3072]{2,1,0:T(8,128)(2,1)} %param.8) | copy-start | bytes 14155780
  11.4 2.9 %copy-start.10 = (f32[16,1536]{1,0:T(8,128)}, f32[16,1536]{1,0:T(8,128)S(1)}, u32[]{:S(2)}) copy-start(f32[16,1536]{1,0:T(8,128)S(1)} %get-tuple-element.15.own) | copy-start | bytes 294916
  11.4 4.8 %copy-start.14 = (s32[1,6,8]{2,0,1:T(1,128)S(1)}, s32[1,6,8]{2,0,1:T(1,128)}, u32[]{:S(2)}) copy-start(s32[1,6,8]{2,0,1:T(1,128)} %param.9) | copy-start | bytes 580
  11.4 17.7 %collective-permute-start.7 = (bf16[6,8,2,128,128]{4,3,2,1,0:T(8,128)(2,1)}, bf16[6,8,2,128,128]{4,3,2,1,0:T(8,128)(2,1)}, u32[]{:S(2)}, u32[]{:S(2)}) collective-permute-start(bf16[6,8,2,128,128]{4,3,2,1,0:T(8,128)(2,1)} %get-tuple-element.24), channel_id=1, source_target_pairs={{0,1},{1,0},{2,3},{3,2},{4,5},{5,4},{6,7},{7,6},{8,9},{9,8},{10,11... | collective-permute-start | bytes 9437192 | tf_op jit(solution)/shard_map/ppermute | solution.py:142
  12.1 10.1 %collective-permute-start.4 = (bf16[6,2,128,128]{3,2,1,0:T(8,128)(2,1)}, bf16[6,2,128,128]{3,2,1,0:T(8,128)(2,1)}, u32[]{:S(2)}, u32[]{:S(2)}) collective-permute-start(bf16[6,2,128,128]{3,2,1,0:T(8,128)(2,1)} %get-tuple-element.20), channel_id=1, source_target_pairs={{0,1},{1,0},{2,3},{3,2},{4,5},{5,4},{6,7},{7,6},{8,9},{9,8},{10,11... | collective-permute-start | bytes 1179656 | tf_op jit(solution)/shard_map/ppermute | solution.py:142
  12.2 10.0 %collective-permute-start.1 = (bf16[16,1536]{1,0:T(8,128)(2,1)}, bf16[16,1536]{1,0:T(8,128)(2,1)}, u32[]{:S(2)}, u32[]{:S(2)}) collective-permute-start(bf16[16,1536]{1,0:T(8,128)(2,1)} %get-tuple-element.16), channel_id=1, source_target_pairs={{0,1},{1,0},{2,3},{3,2},{4,5},{5,4},{6,7},{7,6},{8,9},{9,8},{10,11... | collective-permute-start | bytes 147464 | tf_op jit(solution)/shard_map/ppermute | solution.py:142
  14.3 0.6 copy-start.13
  14.9 7.3 %collective-permute-start.2 = (bf16[16,1536]{1,0:T(8,128)(2,1)}, bf16[16,1536]{1,0:T(8,128)(2,1)}, u32[]{:S(2)}, u32[]{:S(2)}) collective-permute-start(bf16[16,1536]{1,0:T(8,128)(2,1)} %get-tuple-element.17), channel_id=1, source_target_pairs={{0,2},{1,3},{2,0},{3,1},{4,6},{5,7},{6,4},{7,5},{8,10},{9,11},{10,... | collective-permute-start | bytes 147464 | tf_op jit(solution)/shard_map/ppermute | solution.py:142
  16.1 1.7 %collective-permute-start = (s32[6,8]{1,0:T(8,128)S(1)}, s32[6,8]{1,0:T(8,128)S(1)}, u32[]{:S(2)}, u32[]{:S(2)}) collective-permute-start(s32[6,8]{1,0:T(8,128)S(1)} %bitcast.22), channel_id=1, source_target_pairs={{0,1},{1,0},{2,3},{3,2},{4,5},{5,4},{6,7},{7,6},{8,9},{9,8},{10,11... | collective-permute-start | bytes 584 | tf_op jit(solution)/shard_map/ppermute | solution.py:142
  17.9 4.4 %collective-permute-start.3 = (bf16[16,1536]{1,0:T(8,128)(2,1)}, bf16[16,1536]{1,0:T(8,128)(2,1)}, u32[]{:S(2)}, u32[]{:S(2)}) collective-permute-start(bf16[16,1536]{1,0:T(8,128)(2,1)} %copy-done.13), channel_id=1, source_target_pairs={{0,3},{1,2},{2,1},{3,0},{4,7},{5,6},{6,5},{7,4},{8,11},{9,10},{10,... | collective-permute-start | bytes 147464 | tf_op jit(solution)/shard_map/ppermute | solution.py:142
  22.3 0.9 %copy-start.11 = (f32[16,1536]{1,0:T(8,128)S(1)}, f32[16,1536]{1,0:T(8,128)}, u32[]{:S(2)}) copy-start(f32[16,1536]{1,0:T(8,128)} %copy-done.10) | copy-start | bytes 294916
  24.5 7.1 %copy-start.3 = (f32[16,1536]{1,0:T(8,128)}, f32[16,1536]{1,0:T(8,128)S(1)}, u32[]{:S(2)}) copy-start(f32[16,1536]{1,0:T(8,128)S(1)} %get-tuple-element.22.load) | copy-start | bytes 294916
  24.6 3.9 %collective-permute-start.5 = (bf16[16,1536]{1,0:T(8,128)(2,1)S(1)}, bf16[16,1536]{1,0:T(8,128)(2,1)S(1)}, u32[]{:S(2)}, u32[]{:S(2)}) collective-permute-start(bf16[16,1536]{1,0:T(8,128)(2,1)S(1)} %get-tuple-element.21.previous), channel_id=1, source_target_pairs={{12,0},{13,1},{14,2},{15,3},{28,16},{29,17},{30,18},{31,19}} | collective-permute-start | bytes 147464 | tf_op jit(solution)/shard_map/ppermute | solution.py:150
  26.4 2.6 %collective-permute-start.6 = (bf16[16,1536]{1,0:T(8,128)(2,1)S(1)}, bf16[16,1536]{1,0:T(8,128)(2,1)S(1)}, u32[]{:S(2)}, u32[]{:S(2)}) collective-permute-start(bf16[16,1536]{1,0:T(8,128)(2,1)S(1)} %get-tuple-element.21.previous), channel_id=1, source_target_pairs={{12,2},{13,3},{14,0},{15,1},{28,18},{29,19},{30,16},{31,17}} | collective-permute-start | bytes 147464 | tf_op jit(solution)/shard_map/ppermute | solution.py:150
  31.6 2.5 %collective-permute-start.8 = (bf16[16,1536]{1,0:T(8,128)(2,1)}, bf16[16,1536]{1,0:T(8,128)(2,1)}, u32[]{:S(2)}, u32[]{:S(2)}) collective-permute-start(bf16[16,1536]{1,0:T(8,128)(2,1)} %step.4.previous), channel_id=1, source_target_pairs={{0,4},{1,5},{2,6},{3,7},{16,20},{17,21},{18,22},{19,23}} | collective-permute-start | bytes 147464 | tf_op jit(solution)/shard_map/ppermute | solution.py:150
  32.9 1.3 %collective-permute-start.9 = (bf16[16,1536]{1,0:T(8,128)(2,1)}, bf16[16,1536]{1,0:T(8,128)(2,1)}, u32[]{:S(2)}, u32[]{:S(2)}) collective-permute-start(bf16[16,1536]{1,0:T(8,128)(2,1)} %step.4.previous), channel_id=1, source_target_pairs={{0,6},{1,7},{2,4},{3,5},{16,22},{17,23},{18,20},{19,21}} | collective-permute-start | bytes 147464 | tf_op jit(solution)/shard_map/ppermute | solution.py:150
  34.2 0.9 %copy-start.4 = (f32[16,1536]{1,0:T(8,128)S(1)}, f32[16,1536]{1,0:T(8,128)}, u32[]{:S(2)}) copy-start(f32[16,1536]{1,0:T(8,128)} %copy-done.3) | copy-start | bytes 294916
  37.7 2.5 %collective-permute-start.10 = (bf16[16,1536]{1,0:T(8,128)(2,1)}, bf16[16,1536]{1,0:T(8,128)(2,1)}, u32[]{:S(2)}, u32[]{:S(2)}) collective-permute-start(bf16[16,1536]{1,0:T(8,128)(2,1)} %step.5.previous), channel_id=1, source_target_pairs={{4,8},{5,9},{6,10},{7,11},{20,24},{21,25},{22,26},{23,27}} | collective-permute-start | bytes 147464 | tf_op jit(solution)/shard_map/ppermute | solution.py:150
  39.0 1.3 %collective-permute-start.11 = (bf16[16,1536]{1,0:T(8,128)(2,1)}, bf16[16,1536]{1,0:T(8,128)(2,1)}, u32[]{:S(2)}, u32[]{:S(2)}) collective-permute-start(bf16[16,1536]{1,0:T(8,128)(2,1)} %step.5.previous), channel_id=1, source_target_pairs={{4,10},{5,11},{6,8},{7,9},{20,26},{21,27},{22,24},{23,25}} | collective-permute-start | bytes 147464 | tf_op jit(solution)/shard_map/ppermute | solution.py:150
  40.3 0.9 %copy-start.5 = (f32[16,1536]{1,0:T(8,128)S(1)}, f32[16,1536]{1,0:T(8,128)}, u32[]{:S(2)}) copy-start(f32[16,1536]{1,0:T(8,128)} %copy-done.3) | copy-start | bytes 294916
  43.8 23.4 %collective-permute-start.12 = (bf16[16,1536]{1,0:T(8,128)(2,1)}, bf16[16,1536]{1,0:T(8,128)(2,1)}, u32[]{:S(2)}, u32[]{:S(2)}) collective-permute-start(bf16[16,1536]{1,0:T(8,128)(2,1)} %step.6.previous), channel_id=1, source_target_pairs={{8,12},{9,13},{10,14},{11,15},{24,28},{25,29},{26,30},{27,31}} | collective-permute-start | bytes 147464 | tf_op jit(solution)/shard_map/ppermute | solution.py:150
  45.1 24.4 %collective-permute-start.13 = (bf16[16,1536]{1,0:T(8,128)(2,1)}, bf16[16,1536]{1,0:T(8,128)(2,1)}, u32[]{:S(2)}, u32[]{:S(2)}) collective-permute-start(bf16[16,1536]{1,0:T(8,128)(2,1)} %step.6.previous), channel_id=1, source_target_pairs={{8,14},{9,15},{10,12},{11,13},{24,30},{25,31},{26,28},{27,29}} | collective-permute-start | bytes 147464 | tf_op jit(solution)/shard_map/ppermute | solution.py:150
  69.5 0.9 %copy-start.6 = (f32[16,1536]{1,0:T(8,128)S(1)}, f32[16,1536]{1,0:T(8,128)}, u32[]{:S(2)}) copy-start(f32[16,1536]{1,0:T(8,128)} %copy-done.3) | copy-start | bytes 294916
  75.6 0.6 copy-start.9
  76.2 4.5 %collective-permute-start.14 = (bf16[16,768]{1,0:T(8,128)(2,1)S(1)}, bf16[16,768]{1,0:T(8,128)(2,1)S(1)}, u32[]{:S(2)}, u32[]{:S(2)}) collective-permute-start(bf16[16,768]{1,0:T(8,128)(2,1)S(1)} %slice.8), channel_id=1, source_target_pairs={{0,1},{1,0},{2,3},{3,2},{4,5},{5,4},{6,7},{7,6},{8,9},{9,8},{10,11... | collective-permute-start | bytes 73736 | tf_op jit(solution)/shard_map/ppermute | solution.py:142

commit v2 on v1

v2 whole, which is shorter than its diff:
```python
import functools

import jax
import jax.numpy as jnp
from jax import lax
from jax.experimental import pallas as pl
from jax.experimental.pallas import tpu as pltpu
from jax.sharding import PartitionSpec as P

VMEM = pl.BlockSpec(memory_space=pltpu.VMEM)
SMEM = pl.BlockSpec(memory_space=pltpu.SMEM)
ANY = pl.BlockSpec(memory_space=pl.ANY)
MIB = 1 << 20


def nt_dot(left, right):
    return lax.dot_general(left, right, (((1,), (1,)), ((), ())), preferred_element_type=jnp.float32)


def diagonal(product, freqs):
    rows, cols = product.shape[0] // freqs, product.shape[1] // freqs
    return jnp.concatenate(
        [product[f * rows:(f + 1) * rows, f * cols:(f + 1) * cols] for f in range(freqs)], axis=0
    )


def by_parity(odd, rows):
    half = rows.shape[0] // 2
    return jnp.where(odd, rows[half:], rows[:half]), jnp.where(odd, rows[:half], rows[half:])


def columns_of(coupling, owner, width):
    return coupling.at[:, pl.ds(pl.multiple_of(owner * width, width), width)]


def far_kernel(sec_ref, interior, coupling, piece2, piece3, held, sems):
    sec = sec_ref[0]
    width = held.shape[-1]
    copies = [
        pltpu.make_async_copy(columns_of(coupling, sec ^ d, width), held.at[n], sems.at[n])
        for n, d in enumerate((2, 3))
    ]
    for copy in copies:
        copy.start()
    pieces = {2: piece2, 3: piece3}
    for n, d in enumerate((2, 3)):
        copies[n].wait()
        part = -jnp.dot(interior[...], held[n], preferred_element_type=jnp.float32)
        first, second = by_parity(((sec ^ d) & 1) == 1, part)
        pieces[d][:, :width] = first.astype(jnp.bfloat16)
        pieces[d ^ 1][:, width:] = second.astype(jnp.bfloat16)


def near_kernel(
    sec_ref, interior, edge, coupling, transfer, inverse, after,
    piece1, own, transfer_out, inverse_out, held, sems,
):
    sec = sec_ref[0]
    width = held.shape[-1]
    odd = (sec & 1) == 1
    half = transfer.shape[2] // 2
    other = half - (sec & 1) * half
    copies = [
        pltpu.make_async_copy(columns_of(coupling, sec ^ d, width), held.at[n], sems.at[n])
        for n, d in enumerate((1, 0))
    ]
    moves = [
        pltpu.make_async_copy(inverse.at[:, pl.ds(other, half)], inverse_out, sems.at[2]),
        pltpu.make_async_copy(transfer.at[:, :, pl.ds(other, half)], transfer_out, sems.at[3]),
    ]
    for copy in copies + moves:
        copy.start()
    copies[0].wait()
    part = -jnp.dot(interior[...], held[0], preferred_element_type=jnp.float32)
    first, second = by_parity(jnp.logical_not(odd), part)
    piece1[:, :width] = first.astype(jnp.bfloat16)
    own[:, width:] = second
    copies[1].wait()
    part = edge[...].astype(jnp.float32) - jnp.dot(
        interior[...], held[1], preferred_element_type=jnp.float32
    )
    first, second = by_parity(odd, part)
    own[:, :width] = first
    piece1[:, width:] = second.astype(jnp.bfloat16)
    for move in moves:
        move.wait()


def inverse_kernel(sec_ref, inverse, got, held, sems):
    rows, half = got.shape[:2]
    mine = (sec_ref[0] & 1) * half
    copies = [
        pltpu.make_async_copy(inverse.at[:, pl.ds(mine, half)], held.at[pl.ds(0, rows)], sems.at[0]),
        pltpu.make_async_copy(got, held.at[pl.ds(rows, rows)], sems.at[1]),
    ]
    for copy in copies:
        copy.start()
    for copy in copies:
        copy.wait()


def transfer_kernel(sec_ref, transfer, got, after, held, sems):
    rows, _, half = got.shape[:3]
    mine = (sec_ref[0] & 1) * half
    copies = [
        pltpu.make_async_copy(
            transfer.at[:, :, pl.ds(mine, half)], held.at[pl.ds(0, rows)], sems.at[0]
        ),
        pltpu.make_async_copy(got, held.at[pl.ds(rows, rows)], sems.at[1]),
    ]
    for copy in copies:
        copy.start()
    for copy in copies:
        copy.wait()


def initial_kernel(own, got1, got2, got3, inverse, load, initial):
    rows, freqs, block, _ = inverse.shape
    for r in range(rows):
        cols = slice(r * block, (r + 1) * block)
        total = own[:, cols] + got1[:, cols].astype(jnp.float32)
        total += got2[:, cols].astype(jnp.float32) + got3[:, cols].astype(jnp.float32)
        load[:, cols] = total
        solved = nt_dot(total.astype(jnp.bfloat16), inverse[r].reshape(freqs * block, block))
        initial[:, cols] = diagonal(solved, freqs).astype(jnp.bfloat16)


def step_kernel(step, bay_ref, sec_ref, cols_own, cols_got, near, far, previous, load, transfer, inverse, out, state):
    rows, nonzero, freqs, block, _ = transfer.shape
    part = rows // 2
    sec = sec_ref[0]

    @pl.when(bay_ref[0] == step)
    def _():
        for n in range(2):
            source = (near, far)[n]
            for r in range(rows):
                home = (sec ^ (2 * n + r // part)) * part + r % part
                state[home] = source[:, r * block:(r + 1) * block]
        for r in range(rows):
            cols = slice(r * block, (r + 1) * block)
            ids = cols_own if r < part else cols_got
            picked = jnp.concatenate([state[ids[r % part, k]] for k in range(nonzero)], axis=1)
            matrix = jnp.concatenate(
                [transfer[r, k].reshape(freqs * block, block) for k in range(nonzero)], axis=1
            )
            summed = (load[:, cols] + diagonal(nt_dot(picked, matrix), freqs)).astype(jnp.bfloat16)
            solved = nt_dot(summed, inverse[r].reshape(freqs * block, block))
            out[:, cols] = diagonal(solved, freqs).astype(jnp.bfloat16)

    @pl.when(bay_ref[0] != step)
    def _():
        out[...] = previous[...]


def finish_kernel(sec_ref, state, got, out):
    lines, width = got.shape
    odd = (sec_ref[0] & 1) == 1

    @pl.when(odd)
    def _():
        out[:lines] = got[...]
        out[lines:] = state[:, :width]

    @pl.when(jnp.logical_not(odd))
    def _():
        out[:lines] = state[:, :width]
        out[lines:] = got[...]


def moved(value, distance, offset):
    bays, secs = lax.axis_size("bay"), lax.axis_size("sec")
    route = [
        (b * secs + s, (b + distance) % bays * secs + (s ^ offset))
        for b in range(bays)
        for s in range(secs)
    ]
    return lax.ppermute(value, ("bay", "sec"), route)


def hop(value, source, offset):
    bays, secs = lax.axis_size("bay"), lax.axis_size("sec")
    route = [
        (source * secs + s, (source + 1) % bays * secs + (s ^ offset)) for s in range(secs)
    ]
    return lax.ppermute(value, ("bay", "sec"), route)


def per_device(edge_load, interior_load, coupling, block_cols, transfer, local_inverse):
    _, freqs, cases, width = edge_load.shape
    _, rows, nonzero, _, block, _ = transfer.shape
    inner = interior_load.shape[-1]
    half = freqs // 2
    lines = half * cases
    sec = lax.axis_index("sec").astype(jnp.int32)
    position = lax.axis_index("bay")
    bays = lax.axis_size("bay")
    edge = edge_load.reshape(freqs * cases, width)
    interior = interior_load.reshape(freqs * cases, inner)
    sec_word = sec.reshape(1)
    alone = pltpu.CompilerParams(vmem_limit_bytes=60 * MIB)
    beside = pltpu.CompilerParams(vmem_limit_bytes=48 * MIB)
    small = pltpu.CompilerParams(vmem_limit_bytes=12 * MIB)
    bf16, f32 = jnp.bfloat16, jnp.float32
    wide = (lines, 2 * width)
    matrices = (rows, nonzero, half, block, block)
    inverses = (rows, half, block, block)
    held_block = pltpu.VMEM((2, inner, width), bf16)

    piece2, piece3 = pl.pallas_call(
        far_kernel,
        out_shape=[jax.ShapeDtypeStruct(wide, bf16)] * 2,
        in_specs=[SMEM, VMEM, ANY],
        out_specs=[VMEM] * 2,
        scratch_shapes=[held_block, pltpu.SemaphoreType.DMA((2,))],
        compiler_params=alone,
        name="far",
    )(sec_word, interior, coupling[0])
    got2, got3 = moved(piece2, 0, 2), moved(piece3, 0, 3)
    cols_own = block_cols[0]
    cols_got = moved(cols_own, 0, 1)

    piece1, own, transfer_out, inverse_out = pl.pallas_call(
        near_kernel,
        out_shape=[
            jax.ShapeDtypeStruct(wide, bf16),
            jax.ShapeDtypeStruct(wide, f32),
            jax.ShapeDtypeStruct(matrices, bf16),
            jax.ShapeDtypeStruct(inverses, bf16),
        ],
        in_specs=[SMEM, VMEM, VMEM, ANY, ANY, ANY, ANY],
        out_specs=[VMEM, VMEM, VMEM, VMEM],
        scratch_shapes=[held_block, pltpu.SemaphoreType.DMA((4,))],
        compiler_params=alone,
        name="near",
    )(sec_word, interior, edge, coupling[0], transfer[0], local_inverse[0], piece2)
    got1 = moved(piece1, 0, 1)
    inverse_got = moved(inverse_out, 0, 1)
    transfer_got = moved(transfer_out, 0, 1)

    inverse = pl.pallas_call(
        inverse_kernel,
        out_shape=pltpu.VMEM((2 * rows, half, block, block), bf16),
        in_specs=[SMEM, ANY, ANY],
        out_specs=VMEM,
        scratch_shapes=[pltpu.SemaphoreType.DMA((2,))],
        compiler_params=alone,
        name="inverse",
    )(sec_word, local_inverse[0], inverse_got)

    load, state = pl.pallas_call(
        initial_kernel,
        out_shape=[jax.ShapeDtypeStruct(wide, f32), jax.ShapeDtypeStruct(wide, bf16)],
        in_specs=[VMEM] * 5,
        out_specs=[VMEM] * 2,
        compiler_params=small,
        name="initial",
    )(own, got1, got2, got3, inverse)

    matrix = pl.pallas_call(
        transfer_kernel,
        out_shape=pltpu.VMEM((2 * rows, nonzero, half, block, block), bf16),
        in_specs=[SMEM, ANY, ANY, ANY],
        out_specs=VMEM,
        scratch_shapes=[pltpu.SemaphoreType.DMA((2,))],
        compiler_params=beside,
        name="transfer",
    )(sec_word, transfer[0], transfer_got, state)

    bay_word = position.astype(jnp.int32).reshape(1)
    for step in range(bays):
        source = (step - 1) % bays
        near, far = hop(state, source, 0), hop(state, source, 2)
        state = pl.pallas_call(
            functools.partial(step_kernel, step),
            out_shape=jax.ShapeDtypeStruct(wide, bf16),
            in_specs=[SMEM] * 4 + [VMEM] * 6,
            out_specs=VMEM,
            scratch_shapes=[pltpu.VMEM((4 * rows, lines, block), bf16)],
            compiler_params=small,
            name="step",
        )(bay_word, sec_word, cols_own, cols_got, near, far, state, load, matrix, inverse)

    got = moved(state[:, width:], 0, 1)
    result = pl.pallas_call(
        finish_kernel,
        out_shape=jax.ShapeDtypeStruct((2 * lines, width), bf16),
        in_specs=[SMEM, VMEM, VMEM],
        out_specs=VMEM,
        compiler_params=small,
        name="finish",
    )(sec_word, state, got)
    return result.reshape(1, freqs, cases, width)


def solution(mesh):
    in_specs = (
        P(("groups", "bay"), None, None, "sec"),
        P(("groups", "bay"), None, None, "sec"),
        P(("groups", "bay"), "sec", None),
        P(("groups", "bay"), "sec", None),
        P(("groups", "bay"), "sec", None, None, None, None),
        P(("groups", "bay"), "sec", None, None, None),
    )
    out_specs = P(("groups", "bay"), None, None, "sec")
    return jax.shard_map(
        per_device, mesh=mesh, in_specs=in_specs, out_specs=out_specs, check_vma=False
    )
```

time: 82.8 us -> 64 us (0.77)
  local copies, waits for them, and re-layouts: 14.8 us -> 2.47 us
  other arithmetic: 3.17 us -> 0 us
  starting transfers between devices: 18.4 us -> 16.3 us
  waiting for transfers between devices: 25.9 us -> 24.9 us
    unnamed x31 -> x15, local copies, waits for them, and re-layouts: 12.7 us -> 2.47 us
    ppermute x8, waiting for transfers between devices: 23.7 us -> 20.3 us  [hop(): return lax.ppermute(value, ('bay', 'sec'), route)]
    pallas_call x4 -> x7, Pallas kernels: 13.1 us -> 10.5 us  [the longest x4 5.86 us: per_device(): pl.pallas_call(functools.partial(step_kernel, step), out_shape=jax.ShapeD...]
    ppermute x7, waiting for transfers between devices: 2.23 us -> 4.64 us  [moved(): return lax.ppermute(value, ('bay', 'sec'), route)]
    pallas_call x1, Pallas kernels: 3.5 us -> 5.43 us  [per_device(): pl.pallas_call(near_kernel, out_shape=[jax.ShapeDtypeStruct(wide, bf16),...]
    pallas_call x1, Pallas kernels: 1.64 us -> 3.43 us  [per_device(): pl.pallas_call(far_kernel, out_shape=[jax.ShapeDtypeStruct(wide, bf16)] *...]
    ppermute x8, starting transfers between devices: 11 us -> 9.31 us  [hop(): return lax.ppermute(value, ('bay', 'sec'), route)]
    pallas_call x1, Pallas kernels: 1.39 us -> 0.3 us  [per_device(): pl.pallas_call(initial_kernel, out_shape=[jax.ShapeDtypeStruct(wide, f32)...]
  transfers between devices with their start and end apart: 15 -> 15, of which waited for: 5 -> 4; matrix products, arithmetic and copies ran while one was open for 5% -> 0% of each run, Pallas kernels for 4% -> 7%
where the time goes in v2:
time: 64 us; the launch traced here: 63.6 us
  waiting for transfers between devices  24.9 us (39%)
  Pallas kernels  19.6 us (31%)
  starting transfers between devices  16.3 us (25%)
  local copies, waits for them, and re-layouts  2.47 us (4%)
    ppermute x8, waiting for transfers between devices, hop(): return lax.ppermute(value, ('bay', 'sec'), route)  20.3 us
    ppermute x8, starting transfers between devices, hop(): return lax.ppermute(value, ('bay', 'sec'), route)  9.31 us
    ppermute x7, starting transfers between devices, moved(): return lax.ppermute(value, ('bay', 'sec'), route)  6.96 us
    pallas_call x4, Pallas kernels, per_device(): pl.pallas_call(functools.partial(step_kernel, step), out_shape=jax.ShapeD...  5.86 us
    pallas_call x1, Pallas kernels, per_device(): pl.pallas_call(near_kernel, out_shape=[jax.ShapeDtypeStruct(wide, bf16),...  5.43 us
    ppermute x7, waiting for transfers between devices, moved(): return lax.ppermute(value, ('bay', 'sec'), route)  4.64 us
    pallas_call x1, Pallas kernels, per_device(): pl.pallas_call(far_kernel, out_shape=[jax.ShapeDtypeStruct(wide, bf16)] *...  3.43 us
    pallas_call x1, Pallas kernels, per_device(): pl.pallas_call(transfer_kernel, out_shape=pltpu.VMEM((2 * rows, nonzero,...  2.86 us
  transfers between devices with their start and end apart: 15, of which 4 were waited for; matrix products, arithmetic and copies ran while one was open for 0% of the time, Pallas kernels for 7%

profile of v2, /device:TPU:29, one launch (start us, length us, event | category | flops | bytes accessed | tf_op | source)
XLA Modules:
  0.0 63.6 jit_solution(9523316615684293152)
XLA Ops:
  0.0 3.4 %far.1 = (bf16[16,1536]{1,0:T(8,128)(2,1)}, bf16[16,1536]{1,0:T(8,128)(2,1)}) custom-call(s32[1]{0:T(128)} %bitcast.sec_ref, bf16[32,768]{1,0:T(8,128)(2,1)} %bitcast.22, bf16[768,3072]{1,0:T(8,128)(2,1)} %bitcast.18), custom_call_target="tpu_custom_call" | custom-call | tf_op jit(solution)/shard_map/far/pallas_call | solution.py:210
  3.4 0.0 copy-start.4
  3.4 0.0 copy-start.6
  3.5 0.0 copy-start.5
  3.5 5.4 %near.1 = (bf16[16,1536]{1,0:T(8,128)(2,1)}, f32[16,1536]{1,0:T(8,128)}, bf16[6,8,2,128,128]{4,3,2,1,0:T(8,128)(2,1)}, bf16[6,2,128,128]{3,2,1,0:T(8,128)(2,1)}) custom-call(s32[1]{0:T(128)} %bitcast.sec_ref, bf16[32,768]{1,0:T(8,128)(2,1)} %bitcast.23, bf16[32,768]{1,0:T(8,128)(2,1)} %bitcast.24, bf16[768,3072]{1,0:T(8,128)(2,1)} %bitcast.19, ...), custom_call_target="tpu_custom_call" | custom-call | tf_op jit(solution)/shard_map/near/pallas_call | solution.py:223
  8.9 0.7 %collective-permute-start.7 = (bf16[6,8,2,128,128]{4,3,2,1,0:T(8,128)(2,1)}, bf16[6,8,2,128,128]{4,3,2,1,0:T(8,128)(2,1)}, u32[]{:S(2)}, u32[]{:S(2)}) collective-permute-start(bf16[6,8,2,128,128]{4,3,2,1,0:T(8,128)(2,1)} %get-tuple-element.20), channel_id=1, source_target_pairs={{0,1},{1,0},{2,3},{3,2},{4,5},{5,4},{6,7},{7,6},{8,9},{9,8},{10,11... | collective-permute-start | bytes 9437192 | tf_op jit(solution)/shard_map/ppermute | solution.py:178
  9.7 0.1 collective-permute-start.4
  9.7 0.0 copy-done.4
  9.7 1.2 %collective-permute-start.2 = (bf16[16,1536]{1,0:T(8,128)(2,1)S(1)}, bf16[16,1536]{1,0:T(8,128)(2,1)S(1)}, u32[]{:S(2)}, u32[]{:S(2)}) collective-permute-start(bf16[16,1536]{1,0:T(8,128)(2,1)S(1)} %copy-done.4), channel_id=1, source_target_pairs={{0,2},{1,3},{2,0},{3,1},{4,6},{5,7},{6,4},{7,5},{8,10},{9,11},{10,... | collective-permute-start | bytes 147464 | tf_op jit(solution)/shard_map/ppermute | solution.py:178
  10.9 0.7 %collective-permute-start.1 = (bf16[16,1536]{1,0:T(8,128)(2,1)}, bf16[16,1536]{1,0:T(8,128)(2,1)S(1)}, u32[]{:S(2)}, u32[]{:S(2)}) collective-permute-start(bf16[16,1536]{1,0:T(8,128)(2,1)} %get-tuple-element.15), channel_id=1, source_target_pairs={{0,1},{1,0},{2,3},{3,2},{4,5},{5,4},{6,7},{7,6},{8,9},{9,8},{10,11... | collective-permute-start | bytes 147464 | tf_op jit(solution)/shard_map/ppermute | solution.py:178
  11.7 0.0 copy-done.6
  11.7 0.1 collective-permute-start.3
  11.8 3.8 %collective-permute-done.4.got = bf16[6,2,128,128]{3,2,1,0:T(8,128)(2,1)S(1)} collective-permute-done((bf16[6,2,128,128]{3,2,1,0:T(8,128)(2,1)}, bf16[6,2,128,128]{3,2,1,0:T(8,128)(2,1)S(1)}, u32[]{:S(2)}, u32[]{:S(2)}) %collective-permute-start.4) | collective-permute-done | bytes 393248 | tf_op jit(solution)/shard_map/ppermute | solution.py:178
  15.6 0.0 copy-start.3
  15.6 0.8 %copy-done.3 = bf16[6,2,128,128]{3,2,1,0:T(8,128)(2,1)} copy-done((bf16[6,2,128,128]{3,2,1,0:T(8,128)(2,1)}, bf16[6,2,128,128]{3,2,1,0:T(8,128)(2,1)S(1)}, u32[]{:S(2)}) %copy-start.3) | copy-done | bytes 393240
  16.3 1.1 %inverse.1 = bf16[12,2,128,128]{3,2,1,0:T(8,128)(2,1)S(1)} custom-call(s32[1]{0:T(128)} %bitcast.sec_ref, bf16[6,4,128,128]{3,2,1,0:T(8,128)(2,1)} %bitcast.21, bf16[6,2,128,128]{3,2,1,0:T(8,128)(2,1)} %copy-done.3), custom_call_target="tpu_custom_call" | custom-call | tf_op jit(solution)/shard_map/inverse/pallas_call | solution.py:241
  17.5 0.0 collective-permute-done.1.got1
  17.5 0.0 collective-permute-done.2.got2
  17.5 0.0 collective-permute-done.3.got3
  17.5 0.0 copy-start.2
  17.5 0.9 %copy-done.2 = f32[16,1536]{1,0:T(8,128)S(1)} copy-done((f32[16,1536]{1,0:T(8,128)S(1)}, f32[16,1536]{1,0:T(8,128)}, u32[]{:S(2)}) %copy-start.2) | copy-done | bytes 98328
  18.4 0.3 initial.1
  18.7 0.0 copy-start
  18.7 1.9 %collective-permute-start.5 = (bf16[16,1536]{1,0:T(8,128)(2,1)S(1)}, bf16[16,1536]{1,0:T(8,128)(2,1)S(1)}, u32[]{:S(2)}, u32[]{:S(2)}) collective-permute-start(bf16[16,1536]{1,0:T(8,128)(2,1)S(1)} %get-tuple-element.18.after.previous), channel_id=1, source_target_pairs={{12,0},{13,1},{14,2},{15,3},{28,16},{29,17},{30,18},{31,19}} | collective-permute-start | bytes 147464 | tf_op jit(solution)/shard_map/ppermute | solution.py:186
  20.6 2.2 %collective-permute-start.6 = (bf16[16,1536]{1,0:T(8,128)(2,1)S(1)}, bf16[16,1536]{1,0:T(8,128)(2,1)S(1)}, u32[]{:S(2)}, u32[]{:S(2)}) collective-permute-start(bf16[16,1536]{1,0:T(8,128)(2,1)S(1)} %get-tuple-element.18.after.previous), channel_id=1, source_target_pairs={{12,2},{13,3},{14,0},{15,1},{28,18},{29,19},{30,16},{31,17}} | collective-permute-start | bytes 147464 | tf_op jit(solution)/shard_map/ppermute | solution.py:186
  22.8 0.0 copy-done.5
  22.8 0.5 collective-permute-start
  23.3 0.0 collective-permute-done.7.got
  23.3 0.0 copy-done
  23.3 2.9 %transfer.1 = bf16[12,8,2,128,128]{4,3,2,1,0:T(8,128)(2,1)S(1)} custom-call(s32[1]{0:T(128)} %bitcast.sec_ref, bf16[6,8,4,128,128]{4,3,2,1,0:T(8,128)(2,1)} %bitcast.17, bf16[6,8,2,128,128]{4,3,2,1,0:T(8,128)(2,1)} %collective-permute-done.7.got, bf16[16,1536]{1,0:T(8,128)(2,1)} %copy-done), custom_call_target="tpu_custom_call" | custom-call | tf_op jit(solution)/shard_map/transfer/pallas_call | solution.py:260
  26.2 0.0 collective-permute-done.cols_got
  26.2 0.0 collective-permute-done.5.near
  26.2 0.0 collective-permute-done.6.far
  26.2 0.0 copy-start.1
  26.2 0.8 %copy-done.1 = bf16[16,1536]{1,0:T(8,128)(2,1)S(1)} copy-done((bf16[16,1536]{1,0:T(8,128)(2,1)S(1)}, bf16[16,1536]{1,0:T(8,128)(2,1)}, u32[]{:S(2)}) %copy-start.1) | copy-done | bytes 49176
  27.0 0.7 %step.4.previous = bf16[16,1536]{1,0:T(8,128)(2,1)S(1)} custom-call(s32[1]{0:T(128)} %bitcast.1.bay_ref, s32[1]{0:T(128)} %bitcast.sec_ref, s32[6,8]{1,0:T(8,128)S(1)} %bitcast.12, s32[6,8]{1,0:T(8,128)S(1)} %collective-permute-done.cols_got, bf16[16,1536]{1,0:T(8,128)(2,1)S(1)} %collective-permute-done.5.near, ...), custom_call_target="tpu_custom_call" | custom-call | tf_op jit(solution)/shard_map/step/pallas_call | solution.py:274
  27.7 0.7 %collective-permute-start.8 = (bf16[16,1536]{1,0:T(8,128)(2,1)S(1)}, bf16[16,1536]{1,0:T(8,128)(2,1)S(1)}, u32[]{:S(2)}, u32[]{:S(2)}) collective-permute-start(bf16[16,1536]{1,0:T(8,128)(2,1)S(1)} %step.4.previous), channel_id=1, source_target_pairs={{0,4},{1,5},{2,6},{3,7},{16,20},{17,21},{18,22},{19,23}} | collective-permute-start | bytes 147464 | tf_op jit(solution)/shard_map/ppermute | solution.py:186
  28.4 0.7 %collective-permute-start.9 = (bf16[16,1536]{1,0:T(8,128)(2,1)S(1)}, bf16[16,1536]{1,0:T(8,128)(2,1)S(1)}, u32[]{:S(2)}, u32[]{:S(2)}) collective-permute-start(bf16[16,1536]{1,0:T(8,128)(2,1)S(1)} %step.4.previous), channel_id=1, source_target_pairs={{0,6},{1,7},{2,4},{3,5},{16,22},{17,23},{18,20},{19,21}} | collective-permute-start | bytes 147464 | tf_op jit(solution)/shard_map/ppermute | solution.py:186
  29.1 0.0 collective-permute-done.8.near
  29.1 0.0 collective-permute-done.9.far
  29.1 0.7 %step.5.previous = bf16[16,1536]{1,0:T(8,128)(2,1)S(1)} custom-call(s32[1]{0:T(128)} %bitcast.1.bay_ref, s32[1]{0:T(128)} %bitcast.sec_ref, s32[6,8]{1,0:T(8,128)S(1)} %bitcast.13, s32[6,8]{1,0:T(8,128)S(1)} %collective-permute-done.cols_got, bf16[16,1536]{1,0:T(8,128)(2,1)S(1)} %collective-permute-done.8.near, ...), custom_call_target="tpu_custom_call" | custom-call | tf_op jit(solution)/shard_map/step/pallas_call | solution.py:274
  29.8 0.7 %collective-permute-start.10 = (bf16[16,1536]{1,0:T(8,128)(2,1)S(1)}, bf16[16,1536]{1,0:T(8,128)(2,1)S(1)}, u32[]{:S(2)}, u32[]{:S(2)}) collective-permute-start(bf16[16,1536]{1,0:T(8,128)(2,1)S(1)} %step.5.previous), channel_id=1, source_target_pairs={{4,8},{5,9},{6,10},{7,11},{20,24},{21,25},{22,26},{23,27}} | collective-permute-start | bytes 147464 | tf_op jit(solution)/shard_map/ppermute | solution.py:186
  30.4 0.7 %collective-permute-start.11 = (bf16[16,1536]{1,0:T(8,128)(2,1)S(1)}, bf16[16,1536]{1,0:T(8,128)(2,1)S(1)}, u32[]{:S(2)}, u32[]{:S(2)}) collective-permute-start(bf16[16,1536]{1,0:T(8,128)(2,1)S(1)} %step.5.previous), channel_id=1, source_target_pairs={{4,10},{5,11},{6,8},{7,9},{20,26},{21,27},{22,24},{23,25}} | collective-permute-start | bytes 147464 | tf_op jit(solution)/shard_map/ppermute | solution.py:186
  31.1 0.0 collective-permute-done.10.near
  31.1 0.0 collective-permute-done.11.far
  31.1 0.7 %step.6.previous = bf16[16,1536]{1,0:T(8,128)(2,1)S(1)} custom-call(s32[1]{0:T(128)} %bitcast.1.bay_ref, s32[1]{0:T(128)} %bitcast.sec_ref, s32[6,8]{1,0:T(8,128)S(1)} %bitcast.14, s32[6,8]{1,0:T(8,128)S(1)} %collective-permute-done.cols_got, bf16[16,1536]{1,0:T(8,128)(2,1)S(1)} %collective-permute-done.10.near, ...), custom_call_target="tpu_custom_call" | custom-call | tf_op jit(solution)/shard_map/step/pallas_call | solution.py:274
  31.8 1.3 %collective-permute-start.12 = (bf16[16,1536]{1,0:T(8,128)(2,1)S(1)}, bf16[16,1536]{1,0:T(8,128)(2,1)S(1)}, u32[]{:S(2)}, u32[]{:S(2)}) collective-permute-start(bf16[16,1536]{1,0:T(8,128)(2,1)S(1)} %step.6.previous), channel_id=1, source_target_pairs={{8,12},{9,13},{10,14},{11,15},{24,28},{25,29},{26,30},{27,31}} | collective-permute-start | bytes 147464 | tf_op jit(solution)/shard_map/ppermute | solution.py:186
  33.1 1.3 %collective-permute-start.13 = (bf16[16,1536]{1,0:T(8,128)(2,1)S(1)}, bf16[16,1536]{1,0:T(8,128)(2,1)S(1)}, u32[]{:S(2)}, u32[]{:S(2)}) collective-permute-start(bf16[16,1536]{1,0:T(8,128)(2,1)S(1)} %step.6.previous), channel_id=1, source_target_pairs={{8,14},{9,15},{10,12},{11,13},{24,30},{25,31},{26,28},{27,29}} | collective-permute-start | bytes 147464 | tf_op jit(solution)/shard_map/ppermute | solution.py:186
  34.4 18.1 %collective-permute-done.12.near = bf16[16,1536]{1,0:T(8,128)(2,1)S(1)} collective-permute-done((bf16[16,1536]{1,0:T(8,128)(2,1)S(1)}, bf16[16,1536]{1,0:T(8,128)(2,1)S(1)}, u32[]{:S(2)}, u32[]{:S(2)}) %collective-permute-start.12) | collective-permute-done | bytes 49184 | tf_op jit(solution)/shard_map/ppermute | solution.py:186
  52.5 2.2 %collective-permute-done.13.far = bf16[16,1536]{1,0:T(8,128)(2,1)S(1)} collective-permute-done((bf16[16,1536]{1,0:T(8,128)(2,1)S(1)}, bf16[16,1536]{1,0:T(8,128)(2,1)S(1)}, u32[]{:S(2)}, u32[]{:S(2)}) %collective-permute-start.13) | collective-permute-done | bytes 49184 | tf_op jit(solution)/shard_map/ppermute | solution.py:186
  54.7 3.8 %step.7.state = bf16[16,1536]{1,0:T(8,128)(2,1)S(1)} custom-call(s32[1]{0:T(128)} %bitcast.1.bay_ref, s32[1]{0:T(128)} %bitcast.sec_ref, s32[6,8]{1,0:T(8,128)S(1)} %bitcast.15, s32[6,8]{1,0:T(8,128)S(1)} %collective-permute-done.cols_got, bf16[16,1536]{1,0:T(8,128)(2,1)S(1)} %collective-permute-done.12.near, ...), custom_call_target="tpu_custom_call" | custom-call | tf_op jit(solution)/shard_map/step/pallas_call | solution.py:274
  58.5 3.6 %collective-permute-start.14 = (bf16[16,768]{1,0:T(8,128)(2,1)S(1)}, bf16[16,768]{1,0:T(8,128)(2,1)S(1)}, u32[]{:S(2)}, u32[]{:S(2)}) collective-permute-start(bf16[16,768]{1,0:T(8,128)(2,1)S(1)} %slice.4), channel_id=1, source_target_pairs={{0,1},{1,0},{2,3},{3,2},{4,5},{5,4},{6,7},{7,6},{8,9},{9,8},{10,11... | collective-permute-start | bytes 73736 | tf_op jit(solution)/shard_map/ppermute | solution.py:178
  62.1 0.8 %collective-permute-done.14.got = bf16[16,768]{1,0:T(8,128)(2,1)S(1)} collective-permute-done((bf16[16,768]{1,0:T(8,128)(2,1)S(1)}, bf16[16,768]{1,0:T(8,128)(2,1)S(1)}, u32[]{:S(2)}, u32[]{:S(2)}) %collective-permute-start.14) | collective-permute-done | bytes 24608 | tf_op jit(solution)/shard_map/ppermute | solution.py:178
  62.9 0.6 finish.1
  (2 shorter events, 0.0 us)
Async XLA Ops:
  3.4 6.3 %copy-start.4 = (bf16[16,1536]{1,0:T(8,128)(2,1)S(1)}, bf16[16,1536]{1,0:T(8,128)(2,1)}, u32[]{:S(2)}) copy-start(bf16[16,1536]{1,0:T(8,128)(2,1)} %get-tuple-element.13.after) | copy-start | bytes 147460
  3.4 8.2 %copy-start.6 = (bf16[16,1536]{1,0:T(8,128)(2,1)S(1)}, bf16[16,1536]{1,0:T(8,128)(2,1)}, u32[]{:S(2)}) copy-start(bf16[16,1536]{1,0:T(8,128)(2,1)} %get-tuple-element.16) | copy-start | bytes 147460
  3.5 19.4 %copy-start.5 = (s32[1,6,8]{2,0,1:T(1,128)S(1)}, s32[1,6,8]{2,0,1:T(1,128)}, u32[]{:S(2)}) copy-start(s32[1,6,8]{2,0,1:T(1,128)} %param.9) | copy-start | bytes 580
  8.9 14.4 %collective-permute-start.7 = (bf16[6,8,2,128,128]{4,3,2,1,0:T(8,128)(2,1)}, bf16[6,8,2,128,128]{4,3,2,1,0:T(8,128)(2,1)}, u32[]{:S(2)}, u32[]{:S(2)}) collective-permute-start(bf16[6,8,2,128,128]{4,3,2,1,0:T(8,128)(2,1)} %get-tuple-element.20), channel_id=1, source_target_pairs={{0,1},{1,0},{2,3},{3,2},{4,5},{5,4},{6,7},{7,6},{8,9},{9,8},{10,11... | collective-permute-start | bytes 9437192 | tf_op jit(solution)/shard_map/ppermute | solution.py:178
  9.7 5.9 %collective-permute-start.4 = (bf16[6,2,128,128]{3,2,1,0:T(8,128)(2,1)}, bf16[6,2,128,128]{3,2,1,0:T(8,128)(2,1)S(1)}, u32[]{:S(2)}, u32[]{:S(2)}) collective-permute-start(bf16[6,2,128,128]{3,2,1,0:T(8,128)(2,1)} %get-tuple-element.17), channel_id=1, source_target_pairs={{0,1},{1,0},{2,3},{3,2},{4,5},{5,4},{6,7},{7,6},{8,9},{9,8},{10,11... | collective-permute-start | bytes 1179656 | tf_op jit(solution)/shard_map/ppermute | solution.py:178
  9.7 7.8 %collective-permute-start.2 = (bf16[16,1536]{1,0:T(8,128)(2,1)S(1)}, bf16[16,1536]{1,0:T(8,128)(2,1)S(1)}, u32[]{:S(2)}, u32[]{:S(2)}) collective-permute-start(bf16[16,1536]{1,0:T(8,128)(2,1)S(1)} %copy-done.4), channel_id=1, source_target_pairs={{0,2},{1,3},{2,0},{3,1},{4,6},{5,7},{6,4},{7,5},{8,10},{9,11},{10,... | collective-permute-start | bytes 147464 | tf_op jit(solution)/shard_map/ppermute | solution.py:178
  10.9 6.5 %collective-permute-start.1 = (bf16[16,1536]{1,0:T(8,128)(2,1)}, bf16[16,1536]{1,0:T(8,128)(2,1)S(1)}, u32[]{:S(2)}, u32[]{:S(2)}) collective-permute-start(bf16[16,1536]{1,0:T(8,128)(2,1)} %get-tuple-element.15), channel_id=1, source_target_pairs={{0,1},{1,0},{2,3},{3,2},{4,5},{5,4},{6,7},{7,6},{8,9},{9,8},{10,11... | collective-permute-start | bytes 147464 | tf_op jit(solution)/shard_map/ppermute | solution.py:178
  11.7 5.9 %collective-permute-start.3 = (bf16[16,1536]{1,0:T(8,128)(2,1)S(1)}, bf16[16,1536]{1,0:T(8,128)(2,1)S(1)}, u32[]{:S(2)}, u32[]{:S(2)}) collective-permute-start(bf16[16,1536]{1,0:T(8,128)(2,1)S(1)} %copy-done.6), channel_id=1, source_target_pairs={{0,3},{1,2},{2,1},{3,0},{4,7},{5,6},{6,5},{7,4},{8,11},{9,10},{10,... | collective-permute-start | bytes 147464 | tf_op jit(solution)/shard_map/ppermute | solution.py:178
  15.6 0.8 %copy-start.3 = (bf16[6,2,128,128]{3,2,1,0:T(8,128)(2,1)}, bf16[6,2,128,128]{3,2,1,0:T(8,128)(2,1)S(1)}, u32[]{:S(2)}) copy-start(bf16[6,2,128,128]{3,2,1,0:T(8,128)(2,1)S(1)} %collective-permute-done.4.got) | copy-start | bytes 1179652
  17.5 0.9 %copy-start.2 = (f32[16,1536]{1,0:T(8,128)S(1)}, f32[16,1536]{1,0:T(8,128)}, u32[]{:S(2)}) copy-start(f32[16,1536]{1,0:T(8,128)} %get-tuple-element.14.own) | copy-start | bytes 294916
  18.7 4.6 %copy-start = (bf16[16,1536]{1,0:T(8,128)(2,1)}, bf16[16,1536]{1,0:T(8,128)(2,1)S(1)}, u32[]{:S(2)}) copy-start(bf16[16,1536]{1,0:T(8,128)(2,1)S(1)} %get-tuple-element.18.after.previous) | copy-start | bytes 147460
  18.7 7.5 %collective-permute-start.5 = (bf16[16,1536]{1,0:T(8,128)(2,1)S(1)}, bf16[16,1536]{1,0:T(8,128)(2,1)S(1)}, u32[]{:S(2)}, u32[]{:S(2)}) collective-permute-start(bf16[16,1536]{1,0:T(8,128)(2,1)S(1)} %get-tuple-element.18.after.previous), channel_id=1, source_target_pairs={{12,0},{13,1},{14,2},{15,3},{28,16},{29,17},{30,18},{31,19}} | collective-permute-start | bytes 147464 | tf_op jit(solution)/shard_map/ppermute | solution.py:186
  20.6 5.6 %collective-permute-start.6 = (bf16[16,1536]{1,0:T(8,128)(2,1)S(1)}, bf16[16,1536]{1,0:T(8,128)(2,1)S(1)}, u32[]{:S(2)}, u32[]{:S(2)}) collective-permute-start(bf16[16,1536]{1,0:T(8,128)(2,1)S(1)} %get-tuple-element.18.after.previous), channel_id=1, source_target_pairs={{12,2},{13,3},{14,0},{15,1},{28,18},{29,19},{30,16},{31,17}} | collective-permute-start | bytes 147464 | tf_op jit(solution)/shard_map/ppermute | solution.py:186
  22.8 3.4 %collective-permute-start = (s32[6,8]{1,0:T(8,128)S(1)}, s32[6,8]{1,0:T(8,128)S(1)}, u32[]{:S(2)}, u32[]{:S(2)}) collective-permute-start(s32[6,8]{1,0:T(8,128)S(1)} %bitcast.11), channel_id=1, source_target_pairs={{0,1},{1,0},{2,3},{3,2},{4,5},{5,4},{6,7},{7,6},{8,9},{9,8},{10,11... | collective-permute-start | bytes 584 | tf_op jit(solution)/shard_map/ppermute | solution.py:178
  26.2 0.8 %copy-start.1 = (bf16[16,1536]{1,0:T(8,128)(2,1)S(1)}, bf16[16,1536]{1,0:T(8,128)(2,1)}, u32[]{:S(2)}) copy-start(bf16[16,1536]{1,0:T(8,128)(2,1)} %copy-done) | copy-start | bytes 147460
  27.7 1.3 %collective-permute-start.8 = (bf16[16,1536]{1,0:T(8,128)(2,1)S(1)}, bf16[16,1536]{1,0:T(8,128)(2,1)S(1)}, u32[]{:S(2)}, u32[]{:S(2)}) collective-permute-start(bf16[16,1536]{1,0:T(8,128)(2,1)S(1)} %step.4.previous), channel_id=1, source_target_pairs={{0,4},{1,5},{2,6},{3,7},{16,20},{17,21},{18,22},{19,23}} | collective-permute-start | bytes 147464 | tf_op jit(solution)/shard_map/ppermute | solution.py:186
  28.4 0.7 %collective-permute-start.9 = (bf16[16,1536]{1,0:T(8,128)(2,1)S(1)}, bf16[16,1536]{1,0:T(8,128)(2,1)S(1)}, u32[]{:S(2)}, u32[]{:S(2)}) collective-permute-start(bf16[16,1536]{1,0:T(8,128)(2,1)S(1)} %step.4.previous), channel_id=1, source_target_pairs={{0,6},{1,7},{2,4},{3,5},{16,22},{17,23},{18,20},{19,21}} | collective-permute-start | bytes 147464 | tf_op jit(solution)/shard_map/ppermute | solution.py:186
  29.8 1.3 %collective-permute-start.10 = (bf16[16,1536]{1,0:T(8,128)(2,1)S(1)}, bf16[16,1536]{1,0:T(8,128)(2,1)S(1)}, u32[]{:S(2)}, u32[]{:S(2)}) collective-permute-start(bf16[16,1536]{1,0:T(8,128)(2,1)S(1)} %step.5.previous), channel_id=1, source_target_pairs={{4,8},{5,9},{6,10},{7,11},{20,24},{21,25},{22,26},{23,27}} | collective-permute-start | bytes 147464 | tf_op jit(solution)/shard_map/ppermute | solution.py:186
  30.4 0.7 %collective-permute-start.11 = (bf16[16,1536]{1,0:T(8,128)(2,1)S(1)}, bf16[16,1536]{1,0:T(8,128)(2,1)S(1)}, u32[]{:S(2)}, u32[]{:S(2)}) collective-permute-start(bf16[16,1536]{1,0:T(8,128)(2,1)S(1)} %step.5.previous), channel_id=1, source_target_pairs={{4,10},{5,11},{6,8},{7,9},{20,26},{21,27},{22,24},{23,25}} | collective-permute-start | bytes 147464 | tf_op jit(solution)/shard_map/ppermute | solution.py:186
  31.8 20.7 %collective-permute-start.12 = (bf16[16,1536]{1,0:T(8,128)(2,1)S(1)}, bf16[16,1536]{1,0:T(8,128)(2,1)S(1)}, u32[]{:S(2)}, u32[]{:S(2)}) collective-permute-start(bf16[16,1536]{1,0:T(8,128)(2,1)S(1)} %step.6.previous), channel_id=1, source_target_pairs={{8,12},{9,13},{10,14},{11,15},{24,28},{25,29},{26,30},{27,31}} | collective-permute-start | bytes 147464 | tf_op jit(solution)/shard_map/ppermute | solution.py:186
  33.1 21.6 %collective-permute-start.13 = (bf16[16,1536]{1,0:T(8,128)(2,1)S(1)}, bf16[16,1536]{1,0:T(8,128)(2,1)S(1)}, u32[]{:S(2)}, u32[]{:S(2)}) collective-permute-start(bf16[16,1536]{1,0:T(8,128)(2,1)S(1)} %step.6.previous), channel_id=1, source_target_pairs={{8,14},{9,15},{10,12},{11,13},{24,30},{25,31},{26,28},{27,29}} | collective-permute-start | bytes 147464 | tf_op jit(solution)/shard_map/ppermute | solution.py:186
  58.5 4.4 %collective-permute-start.14 = (bf16[16,768]{1,0:T(8,128)(2,1)S(1)}, bf16[16,768]{1,0:T(8,128)(2,1)S(1)}, u32[]{:S(2)}, u32[]{:S(2)}) collective-permute-start(bf16[16,768]{1,0:T(8,128)(2,1)S(1)} %slice.4), channel_id=1, source_target_pairs={{0,1},{1,0},{2,3},{3,2},{4,5},{5,4},{6,7},{7,6},{8,9},{9,8},{10,11... | collective-permute-start | bytes 73736 | tf_op jit(solution)/shard_map/ppermute | solution.py:178

commit v3 on v2

v3 whole, which is shorter than its diff:
```python
import functools

import jax
import jax.numpy as jnp
from jax import lax
from jax.experimental import pallas as pl
from jax.experimental.pallas import tpu as pltpu
from jax.sharding import PartitionSpec as P

VMEM = pl.BlockSpec(memory_space=pltpu.VMEM)
SMEM = pl.BlockSpec(memory_space=pltpu.SMEM)
ANY = pl.BlockSpec(memory_space=pl.ANY)
MIB = 1 << 20


def nt_dot(left, right):
    return lax.dot_general(left, right, (((1,), (1,)), ((), ())), preferred_element_type=jnp.float32)


def diagonal(product, freqs):
    rows, cols = product.shape[0] // freqs, product.shape[1] // freqs
    return jnp.concatenate(
        [product[f * rows:(f + 1) * rows, f * cols:(f + 1) * cols] for f in range(freqs)], axis=0
    )


def by_parity(odd, rows):
    half = rows.shape[0] // 2
    return jnp.where(odd, rows[half:], rows[:half]), jnp.where(odd, rows[:half], rows[half:])


def columns_of(coupling, owner, width):
    return coupling.at[:, pl.ds(pl.multiple_of(owner * width, width), width)]


def force_kernel(
    sec_ref, bay_ref, cols, interior, edge, coupling, inverse,
    piece1, piece2, piece3, own, inverse_own, inverse_out, loads, held, sems,
):
    sec = sec_ref[0]
    width = held.shape[-1]
    half = inverse.shape[1] // 2
    mine = (sec & 1) * half
    loads_in = pltpu.make_async_copy(interior, loads.at[0], sems.at[4])
    edge_in = pltpu.make_async_copy(edge, loads.at[1], sems.at[5])
    loads_in.start()
    order = (2, 3, 1, 0)
    copies = [
        pltpu.make_async_copy(columns_of(coupling, sec ^ d, width), held.at[n], sems.at[n])
        for n, d in enumerate(order)
    ]
    for copy in copies:
        copy.start()
    edge_in.start()
    moves = [
        pltpu.make_async_copy(inverse.at[:, pl.ds(half - mine, half)], inverse_out, sems.at[6]),
        pltpu.make_async_copy(inverse.at[:, pl.ds(mine, half)], inverse_own, sems.at[7]),
    ]
    for move in moves:
        move.start()
    loads_in.wait()
    pieces = (own, piece1, piece2, piece3)
    for n, d in enumerate(order):
        copies[n].wait()
        part = -jnp.dot(loads[0], held[n], preferred_element_type=jnp.float32)
        if d == 0:
            edge_in.wait()
            part += loads[1].astype(jnp.float32)
        first, second = by_parity(((sec ^ d) & 1) == 1, part)
        pieces[d][:, :width] = first.astype(pieces[d].dtype)
        pieces[d ^ 1][:, width:] = second.astype(pieces[d ^ 1].dtype)
    for move in moves:
        move.wait()


def transfer_kernel(sec_ref, transfer, after, transfer_out, transfer_own, sems):
    half = transfer_own.shape[2]
    mine = (sec_ref[0] & 1) * half
    copies = [
        pltpu.make_async_copy(transfer.at[:, :, pl.ds(half - mine, half)], transfer_out, sems.at[0]),
        pltpu.make_async_copy(transfer.at[:, :, pl.ds(mine, half)], transfer_own, sems.at[1]),
    ]
    for copy in copies:
        copy.start()
    for copy in copies:
        copy.wait()


def initial_kernel(own, got1, got2, got3, inverse_own, inverse_got, after, load, initial):
    part, freqs, block, _ = inverse_own.shape
    for r in range(2 * part):
        inverse = inverse_own if r < part else inverse_got
        cols = slice(r * block, (r + 1) * block)
        total = own[:, cols] + got1[:, cols].astype(jnp.float32)
        total += got2[:, cols].astype(jnp.float32) + got3[:, cols].astype(jnp.float32)
        load[:, cols] = total
        solved = nt_dot(total.astype(jnp.bfloat16), inverse[r % part].reshape(freqs * block, block))
        initial[:, cols] = diagonal(solved, freqs).astype(jnp.bfloat16)


def step_kernel(
    step, bay_ref, sec_ref, cols_own, cols_got, near, far, previous, load,
    transfer_own, transfer_got, inverse_own, inverse_got, out, state,
):
    part, nonzero, freqs, block, _ = transfer_own.shape
    rows = 2 * part
    sec = sec_ref[0]

    @pl.when(bay_ref[0] == step)
    def _():
        for n in range(2):
            source = (near, far)[n]
            for r in range(rows):
                home = (sec ^ (2 * n + r // part)) * part + r % part
                state[home] = source[:, r * block:(r + 1) * block]
        for r in range(rows):
            cols = slice(r * block, (r + 1) * block)
            own = r < part
            ids = cols_own if own else cols_got
            transfer = transfer_own if own else transfer_got
            inverse = inverse_own if own else inverse_got
            picked = jnp.concatenate([state[ids[r % part, k]] for k in range(nonzero)], axis=1)
            matrix = jnp.concatenate(
                [transfer[r % part, k].reshape(freqs * block, block) for k in range(nonzero)], axis=1
            )
            summed = (load[:, cols] + diagonal(nt_dot(picked, matrix), freqs)).astype(jnp.bfloat16)
            solved = nt_dot(summed, inverse[r % part].reshape(freqs * block, block))
            out[:, cols] = diagonal(solved, freqs).astype(jnp.bfloat16)

    @pl.when(bay_ref[0] != step)
    def _():
        out[...] = previous[...]


def finish_kernel(sec_ref, state, got, out):
    lines, width = got.shape
    odd = (sec_ref[0] & 1) == 1

    @pl.when(odd)
    def _():
        out[:lines] = got[...]
        out[lines:] = state[:, :width]

    @pl.when(jnp.logical_not(odd))
    def _():
        out[:lines] = state[:, :width]
        out[lines:] = got[...]


def in_hbm(value):
    return pltpu.with_memory_space_constraint(value, pltpu.HBM)


def moved(value, distance, offset):
    bays, secs = lax.axis_size("bay"), lax.axis_size("sec")
    route = [
        (b * secs + s, (b + distance) % bays * secs + (s ^ offset))
        for b in range(bays)
        for s in range(secs)
    ]
    return lax.ppermute(value, ("bay", "sec"), route)


def hop(value, source, offset):
    return moved(value, 1, offset)


def per_device(edge_load, interior_load, coupling, block_cols, transfer, local_inverse):
    _, freqs, cases, width = edge_load.shape
    _, rows, nonzero, _, block, _ = transfer.shape
    inner = interior_load.shape[-1]
    half = freqs // 2
    lines = half * cases
    sec = lax.axis_index("sec").astype(jnp.int32)
    position = lax.axis_index("bay")
    bays = lax.axis_size("bay")
    edge = edge_load.reshape(freqs * cases, width)
    interior = interior_load.reshape(freqs * cases, inner)
    sec_word = sec.reshape(1)
    bay_word = position.astype(jnp.int32).reshape(1)
    params = pltpu.CompilerParams(vmem_limit_bytes=16 * MIB)
    bf16, f32 = jnp.bfloat16, jnp.float32
    wide = (lines, 2 * width)
    matrices = (rows, nonzero, half, block, block)
    inverses = (rows, half, block, block)

    cols_own = block_cols[0]
    piece1, piece2, piece3, own, inverse_own, inverse_out = pl.pallas_call(
        force_kernel,
        out_shape=[jax.ShapeDtypeStruct(wide, bf16)] * 3
        + [jax.ShapeDtypeStruct(wide, f32)]
        + [pltpu.VMEM(inverses, bf16)] * 2,
        in_specs=[SMEM, SMEM, SMEM, ANY, ANY, ANY, ANY],
        out_specs=[VMEM] * 6,
        scratch_shapes=[
            pltpu.VMEM((2, 2 * lines, inner), bf16),
            pltpu.VMEM((4, inner, width), bf16),
            pltpu.SemaphoreType.DMA((8,)),
        ],
        compiler_params=params,
        name="force",
    )(sec_word, bay_word, cols_own, in_hbm(interior), in_hbm(edge), in_hbm(coupling[0]), in_hbm(local_inverse[0]))
    got2, got3, got1 = moved(piece2, 0, 2), moved(piece3, 0, 3), moved(piece1, 0, 1)
    inverse_got = moved(inverse_out, 0, 1)
    cols_got = moved(cols_own, 0, 1)

    transfer_out, transfer_own = pl.pallas_call(
        transfer_kernel,
        out_shape=[pltpu.VMEM(matrices, bf16)] * 2,
        in_specs=[SMEM, ANY, ANY],
        out_specs=[VMEM] * 2,
        scratch_shapes=[pltpu.SemaphoreType.DMA((2,))],
        compiler_params=params,
        name="transfer",
    )(sec_word, in_hbm(transfer[0]), piece2)
    transfer_got = moved(transfer_out, 0, 1)

    load, state = pl.pallas_call(
        initial_kernel,
        out_shape=[jax.ShapeDtypeStruct(wide, f32), jax.ShapeDtypeStruct(wide, bf16)],
        in_specs=[VMEM] * 6 + [ANY],
        out_specs=[VMEM] * 2,
        compiler_params=params,
        name="initial",
    )(own, got1, got2, got3, inverse_own, inverse_got, transfer_own)

    for step in range(bays):
        source = (step - 1) % bays
        near, far = hop(state, source, 0), hop(state, source, 2)
        state = pl.pallas_call(
            functools.partial(step_kernel, step),
            out_shape=jax.ShapeDtypeStruct(wide, bf16),
            in_specs=[SMEM] * 4 + [VMEM] * 8,
            out_specs=VMEM,
            scratch_shapes=[pltpu.VMEM((4 * rows, lines, block), bf16)],
            compiler_params=params,
            name="step",
        )(bay_word, sec_word, cols_own, cols_got, near, far, state, load,
          transfer_own, transfer_got, inverse_own, inverse_got)

    got = moved(state[:, width:], 0, 1)
    result = pl.pallas_call(
        finish_kernel,
        out_shape=jax.ShapeDtypeStruct((2 * lines, width), bf16),
        in_specs=[SMEM, VMEM, VMEM],
        out_specs=VMEM,
        compiler_params=params,
        name="finish",
    )(sec_word, state, got)
    return result.reshape(1, freqs, cases, width)


def solution(mesh):
    in_specs = (
        P(("groups", "bay"), None, None, "sec"),
        P(("groups", "bay"), None, None, "sec"),
        P(("groups", "bay"), "sec", None),
        P(("groups", "bay"), "sec", None),
        P(("groups", "bay"), "sec", None, None, None, None),
        P(("groups", "bay"), "sec", None, None, None),
    )
    out_specs = P(("groups", "bay"), None, None, "sec")
    return jax.shard_map(
        per_device, mesh=mesh, in_specs=in_specs, out_specs=out_specs, check_vma=False
    )
```

time: 64 us -> 54.2 us (0.85)
  waiting for transfers between devices: 24.9 us -> 15.3 us
  starting transfers between devices: 16.3 us -> 24.8 us
  Pallas kernels: 19.6 us -> 13.1 us
  local copies, waits for them, and re-layouts: 2.47 us -> 0.69 us
    ppermute x8 -> x0, waiting for transfers between devices: 20.3 us -> none  [hop(): return lax.ppermute(value, ('bay', 'sec'), route)]
    ppermute x7 -> x15, starting transfers between devices: 6.96 us -> 24.8 us  [moved(): return lax.ppermute(value, ('bay', 'sec'), route)]
    ppermute x7 -> x15, waiting for transfers between devices: 4.64 us -> 15.3 us  [moved(): return lax.ppermute(value, ('bay', 'sec'), route)]
    ppermute x8 -> x0, starting transfers between devices: 9.31 us -> none  [hop(): return lax.ppermute(value, ('bay', 'sec'), route)]
    pallas_call x4 -> x2, Pallas kernels: 12.9 us -> 6.29 us  [the longest x1 3.42 us: per_device(): pl.pallas_call(force_kernel, out_shape=[jax.ShapeDtypeStruct(wide, bf16)]...]
    unnamed x15 -> x1, local copies, waits for them, and re-layouts: 2.47 us -> 0.68 us
  transfers between devices with their start and end apart: 15 -> 15, of which waited for: 4 -> 10; matrix products, arithmetic and copies ran while one was open for 0% -> 0% of each run, Pallas kernels for 7% -> 1%
where the time goes in v3:
time: 54.2 us; the launch traced here: 54 us
  starting transfers between devices  24.8 us (46%)
  waiting for transfers between devices  15.3 us (28%)
  Pallas kernels  13.1 us (24%)
  local copies, waits for them, and re-layouts  0.69 us (1%)
    ppermute x15, starting transfers between devices, moved(): return lax.ppermute(value, ('bay', 'sec'), route)  24.8 us
    ppermute x15, waiting for transfers between devices, moved(): return lax.ppermute(value, ('bay', 'sec'), route)  15.3 us
    pallas_call x4, Pallas kernels, per_device(): pl.pallas_call(functools.partial(step_kernel, step), out_shape=jax.ShapeD...  5.85 us
    pallas_call x1, Pallas kernels, per_device(): pl.pallas_call(force_kernel, out_shape=[jax.ShapeDtypeStruct(wide, bf16)]...  3.42 us
    pallas_call x1, Pallas kernels, per_device(): pl.pallas_call(transfer_kernel, out_shape=[pltpu.VMEM(matrices, bf16)] *...  2.87 us
  transfers between devices with their start and end apart: 15, of which 10 were waited for; matrix products, arithmetic and copies ran while one was open for 0% of the time, Pallas kernels for 1%

profile of v3, /device:TPU:29, one launch (start us, length us, event | category | flops | bytes accessed | tf_op | source)
XLA Modules:
  0.0 54.0 jit_solution(8246956070094953431)
XLA Ops:
  0.0 0.7 %copy.9 = s32[1,6,8]{2,1,0:T(8,128)S(1)} copy(s32[1,6,8]{2,0,1:T(1,128)} %param.9) | data formatting | bytes 384
  0.7 3.4 %force.1 = (bf16[16,1536]{1,0:T(8,128)(2,1)S(1)}, bf16[16,1536]{1,0:T(8,128)(2,1)S(1)}, bf16[16,1536]{1,0:T(8,128)(2,1)S(1)}, f32[16,1536]{1,0:T(8,128)S(1)}, bf...) custom-call(s32[1]{0:T(128)} %bitcast.sec_ref, s32[1]{0:T(128)} %bitcast.1.bay_ref, ...), custom_call_target="tpu_custom_call" | custom-call | tf_op jit(solution)/shard_map/force/pallas_call | solution.py:188
  4.1 2.9 %transfer.1 = (bf16[6,8,2,128,128]{4,3,2,1,0:T(8,128)(2,1)S(1)}, bf16[6,8,2,128,128]{4,3,2,1,0:T(8,128)(2,1)S(1)}) custom-call(s32[1]{0:T(128)} %bitcast.sec_ref, bf16[6,8,4,128,128]{4,3,2,1,0:T(8,128)(2,1)} %bitcast.17, bf16[16,1536]{1,0:T(8,128)(2,1)S(1)} %get-tuple-element.17.after), custom_call_target="tpu_custom_call" | custom-call | tf_op jit(solution)/shard_map/transfer/pallas_call | solution.py:207
  7.0 0.7 %collective-permute-start.7 = (bf16[6,8,2,128,128]{4,3,2,1,0:T(8,128)(2,1)S(1)}, bf16[6,8,2,128,128]{4,3,2,1,0:T(8,128)(2,1)S(1)}, u32[]{:S(2)}, u32[]{:S(2)}) collective-permute-start(bf16[6,8,2,128,128]{4,3,2,1,0:T(8,128)(2,1)S(1)} %get-tuple-element.24), channel_id=1, source_target_pairs={{0,1},{1,0},{2,3},{3,2},{4,5},{5,4},{6,7},{7,6},{8,9},{9,8},{10,11... | collective-permute-start | bytes 9437192 | tf_op jit(solution)/shard_map/ppermute | solution.py:161
  7.7 0.1 collective-permute-start.4
  7.8 1.2 %collective-permute-start.2 = (bf16[16,1536]{1,0:T(8,128)(2,1)S(1)}, bf16[16,1536]{1,0:T(8,128)(2,1)S(1)}, u32[]{:S(2)}, u32[]{:S(2)}) collective-permute-start(bf16[16,1536]{1,0:T(8,128)(2,1)S(1)} %get-tuple-element.17.after), channel_id=1, source_target_pairs={{0,2},{1,3},{2,0},{3,1},{4,6},{5,7},{6,4},{7,5},{8,10},{9,11},{10,... | collective-permute-start | bytes 147464 | tf_op jit(solution)/shard_map/ppermute | solution.py:161
  9.0 0.7 %collective-permute-start.1 = (bf16[16,1536]{1,0:T(8,128)(2,1)S(1)}, bf16[16,1536]{1,0:T(8,128)(2,1)S(1)}, u32[]{:S(2)}, u32[]{:S(2)}) collective-permute-start(bf16[16,1536]{1,0:T(8,128)(2,1)S(1)} %get-tuple-element.16), channel_id=1, source_target_pairs={{0,1},{1,0},{2,3},{3,2},{4,5},{5,4},{6,7},{7,6},{8,9},{9,8},{10,11... | collective-permute-start | bytes 147464 | tf_op jit(solution)/shard_map/ppermute | solution.py:161
  9.7 0.1 collective-permute-start.3
  9.9 0.9 %collective-permute-done.2.got2 = bf16[16,1536]{1,0:T(8,128)(2,1)S(1)} collective-permute-done((bf16[16,1536]{1,0:T(8,128)(2,1)S(1)}, bf16[16,1536]{1,0:T(8,128)(2,1)S(1)}, u32[]{:S(2)}, u32[]{:S(2)}) %collective-permute-start.2) | collective-permute-done | bytes 49184 | tf_op jit(solution)/shard_map/ppermute | solution.py:161
  10.7 2.9 %collective-permute-done.1.got1 = bf16[16,1536]{1,0:T(8,128)(2,1)S(1)} collective-permute-done((bf16[16,1536]{1,0:T(8,128)(2,1)S(1)}, bf16[16,1536]{1,0:T(8,128)(2,1)S(1)}, u32[]{:S(2)}, u32[]{:S(2)}) %collective-permute-start.1) | collective-permute-done | bytes 49184 | tf_op jit(solution)/shard_map/ppermute | solution.py:161
  13.6 0.0 collective-permute-done.3.got3
  13.7 0.0 collective-permute-done.4.inverse_got
  13.7 0.3 initial.1
  14.0 0.0 collective-permute-start.5
  14.0 2.2 %collective-permute-start.6 = (bf16[16,1536]{1,0:T(8,128)(2,1)S(1)}, bf16[16,1536]{1,0:T(8,128)(2,1)S(1)}, u32[]{:S(2)}, u32[]{:S(2)}) collective-permute-start(bf16[16,1536]{1,0:T(8,128)(2,1)S(1)} %get-tuple-element.22.previous), channel_id=1, source_target_pairs={{0,6},{1,7},{2,4},{3,5},{4,10},{5,11},{6,8},{7,9},{8,14},{9,15},{1... | collective-permute-start | bytes 147464 | tf_op jit(solution)/shard_map/ppermute | solution.py:161
  16.1 0.9 %collective-permute-start = (s32[6,8]{1,0:T(8,128)S(1)}, s32[6,8]{1,0:T(8,128)S(1)}, u32[]{:S(2)}, u32[]{:S(2)}) collective-permute-start(s32[6,8]{1,0:T(8,128)S(1)} %bitcast.12), channel_id=1, source_target_pairs={{0,1},{1,0},{2,3},{3,2},{4,5},{5,4},{6,7},{7,6},{8,9},{9,8},{10,11... | collective-permute-start | bytes 584 | tf_op jit(solution)/shard_map/ppermute | solution.py:161
  17.1 0.8 %collective-permute-done.cols_got = s32[6,8]{1,0:T(8,128)S(1)} collective-permute-done((s32[6,8]{1,0:T(8,128)S(1)}, s32[6,8]{1,0:T(8,128)S(1)}, u32[]{:S(2)}, u32[]{:S(2)}) %collective-permute-start) | collective-permute-done | bytes 224 | tf_op jit(solution)/shard_map/ppermute | solution.py:161
  17.9 0.0 collective-permute-done.5.near
  17.9 0.7 %collective-permute-done.6.far = bf16[16,1536]{1,0:T(8,128)(2,1)S(1)} collective-permute-done((bf16[16,1536]{1,0:T(8,128)(2,1)S(1)}, bf16[16,1536]{1,0:T(8,128)(2,1)S(1)}, u32[]{:S(2)}, u32[]{:S(2)}) %collective-permute-start.6) | collective-permute-done | bytes 49184 | tf_op jit(solution)/shard_map/ppermute | solution.py:161
  18.6 0.0 collective-permute-done.7.transfer_got
  18.6 0.7 %step.4.previous = bf16[16,1536]{1,0:T(8,128)(2,1)S(1)} custom-call(s32[1]{0:T(128)} %bitcast.1.bay_ref, s32[1]{0:T(128)} %bitcast.sec_ref, s32[6,8]{1,0:T(8,128)S(1)} %bitcast.13, s32[6,8]{1,0:T(8,128)S(1)} %collective-permute-done.cols_got, bf16[16,1536]{1,0:T(8,128)(2,1)S(1)} %collective-permute-done.5.near, ...), custom_call_target="tpu_custom_call" | custom-call | tf_op jit(solution)/shard_map/step/pallas_call | solution.py:230
  19.3 5.5 %collective-permute-start.8 = (bf16[16,1536]{1,0:T(8,128)(2,1)S(1)}, bf16[16,1536]{1,0:T(8,128)(2,1)S(1)}, u32[]{:S(2)}, u32[]{:S(2)}) collective-permute-start(bf16[16,1536]{1,0:T(8,128)(2,1)S(1)} %step.4.previous), channel_id=1, source_target_pairs={{0,4},{1,5},{2,6},{3,7},{4,8},{5,9},{6,10},{7,11},{8,12},{9,13},{1... | collective-permute-start | bytes 147464 | tf_op jit(solution)/shard_map/ppermute | solution.py:161
  24.8 0.8 %collective-permute-start.9 = (bf16[16,1536]{1,0:T(8,128)(2,1)S(1)}, bf16[16,1536]{1,0:T(8,128)(2,1)S(1)}, u32[]{:S(2)}, u32[]{:S(2)}) collective-permute-start(bf16[16,1536]{1,0:T(8,128)(2,1)S(1)} %step.4.previous), channel_id=1, source_target_pairs={{0,6},{1,7},{2,4},{3,5},{4,10},{5,11},{6,8},{7,9},{8,14},{9,15},{1... | collective-permute-start | bytes 147464 | tf_op jit(solution)/shard_map/ppermute | solution.py:161
  25.6 0.3 collective-permute-done.8.near
  26.0 2.7 %collective-permute-done.9.far = bf16[16,1536]{1,0:T(8,128)(2,1)S(1)} collective-permute-done((bf16[16,1536]{1,0:T(8,128)(2,1)S(1)}, bf16[16,1536]{1,0:T(8,128)(2,1)S(1)}, u32[]{:S(2)}, u32[]{:S(2)}) %collective-permute-start.9) | collective-permute-done | bytes 49184 | tf_op jit(solution)/shard_map/ppermute | solution.py:161
  28.6 0.7 %step.5.previous = bf16[16,1536]{1,0:T(8,128)(2,1)S(1)} custom-call(s32[1]{0:T(128)} %bitcast.1.bay_ref, s32[1]{0:T(128)} %bitcast.sec_ref, s32[6,8]{1,0:T(8,128)S(1)} %bitcast.14, s32[6,8]{1,0:T(8,128)S(1)} %collective-permute-done.cols_got, bf16[16,1536]{1,0:T(8,128)(2,1)S(1)} %collective-permute-done.8.near, ...), custom_call_target="tpu_custom_call" | custom-call | tf_op jit(solution)/shard_map/step/pallas_call | solution.py:230
  29.3 2.3 %collective-permute-start.10 = (bf16[16,1536]{1,0:T(8,128)(2,1)S(1)}, bf16[16,1536]{1,0:T(8,128)(2,1)S(1)}, u32[]{:S(2)}, u32[]{:S(2)}) collective-permute-start(bf16[16,1536]{1,0:T(8,128)(2,1)S(1)} %step.5.previous), channel_id=1, source_target_pairs={{0,4},{1,5},{2,6},{3,7},{4,8},{5,9},{6,10},{7,11},{8,12},{9,13},{1... | collective-permute-start | bytes 147464 | tf_op jit(solution)/shard_map/ppermute | solution.py:161
  31.6 1.4 %collective-permute-start.11 = (bf16[16,1536]{1,0:T(8,128)(2,1)S(1)}, bf16[16,1536]{1,0:T(8,128)(2,1)S(1)}, u32[]{:S(2)}, u32[]{:S(2)}) collective-permute-start(bf16[16,1536]{1,0:T(8,128)(2,1)S(1)} %step.5.previous), channel_id=1, source_target_pairs={{0,6},{1,7},{2,4},{3,5},{4,10},{5,11},{6,8},{7,9},{8,14},{9,15},{1... | collective-permute-start | bytes 147464 | tf_op jit(solution)/shard_map/ppermute | solution.py:161
  33.0 0.0 collective-permute-done.10.near
  33.0 2.5 %collective-permute-done.11.far = bf16[16,1536]{1,0:T(8,128)(2,1)S(1)} collective-permute-done((bf16[16,1536]{1,0:T(8,128)(2,1)S(1)}, bf16[16,1536]{1,0:T(8,128)(2,1)S(1)}, u32[]{:S(2)}, u32[]{:S(2)}) %collective-permute-start.11) | collective-permute-done | bytes 49184 | tf_op jit(solution)/shard_map/ppermute | solution.py:161
  35.5 0.7 %step.6.previous = bf16[16,1536]{1,0:T(8,128)(2,1)S(1)} custom-call(s32[1]{0:T(128)} %bitcast.1.bay_ref, s32[1]{0:T(128)} %bitcast.sec_ref, s32[6,8]{1,0:T(8,128)S(1)} %bitcast.15, s32[6,8]{1,0:T(8,128)S(1)} %collective-permute-done.cols_got, bf16[16,1536]{1,0:T(8,128)(2,1)S(1)} %collective-permute-done.10.near, ...), custom_call_target="tpu_custom_call" | custom-call | tf_op jit(solution)/shard_map/step/pallas_call | solution.py:230
  36.2 3.2 %collective-permute-start.12 = (bf16[16,1536]{1,0:T(8,128)(2,1)S(1)}, bf16[16,1536]{1,0:T(8,128)(2,1)S(1)}, u32[]{:S(2)}, u32[]{:S(2)}) collective-permute-start(bf16[16,1536]{1,0:T(8,128)(2,1)S(1)} %step.6.previous), channel_id=1, source_target_pairs={{0,4},{1,5},{2,6},{3,7},{4,8},{5,9},{6,10},{7,11},{8,12},{9,13},{1... | collective-permute-start | bytes 147464 | tf_op jit(solution)/shard_map/ppermute | solution.py:161
  39.3 0.1 collective-permute-start.13
  39.4 1.0 %collective-permute-done.12.near = bf16[16,1536]{1,0:T(8,128)(2,1)S(1)} collective-permute-done((bf16[16,1536]{1,0:T(8,128)(2,1)S(1)}, bf16[16,1536]{1,0:T(8,128)(2,1)S(1)}, u32[]{:S(2)}, u32[]{:S(2)}) %collective-permute-start.12) | collective-permute-done | bytes 49184 | tf_op jit(solution)/shard_map/ppermute | solution.py:161
  40.5 2.7 %collective-permute-done.13.far = bf16[16,1536]{1,0:T(8,128)(2,1)S(1)} collective-permute-done((bf16[16,1536]{1,0:T(8,128)(2,1)S(1)}, bf16[16,1536]{1,0:T(8,128)(2,1)S(1)}, u32[]{:S(2)}, u32[]{:S(2)}) %collective-permute-start.13) | collective-permute-done | bytes 49184 | tf_op jit(solution)/shard_map/ppermute | solution.py:161
  43.2 3.8 %step.7.state = bf16[16,1536]{1,0:T(8,128)(2,1)S(1)} custom-call(s32[1]{0:T(128)} %bitcast.1.bay_ref, s32[1]{0:T(128)} %bitcast.sec_ref, s32[6,8]{1,0:T(8,128)S(1)} %bitcast.16, s32[6,8]{1,0:T(8,128)S(1)} %collective-permute-done.cols_got, bf16[16,1536]{1,0:T(8,128)(2,1)S(1)} %collective-permute-done.12.near, ...), custom_call_target="tpu_custom_call" | custom-call | tf_op jit(solution)/shard_map/step/pallas_call | solution.py:230
  47.0 5.6 %collective-permute-start.14 = (bf16[16,768]{1,0:T(8,128)(2,1)S(1)}, bf16[16,768]{1,0:T(8,128)(2,1)S(1)}, u32[]{:S(2)}, u32[]{:S(2)}) collective-permute-start(bf16[16,768]{1,0:T(8,128)(2,1)S(1)} %slice.4), channel_id=1, source_target_pairs={{0,1},{1,0},{2,3},{3,2},{4,5},{5,4},{6,7},{7,6},{8,9},{9,8},{10,11... | collective-permute-start | bytes 73736 | tf_op jit(solution)/shard_map/ppermute | solution.py:161
  52.5 0.8 %collective-permute-done.14.got = bf16[16,768]{1,0:T(8,128)(2,1)S(1)} collective-permute-done((bf16[16,768]{1,0:T(8,128)(2,1)S(1)}, bf16[16,768]{1,0:T(8,128)(2,1)S(1)}, u32[]{:S(2)}, u32[]{:S(2)}) %collective-permute-start.14) | collective-permute-done | bytes 24608 | tf_op jit(solution)/shard_map/ppermute | solution.py:161
  53.4 0.6 %finish.1 = bf16[32,768]{1,0:T(8,128)(2,1)} custom-call(s32[1]{0:T(128)} %bitcast.sec_ref, bf16[16,1536]{1,0:T(8,128)(2,1)S(1)} %step.7.state, bf16[16,768]{1,0:T(8,128)(2,1)S(1)} %collective-permute-done.14.got), custom_call_target="tpu_custom_call" | custom-call | tf_op jit(solution)/shard_map/finish/pallas_call | solution.py:242
  (1 shorter events, 0.0 us)
Async XLA Ops:
  7.0 11.6 %collective-permute-start.7 = (bf16[6,8,2,128,128]{4,3,2,1,0:T(8,128)(2,1)S(1)}, bf16[6,8,2,128,128]{4,3,2,1,0:T(8,128)(2,1)S(1)}, u32[]{:S(2)}, u32[]{:S(2)}) collective-permute-start(bf16[6,8,2,128,128]{4,3,2,1,0:T(8,128)(2,1)S(1)} %get-tuple-element.24), channel_id=1, source_target_pairs={{0,1},{1,0},{2,3},{3,2},{4,5},{5,4},{6,7},{7,6},{8,9},{9,8},{10,11... | collective-permute-start | bytes 9437192 | tf_op jit(solution)/shard_map/ppermute | solution.py:161
  7.7 5.9 %collective-permute-start.4 = (bf16[6,2,128,128]{3,2,1,0:T(8,128)(2,1)S(1)}, bf16[6,2,128,128]{3,2,1,0:T(8,128)(2,1)S(1)}, u32[]{:S(2)}, u32[]{:S(2)}) collective-permute-start(bf16[6,2,128,128]{3,2,1,0:T(8,128)(2,1)S(1)} %get-tuple-element.20), channel_id=1, source_target_pairs={{0,1},{1,0},{2,3},{3,2},{4,5},{5,4},{6,7},{7,6},{8,9},{9,8},{10,11... | collective-permute-start | bytes 1179656 | tf_op jit(solution)/shard_map/ppermute | solution.py:161
  7.8 2.9 %collective-permute-start.2 = (bf16[16,1536]{1,0:T(8,128)(2,1)S(1)}, bf16[16,1536]{1,0:T(8,128)(2,1)S(1)}, u32[]{:S(2)}, u32[]{:S(2)}) collective-permute-start(bf16[16,1536]{1,0:T(8,128)(2,1)S(1)} %get-tuple-element.17.after), channel_id=1, source_target_pairs={{0,2},{1,3},{2,0},{3,1},{4,6},{5,7},{6,4},{7,5},{8,10},{9,11},{10,... | collective-permute-start | bytes 147464 | tf_op jit(solution)/shard_map/ppermute | solution.py:161
  9.0 4.6 %collective-permute-start.1 = (bf16[16,1536]{1,0:T(8,128)(2,1)S(1)}, bf16[16,1536]{1,0:T(8,128)(2,1)S(1)}, u32[]{:S(2)}, u32[]{:S(2)}) collective-permute-start(bf16[16,1536]{1,0:T(8,128)(2,1)S(1)} %get-tuple-element.16), channel_id=1, source_target_pairs={{0,1},{1,0},{2,3},{3,2},{4,5},{5,4},{6,7},{7,6},{8,9},{9,8},{10,11... | collective-permute-start | bytes 147464 | tf_op jit(solution)/shard_map/ppermute | solution.py:161
  9.7 3.9 %collective-permute-start.3 = (bf16[16,1536]{1,0:T(8,128)(2,1)S(1)}, bf16[16,1536]{1,0:T(8,128)(2,1)S(1)}, u32[]{:S(2)}, u32[]{:S(2)}) collective-permute-start(bf16[16,1536]{1,0:T(8,128)(2,1)S(1)} %get-tuple-element.18), channel_id=1, source_target_pairs={{0,3},{1,2},{2,1},{3,0},{4,7},{5,6},{6,5},{7,4},{8,11},{9,10},{10,... | collective-permute-start | bytes 147464 | tf_op jit(solution)/shard_map/ppermute | solution.py:161
  14.0 4.0 %collective-permute-start.5 = (bf16[16,1536]{1,0:T(8,128)(2,1)S(1)}, bf16[16,1536]{1,0:T(8,128)(2,1)S(1)}, u32[]{:S(2)}, u32[]{:S(2)}) collective-permute-start(bf16[16,1536]{1,0:T(8,128)(2,1)S(1)} %get-tuple-element.22.previous), channel_id=1, source_target_pairs={{0,4},{1,5},{2,6},{3,7},{4,8},{5,9},{6,10},{7,11},{8,12},{9,13},{1... | collective-permute-start | bytes 147464 | tf_op jit(solution)/shard_map/ppermute | solution.py:161
  14.0 4.6 %collective-permute-start.6 = (bf16[16,1536]{1,0:T(8,128)(2,1)S(1)}, bf16[16,1536]{1,0:T(8,128)(2,1)S(1)}, u32[]{:S(2)}, u32[]{:S(2)}) collective-permute-start(bf16[16,1536]{1,0:T(8,128)(2,1)S(1)} %get-tuple-element.22.previous), channel_id=1, source_target_pairs={{0,6},{1,7},{2,4},{3,5},{4,10},{5,11},{6,8},{7,9},{8,14},{9,15},{1... | collective-permute-start | bytes 147464 | tf_op jit(solution)/shard_map/ppermute | solution.py:161
  16.1 1.8 %collective-permute-start = (s32[6,8]{1,0:T(8,128)S(1)}, s32[6,8]{1,0:T(8,128)S(1)}, u32[]{:S(2)}, u32[]{:S(2)}) collective-permute-start(s32[6,8]{1,0:T(8,128)S(1)} %bitcast.12), channel_id=1, source_target_pairs={{0,1},{1,0},{2,3},{3,2},{4,5},{5,4},{6,7},{7,6},{8,9},{9,8},{10,11... | collective-permute-start | bytes 584 | tf_op jit(solution)/shard_map/ppermute | solution.py:161
  19.3 6.7 %collective-permute-start.8 = (bf16[16,1536]{1,0:T(8,128)(2,1)S(1)}, bf16[16,1536]{1,0:T(8,128)(2,1)S(1)}, u32[]{:S(2)}, u32[]{:S(2)}) collective-permute-start(bf16[16,1536]{1,0:T(8,128)(2,1)S(1)} %step.4.previous), channel_id=1, source_target_pairs={{0,4},{1,5},{2,6},{3,7},{4,8},{5,9},{6,10},{7,11},{8,12},{9,13},{1... | collective-permute-start | bytes 147464 | tf_op jit(solution)/shard_map/ppermute | solution.py:161
  24.8 3.8 %collective-permute-start.9 = (bf16[16,1536]{1,0:T(8,128)(2,1)S(1)}, bf16[16,1536]{1,0:T(8,128)(2,1)S(1)}, u32[]{:S(2)}, u32[]{:S(2)}) collective-permute-start(bf16[16,1536]{1,0:T(8,128)(2,1)S(1)} %step.4.previous), channel_id=1, source_target_pairs={{0,6},{1,7},{2,4},{3,5},{4,10},{5,11},{6,8},{7,9},{8,14},{9,15},{1... | collective-permute-start | bytes 147464 | tf_op jit(solution)/shard_map/ppermute | solution.py:161
  29.3 3.7 %collective-permute-start.10 = (bf16[16,1536]{1,0:T(8,128)(2,1)S(1)}, bf16[16,1536]{1,0:T(8,128)(2,1)S(1)}, u32[]{:S(2)}, u32[]{:S(2)}) collective-permute-start(bf16[16,1536]{1,0:T(8,128)(2,1)S(1)} %step.5.previous), channel_id=1, source_target_pairs={{0,4},{1,5},{2,6},{3,7},{4,8},{5,9},{6,10},{7,11},{8,12},{9,13},{1... | collective-permute-start | bytes 147464 | tf_op jit(solution)/shard_map/ppermute | solution.py:161
  31.6 3.8 %collective-permute-start.11 = (bf16[16,1536]{1,0:T(8,128)(2,1)S(1)}, bf16[16,1536]{1,0:T(8,128)(2,1)S(1)}, u32[]{:S(2)}, u32[]{:S(2)}) collective-permute-start(bf16[16,1536]{1,0:T(8,128)(2,1)S(1)} %step.5.previous), channel_id=1, source_target_pairs={{0,6},{1,7},{2,4},{3,5},{4,10},{5,11},{6,8},{7,9},{8,14},{9,15},{1... | collective-permute-start | bytes 147464 | tf_op jit(solution)/shard_map/ppermute | solution.py:161
  36.2 4.3 %collective-permute-start.12 = (bf16[16,1536]{1,0:T(8,128)(2,1)S(1)}, bf16[16,1536]{1,0:T(8,128)(2,1)S(1)}, u32[]{:S(2)}, u32[]{:S(2)}) collective-permute-start(bf16[16,1536]{1,0:T(8,128)(2,1)S(1)} %step.6.previous), channel_id=1, source_target_pairs={{0,4},{1,5},{2,6},{3,7},{4,8},{5,9},{6,10},{7,11},{8,12},{9,13},{1... | collective-permute-start | bytes 147464 | tf_op jit(solution)/shard_map/ppermute | solution.py:161
  39.3 3.8 %collective-permute-start.13 = (bf16[16,1536]{1,0:T(8,128)(2,1)S(1)}, bf16[16,1536]{1,0:T(8,128)(2,1)S(1)}, u32[]{:S(2)}, u32[]{:S(2)}) collective-permute-start(bf16[16,1536]{1,0:T(8,128)(2,1)S(1)} %step.6.previous), channel_id=1, source_target_pairs={{0,6},{1,7},{2,4},{3,5},{4,10},{5,11},{6,8},{7,9},{8,14},{9,15},{1... | collective-permute-start | bytes 147464 | tf_op jit(solution)/shard_map/ppermute | solution.py:161
  47.0 6.4 %collective-permute-start.14 = (bf16[16,768]{1,0:T(8,128)(2,1)S(1)}, bf16[16,768]{1,0:T(8,128)(2,1)S(1)}, u32[]{:S(2)}, u32[]{:S(2)}) collective-permute-start(bf16[16,768]{1,0:T(8,128)(2,1)S(1)} %slice.4), channel_id=1, source_target_pairs={{0,1},{1,0},{2,3},{3,2},{4,5},{5,4},{6,7},{7,6},{8,9},{9,8},{10,11... | collective-permute-start | bytes 73736 | tf_op jit(solution)/shard_map/ppermute | solution.py:161

commit v4 on v3

--- a/solution.py
+++ b/solution.py
@@ -34,10 +34,10 @@
 
 
 def force_kernel(
-    sec_ref, bay_ref, cols, interior, edge, coupling, inverse,
+    interior, edge, coupling, inverse,
     piece1, piece2, piece3, own, inverse_own, inverse_out, loads, held, sems,
 ):
-    sec = sec_ref[0]
+    sec = lax.axis_index("sec")
     width = held.shape[-1]
     half = inverse.shape[1] // 2
     mine = (sec & 1) * half
@@ -73,9 +73,9 @@
         move.wait()
 
 
-def transfer_kernel(sec_ref, transfer, after, transfer_out, transfer_own, sems):
+def transfer_kernel(transfer, after, transfer_out, transfer_own, sems):
     half = transfer_own.shape[2]
-    mine = (sec_ref[0] & 1) * half
+    mine = (lax.axis_index("sec") & 1) * half
     copies = [
         pltpu.make_async_copy(transfer.at[:, :, pl.ds(half - mine, half)], transfer_out, sems.at[0]),
         pltpu.make_async_copy(transfer.at[:, :, pl.ds(mine, half)], transfer_own, sems.at[1]),
@@ -86,7 +86,7 @@
         copy.wait()
 
 
-def initial_kernel(own, got1, got2, got3, inverse_own, inverse_got, after, load, initial):
+def initial_kernel(own, got1, got2, got3, inverse_own, inverse_got, after, load, initial, passed):
     part, freqs, block, _ = inverse_own.shape
     for r in range(2 * part):
         inverse = inverse_own if r < part else inverse_got
@@ -99,14 +99,15 @@
 
 
 def step_kernel(
-    step, bay_ref, sec_ref, cols_own, cols_got, near, far, previous, load,
+    step, cols_own, cols_got, near, far, previous, load,
     transfer_own, transfer_got, inverse_own, inverse_got, out, state,
 ):
     part, nonzero, freqs, block, _ = transfer_own.shape
     rows = 2 * part
-    sec = sec_ref[0]
-
-    @pl.when(bay_ref[0] == step)
+    sec = lax.axis_index("sec")
+    bay = lax.axis_index("bay")
+
+    @pl.when(bay == step)
     def _():
         for n in range(2):
             source = (near, far)[n]
@@ -119,7 +120,7 @@
             ids = cols_own if own else cols_got
             transfer = transfer_own if own else transfer_got
             inverse = inverse_own if own else inverse_got
-            picked = jnp.concatenate([state[ids[r % part, k]] for k in range(nonzero)], axis=1)
+            picked = jnp.concatenate([state[ids[r % part, 0, k]] for k in range(nonzero)], axis=1)
             matrix = jnp.concatenate(
                 [transfer[r % part, k].reshape(freqs * block, block) for k in range(nonzero)], axis=1
             )
@@ -127,14 +128,14 @@
             solved = nt_dot(summed, inverse[r % part].reshape(freqs * block, block))
             out[:, cols] = diagonal(solved, freqs).astype(jnp.bfloat16)
 
-    @pl.when(bay_ref[0] != step)
+    @pl.when(bay != step)
     def _():
         out[...] = previous[...]
 
 
-def finish_kernel(sec_ref, state, got, out):
+def finish_kernel(state, got, out):
     lines, width = got.shape
-    odd = (sec_ref[0] & 1) == 1
+    odd = (lax.axis_index("sec") & 1) == 1
 
     @pl.when(odd)
     def _():
@@ -171,26 +172,22 @@
     inner = interior_load.shape[-1]
     half = freqs // 2
     lines = half * cases
-    sec = lax.axis_index("sec").astype(jnp.int32)
-    position = lax.axis_index("bay")
     bays = lax.axis_size("bay")
     edge = edge_load.reshape(freqs * cases, width)
     interior = interior_load.reshape(freqs * cases, inner)
-    sec_word = sec.reshape(1)
-    bay_word = position.astype(jnp.int32).reshape(1)
     params = pltpu.CompilerParams(vmem_limit_bytes=16 * MIB)
     bf16, f32 = jnp.bfloat16, jnp.float32
     wide = (lines, 2 * width)
     matrices = (rows, nonzero, half, block, block)
     inverses = (rows, half, block, block)
 
-    cols_own = block_cols[0]
+    cols_own = jnp.transpose(block_cols, (1, 0, 2))
     piece1, piece2, piece3, own, inverse_own, inverse_out = pl.pallas_call(
         force_kernel,
         out_shape=[jax.ShapeDtypeStruct(wide, bf16)] * 3
         + [jax.ShapeDtypeStruct(wide, f32)]
         + [pltpu.VMEM(inverses, bf16)] * 2,
-        in_specs=[SMEM, SMEM, SMEM, ANY, ANY, ANY, ANY],
+        in_specs=[ANY] * 4,
         out_specs=[VMEM] * 6,
         scratch_shapes=[
             pltpu.VMEM((2, 2 * lines, inner), bf16),
@@ -199,7 +196,7 @@
         ],
         compiler_params=params,
         name="force",
-    )(sec_word, bay_word, cols_own, in_hbm(interior), in_hbm(edge), in_hbm(coupling[0]), in_hbm(local_inverse[0]))
+    )(in_hbm(interior), in_hbm(edge), in_hbm(coupling[0]), in_hbm(local_inverse[0]))
     got2, got3, got1 = moved(piece2, 0, 2), moved(piece3, 0, 3), moved(piece1, 0, 1)
     inverse_got = moved(inverse_out, 0, 1)
     cols_got = moved(cols_own, 0, 1)
@@ -207,22 +204,26 @@
     transfer_out, transfer_own = pl.pallas_call(
         transfer_kernel,
         out_shape=[pltpu.VMEM(matrices, bf16)] * 2,
-        in_specs=[SMEM, ANY, ANY],
+        in_specs=[ANY, ANY],
         out_specs=[VMEM] * 2,
         scratch_shapes=[pltpu.SemaphoreType.DMA((2,))],
         compiler_params=params,
         name="transfer",
-    )(sec_word, in_hbm(transfer[0]), piece2)
+    )(in_hbm(transfer[0]), got1)
+    load, state, transfer_out = pl.pallas_call(
+        initial_kernel,
+        out_shape=[
+            jax.ShapeDtypeStruct(wide, f32),
+            jax.ShapeDtypeStruct(wide, bf16),
+            pltpu.VMEM(matrices, bf16),
+        ],
+        in_specs=[VMEM] * 6 + [ANY],
+        out_specs=[VMEM, VMEM, ANY],
+        input_output_aliases={6: 2},
+        compiler_params=params,
+        name="initial",
+    )(own, got1, got2, got3, inverse_own, inverse_got, transfer_out)
     transfer_got = moved(transfer_out, 0, 1)
-
-    load, state = pl.pallas_call(
-        initial_kernel,
-        out_shape=[jax.ShapeDtypeStruct(wide, f32), jax.ShapeDtypeStruct(wide, bf16)],
-        in_specs=[VMEM] * 6 + [ANY],
-        out_specs=[VMEM] * 2,
-        compiler_params=params,
-        name="initial",
-    )(own, got1, got2, got3, inverse_own, inverse_got, transfer_own)
 
     for step in range(bays):
         source = (step - 1) % bays
@@ -230,23 +231,23 @@
         state = pl.pallas_call(
             functools.partial(step_kernel, step),
             out_shape=jax.ShapeDtypeStruct(wide, bf16),
-            in_specs=[SMEM] * 4 + [VMEM] * 8,
+            in_specs=[SMEM] * 2 + [VMEM] * 8,
             out_specs=VMEM,
             scratch_shapes=[pltpu.VMEM((4 * rows, lines, block), bf16)],
             compiler_params=params,
             name="step",
-        )(bay_word, sec_word, cols_own, cols_got, near, far, state, load,
+        )(cols_own, cols_got, near, far, state, load,
           transfer_own, transfer_got, inverse_own, inverse_got)
 
     got = moved(state[:, width:], 0, 1)
     result = pl.pallas_call(
         finish_kernel,
         out_shape=jax.ShapeDtypeStruct((2 * lines, width), bf16),
-        in_specs=[SMEM, VMEM, VMEM],
+        in_specs=[VMEM, VMEM],
         out_specs=VMEM,
         compiler_params=params,
         name="finish",
-    )(sec_word, state, got)
+    )(state, got)
     return result.reshape(1, freqs, cases, width)
 
 

time: 54.2 us -> 49.2 us (0.908)
  waiting for transfers between devices: 15.3 us -> 13.2 us
  starting transfers between devices: 24.8 us -> 23.4 us
  Pallas kernels: 13.1 us -> 12.3 us
  local copies, waits for them, and re-layouts: 0.69 us -> 0.01 us
    ppermute x15, waiting for transfers between devices: 15.3 us -> 13.2 us  [moved(): return lax.ppermute(value, ('bay', 'sec'), route)]
    ppermute x15, starting transfers between devices: 24.8 us -> 23.4 us  [moved(): return lax.ppermute(value, ('bay', 'sec'), route)]
    unnamed x1 -> x2, local copies, waits for them, and re-layouts: 0.68 us -> 0.01 us
    pallas_call x1, Pallas kernels: 3.42 us -> 2.82 us  [per_device(): pl.pallas_call(force_kernel, out_shape=[jax.ShapeDtypeStruct(wide, bf16)]...]
  transfers between devices with their start and end apart: 15 -> 15, of which waited for: 10 -> 8; matrix products, arithmetic and copies ran while one was open for 0% -> 0% of each run, Pallas kernels for 1% -> 6%
where the time goes in v4:
time: 49.2 us; the launch traced here: 49 us
  starting transfers between devices  23.4 us (48%)
  waiting for transfers between devices  13.2 us (27%)
  Pallas kernels  12.3 us (25%)
    ppermute x15, starting transfers between devices, moved(): return lax.ppermute(value, ('bay', 'sec'), route)  23.4 us
    ppermute x15, waiting for transfers between devices, moved(): return lax.ppermute(value, ('bay', 'sec'), route)  13.2 us
    pallas_call x4, Pallas kernels, per_device(): pl.pallas_call(functools.partial(step_kernel, step), out_shape=jax.ShapeD...  5.73 us
    pallas_call x1, Pallas kernels, per_device(): pl.pallas_call(transfer_kernel, out_shape=[pltpu.VMEM(matrices, bf16)] *...  2.86 us
    pallas_call x1, Pallas kernels, per_device(): pl.pallas_call(force_kernel, out_shape=[jax.ShapeDtypeStruct(wide, bf16)]...  2.82 us
  transfers between devices with their start and end apart: 15, of which 8 were waited for; matrix products, arithmetic and copies ran while one was open for 0% of the time, Pallas kernels for 6%

profile of v4, /device:TPU:29, one launch (start us, length us, event | category | flops | bytes accessed | tf_op | source)
XLA Modules:
  0.0 49.0 jit_solution(62815633980379763)
XLA Ops:
  0.0 2.8 %force.1 = (bf16[16,1536]{1,0:T(8,128)(2,1)S(1)}, bf16[16,1536]{1,0:T(8,128)(2,1)S(1)}, bf16[16,1536]{1,0:T(8,128)(2,1)S(1)}, f32[16,1536]{1,0:T(8,128)S(1)}, bf...) custom-call(bf16[32,768]{1,0:T(8,128)(2,1)} %bitcast.15, bf16[32,768]{1,0:T(8,128)(2,1)} %bitcast.16, ...), custom_call_target="tpu_custom_call" | custom-call | tf_op jit(solution)/shard_map/force/pallas_call | solution.py:185
  2.8 0.7 %collective-permute-start.4 = (bf16[6,2,128,128]{3,2,1,0:T(8,128)(2,1)S(1)}, bf16[6,2,128,128]{3,2,1,0:T(8,128)(2,1)S(1)}, u32[]{:S(2)}, u32[]{:S(2)}) collective-permute-start(bf16[6,2,128,128]{3,2,1,0:T(8,128)(2,1)S(1)} %get-tuple-element.21), channel_id=1, source_target_pairs={{0,1},{1,0},{2,3},{3,2},{4,5},{5,4},{6,7},{7,6},{8,9},{9,8},{10,11... | collective-permute-start | bytes 1179656 | tf_op jit(solution)/shard_map/ppermute | solution.py:162
  3.6 0.1 collective-permute-start.1
  3.6 1.2 %collective-permute-start.2 = (bf16[16,1536]{1,0:T(8,128)(2,1)S(1)}, bf16[16,1536]{1,0:T(8,128)(2,1)S(1)}, u32[]{:S(2)}, u32[]{:S(2)}) collective-permute-start(bf16[16,1536]{1,0:T(8,128)(2,1)S(1)} %get-tuple-element.18), channel_id=1, source_target_pairs={{0,2},{1,3},{2,0},{3,1},{4,6},{5,7},{6,4},{7,5},{8,10},{9,11},{10,... | collective-permute-start | bytes 147464 | tf_op jit(solution)/shard_map/ppermute | solution.py:162
  4.9 0.9 %collective-permute-start.3 = (bf16[16,1536]{1,0:T(8,128)(2,1)S(1)}, bf16[16,1536]{1,0:T(8,128)(2,1)S(1)}, u32[]{:S(2)}, u32[]{:S(2)}) collective-permute-start(bf16[16,1536]{1,0:T(8,128)(2,1)S(1)} %get-tuple-element.19), channel_id=1, source_target_pairs={{0,3},{1,2},{2,1},{3,0},{4,7},{5,6},{6,5},{7,4},{8,11},{9,10},{10,... | collective-permute-start | bytes 147464 | tf_op jit(solution)/shard_map/ppermute | solution.py:162
  5.7 0.0 collective-permute-done.1.after.got1
  5.7 2.9 %transfer.1 = (bf16[6,8,2,128,128]{4,3,2,1,0:T(8,128)(2,1)S(1)}, bf16[6,8,2,128,128]{4,3,2,1,0:T(8,128)(2,1)S(1)}) custom-call(bf16[6,8,4,128,128]{4,3,2,1,0:T(8,128)(2,1)} %bitcast.12, bf16[16,1536]{1,0:T(8,128)(2,1)S(1)} %collective-permute-done.1.after.got1), custom_call_target="tpu_custom_call" | custom-call | tf_op jit(solution)/shard_map/transfer/pallas_call | solution.py:204
  8.6 0.0 copy-start
  8.6 0.0 collective-permute-done.2.got2
  8.6 0.6 %collective-permute-done.3.got3 = bf16[16,1536]{1,0:T(8,128)(2,1)S(1)} collective-permute-done((bf16[16,1536]{1,0:T(8,128)(2,1)S(1)}, bf16[16,1536]{1,0:T(8,128)(2,1)S(1)}, u32[]{:S(2)}, u32[]{:S(2)}) %collective-permute-start.3) | collective-permute-done | bytes 49184 | tf_op jit(solution)/shard_map/ppermute | solution.py:162
  9.2 0.0 collective-permute-done.4.inverse_got
  9.2 0.3 initial.1
  9.5 0.5 collective-permute-start.7
  9.9 0.0 collective-permute-start.5
  9.9 1.3 %collective-permute-start.6 = (bf16[16,1536]{1,0:T(8,128)(2,1)S(1)}, bf16[16,1536]{1,0:T(8,128)(2,1)S(1)}, u32[]{:S(2)}, u32[]{:S(2)}) collective-permute-start(bf16[16,1536]{1,0:T(8,128)(2,1)S(1)} %get-tuple-element.23.previous), channel_id=1, source_target_pairs={{0,6},{1,7},{2,4},{3,5},{4,10},{5,11},{6,8},{7,9},{8,14},{9,15},{1... | collective-permute-start | bytes 147464 | tf_op jit(solution)/shard_map/ppermute | solution.py:162
  11.2 0.0 copy-done
  11.2 1.0 %collective-permute-start = (s32[6,1,8]{2,1,0:T(1,128)S(1)}, s32[6,1,8]{2,1,0:T(1,128)S(1)}, u32[]{:S(2)}, u32[]{:S(2)}) collective-permute-start(s32[6,1,8]{2,1,0:T(1,128)S(1)} %bitcast.7), channel_id=1, source_target_pairs={{0,1},{1,0},{2,3},{3,2},{4,5},{5,4},{6,7},{7,6},{8,9},{9,8},{10,11... | collective-permute-start | bytes 584 | tf_op jit(solution)/shard_map/ppermute | solution.py:162
  12.2 3.0 %collective-permute-done.cols_got = s32[6,1,8]{2,1,0:T(1,128)S(1)} collective-permute-done((s32[6,1,8]{2,1,0:T(1,128)S(1)}, s32[6,1,8]{2,1,0:T(1,128)S(1)}, u32[]{:S(2)}, u32[]{:S(2)}) %collective-permute-start) | collective-permute-done | bytes 224 | tf_op jit(solution)/shard_map/ppermute | solution.py:162
  15.2 0.0 collective-permute-done.5.near
  15.2 0.0 collective-permute-done.6.far
  15.2 0.0 collective-permute-done.7.transfer_got
  15.2 0.7 %step.4.previous = bf16[16,1536]{1,0:T(8,128)(2,1)S(1)} custom-call(s32[6,1,8]{2,1,0:T(1,128)S(1)} %bitcast.8, s32[6,1,8]{2,1,0:T(1,128)S(1)} %collective-permute-done.cols_got, bf16[16,1536]{1,0:T(8,128)(2,1)S(1)} %collective-permute-done.5.near, bf16[16,1536]{1,0:T(8,128)(2,1)S(1)} %collective-permute-done.6.far, ...), custom_call_target="tpu_custom_call" | custom-call | tf_op jit(solution)/shard_map/step/pallas_call | solution.py:231
  15.9 4.7 %collective-permute-start.8 = (bf16[16,1536]{1,0:T(8,128)(2,1)S(1)}, bf16[16,1536]{1,0:T(8,128)(2,1)S(1)}, u32[]{:S(2)}, u32[]{:S(2)}) collective-permute-start(bf16[16,1536]{1,0:T(8,128)(2,1)S(1)} %step.4.previous), channel_id=1, source_target_pairs={{0,4},{1,5},{2,6},{3,7},{4,8},{5,9},{6,10},{7,11},{8,12},{9,13},{1... | collective-permute-start | bytes 147464 | tf_op jit(solution)/shard_map/ppermute | solution.py:162
  20.6 0.0 collective-permute-start.9
  20.7 1.2 %collective-permute-done.8.near = bf16[16,1536]{1,0:T(8,128)(2,1)S(1)} collective-permute-done((bf16[16,1536]{1,0:T(8,128)(2,1)S(1)}, bf16[16,1536]{1,0:T(8,128)(2,1)S(1)}, u32[]{:S(2)}, u32[]{:S(2)}) %collective-permute-start.8) | collective-permute-done | bytes 49184 | tf_op jit(solution)/shard_map/ppermute | solution.py:162
  21.8 2.7 %collective-permute-done.9.far = bf16[16,1536]{1,0:T(8,128)(2,1)S(1)} collective-permute-done((bf16[16,1536]{1,0:T(8,128)(2,1)S(1)}, bf16[16,1536]{1,0:T(8,128)(2,1)S(1)}, u32[]{:S(2)}, u32[]{:S(2)}) %collective-permute-start.9) | collective-permute-done | bytes 49184 | tf_op jit(solution)/shard_map/ppermute | solution.py:162
  24.5 0.6 %step.5.previous = bf16[16,1536]{1,0:T(8,128)(2,1)S(1)} custom-call(s32[6,1,8]{2,1,0:T(1,128)S(1)} %bitcast.9, s32[6,1,8]{2,1,0:T(1,128)S(1)} %collective-permute-done.cols_got, bf16[16,1536]{1,0:T(8,128)(2,1)S(1)} %collective-permute-done.8.near, bf16[16,1536]{1,0:T(8,128)(2,1)S(1)} %collective-permute-done.9.far, bf16[16,1536]{1,0:T(8,128)(2,1)S(1)} %step.4.previous, ...), custom_call_target="tpu_custom_call" | custom-call | tf_op jit(solution)/shard_map/step/pallas_call | solution.py:231
  25.1 1.9 %collective-permute-start.10 = (bf16[16,1536]{1,0:T(8,128)(2,1)S(1)}, bf16[16,1536]{1,0:T(8,128)(2,1)S(1)}, u32[]{:S(2)}, u32[]{:S(2)}) collective-permute-start(bf16[16,1536]{1,0:T(8,128)(2,1)S(1)} %step.5.previous), channel_id=1, source_target_pairs={{0,4},{1,5},{2,6},{3,7},{4,8},{5,9},{6,10},{7,11},{8,12},{9,13},{1... | collective-permute-start | bytes 147464 | tf_op jit(solution)/shard_map/ppermute | solution.py:162
  27.0 1.8 %collective-permute-start.11 = (bf16[16,1536]{1,0:T(8,128)(2,1)S(1)}, bf16[16,1536]{1,0:T(8,128)(2,1)S(1)}, u32[]{:S(2)}, u32[]{:S(2)}) collective-permute-start(bf16[16,1536]{1,0:T(8,128)(2,1)S(1)} %step.5.previous), channel_id=1, source_target_pairs={{0,6},{1,7},{2,4},{3,5},{4,10},{5,11},{6,8},{7,9},{8,14},{9,15},{1... | collective-permute-start | bytes 147464 | tf_op jit(solution)/shard_map/ppermute | solution.py:162
  28.8 0.0 collective-permute-done.10.near
  28.8 2.0 %collective-permute-done.11.far = bf16[16,1536]{1,0:T(8,128)(2,1)S(1)} collective-permute-done((bf16[16,1536]{1,0:T(8,128)(2,1)S(1)}, bf16[16,1536]{1,0:T(8,128)(2,1)S(1)}, u32[]{:S(2)}, u32[]{:S(2)}) %collective-permute-start.11) | collective-permute-done | bytes 49184 | tf_op jit(solution)/shard_map/ppermute | solution.py:162
  30.8 0.6 %step.6.previous = bf16[16,1536]{1,0:T(8,128)(2,1)S(1)} custom-call(s32[6,1,8]{2,1,0:T(1,128)S(1)} %bitcast.10, s32[6,1,8]{2,1,0:T(1,128)S(1)} %collective-permute-done.cols_got, bf16[16,1536]{1,0:T(8,128)(2,1)S(1)} %collective-permute-done.10.near, bf16[16,1536]{1,0:T(8,128)(2,1)S(1)} %collective-permute-done.11.far, bf16[16,1536]{1,0:T(8,128)(2,1)S(1)} %step.5.previous, ...), custom_call_target="tpu_custom_call" | custom-call | tf_op jit(solution)/shard_map/step/pallas_call | solution.py:231
  31.5 2.8 %collective-permute-start.12 = (bf16[16,1536]{1,0:T(8,128)(2,1)S(1)}, bf16[16,1536]{1,0:T(8,128)(2,1)S(1)}, u32[]{:S(2)}, u32[]{:S(2)}) collective-permute-start(bf16[16,1536]{1,0:T(8,128)(2,1)S(1)} %step.6.previous), channel_id=1, source_target_pairs={{0,4},{1,5},{2,6},{3,7},{4,8},{5,9},{6,10},{7,11},{8,12},{9,13},{1... | collective-permute-start | bytes 147464 | tf_op jit(solution)/shard_map/ppermute | solution.py:162
  34.3 0.9 %collective-permute-start.13 = (bf16[16,1536]{1,0:T(8,128)(2,1)S(1)}, bf16[16,1536]{1,0:T(8,128)(2,1)S(1)}, u32[]{:S(2)}, u32[]{:S(2)}) collective-permute-start(bf16[16,1536]{1,0:T(8,128)(2,1)S(1)} %step.6.previous), channel_id=1, source_target_pairs={{0,6},{1,7},{2,4},{3,5},{4,10},{5,11},{6,8},{7,9},{8,14},{9,15},{1... | collective-permute-start | bytes 147464 | tf_op jit(solution)/shard_map/ppermute | solution.py:162
  35.2 0.5 %collective-permute-done.12.near = bf16[16,1536]{1,0:T(8,128)(2,1)S(1)} collective-permute-done((bf16[16,1536]{1,0:T(8,128)(2,1)S(1)}, bf16[16,1536]{1,0:T(8,128)(2,1)S(1)}, u32[]{:S(2)}, u32[]{:S(2)}) %collective-permute-start.12) | collective-permute-done | bytes 49184 | tf_op jit(solution)/shard_map/ppermute | solution.py:162
  35.8 2.3 %collective-permute-done.13.far = bf16[16,1536]{1,0:T(8,128)(2,1)S(1)} collective-permute-done((bf16[16,1536]{1,0:T(8,128)(2,1)S(1)}, bf16[16,1536]{1,0:T(8,128)(2,1)S(1)}, u32[]{:S(2)}, u32[]{:S(2)}) %collective-permute-start.13) | collective-permute-done | bytes 49184 | tf_op jit(solution)/shard_map/ppermute | solution.py:162
  38.1 3.8 %step.7.state = bf16[16,1536]{1,0:T(8,128)(2,1)S(1)} custom-call(s32[6,1,8]{2,1,0:T(1,128)S(1)} %bitcast.11, s32[6,1,8]{2,1,0:T(1,128)S(1)} %collective-permute-done.cols_got, bf16[16,1536]{1,0:T(8,128)(2,1)S(1)} %collective-permute-done.12.near, bf16[16,1536]{1,0:T(8,128)(2,1)S(1)} %collective-permute-done.13.far, bf16[16,1536]{1,0:T(8,128)(2,1)S(1)} %step.6.previous, ...), custom_call_target="tpu_custom_call" | custom-call | tf_op jit(solution)/shard_map/step/pallas_call | solution.py:231
  41.9 5.6 %collective-permute-start.14 = (bf16[16,768]{1,0:T(8,128)(2,1)S(1)}, bf16[16,768]{1,0:T(8,128)(2,1)S(1)}, u32[]{:S(2)}, u32[]{:S(2)}) collective-permute-start(bf16[16,768]{1,0:T(8,128)(2,1)S(1)} %slice.4), channel_id=1, source_target_pairs={{0,1},{1,0},{2,3},{3,2},{4,5},{5,4},{6,7},{7,6},{8,9},{9,8},{10,11... | collective-permute-start | bytes 73736 | tf_op jit(solution)/shard_map/ppermute | solution.py:162
  47.5 0.8 %collective-permute-done.14.got = bf16[16,768]{1,0:T(8,128)(2,1)S(1)} collective-permute-done((bf16[16,768]{1,0:T(8,128)(2,1)S(1)}, bf16[16,768]{1,0:T(8,128)(2,1)S(1)}, u32[]{:S(2)}, u32[]{:S(2)}) %collective-permute-start.14) | collective-permute-done | bytes 24608 | tf_op jit(solution)/shard_map/ppermute | solution.py:162
  48.4 0.6 %finish.1 = bf16[32,768]{1,0:T(8,128)(2,1)} custom-call(bf16[16,1536]{1,0:T(8,128)(2,1)S(1)} %step.7.state, bf16[16,768]{1,0:T(8,128)(2,1)S(1)} %collective-permute-done.14.got), custom_call_target="tpu_custom_call" | custom-call | tf_op jit(solution)/shard_map/finish/pallas_call | solution.py:243
  (1 shorter events, 0.0 us)
Async XLA Ops:
  2.8 6.3 %collective-permute-start.4 = (bf16[6,2,128,128]{3,2,1,0:T(8,128)(2,1)S(1)}, bf16[6,2,128,128]{3,2,1,0:T(8,128)(2,1)S(1)}, u32[]{:S(2)}, u32[]{:S(2)}) collective-permute-start(bf16[6,2,128,128]{3,2,1,0:T(8,128)(2,1)S(1)} %get-tuple-element.21), channel_id=1, source_target_pairs={{0,1},{1,0},{2,3},{3,2},{4,5},{5,4},{6,7},{7,6},{8,9},{9,8},{10,11... | collective-permute-start | bytes 1179656 | tf_op jit(solution)/shard_map/ppermute | solution.py:162
  3.6 2.1 %collective-permute-start.1 = (bf16[16,1536]{1,0:T(8,128)(2,1)S(1)}, bf16[16,1536]{1,0:T(8,128)(2,1)S(1)}, u32[]{:S(2)}, u32[]{:S(2)}) collective-permute-start(bf16[16,1536]{1,0:T(8,128)(2,1)S(1)} %get-tuple-element.17), channel_id=1, source_target_pairs={{0,1},{1,0},{2,3},{3,2},{4,5},{5,4},{6,7},{7,6},{8,9},{9,8},{10,11... | collective-permute-start | bytes 147464 | tf_op jit(solution)/shard_map/ppermute | solution.py:162
  3.6 5.0 %collective-permute-start.2 = (bf16[16,1536]{1,0:T(8,128)(2,1)S(1)}, bf16[16,1536]{1,0:T(8,128)(2,1)S(1)}, u32[]{:S(2)}, u32[]{:S(2)}) collective-permute-start(bf16[16,1536]{1,0:T(8,128)(2,1)S(1)} %get-tuple-element.18), channel_id=1, source_target_pairs={{0,2},{1,3},{2,0},{3,1},{4,6},{5,7},{6,4},{7,5},{8,10},{9,11},{10,... | collective-permute-start | bytes 147464 | tf_op jit(solution)/shard_map/ppermute | solution.py:162
  4.9 4.3 %collective-permute-start.3 = (bf16[16,1536]{1,0:T(8,128)(2,1)S(1)}, bf16[16,1536]{1,0:T(8,128)(2,1)S(1)}, u32[]{:S(2)}, u32[]{:S(2)}) collective-permute-start(bf16[16,1536]{1,0:T(8,128)(2,1)S(1)} %get-tuple-element.19), channel_id=1, source_target_pairs={{0,3},{1,2},{2,1},{3,0},{4,7},{5,6},{6,5},{7,4},{8,11},{9,10},{10,... | collective-permute-start | bytes 147464 | tf_op jit(solution)/shard_map/ppermute | solution.py:162
  8.6 2.6 %copy-start = (s32[1,6,8]{2,0,1:T(1,128)S(1)}, s32[1,6,8]{2,0,1:T(1,128)}, u32[]{:S(2)}) copy-start(s32[1,6,8]{2,0,1:T(1,128)} %param.9) | copy-start | bytes 580
  9.5 5.8 %collective-permute-start.7 = (bf16[6,8,2,128,128]{4,3,2,1,0:T(8,128)(2,1)S(1)}, bf16[6,8,2,128,128]{4,3,2,1,0:T(8,128)(2,1)S(1)}, u32[]{:S(2)}, u32[]{:S(2)}) collective-permute-start(bf16[6,8,2,128,128]{4,3,2,1,0:T(8,128)(2,1)S(1)} %get-tuple-element.26), channel_id=1, source_target_pairs={{0,1},{1,0},{2,3},{3,2},{4,5},{5,4},{6,7},{7,6},{8,9},{9,8},{10,11... | collective-permute-start | bytes 9437192 | tf_op jit(solution)/shard_map/ppermute | solution.py:162
  9.9 5.3 %collective-permute-start.5 = (bf16[16,1536]{1,0:T(8,128)(2,1)S(1)}, bf16[16,1536]{1,0:T(8,128)(2,1)S(1)}, u32[]{:S(2)}, u32[]{:S(2)}) collective-permute-start(bf16[16,1536]{1,0:T(8,128)(2,1)S(1)} %get-tuple-element.23.previous), channel_id=1, source_target_pairs={{0,4},{1,5},{2,6},{3,7},{4,8},{5,9},{6,10},{7,11},{8,12},{9,13},{1... | collective-permute-start | bytes 147464 | tf_op jit(solution)/shard_map/ppermute | solution.py:162
  9.9 5.3 %collective-permute-start.6 = (bf16[16,1536]{1,0:T(8,128)(2,1)S(1)}, bf16[16,1536]{1,0:T(8,128)(2,1)S(1)}, u32[]{:S(2)}, u32[]{:S(2)}) collective-permute-start(bf16[16,1536]{1,0:T(8,128)(2,1)S(1)} %get-tuple-element.23.previous), channel_id=1, source_target_pairs={{0,6},{1,7},{2,4},{3,5},{4,10},{5,11},{6,8},{7,9},{8,14},{9,15},{1... | collective-permute-start | bytes 147464 | tf_op jit(solution)/shard_map/ppermute | solution.py:162
  11.2 4.0 %collective-permute-start = (s32[6,1,8]{2,1,0:T(1,128)S(1)}, s32[6,1,8]{2,1,0:T(1,128)S(1)}, u32[]{:S(2)}, u32[]{:S(2)}) collective-permute-start(s32[6,1,8]{2,1,0:T(1,128)S(1)} %bitcast.7), channel_id=1, source_target_pairs={{0,1},{1,0},{2,3},{3,2},{4,5},{5,4},{6,7},{7,6},{8,9},{9,8},{10,11... | collective-permute-start | bytes 584 | tf_op jit(solution)/shard_map/ppermute | solution.py:162
  15.9 5.9 %collective-permute-start.8 = (bf16[16,1536]{1,0:T(8,128)(2,1)S(1)}, bf16[16,1536]{1,0:T(8,128)(2,1)S(1)}, u32[]{:S(2)}, u32[]{:S(2)}) collective-permute-start(bf16[16,1536]{1,0:T(8,128)(2,1)S(1)} %step.4.previous), channel_id=1, source_target_pairs={{0,4},{1,5},{2,6},{3,7},{4,8},{5,9},{6,10},{7,11},{8,12},{9,13},{1... | collective-permute-start | bytes 147464 | tf_op jit(solution)/shard_map/ppermute | solution.py:162
  20.6 3.8 %collective-permute-start.9 = (bf16[16,1536]{1,0:T(8,128)(2,1)S(1)}, bf16[16,1536]{1,0:T(8,128)(2,1)S(1)}, u32[]{:S(2)}, u32[]{:S(2)}) collective-permute-start(bf16[16,1536]{1,0:T(8,128)(2,1)S(1)} %step.4.previous), channel_id=1, source_target_pairs={{0,6},{1,7},{2,4},{3,5},{4,10},{5,11},{6,8},{7,9},{8,14},{9,15},{1... | collective-permute-start | bytes 147464 | tf_op jit(solution)/shard_map/ppermute | solution.py:162
  25.1 3.7 %collective-permute-start.10 = (bf16[16,1536]{1,0:T(8,128)(2,1)S(1)}, bf16[16,1536]{1,0:T(8,128)(2,1)S(1)}, u32[]{:S(2)}, u32[]{:S(2)}) collective-permute-start(bf16[16,1536]{1,0:T(8,128)(2,1)S(1)} %step.5.previous), channel_id=1, source_target_pairs={{0,4},{1,5},{2,6},{3,7},{4,8},{5,9},{6,10},{7,11},{8,12},{9,13},{1... | collective-permute-start | bytes 147464 | tf_op jit(solution)/shard_map/ppermute | solution.py:162
  27.0 3.8 %collective-permute-start.11 = (bf16[16,1536]{1,0:T(8,128)(2,1)S(1)}, bf16[16,1536]{1,0:T(8,128)(2,1)S(1)}, u32[]{:S(2)}, u32[]{:S(2)}) collective-permute-start(bf16[16,1536]{1,0:T(8,128)(2,1)S(1)} %step.5.previous), channel_id=1, source_target_pairs={{0,6},{1,7},{2,4},{3,5},{4,10},{5,11},{6,8},{7,9},{8,14},{9,15},{1... | collective-permute-start | bytes 147464 | tf_op jit(solution)/shard_map/ppermute | solution.py:162
  31.5 4.3 %collective-permute-start.12 = (bf16[16,1536]{1,0:T(8,128)(2,1)S(1)}, bf16[16,1536]{1,0:T(8,128)(2,1)S(1)}, u32[]{:S(2)}, u32[]{:S(2)}) collective-permute-start(bf16[16,1536]{1,0:T(8,128)(2,1)S(1)} %step.6.previous), channel_id=1, source_target_pairs={{0,4},{1,5},{2,6},{3,7},{4,8},{5,9},{6,10},{7,11},{8,12},{9,13},{1... | collective-permute-start | bytes 147464 | tf_op jit(solution)/shard_map/ppermute | solution.py:162
  34.3 3.8 %collective-permute-start.13 = (bf16[16,1536]{1,0:T(8,128)(2,1)S(1)}, bf16[16,1536]{1,0:T(8,128)(2,1)S(1)}, u32[]{:S(2)}, u32[]{:S(2)}) collective-permute-start(bf16[16,1536]{1,0:T(8,128)(2,1)S(1)} %step.6.previous), channel_id=1, source_target_pairs={{0,6},{1,7},{2,4},{3,5},{4,10},{5,11},{6,8},{7,9},{8,14},{9,15},{1... | collective-permute-start | bytes 147464 | tf_op jit(solution)/shard_map/ppermute | solution.py:162
  41.9 6.5 %collective-permute-start.14 = (bf16[16,768]{1,0:T(8,128)(2,1)S(1)}, bf16[16,768]{1,0:T(8,128)(2,1)S(1)}, u32[]{:S(2)}, u32[]{:S(2)}) collective-permute-start(bf16[16,768]{1,0:T(8,128)(2,1)S(1)} %slice.4), channel_id=1, source_target_pairs={{0,1},{1,0},{2,3},{3,2},{4,5},{5,4},{6,7},{7,6},{8,9},{9,8},{10,11... | collective-permute-start | bytes 73736 | tf_op jit(solution)/shard_map/ppermute | solution.py:162

commit v5 on v4

--- a/solution.py
+++ b/solution.py
@@ -15,6 +15,10 @@
 
 def nt_dot(left, right):
     return lax.dot_general(left, right, (((1,), (1,)), ((), ())), preferred_element_type=jnp.float32)
+
+
+def nn_dot(left, right):
+    return jnp.dot(left, right, preferred_element_type=jnp.float32)
 
 
 def diagonal(product, freqs):
@@ -73,17 +77,31 @@
         move.wait()
 
 
-def transfer_kernel(transfer, after, transfer_out, transfer_own, sems):
-    half = transfer_own.shape[2]
+def transfer_kernel(
+    transfer, inverse_own, inverse_got, after, transfer_out, transfer_own, turned, raw, sems,
+):
+    rows, nonzero, half = transfer_own.shape[:3]
     mine = (lax.axis_index("sec") & 1) * half
+    targets = [(transfer_out, half - mine), (transfer_own, mine)]
     copies = [
-        pltpu.make_async_copy(transfer.at[:, :, pl.ds(half - mine, half)], transfer_out, sems.at[0]),
-        pltpu.make_async_copy(transfer.at[:, :, pl.ds(mine, half)], transfer_own, sems.at[1]),
+        pltpu.make_async_copy(
+            transfer.at[r, :, pl.ds(first, half)], raw.at[n * rows + r], sems.at[n * rows + r]
+        )
+        for n, (_, first) in enumerate(targets)
+        for r in range(rows)
     ]
     for copy in copies:
         copy.start()
-    for copy in copies:
-        copy.wait()
+    for r in range(rows):
+        for f in range(half):
+            turned[r, f] = inverse_own[r, f].T
+            turned[rows + r, f] = inverse_got[r, f].T
+    for n, (target, _) in enumerate(targets):
+        for r in range(rows):
+            copies[n * rows + r].wait()
+            for k in range(nonzero):
+                for f in range(half):
+                    target[r, k, f] = raw[n * rows + r, k, f].T
 
 
 def initial_kernel(own, got1, got2, got3, inverse_own, inverse_got, after, load, initial, passed):
@@ -99,8 +117,8 @@
 
 
 def step_kernel(
-    step, cols_own, cols_got, near, far, previous, load,
-    transfer_own, transfer_got, inverse_own, inverse_got, out, state,
+    step, near, far, previous, load,
+    transfer_own, transfer_got, inverse, cols_own, cols_got, out, state, ids, sems,
 ):
     part, nonzero, freqs, block, _ = transfer_own.shape
     rows = 2 * part
@@ -109,23 +127,28 @@
 
     @pl.when(bay == step)
     def _():
+        copies = [
+            pltpu.make_async_copy(cols, ids.at[n], sems.at[n]) for n, cols in enumerate((cols_own, cols_got))
+        ]
+        for copy in copies:
+            copy.start()
         for n in range(2):
             source = (near, far)[n]
             for r in range(rows):
                 home = (sec ^ (2 * n + r // part)) * part + r % part
                 state[home] = source[:, r * block:(r + 1) * block]
+        for copy in copies:
+            copy.wait()
         for r in range(rows):
             cols = slice(r * block, (r + 1) * block)
-            own = r < part
-            ids = cols_own if own else cols_got
-            transfer = transfer_own if own else transfer_got
-            inverse = inverse_own if own else inverse_got
-            picked = jnp.concatenate([state[ids[r % part, 0, k]] for k in range(nonzero)], axis=1)
+            transfer = transfer_own if r < part else transfer_got
+            picked = jnp.concatenate([state[ids[r // part, r % part, 0, k]] for k in range(nonzero)], axis=1)
             matrix = jnp.concatenate(
-                [transfer[r % part, k].reshape(freqs * block, block) for k in range(nonzero)], axis=1
+                [jnp.concatenate([transfer[r % part, k, f] for f in range(freqs)], axis=1) for k in range(nonzero)],
+                axis=0,
             )
-            summed = (load[:, cols] + diagonal(nt_dot(picked, matrix), freqs)).astype(jnp.bfloat16)
-            solved = nt_dot(summed, inverse[r % part].reshape(freqs * block, block))
+            summed = (load[:, cols] + diagonal(nn_dot(picked, matrix), freqs)).astype(jnp.bfloat16)
+            solved = nn_dot(summed, jnp.concatenate([inverse[r, f] for f in range(freqs)], axis=1))
             out[:, cols] = diagonal(solved, freqs).astype(jnp.bfloat16)
 
     @pl.when(bay != step)
@@ -175,7 +198,7 @@
     bays = lax.axis_size("bay")
     edge = edge_load.reshape(freqs * cases, width)
     interior = interior_load.reshape(freqs * cases, inner)
-    params = pltpu.CompilerParams(vmem_limit_bytes=16 * MIB)
+    params = pltpu.CompilerParams(vmem_limit_bytes=20 * MIB)
     bf16, f32 = jnp.bfloat16, jnp.float32
     wide = (lines, 2 * width)
     matrices = (rows, nonzero, half, block, block)
@@ -201,15 +224,19 @@
     inverse_got = moved(inverse_out, 0, 1)
     cols_got = moved(cols_own, 0, 1)
 
-    transfer_out, transfer_own = pl.pallas_call(
+    transfer_out, transfer_own, turned = pl.pallas_call(
         transfer_kernel,
-        out_shape=[pltpu.VMEM(matrices, bf16)] * 2,
-        in_specs=[ANY, ANY],
-        out_specs=[VMEM] * 2,
-        scratch_shapes=[pltpu.SemaphoreType.DMA((2,))],
+        out_shape=[pltpu.VMEM(matrices, bf16)] * 2
+        + [pltpu.VMEM((2 * rows,) + inverses[1:], bf16)],
+        in_specs=[ANY, VMEM, VMEM, ANY],
+        out_specs=[VMEM] * 3,
+        scratch_shapes=[
+            pltpu.VMEM((2 * rows,) + matrices[1:], bf16),
+            pltpu.SemaphoreType.DMA((2 * rows,)),
+        ],
         compiler_params=params,
         name="transfer",
-    )(in_hbm(transfer[0]), got1)
+    )(in_hbm(transfer[0]), inverse_own, inverse_got, got1)
     load, state, transfer_out = pl.pallas_call(
         initial_kernel,
         out_shape=[
@@ -231,13 +258,16 @@
         state = pl.pallas_call(
             functools.partial(step_kernel, step),
             out_shape=jax.ShapeDtypeStruct(wide, bf16),
-            in_specs=[SMEM] * 2 + [VMEM] * 8,
+            in_specs=[VMEM] * 9,
             out_specs=VMEM,
-            scratch_shapes=[pltpu.VMEM((4 * rows, lines, block), bf16)],
+            scratch_shapes=[
+                pltpu.VMEM((4 * rows, lines, block), bf16),
+                pltpu.SMEM((2,) + cols_own.shape, jnp.int32),
+                pltpu.SemaphoreType.DMA((2,)),
+            ],
             compiler_params=params,
             name="step",
-        )(cols_own, cols_got, near, far, state, load,
-          transfer_own, transfer_got, inverse_own, inverse_got)
+        )(near, far, state, load, transfer_own, transfer_got, turned, cols_own, cols_got)
 
     got = moved(state[:, width:], 0, 1)
     result = pl.pallas_call(

time: 49.2 us -> 46.9 us (0.953)
  Pallas kernels: 12.3 us -> 10.3 us
  waiting for transfers between devices: 13.2 us -> 12.3 us
  starting transfers between devices: 23.4 us -> 24 us
    pallas_call x4, Pallas kernels: 5.73 us -> 3.09 us  [per_device(): pl.pallas_call(functools.partial(step_kernel, step), out_shape=jax.ShapeD...]
    ppermute x15, waiting for transfers between devices: 13.2 us -> 12.3 us  [moved(): return lax.ppermute(value, ('bay', 'sec'), route)]
    ppermute x15, starting transfers between devices: 23.4 us -> 24 us  [moved(): return lax.ppermute(value, ('bay', 'sec'), route)]
    pallas_call x1, Pallas kernels: 2.86 us -> 3.44 us  [per_device(): pl.pallas_call(transfer_kernel, out_shape=[pltpu.VMEM(matrices, bf16)] *...]
  transfers between devices with their start and end apart: 15 -> 15, of which waited for: 8 -> 7; matrix products, arithmetic and copies ran while one was open for 0% -> 0% of each run, Pallas kernels for 6% -> 7%
where the time goes in v5:
time: 46.9 us; the launch traced here: 46.7 us
  starting transfers between devices  24 us (51%)
  waiting for transfers between devices  12.3 us (26%)
  Pallas kernels  10.3 us (22%)
    ppermute x15, starting transfers between devices, moved(): return lax.ppermute(value, ('bay', 'sec'), route)  24 us
    ppermute x15, waiting for transfers between devices, moved(): return lax.ppermute(value, ('bay', 'sec'), route)  12.3 us
    pallas_call x1, Pallas kernels, per_device(): pl.pallas_call(transfer_kernel, out_shape=[pltpu.VMEM(matrices, bf16)] *...  3.44 us
    pallas_call x4, Pallas kernels, per_device(): pl.pallas_call(functools.partial(step_kernel, step), out_shape=jax.ShapeD...  3.09 us
    pallas_call x1, Pallas kernels, per_device(): pl.pallas_call(force_kernel, out_shape=[jax.ShapeDtypeStruct(wide, bf16)]...  2.82 us
  transfers between devices with their start and end apart: 15, of which 7 were waited for; matrix products, arithmetic and copies ran while one was open for 0% of the time, Pallas kernels for 7%

profile of v5, /device:TPU:29, one launch (start us, length us, event | category | flops | bytes accessed | tf_op | source)
XLA Modules:
  0.0 46.7 jit_solution(8393037411230035187)
XLA Ops:
  0.0 2.8 %force.1 = (bf16[16,1536]{1,0:T(8,128)(2,1)S(1)}, bf16[16,1536]{1,0:T(8,128)(2,1)S(1)}, bf16[16,1536]{1,0:T(8,128)(2,1)S(1)}, f32[16,1536]{1,0:T(8,128)S(1)}, bf...) custom-call(bf16[32,768]{1,0:T(8,128)(2,1)} %bitcast.15, bf16[32,768]{1,0:T(8,128)(2,1)} %bitcast.16, ...), custom_call_target="tpu_custom_call" | custom-call | tf_op jit(solution)/shard_map/force/pallas_call | solution.py:208
  2.8 0.7 %collective-permute-start.3 = (bf16[6,2,128,128]{3,2,1,0:T(8,128)(2,1)S(1)}, bf16[6,2,128,128]{3,2,1,0:T(8,128)(2,1)S(1)}, u32[]{:S(2)}, u32[]{:S(2)}) collective-permute-start(bf16[6,2,128,128]{3,2,1,0:T(8,128)(2,1)S(1)} %get-tuple-element.22), channel_id=1, source_target_pairs={{0,1},{1,0},{2,3},{3,2},{4,5},{5,4},{6,7},{7,6},{8,9},{9,8},{10,11... | collective-permute-start | bytes 1179656 | tf_op jit(solution)/shard_map/ppermute | solution.py:185
  3.6 0.1 collective-permute-start
  3.6 1.2 %collective-permute-start.1 = (bf16[16,1536]{1,0:T(8,128)(2,1)S(1)}, bf16[16,1536]{1,0:T(8,128)(2,1)S(1)}, u32[]{:S(2)}, u32[]{:S(2)}) collective-permute-start(bf16[16,1536]{1,0:T(8,128)(2,1)S(1)} %get-tuple-element.19), channel_id=1, source_target_pairs={{0,2},{1,3},{2,0},{3,1},{4,6},{5,7},{6,4},{7,5},{8,10},{9,11},{10,... | collective-permute-start | bytes 147464 | tf_op jit(solution)/shard_map/ppermute | solution.py:185
  4.9 0.9 %collective-permute-start.2 = (bf16[16,1536]{1,0:T(8,128)(2,1)S(1)}, bf16[16,1536]{1,0:T(8,128)(2,1)S(1)}, u32[]{:S(2)}, u32[]{:S(2)}) collective-permute-start(bf16[16,1536]{1,0:T(8,128)(2,1)S(1)} %get-tuple-element.20), channel_id=1, source_target_pairs={{0,3},{1,2},{2,1},{3,0},{4,7},{5,6},{6,5},{7,4},{8,11},{9,10},{10,... | collective-permute-start | bytes 147464 | tf_op jit(solution)/shard_map/ppermute | solution.py:185
  5.7 0.0 collective-permute-done.after.got1
  5.7 0.0 collective-permute-done.3.inverse_got
  5.7 3.4 %transfer.1 = (bf16[6,8,2,128,128]{4,3,2,1,0:T(8,128)(2,1)S(1)}, bf16[6,8,2,128,128]{4,3,2,1,0:T(8,128)(2,1)S(1)}, bf16[12,2,128,128]{3,2,1,0:T(8,128)(2,1)S(1)}) custom-call(bf16[6,8,4,128,128]{4,3,2,1,0:T(8,128)(2,1)} %bitcast.12, bf16[6,2,128,128]{3,2,1,0:T(8,128)(2,1)S(1)} %get-tuple-element.21.inverse_own, ...), custom_call_target="tpu_custom_call" | custom-call | tf_op jit(solution)/shard_map/transfer/pallas_call | solution.py:227
  9.2 0.0 copy-start
  9.2 0.0 collective-permute-done.1.got2
  9.2 0.0 collective-permute-done.2.got3
  9.2 0.3 initial.1
  9.5 0.4 collective-permute-start.6
  9.9 0.0 collective-permute-start.4
  9.9 1.8 %collective-permute-start.5 = (bf16[16,1536]{1,0:T(8,128)(2,1)S(1)}, bf16[16,1536]{1,0:T(8,128)(2,1)S(1)}, u32[]{:S(2)}, u32[]{:S(2)}) collective-permute-start(bf16[16,1536]{1,0:T(8,128)(2,1)S(1)} %get-tuple-element.24.previous), channel_id=1, source_target_pairs={{0,6},{1,7},{2,4},{3,5},{4,10},{5,11},{6,8},{7,9},{8,14},{9,15},{1... | collective-permute-start | bytes 147464 | tf_op jit(solution)/shard_map/ppermute | solution.py:185
  11.8 0.0 copy-done
  11.8 1.0 %collective-permute-start.7 = (s32[6,1,8]{2,1,0:T(1,128)S(1)}, s32[6,1,8]{2,1,0:T(1,128)S(1)}, u32[]{:S(2)}, u32[]{:S(2)}) collective-permute-start(s32[6,1,8]{2,1,0:T(1,128)S(1)} %bitcast.7), channel_id=1, source_target_pairs={{0,1},{1,0},{2,3},{3,2},{4,5},{5,4},{6,7},{7,6},{8,9},{9,8},{10,11... | collective-permute-start | bytes 584 | tf_op jit(solution)/shard_map/ppermute | solution.py:185
  12.8 2.4 %collective-permute-done.7.cols_got = s32[6,1,8]{2,1,0:T(1,128)S(1)} collective-permute-done((s32[6,1,8]{2,1,0:T(1,128)S(1)}, s32[6,1,8]{2,1,0:T(1,128)S(1)}, u32[]{:S(2)}, u32[]{:S(2)}) %collective-permute-start.7) | collective-permute-done | bytes 224 | tf_op jit(solution)/shard_map/ppermute | solution.py:185
  15.2 0.0 collective-permute-done.4.near
  15.2 0.0 collective-permute-done.5.far
  15.2 0.0 collective-permute-done.6.transfer_got
  15.3 4.6 %collective-permute-start.8 = (bf16[16,1536]{1,0:T(8,128)(2,1)S(1)}, bf16[16,1536]{1,0:T(8,128)(2,1)S(1)}, u32[]{:S(2)}, u32[]{:S(2)}) collective-permute-start(bf16[16,1536]{1,0:T(8,128)(2,1)S(1)} %step.4.previous), channel_id=1, source_target_pairs={{0,4},{1,5},{2,6},{3,7},{4,8},{5,9},{6,10},{7,11},{8,12},{9,13},{1... | collective-permute-start | bytes 147464 | tf_op jit(solution)/shard_map/ppermute | solution.py:185
  19.9 0.7 %collective-permute-start.9 = (bf16[16,1536]{1,0:T(8,128)(2,1)S(1)}, bf16[16,1536]{1,0:T(8,128)(2,1)S(1)}, u32[]{:S(2)}, u32[]{:S(2)}) collective-permute-start(bf16[16,1536]{1,0:T(8,128)(2,1)S(1)} %step.4.previous), channel_id=1, source_target_pairs={{0,6},{1,7},{2,4},{3,5},{4,10},{5,11},{6,8},{7,9},{8,14},{9,15},{1... | collective-permute-start | bytes 147464 | tf_op jit(solution)/shard_map/ppermute | solution.py:185
  20.6 0.5 %collective-permute-done.8.near = bf16[16,1536]{1,0:T(8,128)(2,1)S(1)} collective-permute-done((bf16[16,1536]{1,0:T(8,128)(2,1)S(1)}, bf16[16,1536]{1,0:T(8,128)(2,1)S(1)}, u32[]{:S(2)}, u32[]{:S(2)}) %collective-permute-start.8) | collective-permute-done | bytes 49184 | tf_op jit(solution)/shard_map/ppermute | solution.py:185
  21.1 2.7 %collective-permute-done.9.far = bf16[16,1536]{1,0:T(8,128)(2,1)S(1)} collective-permute-done((bf16[16,1536]{1,0:T(8,128)(2,1)S(1)}, bf16[16,1536]{1,0:T(8,128)(2,1)S(1)}, u32[]{:S(2)}, u32[]{:S(2)}) %collective-permute-start.9) | collective-permute-done | bytes 49184 | tf_op jit(solution)/shard_map/ppermute | solution.py:185
  23.7 2.1 %collective-permute-start.10 = (bf16[16,1536]{1,0:T(8,128)(2,1)S(1)}, bf16[16,1536]{1,0:T(8,128)(2,1)S(1)}, u32[]{:S(2)}, u32[]{:S(2)}) collective-permute-start(bf16[16,1536]{1,0:T(8,128)(2,1)S(1)} %step.5.previous), channel_id=1, source_target_pairs={{0,4},{1,5},{2,6},{3,7},{4,8},{5,9},{6,10},{7,11},{8,12},{9,13},{1... | collective-permute-start | bytes 147464 | tf_op jit(solution)/shard_map/ppermute | solution.py:185
  25.8 1.5 %collective-permute-start.11 = (bf16[16,1536]{1,0:T(8,128)(2,1)S(1)}, bf16[16,1536]{1,0:T(8,128)(2,1)S(1)}, u32[]{:S(2)}, u32[]{:S(2)}) collective-permute-start(bf16[16,1536]{1,0:T(8,128)(2,1)S(1)} %step.5.previous), channel_id=1, source_target_pairs={{0,6},{1,7},{2,4},{3,5},{4,10},{5,11},{6,8},{7,9},{8,14},{9,15},{1... | collective-permute-start | bytes 147464 | tf_op jit(solution)/shard_map/ppermute | solution.py:185
  27.3 0.0 collective-permute-done.10.near
  27.3 2.4 %collective-permute-done.11.far = bf16[16,1536]{1,0:T(8,128)(2,1)S(1)} collective-permute-done((bf16[16,1536]{1,0:T(8,128)(2,1)S(1)}, bf16[16,1536]{1,0:T(8,128)(2,1)S(1)}, u32[]{:S(2)}, u32[]{:S(2)}) %collective-permute-start.11) | collective-permute-done | bytes 49184 | tf_op jit(solution)/shard_map/ppermute | solution.py:185
  29.7 3.0 %collective-permute-start.12 = (bf16[16,1536]{1,0:T(8,128)(2,1)S(1)}, bf16[16,1536]{1,0:T(8,128)(2,1)S(1)}, u32[]{:S(2)}, u32[]{:S(2)}) collective-permute-start(bf16[16,1536]{1,0:T(8,128)(2,1)S(1)} %step.6.previous), channel_id=1, source_target_pairs={{0,4},{1,5},{2,6},{3,7},{4,8},{5,9},{6,10},{7,11},{8,12},{9,13},{1... | collective-permute-start | bytes 147464 | tf_op jit(solution)/shard_map/ppermute | solution.py:185
  32.7 0.4 collective-permute-start.13
  33.1 0.8 %collective-permute-done.12.near = bf16[16,1536]{1,0:T(8,128)(2,1)S(1)} collective-permute-done((bf16[16,1536]{1,0:T(8,128)(2,1)S(1)}, bf16[16,1536]{1,0:T(8,128)(2,1)S(1)}, u32[]{:S(2)}, u32[]{:S(2)}) %collective-permute-start.12) | collective-permute-done | bytes 49184 | tf_op jit(solution)/shard_map/ppermute | solution.py:185
  33.9 2.7 %collective-permute-done.13.far = bf16[16,1536]{1,0:T(8,128)(2,1)S(1)} collective-permute-done((bf16[16,1536]{1,0:T(8,128)(2,1)S(1)}, bf16[16,1536]{1,0:T(8,128)(2,1)S(1)}, u32[]{:S(2)}, u32[]{:S(2)}) %collective-permute-start.13) | collective-permute-done | bytes 49184 | tf_op jit(solution)/shard_map/ppermute | solution.py:185
  36.6 3.0 %step.7.state = bf16[16,1536]{1,0:T(8,128)(2,1)S(1)} custom-call(bf16[16,1536]{1,0:T(8,128)(2,1)S(1)} %collective-permute-done.12.near, bf16[16,1536]{1,0:T(8,128)(2,1)S(1)} %collective-permute-done.13.far, bf16[16,1536]{1,0:T(8,128)(2,1)S(1)} %step.6.previous, f32[16,1536]{1,0:T(8,128)S(1)} %get-tuple-element.25.load, ...), custom_call_target="tpu_custom_call" | custom-call | tf_op jit(solution)/shard_map/step/pallas_call | solution.py:258
  39.6 5.7 %collective-permute-start.14 = (bf16[16,768]{1,0:T(8,128)(2,1)S(1)}, bf16[16,768]{1,0:T(8,128)(2,1)S(1)}, u32[]{:S(2)}, u32[]{:S(2)}) collective-permute-start(bf16[16,768]{1,0:T(8,128)(2,1)S(1)} %slice.4), channel_id=1, source_target_pairs={{0,1},{1,0},{2,3},{3,2},{4,5},{5,4},{6,7},{7,6},{8,9},{9,8},{10,11... | collective-permute-start | bytes 73736 | tf_op jit(solution)/shard_map/ppermute | solution.py:185
  45.3 0.8 %collective-permute-done.14.got = bf16[16,768]{1,0:T(8,128)(2,1)S(1)} collective-permute-done((bf16[16,768]{1,0:T(8,128)(2,1)S(1)}, bf16[16,768]{1,0:T(8,128)(2,1)S(1)}, u32[]{:S(2)}, u32[]{:S(2)}) %collective-permute-start.14) | collective-permute-done | bytes 24608 | tf_op jit(solution)/shard_map/ppermute | solution.py:185
  46.1 0.6 %finish.1 = bf16[32,768]{1,0:T(8,128)(2,1)} custom-call(bf16[16,1536]{1,0:T(8,128)(2,1)S(1)} %step.7.state, bf16[16,768]{1,0:T(8,128)(2,1)S(1)} %collective-permute-done.14.got), custom_call_target="tpu_custom_call" | custom-call | tf_op jit(solution)/shard_map/finish/pallas_call | solution.py:273
  (4 shorter events, 0.1 us)
Async XLA Ops:
  2.8 2.9 %collective-permute-start.3 = (bf16[6,2,128,128]{3,2,1,0:T(8,128)(2,1)S(1)}, bf16[6,2,128,128]{3,2,1,0:T(8,128)(2,1)S(1)}, u32[]{:S(2)}, u32[]{:S(2)}) collective-permute-start(bf16[6,2,128,128]{3,2,1,0:T(8,128)(2,1)S(1)} %get-tuple-element.22), channel_id=1, source_target_pairs={{0,1},{1,0},{2,3},{3,2},{4,5},{5,4},{6,7},{7,6},{8,9},{9,8},{10,11... | collective-permute-start | bytes 1179656 | tf_op jit(solution)/shard_map/ppermute | solution.py:185
  3.6 2.1 %collective-permute-start = (bf16[16,1536]{1,0:T(8,128)(2,1)S(1)}, bf16[16,1536]{1,0:T(8,128)(2,1)S(1)}, u32[]{:S(2)}, u32[]{:S(2)}) collective-permute-start(bf16[16,1536]{1,0:T(8,128)(2,1)S(1)} %get-tuple-element.18), channel_id=1, source_target_pairs={{0,1},{1,0},{2,3},{3,2},{4,5},{5,4},{6,7},{7,6},{8,9},{9,8},{10,11... | collective-permute-start | bytes 147464 | tf_op jit(solution)/shard_map/ppermute | solution.py:185
  3.6 5.5 %collective-permute-start.1 = (bf16[16,1536]{1,0:T(8,128)(2,1)S(1)}, bf16[16,1536]{1,0:T(8,128)(2,1)S(1)}, u32[]{:S(2)}, u32[]{:S(2)}) collective-permute-start(bf16[16,1536]{1,0:T(8,128)(2,1)S(1)} %get-tuple-element.19), channel_id=1, source_target_pairs={{0,2},{1,3},{2,0},{3,1},{4,6},{5,7},{6,4},{7,5},{8,10},{9,11},{10,... | collective-permute-start | bytes 147464 | tf_op jit(solution)/shard_map/ppermute | solution.py:185
  4.9 4.3 %collective-permute-start.2 = (bf16[16,1536]{1,0:T(8,128)(2,1)S(1)}, bf16[16,1536]{1,0:T(8,128)(2,1)S(1)}, u32[]{:S(2)}, u32[]{:S(2)}) collective-permute-start(bf16[16,1536]{1,0:T(8,128)(2,1)S(1)} %get-tuple-element.20), channel_id=1, source_target_pairs={{0,3},{1,2},{2,1},{3,0},{4,7},{5,6},{6,5},{7,4},{8,11},{9,10},{10,... | collective-permute-start | bytes 147464 | tf_op jit(solution)/shard_map/ppermute | solution.py:185
  9.2 2.6 %copy-start = (s32[1,6,8]{2,0,1:T(1,128)S(1)}, s32[1,6,8]{2,0,1:T(1,128)}, u32[]{:S(2)}) copy-start(s32[1,6,8]{2,0,1:T(1,128)} %param.9) | copy-start | bytes 580
  9.5 5.7 %collective-permute-start.6 = (bf16[6,8,2,128,128]{4,3,2,1,0:T(8,128)(2,1)S(1)}, bf16[6,8,2,128,128]{4,3,2,1,0:T(8,128)(2,1)S(1)}, u32[]{:S(2)}, u32[]{:S(2)}) collective-permute-start(bf16[6,8,2,128,128]{4,3,2,1,0:T(8,128)(2,1)S(1)} %get-tuple-element.27), channel_id=1, source_target_pairs={{0,1},{1,0},{2,3},{3,2},{4,5},{5,4},{6,7},{7,6},{8,9},{9,8},{10,11... | collective-permute-start | bytes 9437192 | tf_op jit(solution)/shard_map/ppermute | solution.py:185
  9.9 5.3 %collective-permute-start.4 = (bf16[16,1536]{1,0:T(8,128)(2,1)S(1)}, bf16[16,1536]{1,0:T(8,128)(2,1)S(1)}, u32[]{:S(2)}, u32[]{:S(2)}) collective-permute-start(bf16[16,1536]{1,0:T(8,128)(2,1)S(1)} %get-tuple-element.24.previous), channel_id=1, source_target_pairs={{0,4},{1,5},{2,6},{3,7},{4,8},{5,9},{6,10},{7,11},{8,12},{9,13},{1... | collective-permute-start | bytes 147464 | tf_op jit(solution)/shard_map/ppermute | solution.py:185
  9.9 5.3 %collective-permute-start.5 = (bf16[16,1536]{1,0:T(8,128)(2,1)S(1)}, bf16[16,1536]{1,0:T(8,128)(2,1)S(1)}, u32[]{:S(2)}, u32[]{:S(2)}) collective-permute-start(bf16[16,1536]{1,0:T(8,128)(2,1)S(1)} %get-tuple-element.24.previous), channel_id=1, source_target_pairs={{0,6},{1,7},{2,4},{3,5},{4,10},{5,11},{6,8},{7,9},{8,14},{9,15},{1... | collective-permute-start | bytes 147464 | tf_op jit(solution)/shard_map/ppermute | solution.py:185
  11.8 3.4 %collective-permute-start.7 = (s32[6,1,8]{2,1,0:T(1,128)S(1)}, s32[6,1,8]{2,1,0:T(1,128)S(1)}, u32[]{:S(2)}, u32[]{:S(2)}) collective-permute-start(s32[6,1,8]{2,1,0:T(1,128)S(1)} %bitcast.7), channel_id=1, source_target_pairs={{0,1},{1,0},{2,3},{3,2},{4,5},{5,4},{6,7},{7,6},{8,9},{9,8},{10,11... | collective-permute-start | bytes 584 | tf_op jit(solution)/shard_map/ppermute | solution.py:185
  15.3 5.8 %collective-permute-start.8 = (bf16[16,1536]{1,0:T(8,128)(2,1)S(1)}, bf16[16,1536]{1,0:T(8,128)(2,1)S(1)}, u32[]{:S(2)}, u32[]{:S(2)}) collective-permute-start(bf16[16,1536]{1,0:T(8,128)(2,1)S(1)} %step.4.previous), channel_id=1, source_target_pairs={{0,4},{1,5},{2,6},{3,7},{4,8},{5,9},{6,10},{7,11},{8,12},{9,13},{1... | collective-permute-start | bytes 147464 | tf_op jit(solution)/shard_map/ppermute | solution.py:185
  19.9 3.8 %collective-permute-start.9 = (bf16[16,1536]{1,0:T(8,128)(2,1)S(1)}, bf16[16,1536]{1,0:T(8,128)(2,1)S(1)}, u32[]{:S(2)}, u32[]{:S(2)}) collective-permute-start(bf16[16,1536]{1,0:T(8,128)(2,1)S(1)} %step.4.previous), channel_id=1, source_target_pairs={{0,6},{1,7},{2,4},{3,5},{4,10},{5,11},{6,8},{7,9},{8,14},{9,15},{1... | collective-permute-start | bytes 147464 | tf_op jit(solution)/shard_map/ppermute | solution.py:185
  23.7 3.6 %collective-permute-start.10 = (bf16[16,1536]{1,0:T(8,128)(2,1)S(1)}, bf16[16,1536]{1,0:T(8,128)(2,1)S(1)}, u32[]{:S(2)}, u32[]{:S(2)}) collective-permute-start(bf16[16,1536]{1,0:T(8,128)(2,1)S(1)} %step.5.previous), channel_id=1, source_target_pairs={{0,4},{1,5},{2,6},{3,7},{4,8},{5,9},{6,10},{7,11},{8,12},{9,13},{1... | collective-permute-start | bytes 147464 | tf_op jit(solution)/shard_map/ppermute | solution.py:185
  25.8 3.8 %collective-permute-start.11 = (bf16[16,1536]{1,0:T(8,128)(2,1)S(1)}, bf16[16,1536]{1,0:T(8,128)(2,1)S(1)}, u32[]{:S(2)}, u32[]{:S(2)}) collective-permute-start(bf16[16,1536]{1,0:T(8,128)(2,1)S(1)} %step.5.previous), channel_id=1, source_target_pairs={{0,6},{1,7},{2,4},{3,5},{4,10},{5,11},{6,8},{7,9},{8,14},{9,15},{1... | collective-permute-start | bytes 147464 | tf_op jit(solution)/shard_map/ppermute | solution.py:185
  29.7 4.2 %collective-permute-start.12 = (bf16[16,1536]{1,0:T(8,128)(2,1)S(1)}, bf16[16,1536]{1,0:T(8,128)(2,1)S(1)}, u32[]{:S(2)}, u32[]{:S(2)}) collective-permute-start(bf16[16,1536]{1,0:T(8,128)(2,1)S(1)} %step.6.previous), channel_id=1, source_target_pairs={{0,4},{1,5},{2,6},{3,7},{4,8},{5,9},{6,10},{7,11},{8,12},{9,13},{1... | collective-permute-start | bytes 147464 | tf_op jit(solution)/shard_map/ppermute | solution.py:185
  32.7 3.8 %collective-permute-start.13 = (bf16[16,1536]{1,0:T(8,128)(2,1)S(1)}, bf16[16,1536]{1,0:T(8,128)(2,1)S(1)}, u32[]{:S(2)}, u32[]{:S(2)}) collective-permute-start(bf16[16,1536]{1,0:T(8,128)(2,1)S(1)} %step.6.previous), channel_id=1, source_target_pairs={{0,6},{1,7},{2,4},{3,5},{4,10},{5,11},{6,8},{7,9},{8,14},{9,15},{1... | collective-permute-start | bytes 147464 | tf_op jit(solution)/shard_map/ppermute | solution.py:185
  39.6 6.5 %collective-permute-start.14 = (bf16[16,768]{1,0:T(8,128)(2,1)S(1)}, bf16[16,768]{1,0:T(8,128)(2,1)S(1)}, u32[]{:S(2)}, u32[]{:S(2)}) collective-permute-start(bf16[16,768]{1,0:T(8,128)(2,1)S(1)} %slice.4), channel_id=1, source_target_pairs={{0,1},{1,0},{2,3},{3,2},{4,5},{5,4},{6,7},{7,6},{8,9},{9,8},{10,11... | collective-permute-start | bytes 73736 | tf_op jit(solution)/shard_map/ppermute | solution.py:185

commit v6 on v5

--- a/solution.py
+++ b/solution.py
@@ -186,7 +186,22 @@
 
 
 def hop(value, source, offset):
-    return moved(value, 1, offset)
+    bays, secs = lax.axis_size("bay"), lax.axis_size("sec")
+    target = (source + 1) % bays
+    cycle = list(range(bays))
+    if bays > 3 and target > 0:
+        cycle = [source, target, source + 2]
+        if target == bays - 1:
+            cycle = [source, target, 0, 1]
+        elif target == 1:
+            cycle = [0, 1, 3, 2]
+    goes = {b: cycle[(n + 1) % len(cycle)] for n, b in enumerate(cycle)}
+    route = [
+        (b * secs + s, goes[b] * secs + (s ^ offset) if b in goes else b * secs + (s ^ 1))
+        for b in range(bays)
+        for s in range(secs)
+    ]
+    return lax.ppermute(value, ("bay", "sec"), route)
 
 
 def per_device(edge_load, interior_load, coupling, block_cols, transfer, local_inverse):

time: 46.9 us -> 46 us (0.981)
  the two profiles are of different devices: /device:TPU:29 before, /device:TPU:0 now
where the time goes in v6:
time: 46 us; the launch traced here: 45.9 us
  starting transfers between devices  18.4 us (40%)
  waiting for transfers between devices  17.1 us (37%)
  Pallas kernels  10.3 us (22%)
    ppermute x8, starting transfers between devices, hop(): return lax.ppermute(value, ('bay', 'sec'), route)  14.7 us
    ppermute x8, waiting for transfers between devices, hop(): return lax.ppermute(value, ('bay', 'sec'), route)  13.9 us
    ppermute x7, starting transfers between devices, moved(): return lax.ppermute(value, ('bay', 'sec'), route)  3.72 us
    pallas_call x1, Pallas kernels, per_device(): pl.pallas_call(transfer_kernel, out_shape=[pltpu.VMEM(matrices, bf16)] *...  3.45 us
    ppermute x7, waiting for transfers between devices, moved(): return lax.ppermute(value, ('bay', 'sec'), route)  3.17 us
    pallas_call x4, Pallas kernels, per_device(): pl.pallas_call(functools.partial(step_kernel, step), out_shape=jax.ShapeD...  3.07 us
    pallas_call x1, Pallas kernels, per_device(): pl.pallas_call(force_kernel, out_shape=[jax.ShapeDtypeStruct(wide, bf16)]...  2.82 us
  transfers between devices with their start and end apart: 15, of which 11 were waited for; matrix products, arithmetic and copies ran while one was open for 0% of the time, Pallas kernels for 8%

profile of v6, /device:TPU:0, one launch (start us, length us, event | category | flops | bytes accessed | tf_op | source)
XLA Modules:
  0.0 45.9 jit_solution(13968229550002062314)
XLA Ops:
  0.0 2.8 %force.1 = (bf16[16,1536]{1,0:T(8,128)(2,1)S(1)}, bf16[16,1536]{1,0:T(8,128)(2,1)S(1)}, bf16[16,1536]{1,0:T(8,128)(2,1)S(1)}, f32[16,1536]{1,0:T(8,128)S(1)}, bf...) custom-call(bf16[32,768]{1,0:T(8,128)(2,1)} %bitcast.15, bf16[32,768]{1,0:T(8,128)(2,1)} %bitcast.16, ...), custom_call_target="tpu_custom_call" | custom-call | tf_op jit(solution)/shard_map/force/pallas_call | solution.py:223
  2.8 0.5 %collective-permute-start.3 = (bf16[6,2,128,128]{3,2,1,0:T(8,128)(2,1)S(1)}, bf16[6,2,128,128]{3,2,1,0:T(8,128)(2,1)S(1)}, u32[]{:S(2)}, u32[]{:S(2)}) collective-permute-start(bf16[6,2,128,128]{3,2,1,0:T(8,128)(2,1)S(1)} %get-tuple-element.22), channel_id=1, source_target_pairs={{0,1},{1,0},{2,3},{3,2},{4,5},{5,4},{6,7},{7,6},{8,9},{9,8},{10,11... | collective-permute-start | bytes 1179656 | tf_op jit(solution)/shard_map/ppermute | solution.py:185
  3.3 0.1 collective-permute-start
  3.4 2.9 %collective-permute-start.1 = (bf16[16,1536]{1,0:T(8,128)(2,1)S(1)}, bf16[16,1536]{1,0:T(8,128)(2,1)S(1)}, u32[]{:S(2)}, u32[]{:S(2)}) collective-permute-start(bf16[16,1536]{1,0:T(8,128)(2,1)S(1)} %get-tuple-element.19), channel_id=1, source_target_pairs={{0,2},{1,3},{2,0},{3,1},{4,6},{5,7},{6,4},{7,5},{8,10},{9,11},{10,... | collective-permute-start | bytes 147464 | tf_op jit(solution)/shard_map/ppermute | solution.py:185
  6.3 0.0 collective-permute-start.2
  6.3 0.0 collective-permute-done.after.got1
  6.3 0.0 collective-permute-done.3.inverse_got
  6.4 3.4 %transfer.1 = (bf16[6,8,2,128,128]{4,3,2,1,0:T(8,128)(2,1)S(1)}, bf16[6,8,2,128,128]{4,3,2,1,0:T(8,128)(2,1)S(1)}, bf16[12,2,128,128]{3,2,1,0:T(8,128)(2,1)S(1)}) custom-call(bf16[6,8,4,128,128]{4,3,2,1,0:T(8,128)(2,1)} %bitcast.12, bf16[6,2,128,128]{3,2,1,0:T(8,128)(2,1)S(1)} %get-tuple-element.21.inverse_own, ...), custom_call_target="tpu_custom_call" | custom-call | tf_op jit(solution)/shard_map/transfer/pallas_call | solution.py:242
  9.8 0.0 copy-start
  9.8 0.0 collective-permute-done.1.got2
  9.8 0.5 %collective-permute-done.2.got3 = bf16[16,1536]{1,0:T(8,128)(2,1)S(1)} collective-permute-done((bf16[16,1536]{1,0:T(8,128)(2,1)S(1)}, bf16[16,1536]{1,0:T(8,128)(2,1)S(1)}, u32[]{:S(2)}, u32[]{:S(2)}) %collective-permute-start.2) | collective-permute-done | bytes 49184 | tf_op jit(solution)/shard_map/ppermute | solution.py:185
  10.4 0.3 initial.1
  10.7 0.1 collective-permute-start.6
  10.8 1.6 %collective-permute-start.4 = (bf16[16,1536]{1,0:T(8,128)(2,1)S(1)}, bf16[16,1536]{1,0:T(8,128)(2,1)S(1)}, u32[]{:S(2)}, u32[]{:S(2)}) collective-permute-start(bf16[16,1536]{1,0:T(8,128)(2,1)S(1)} %get-tuple-element.24.previous), channel_id=1, source_target_pairs={{0,4},{1,5},{2,6},{3,7},{4,8},{5,9},{6,10},{7,11},{8,12},{9,13},{1... | collective-permute-start | bytes 147464 | tf_op jit(solution)/shard_map/ppermute | solution.py:204
  12.4 2.5 %collective-permute-start.5 = (bf16[16,1536]{1,0:T(8,128)(2,1)S(1)}, bf16[16,1536]{1,0:T(8,128)(2,1)S(1)}, u32[]{:S(2)}, u32[]{:S(2)}) collective-permute-start(bf16[16,1536]{1,0:T(8,128)(2,1)S(1)} %get-tuple-element.24.previous), channel_id=1, source_target_pairs={{0,6},{1,7},{2,4},{3,5},{4,10},{5,11},{6,8},{7,9},{8,14},{9,15},{1... | collective-permute-start | bytes 147464 | tf_op jit(solution)/shard_map/ppermute | solution.py:204
  14.9 0.0 copy-done
  14.9 0.0 collective-permute-start.7
  14.9 1.4 %collective-permute-done.7.cols_got = s32[6,1,8]{2,1,0:T(1,128)S(1)} collective-permute-done((s32[6,1,8]{2,1,0:T(1,128)S(1)}, s32[6,1,8]{2,1,0:T(1,128)S(1)}, u32[]{:S(2)}, u32[]{:S(2)}) %collective-permute-start.7) | collective-permute-done | bytes 224 | tf_op jit(solution)/shard_map/ppermute | solution.py:185
  16.4 0.4 collective-permute-done.4.near
  16.7 2.5 %collective-permute-done.5.far = bf16[16,1536]{1,0:T(8,128)(2,1)S(1)} collective-permute-done((bf16[16,1536]{1,0:T(8,128)(2,1)S(1)}, bf16[16,1536]{1,0:T(8,128)(2,1)S(1)}, u32[]{:S(2)}, u32[]{:S(2)}) %collective-permute-start.5) | collective-permute-done | bytes 49184 | tf_op jit(solution)/shard_map/ppermute | solution.py:204
  19.2 0.0 collective-permute-done.6.transfer_got
  19.2 3.0 %step.4.previous = bf16[16,1536]{1,0:T(8,128)(2,1)S(1)} custom-call(bf16[16,1536]{1,0:T(8,128)(2,1)S(1)} %collective-permute-done.4.near, bf16[16,1536]{1,0:T(8,128)(2,1)S(1)} %collective-permute-done.5.far, bf16[16,1536]{1,0:T(8,128)(2,1)S(1)} %get-tuple-element.24.previous, f32[16,1536]{1,0:T(8,128)S(1)} %get-tuple-element.25.load, ...), custom_call_target="tpu_custom_call" | custom-call | tf_op jit(solution)/shard_map/step/pallas_call | solution.py:273
  22.2 0.1 collective-permute-start.8
  22.3 0.1 collective-permute-start.9
  22.4 4.9 %collective-permute-done.8.near = bf16[16,1536]{1,0:T(8,128)(2,1)S(1)} collective-permute-done((bf16[16,1536]{1,0:T(8,128)(2,1)S(1)}, bf16[16,1536]{1,0:T(8,128)(2,1)S(1)}, u32[]{:S(2)}, u32[]{:S(2)}) %collective-permute-start.8) | collective-permute-done | bytes 49184 | tf_op jit(solution)/shard_map/ppermute | solution.py:204
  27.3 1.4 %collective-permute-done.9.far = bf16[16,1536]{1,0:T(8,128)(2,1)S(1)} collective-permute-done((bf16[16,1536]{1,0:T(8,128)(2,1)S(1)}, bf16[16,1536]{1,0:T(8,128)(2,1)S(1)}, u32[]{:S(2)}, u32[]{:S(2)}) %collective-permute-start.9) | collective-permute-done | bytes 49184 | tf_op jit(solution)/shard_map/ppermute | solution.py:204
  28.7 0.1 collective-permute-start.10
  28.8 0.5 %collective-permute-start.11 = (bf16[16,1536]{1,0:T(8,128)(2,1)S(1)}, bf16[16,1536]{1,0:T(8,128)(2,1)S(1)}, u32[]{:S(2)}, u32[]{:S(2)}) collective-permute-start(bf16[16,1536]{1,0:T(8,128)(2,1)S(1)} %step.5.previous), channel_id=1, source_target_pairs={{0,1},{1,0},{2,3},{3,2},{4,10},{5,11},{6,8},{7,9},{8,14},{9,15},{1... | collective-permute-start | bytes 147464 | tf_op jit(solution)/shard_map/ppermute | solution.py:204
  29.3 0.7 %collective-permute-done.10.near = bf16[16,1536]{1,0:T(8,128)(2,1)S(1)} collective-permute-done((bf16[16,1536]{1,0:T(8,128)(2,1)S(1)}, bf16[16,1536]{1,0:T(8,128)(2,1)S(1)}, u32[]{:S(2)}, u32[]{:S(2)}) %collective-permute-start.10) | collective-permute-done | bytes 49184 | tf_op jit(solution)/shard_map/ppermute | solution.py:204
  30.0 0.2 collective-permute-done.11.far
  30.2 6.9 %collective-permute-start.12 = (bf16[16,1536]{1,0:T(8,128)(2,1)S(1)}, bf16[16,1536]{1,0:T(8,128)(2,1)S(1)}, u32[]{:S(2)}, u32[]{:S(2)}) collective-permute-start(bf16[16,1536]{1,0:T(8,128)(2,1)S(1)} %step.6.previous), channel_id=1, source_target_pairs={{0,4},{1,5},{2,6},{3,7},{4,8},{5,9},{6,10},{7,11},{8,12},{9,13},{1... | collective-permute-start | bytes 147464 | tf_op jit(solution)/shard_map/ppermute | solution.py:204
  37.2 2.9 %collective-permute-start.13 = (bf16[16,1536]{1,0:T(8,128)(2,1)S(1)}, bf16[16,1536]{1,0:T(8,128)(2,1)S(1)}, u32[]{:S(2)}, u32[]{:S(2)}) collective-permute-start(bf16[16,1536]{1,0:T(8,128)(2,1)S(1)} %step.6.previous), channel_id=1, source_target_pairs={{0,6},{1,7},{2,4},{3,5},{4,10},{5,11},{6,8},{7,9},{8,14},{9,15},{1... | collective-permute-start | bytes 147464 | tf_op jit(solution)/shard_map/ppermute | solution.py:204
  40.1 0.3 collective-permute-done.12.near
  40.4 3.6 %collective-permute-done.13.far = bf16[16,1536]{1,0:T(8,128)(2,1)S(1)} collective-permute-done((bf16[16,1536]{1,0:T(8,128)(2,1)S(1)}, bf16[16,1536]{1,0:T(8,128)(2,1)S(1)}, u32[]{:S(2)}, u32[]{:S(2)}) %collective-permute-start.13) | collective-permute-done | bytes 49184 | tf_op jit(solution)/shard_map/ppermute | solution.py:204
  44.0 0.1 collective-permute-start.14
  44.1 1.2 %collective-permute-done.14.got = bf16[16,768]{1,0:T(8,128)(2,1)S(1)} collective-permute-done((bf16[16,768]{1,0:T(8,128)(2,1)S(1)}, bf16[16,768]{1,0:T(8,128)(2,1)S(1)}, u32[]{:S(2)}, u32[]{:S(2)}) %collective-permute-start.14) | collective-permute-done | bytes 24608 | tf_op jit(solution)/shard_map/ppermute | solution.py:185
  45.2 0.6 %finish.1 = bf16[32,768]{1,0:T(8,128)(2,1)} custom-call(bf16[16,1536]{1,0:T(8,128)(2,1)S(1)} %step.7.state, bf16[16,768]{1,0:T(8,128)(2,1)S(1)} %collective-permute-done.14.got), custom_call_target="tpu_custom_call" | custom-call | tf_op jit(solution)/shard_map/finish/pallas_call | solution.py:288
  (4 shorter events, 0.1 us)
Async XLA Ops:
  2.8 3.5 %collective-permute-start.3 = (bf16[6,2,128,128]{3,2,1,0:T(8,128)(2,1)S(1)}, bf16[6,2,128,128]{3,2,1,0:T(8,128)(2,1)S(1)}, u32[]{:S(2)}, u32[]{:S(2)}) collective-permute-start(bf16[6,2,128,128]{3,2,1,0:T(8,128)(2,1)S(1)} %get-tuple-element.22), channel_id=1, source_target_pairs={{0,1},{1,0},{2,3},{3,2},{4,5},{5,4},{6,7},{7,6},{8,9},{9,8},{10,11... | collective-permute-start | bytes 1179656 | tf_op jit(solution)/shard_map/ppermute | solution.py:185
  3.3 3.0 %collective-permute-start = (bf16[16,1536]{1,0:T(8,128)(2,1)S(1)}, bf16[16,1536]{1,0:T(8,128)(2,1)S(1)}, u32[]{:S(2)}, u32[]{:S(2)}) collective-permute-start(bf16[16,1536]{1,0:T(8,128)(2,1)S(1)} %get-tuple-element.18), channel_id=1, source_target_pairs={{0,1},{1,0},{2,3},{3,2},{4,5},{5,4},{6,7},{7,6},{8,9},{9,8},{10,11... | collective-permute-start | bytes 147464 | tf_op jit(solution)/shard_map/ppermute | solution.py:185
  3.4 6.4 %collective-permute-start.1 = (bf16[16,1536]{1,0:T(8,128)(2,1)S(1)}, bf16[16,1536]{1,0:T(8,128)(2,1)S(1)}, u32[]{:S(2)}, u32[]{:S(2)}) collective-permute-start(bf16[16,1536]{1,0:T(8,128)(2,1)S(1)} %get-tuple-element.19), channel_id=1, source_target_pairs={{0,2},{1,3},{2,0},{3,1},{4,6},{5,7},{6,4},{7,5},{8,10},{9,11},{10,... | collective-permute-start | bytes 147464 | tf_op jit(solution)/shard_map/ppermute | solution.py:185
  6.3 4.0 %collective-permute-start.2 = (bf16[16,1536]{1,0:T(8,128)(2,1)S(1)}, bf16[16,1536]{1,0:T(8,128)(2,1)S(1)}, u32[]{:S(2)}, u32[]{:S(2)}) collective-permute-start(bf16[16,1536]{1,0:T(8,128)(2,1)S(1)} %get-tuple-element.20), channel_id=1, source_target_pairs={{0,3},{1,2},{2,1},{3,0},{4,7},{5,6},{6,5},{7,4},{8,11},{9,10},{10,... | collective-permute-start | bytes 147464 | tf_op jit(solution)/shard_map/ppermute | solution.py:185
  9.8 5.1 %copy-start = (s32[1,6,8]{2,0,1:T(1,128)S(1)}, s32[1,6,8]{2,0,1:T(1,128)}, u32[]{:S(2)}) copy-start(s32[1,6,8]{2,0,1:T(1,128)} %param.9) | copy-start | bytes 580
  10.7 8.6 %collective-permute-start.6 = (bf16[6,8,2,128,128]{4,3,2,1,0:T(8,128)(2,1)S(1)}, bf16[6,8,2,128,128]{4,3,2,1,0:T(8,128)(2,1)S(1)}, u32[]{:S(2)}, u32[]{:S(2)}) collective-permute-start(bf16[6,8,2,128,128]{4,3,2,1,0:T(8,128)(2,1)S(1)} %get-tuple-element.27), channel_id=1, source_target_pairs={{0,1},{1,0},{2,3},{3,2},{4,5},{5,4},{6,7},{7,6},{8,9},{9,8},{10,11... | collective-permute-start | bytes 9437192 | tf_op jit(solution)/shard_map/ppermute | solution.py:185
  10.8 5.9 %collective-permute-start.4 = (bf16[16,1536]{1,0:T(8,128)(2,1)S(1)}, bf16[16,1536]{1,0:T(8,128)(2,1)S(1)}, u32[]{:S(2)}, u32[]{:S(2)}) collective-permute-start(bf16[16,1536]{1,0:T(8,128)(2,1)S(1)} %get-tuple-element.24.previous), channel_id=1, source_target_pairs={{0,4},{1,5},{2,6},{3,7},{4,8},{5,9},{6,10},{7,11},{8,12},{9,13},{1... | collective-permute-start | bytes 147464 | tf_op jit(solution)/shard_map/ppermute | solution.py:204
  12.4 6.8 %collective-permute-start.5 = (bf16[16,1536]{1,0:T(8,128)(2,1)S(1)}, bf16[16,1536]{1,0:T(8,128)(2,1)S(1)}, u32[]{:S(2)}, u32[]{:S(2)}) collective-permute-start(bf16[16,1536]{1,0:T(8,128)(2,1)S(1)} %get-tuple-element.24.previous), channel_id=1, source_target_pairs={{0,6},{1,7},{2,4},{3,5},{4,10},{5,11},{6,8},{7,9},{8,14},{9,15},{1... | collective-permute-start | bytes 147464 | tf_op jit(solution)/shard_map/ppermute | solution.py:204
  14.9 1.5 %collective-permute-start.7 = (s32[6,1,8]{2,1,0:T(1,128)S(1)}, s32[6,1,8]{2,1,0:T(1,128)S(1)}, u32[]{:S(2)}, u32[]{:S(2)}) collective-permute-start(s32[6,1,8]{2,1,0:T(1,128)S(1)} %bitcast.7), channel_id=1, source_target_pairs={{0,1},{1,0},{2,3},{3,2},{4,5},{5,4},{6,7},{7,6},{8,9},{9,8},{10,11... | collective-permute-start | bytes 584 | tf_op jit(solution)/shard_map/ppermute | solution.py:185
  22.2 5.0 %collective-permute-start.8 = (bf16[16,1536]{1,0:T(8,128)(2,1)S(1)}, bf16[16,1536]{1,0:T(8,128)(2,1)S(1)}, u32[]{:S(2)}, u32[]{:S(2)}) collective-permute-start(bf16[16,1536]{1,0:T(8,128)(2,1)S(1)} %step.4.previous), channel_id=1, source_target_pairs={{0,4},{1,5},{2,6},{3,7},{4,12},{5,13},{6,14},{7,15},{8,0},{9,1},{1... | collective-permute-start | bytes 147464 | tf_op jit(solution)/shard_map/ppermute | solution.py:204
  22.3 6.4 %collective-permute-start.9 = (bf16[16,1536]{1,0:T(8,128)(2,1)S(1)}, bf16[16,1536]{1,0:T(8,128)(2,1)S(1)}, u32[]{:S(2)}, u32[]{:S(2)}) collective-permute-start(bf16[16,1536]{1,0:T(8,128)(2,1)S(1)} %step.4.previous), channel_id=1, source_target_pairs={{0,6},{1,7},{2,4},{3,5},{4,14},{5,15},{6,12},{7,13},{8,2},{9,3},{1... | collective-permute-start | bytes 147464 | tf_op jit(solution)/shard_map/ppermute | solution.py:204
  28.7 1.3 %collective-permute-start.10 = (bf16[16,1536]{1,0:T(8,128)(2,1)S(1)}, bf16[16,1536]{1,0:T(8,128)(2,1)S(1)}, u32[]{:S(2)}, u32[]{:S(2)}) collective-permute-start(bf16[16,1536]{1,0:T(8,128)(2,1)S(1)} %step.5.previous), channel_id=1, source_target_pairs={{0,1},{1,0},{2,3},{3,2},{4,8},{5,9},{6,10},{7,11},{8,12},{9,13},{1... | collective-permute-start | bytes 147464 | tf_op jit(solution)/shard_map/ppermute | solution.py:204
  28.8 1.4 %collective-permute-start.11 = (bf16[16,1536]{1,0:T(8,128)(2,1)S(1)}, bf16[16,1536]{1,0:T(8,128)(2,1)S(1)}, u32[]{:S(2)}, u32[]{:S(2)}) collective-permute-start(bf16[16,1536]{1,0:T(8,128)(2,1)S(1)} %step.5.previous), channel_id=1, source_target_pairs={{0,1},{1,0},{2,3},{3,2},{4,10},{5,11},{6,8},{7,9},{8,14},{9,15},{1... | collective-permute-start | bytes 147464 | tf_op jit(solution)/shard_map/ppermute | solution.py:204
  30.2 10.2 %collective-permute-start.12 = (bf16[16,1536]{1,0:T(8,128)(2,1)S(1)}, bf16[16,1536]{1,0:T(8,128)(2,1)S(1)}, u32[]{:S(2)}, u32[]{:S(2)}) collective-permute-start(bf16[16,1536]{1,0:T(8,128)(2,1)S(1)} %step.6.previous), channel_id=1, source_target_pairs={{0,4},{1,5},{2,6},{3,7},{4,8},{5,9},{6,10},{7,11},{8,12},{9,13},{1... | collective-permute-start | bytes 147464 | tf_op jit(solution)/shard_map/ppermute | solution.py:204
  37.2 6.8 %collective-permute-start.13 = (bf16[16,1536]{1,0:T(8,128)(2,1)S(1)}, bf16[16,1536]{1,0:T(8,128)(2,1)S(1)}, u32[]{:S(2)}, u32[]{:S(2)}) collective-permute-start(bf16[16,1536]{1,0:T(8,128)(2,1)S(1)} %step.6.previous), channel_id=1, source_target_pairs={{0,6},{1,7},{2,4},{3,5},{4,10},{5,11},{6,8},{7,9},{8,14},{9,15},{1... | collective-permute-start | bytes 147464 | tf_op jit(solution)/shard_map/ppermute | solution.py:204
  44.0 1.3 %collective-permute-start.14 = (bf16[16,768]{1,0:T(8,128)(2,1)S(1)}, bf16[16,768]{1,0:T(8,128)(2,1)S(1)}, u32[]{:S(2)}, u32[]{:S(2)}) collective-permute-start(bf16[16,768]{1,0:T(8,128)(2,1)S(1)} %slice.4), channel_id=1, source_target_pairs={{0,1},{1,0},{2,3},{3,2},{4,5},{5,4},{6,7},{7,6},{8,9},{9,8},{10,11... | collective-permute-start | bytes 73736 | tf_op jit(solution)/shard_map/ppermute | solution.py:185

commit v7 on v6

--- a/solution.py
+++ b/solution.py
@@ -117,7 +117,7 @@
 
 
 def step_kernel(
-    step, near, far, previous, load,
+    step, far, near, previous, load,
     transfer_own, transfer_got, inverse, cols_own, cols_got, out, state, ids, sems,
 ):
     part, nonzero, freqs, block, _ = transfer_own.shape
@@ -189,12 +189,10 @@
     bays, secs = lax.axis_size("bay"), lax.axis_size("sec")
     target = (source + 1) % bays
     cycle = list(range(bays))
-    if bays > 3 and target > 0:
-        cycle = [source, target, source + 2]
-        if target == bays - 1:
-            cycle = [source, target, 0, 1]
-        elif target == 1:
-            cycle = [0, 1, 3, 2]
+    if bays > 3 and target == 1:
+        cycle = [0, 1, 3, 2]
+    elif bays > 3 and target > 1:
+        cycle = [source, target, target + 1 if target + 1 < bays else source - 1]
     goes = {b: cycle[(n + 1) % len(cycle)] for n, b in enumerate(cycle)}
     route = [
         (b * secs + s, goes[b] * secs + (s ^ offset) if b in goes else b * secs + (s ^ 1))
@@ -269,7 +267,8 @@
 
     for step in range(bays):
         source = (step - 1) % bays
-        near, far = hop(state, source, 0), hop(state, source, 2)
+        far = hop(state, source, 2)
+        near = hop(state, source, 0)
         state = pl.pallas_call(
             functools.partial(step_kernel, step),
             out_shape=jax.ShapeDtypeStruct(wide, bf16),
@@ -282,7 +281,7 @@
             ],
             compiler_params=params,
             name="step",
-        )(near, far, state, load, transfer_own, transfer_got, turned, cols_own, cols_got)
+        )(far, near, state, load, transfer_own, transfer_got, turned, cols_own, cols_got)
 
     got = moved(state[:, width:], 0, 1)
     result = pl.pallas_call(

time: 46 us -> 43.6 us (0.948)
  the two profiles are of different devices: /device:TPU:0 before, /device:TPU:29 now
where the time goes in v7:
time: 43.6 us; the launch traced here: 43.5 us
  starting transfers between devices  23.7 us (54%)
  Pallas kernels  10.3 us (24%)
  waiting for transfers between devices  9.39 us (22%)
    ppermute x8, starting transfers between devices, hop(): return lax.ppermute(value, ('bay', 'sec'), route)  14.7 us
    ppermute x7, starting transfers between devices, moved(): return lax.ppermute(value, ('bay', 'sec'), route)  8.95 us
    ppermute x8, waiting for transfers between devices, hop(): return lax.ppermute(value, ('bay', 'sec'), route)  6.09 us
    pallas_call x1, Pallas kernels, per_device(): pl.pallas_call(transfer_kernel, out_shape=[pltpu.VMEM(matrices, bf16)] *...  3.44 us
    ppermute x7, waiting for transfers between devices, moved(): return lax.ppermute(value, ('bay', 'sec'), route)  3.3 us
    pallas_call x4, Pallas kernels, per_device(): pl.pallas_call(functools.partial(step_kernel, step), out_shape=jax.ShapeD...  3.09 us
    pallas_call x1, Pallas kernels, per_device(): pl.pallas_call(force_kernel, out_shape=[jax.ShapeDtypeStruct(wide, bf16)]...  2.82 us
  transfers between devices with their start and end apart: 15, of which 7 were waited for; matrix products, arithmetic and copies ran while one was open for 0% of the time, Pallas kernels for 8%

profile of v7, /device:TPU:29, one launch (start us, length us, event | category | flops | bytes accessed | tf_op | source)
XLA Modules:
  0.0 43.5 jit_solution(6357855799536023168)
XLA Ops:
  0.0 2.8 %force.1 = (bf16[16,1536]{1,0:T(8,128)(2,1)S(1)}, bf16[16,1536]{1,0:T(8,128)(2,1)S(1)}, bf16[16,1536]{1,0:T(8,128)(2,1)S(1)}, f32[16,1536]{1,0:T(8,128)S(1)}, bf...) custom-call(bf16[32,768]{1,0:T(8,128)(2,1)} %bitcast.15, bf16[32,768]{1,0:T(8,128)(2,1)} %bitcast.16, ...), custom_call_target="tpu_custom_call" | custom-call | tf_op jit(solution)/shard_map/force/pallas_call | solution.py:221
  2.8 0.7 %collective-permute-start.3 = (bf16[6,2,128,128]{3,2,1,0:T(8,128)(2,1)S(1)}, bf16[6,2,128,128]{3,2,1,0:T(8,128)(2,1)S(1)}, u32[]{:S(2)}, u32[]{:S(2)}) collective-permute-start(bf16[6,2,128,128]{3,2,1,0:T(8,128)(2,1)S(1)} %get-tuple-element.22), channel_id=1, source_target_pairs={{0,1},{1,0},{2,3},{3,2},{4,5},{5,4},{6,7},{7,6},{8,9},{9,8},{10,11... | collective-permute-start | bytes 1179656 | tf_op jit(solution)/shard_map/ppermute | solution.py:185
  3.6 0.1 collective-permute-start
  3.6 1.2 %collective-permute-start.1 = (bf16[16,1536]{1,0:T(8,128)(2,1)S(1)}, bf16[16,1536]{1,0:T(8,128)(2,1)S(1)}, u32[]{:S(2)}, u32[]{:S(2)}) collective-permute-start(bf16[16,1536]{1,0:T(8,128)(2,1)S(1)} %get-tuple-element.19), channel_id=1, source_target_pairs={{0,2},{1,3},{2,0},{3,1},{4,6},{5,7},{6,4},{7,5},{8,10},{9,11},{10,... | collective-permute-start | bytes 147464 | tf_op jit(solution)/shard_map/ppermute | solution.py:185
  4.9 0.9 %collective-permute-start.2 = (bf16[16,1536]{1,0:T(8,128)(2,1)S(1)}, bf16[16,1536]{1,0:T(8,128)(2,1)S(1)}, u32[]{:S(2)}, u32[]{:S(2)}) collective-permute-start(bf16[16,1536]{1,0:T(8,128)(2,1)S(1)} %get-tuple-element.20), channel_id=1, source_target_pairs={{0,3},{1,2},{2,1},{3,0},{4,7},{5,6},{6,5},{7,4},{8,11},{9,10},{10,... | collective-permute-start | bytes 147464 | tf_op jit(solution)/shard_map/ppermute | solution.py:185
  5.7 0.0 collective-permute-done.after.got1
  5.7 0.0 collective-permute-done.3.inverse_got
  5.7 3.4 %transfer.1 = (bf16[6,8,2,128,128]{4,3,2,1,0:T(8,128)(2,1)S(1)}, bf16[6,8,2,128,128]{4,3,2,1,0:T(8,128)(2,1)S(1)}, bf16[12,2,128,128]{3,2,1,0:T(8,128)(2,1)S(1)}) custom-call(bf16[6,8,4,128,128]{4,3,2,1,0:T(8,128)(2,1)} %bitcast.12, bf16[6,2,128,128]{3,2,1,0:T(8,128)(2,1)S(1)} %get-tuple-element.21.inverse_own, ...), custom_call_target="tpu_custom_call" | custom-call | tf_op jit(solution)/shard_map/transfer/pallas_call | solution.py:240
  9.2 0.0 copy-start
  9.2 0.0 collective-permute-done.1.got2
  9.2 0.0 collective-permute-done.2.got3
  9.2 0.3 initial.1
  9.5 0.4 collective-permute-start.6
  9.9 0.6 %collective-permute-start.4 = (bf16[16,1536]{1,0:T(8,128)(2,1)S(1)}, bf16[16,1536]{1,0:T(8,128)(2,1)S(1)}, u32[]{:S(2)}, u32[]{:S(2)}) collective-permute-start(bf16[16,1536]{1,0:T(8,128)(2,1)S(1)} %get-tuple-element.24.previous), channel_id=1, source_target_pairs={{0,6},{1,7},{2,4},{3,5},{4,10},{5,11},{6,8},{7,9},{8,14},{9,15},{1... | collective-permute-start | bytes 147464 | tf_op jit(solution)/shard_map/ppermute | solution.py:202
  10.5 1.3 %collective-permute-start.5 = (bf16[16,1536]{1,0:T(8,128)(2,1)S(1)}, bf16[16,1536]{1,0:T(8,128)(2,1)S(1)}, u32[]{:S(2)}, u32[]{:S(2)}) collective-permute-start(bf16[16,1536]{1,0:T(8,128)(2,1)S(1)} %get-tuple-element.24.previous), channel_id=1, source_target_pairs={{0,4},{1,5},{2,6},{3,7},{4,8},{5,9},{6,10},{7,11},{8,12},{9,13},{1... | collective-permute-start | bytes 147464 | tf_op jit(solution)/shard_map/ppermute | solution.py:202
  11.8 0.0 copy-done
  11.8 1.0 %collective-permute-start.7 = (s32[6,1,8]{2,1,0:T(1,128)S(1)}, s32[6,1,8]{2,1,0:T(1,128)S(1)}, u32[]{:S(2)}, u32[]{:S(2)}) collective-permute-start(s32[6,1,8]{2,1,0:T(1,128)S(1)} %bitcast.7), channel_id=1, source_target_pairs={{0,1},{1,0},{2,3},{3,2},{4,5},{5,4},{6,7},{7,6},{8,9},{9,8},{10,11... | collective-permute-start | bytes 584 | tf_op jit(solution)/shard_map/ppermute | solution.py:185
  12.8 2.4 %collective-permute-done.7.cols_got = s32[6,1,8]{2,1,0:T(1,128)S(1)} collective-permute-done((s32[6,1,8]{2,1,0:T(1,128)S(1)}, s32[6,1,8]{2,1,0:T(1,128)S(1)}, u32[]{:S(2)}, u32[]{:S(2)}) %collective-permute-start.7) | collective-permute-done | bytes 224 | tf_op jit(solution)/shard_map/ppermute | solution.py:185
  15.2 0.0 collective-permute-done.4.far
  15.2 0.0 collective-permute-done.5.near
  15.2 0.0 collective-permute-done.6.transfer_got
  15.3 1.1 %collective-permute-start.8 = (bf16[16,1536]{1,0:T(8,128)(2,1)S(1)}, bf16[16,1536]{1,0:T(8,128)(2,1)S(1)}, u32[]{:S(2)}, u32[]{:S(2)}) collective-permute-start(bf16[16,1536]{1,0:T(8,128)(2,1)S(1)} %step.4.previous), channel_id=1, source_target_pairs={{0,6},{1,7},{2,4},{3,5},{4,14},{5,15},{6,12},{7,13},{8,2},{9,3},{1... | collective-permute-start | bytes 147464 | tf_op jit(solution)/shard_map/ppermute | solution.py:202
  16.4 4.0 %collective-permute-start.9 = (bf16[16,1536]{1,0:T(8,128)(2,1)S(1)}, bf16[16,1536]{1,0:T(8,128)(2,1)S(1)}, u32[]{:S(2)}, u32[]{:S(2)}) collective-permute-start(bf16[16,1536]{1,0:T(8,128)(2,1)S(1)} %step.4.previous), channel_id=1, source_target_pairs={{0,4},{1,5},{2,6},{3,7},{4,12},{5,13},{6,14},{7,15},{8,0},{9,1},{1... | collective-permute-start | bytes 147464 | tf_op jit(solution)/shard_map/ppermute | solution.py:202
  20.5 0.0 collective-permute-done.8.far
  20.5 1.2 %collective-permute-done.9.near = bf16[16,1536]{1,0:T(8,128)(2,1)S(1)} collective-permute-done((bf16[16,1536]{1,0:T(8,128)(2,1)S(1)}, bf16[16,1536]{1,0:T(8,128)(2,1)S(1)}, u32[]{:S(2)}, u32[]{:S(2)}) %collective-permute-start.9) | collective-permute-done | bytes 49184 | tf_op jit(solution)/shard_map/ppermute | solution.py:202
  21.7 3.9 %collective-permute-start.10 = (bf16[16,1536]{1,0:T(8,128)(2,1)S(1)}, bf16[16,1536]{1,0:T(8,128)(2,1)S(1)}, u32[]{:S(2)}, u32[]{:S(2)}) collective-permute-start(bf16[16,1536]{1,0:T(8,128)(2,1)S(1)} %step.5.previous), channel_id=1, source_target_pairs={{0,1},{1,0},{2,3},{3,2},{4,10},{5,11},{6,8},{7,9},{8,14},{9,15},{1... | collective-permute-start | bytes 147464 | tf_op jit(solution)/shard_map/ppermute | solution.py:202
  25.5 0.0 collective-permute-start.11
  25.5 1.2 %collective-permute-done.10.far = bf16[16,1536]{1,0:T(8,128)(2,1)S(1)} collective-permute-done((bf16[16,1536]{1,0:T(8,128)(2,1)S(1)}, bf16[16,1536]{1,0:T(8,128)(2,1)S(1)}, u32[]{:S(2)}, u32[]{:S(2)}) %collective-permute-start.10) | collective-permute-done | bytes 49184 | tf_op jit(solution)/shard_map/ppermute | solution.py:202
  26.7 2.6 %collective-permute-done.11.near = bf16[16,1536]{1,0:T(8,128)(2,1)S(1)} collective-permute-done((bf16[16,1536]{1,0:T(8,128)(2,1)S(1)}, bf16[16,1536]{1,0:T(8,128)(2,1)S(1)}, u32[]{:S(2)}, u32[]{:S(2)}) %collective-permute-start.11) | collective-permute-done | bytes 49184 | tf_op jit(solution)/shard_map/ppermute | solution.py:202
  29.3 1.1 %collective-permute-start.12 = (bf16[16,1536]{1,0:T(8,128)(2,1)S(1)}, bf16[16,1536]{1,0:T(8,128)(2,1)S(1)}, u32[]{:S(2)}, u32[]{:S(2)}) collective-permute-start(bf16[16,1536]{1,0:T(8,128)(2,1)S(1)} %step.6.previous), channel_id=1, source_target_pairs={{0,1},{1,0},{2,3},{3,2},{4,10},{5,11},{6,8},{7,9},{8,14},{9,15},{1... | collective-permute-start | bytes 147464 | tf_op jit(solution)/shard_map/ppermute | solution.py:202
  30.4 2.7 %collective-permute-start.13 = (bf16[16,1536]{1,0:T(8,128)(2,1)S(1)}, bf16[16,1536]{1,0:T(8,128)(2,1)S(1)}, u32[]{:S(2)}, u32[]{:S(2)}) collective-permute-start(bf16[16,1536]{1,0:T(8,128)(2,1)S(1)} %step.6.previous), channel_id=1, source_target_pairs={{0,1},{1,0},{2,3},{3,2},{4,8},{5,9},{6,10},{7,11},{8,12},{9,13},{1... | collective-permute-start | bytes 147464 | tf_op jit(solution)/shard_map/ppermute | solution.py:202
  33.2 0.3 collective-permute-done.12.far
  33.5 0.9 %collective-permute-done.13.near = bf16[16,1536]{1,0:T(8,128)(2,1)S(1)} collective-permute-done((bf16[16,1536]{1,0:T(8,128)(2,1)S(1)}, bf16[16,1536]{1,0:T(8,128)(2,1)S(1)}, u32[]{:S(2)}, u32[]{:S(2)}) %collective-permute-start.13) | collective-permute-done | bytes 49184 | tf_op jit(solution)/shard_map/ppermute | solution.py:202
  34.3 3.0 %step.7.state = bf16[16,1536]{1,0:T(8,128)(2,1)S(1)} custom-call(bf16[16,1536]{1,0:T(8,128)(2,1)S(1)} %collective-permute-done.12.far, bf16[16,1536]{1,0:T(8,128)(2,1)S(1)} %collective-permute-done.13.near, bf16[16,1536]{1,0:T(8,128)(2,1)S(1)} %step.6.previous, f32[16,1536]{1,0:T(8,128)S(1)} %get-tuple-element.25.load, ...), custom_call_target="tpu_custom_call" | custom-call | tf_op jit(solution)/shard_map/step/pallas_call | solution.py:272
  37.4 4.6 %collective-permute-start.14 = (bf16[16,768]{1,0:T(8,128)(2,1)S(1)}, bf16[16,768]{1,0:T(8,128)(2,1)S(1)}, u32[]{:S(2)}, u32[]{:S(2)}) collective-permute-start(bf16[16,768]{1,0:T(8,128)(2,1)S(1)} %slice.4), channel_id=1, source_target_pairs={{0,1},{1,0},{2,3},{3,2},{4,5},{5,4},{6,7},{7,6},{8,9},{9,8},{10,11... | collective-permute-start | bytes 73736 | tf_op jit(solution)/shard_map/ppermute | solution.py:185
  42.0 0.8 %collective-permute-done.14.got = bf16[16,768]{1,0:T(8,128)(2,1)S(1)} collective-permute-done((bf16[16,768]{1,0:T(8,128)(2,1)S(1)}, bf16[16,768]{1,0:T(8,128)(2,1)S(1)}, u32[]{:S(2)}, u32[]{:S(2)}) %collective-permute-start.14) | collective-permute-done | bytes 24608 | tf_op jit(solution)/shard_map/ppermute | solution.py:185
  42.8 0.6 %finish.1 = bf16[32,768]{1,0:T(8,128)(2,1)} custom-call(bf16[16,1536]{1,0:T(8,128)(2,1)S(1)} %step.7.state, bf16[16,768]{1,0:T(8,128)(2,1)S(1)} %collective-permute-done.14.got), custom_call_target="tpu_custom_call" | custom-call | tf_op jit(solution)/shard_map/finish/pallas_call | solution.py:287
  (4 shorter events, 0.1 us)
Async XLA Ops:
  2.8 2.9 %collective-permute-start.3 = (bf16[6,2,128,128]{3,2,1,0:T(8,128)(2,1)S(1)}, bf16[6,2,128,128]{3,2,1,0:T(8,128)(2,1)S(1)}, u32[]{:S(2)}, u32[]{:S(2)}) collective-permute-start(bf16[6,2,128,128]{3,2,1,0:T(8,128)(2,1)S(1)} %get-tuple-element.22), channel_id=1, source_target_pairs={{0,1},{1,0},{2,3},{3,2},{4,5},{5,4},{6,7},{7,6},{8,9},{9,8},{10,11... | collective-permute-start | bytes 1179656 | tf_op jit(solution)/shard_map/ppermute | solution.py:185
  3.6 2.1 %collective-permute-start = (bf16[16,1536]{1,0:T(8,128)(2,1)S(1)}, bf16[16,1536]{1,0:T(8,128)(2,1)S(1)}, u32[]{:S(2)}, u32[]{:S(2)}) collective-permute-start(bf16[16,1536]{1,0:T(8,128)(2,1)S(1)} %get-tuple-element.18), channel_id=1, source_target_pairs={{0,1},{1,0},{2,3},{3,2},{4,5},{5,4},{6,7},{7,6},{8,9},{9,8},{10,11... | collective-permute-start | bytes 147464 | tf_op jit(solution)/shard_map/ppermute | solution.py:185
  3.6 5.5 %collective-permute-start.1 = (bf16[16,1536]{1,0:T(8,128)(2,1)S(1)}, bf16[16,1536]{1,0:T(8,128)(2,1)S(1)}, u32[]{:S(2)}, u32[]{:S(2)}) collective-permute-start(bf16[16,1536]{1,0:T(8,128)(2,1)S(1)} %get-tuple-element.19), channel_id=1, source_target_pairs={{0,2},{1,3},{2,0},{3,1},{4,6},{5,7},{6,4},{7,5},{8,10},{9,11},{10,... | collective-permute-start | bytes 147464 | tf_op jit(solution)/shard_map/ppermute | solution.py:185
  4.9 4.3 %collective-permute-start.2 = (bf16[16,1536]{1,0:T(8,128)(2,1)S(1)}, bf16[16,1536]{1,0:T(8,128)(2,1)S(1)}, u32[]{:S(2)}, u32[]{:S(2)}) collective-permute-start(bf16[16,1536]{1,0:T(8,128)(2,1)S(1)} %get-tuple-element.20), channel_id=1, source_target_pairs={{0,3},{1,2},{2,1},{3,0},{4,7},{5,6},{6,5},{7,4},{8,11},{9,10},{10,... | collective-permute-start | bytes 147464 | tf_op jit(solution)/shard_map/ppermute | solution.py:185
  9.2 2.6 %copy-start = (s32[1,6,8]{2,0,1:T(1,128)S(1)}, s32[1,6,8]{2,0,1:T(1,128)}, u32[]{:S(2)}) copy-start(s32[1,6,8]{2,0,1:T(1,128)} %param.9) | copy-start | bytes 580
  9.5 5.7 %collective-permute-start.6 = (bf16[6,8,2,128,128]{4,3,2,1,0:T(8,128)(2,1)S(1)}, bf16[6,8,2,128,128]{4,3,2,1,0:T(8,128)(2,1)S(1)}, u32[]{:S(2)}, u32[]{:S(2)}) collective-permute-start(bf16[6,8,2,128,128]{4,3,2,1,0:T(8,128)(2,1)S(1)} %get-tuple-element.27), channel_id=1, source_target_pairs={{0,1},{1,0},{2,3},{3,2},{4,5},{5,4},{6,7},{7,6},{8,9},{9,8},{10,11... | collective-permute-start | bytes 9437192 | tf_op jit(solution)/shard_map/ppermute | solution.py:185
  9.9 5.3 %collective-permute-start.4 = (bf16[16,1536]{1,0:T(8,128)(2,1)S(1)}, bf16[16,1536]{1,0:T(8,128)(2,1)S(1)}, u32[]{:S(2)}, u32[]{:S(2)}) collective-permute-start(bf16[16,1536]{1,0:T(8,128)(2,1)S(1)} %get-tuple-element.24.previous), channel_id=1, source_target_pairs={{0,6},{1,7},{2,4},{3,5},{4,10},{5,11},{6,8},{7,9},{8,14},{9,15},{1... | collective-permute-start | bytes 147464 | tf_op jit(solution)/shard_map/ppermute | solution.py:202
  10.5 4.7 %collective-permute-start.5 = (bf16[16,1536]{1,0:T(8,128)(2,1)S(1)}, bf16[16,1536]{1,0:T(8,128)(2,1)S(1)}, u32[]{:S(2)}, u32[]{:S(2)}) collective-permute-start(bf16[16,1536]{1,0:T(8,128)(2,1)S(1)} %get-tuple-element.24.previous), channel_id=1, source_target_pairs={{0,4},{1,5},{2,6},{3,7},{4,8},{5,9},{6,10},{7,11},{8,12},{9,13},{1... | collective-permute-start | bytes 147464 | tf_op jit(solution)/shard_map/ppermute | solution.py:202
  11.8 3.4 %collective-permute-start.7 = (s32[6,1,8]{2,1,0:T(1,128)S(1)}, s32[6,1,8]{2,1,0:T(1,128)S(1)}, u32[]{:S(2)}, u32[]{:S(2)}) collective-permute-start(s32[6,1,8]{2,1,0:T(1,128)S(1)} %bitcast.7), channel_id=1, source_target_pairs={{0,1},{1,0},{2,3},{3,2},{4,5},{5,4},{6,7},{7,6},{8,9},{9,8},{10,11... | collective-permute-start | bytes 584 | tf_op jit(solution)/shard_map/ppermute | solution.py:185
  15.3 5.2 %collective-permute-start.8 = (bf16[16,1536]{1,0:T(8,128)(2,1)S(1)}, bf16[16,1536]{1,0:T(8,128)(2,1)S(1)}, u32[]{:S(2)}, u32[]{:S(2)}) collective-permute-start(bf16[16,1536]{1,0:T(8,128)(2,1)S(1)} %step.4.previous), channel_id=1, source_target_pairs={{0,6},{1,7},{2,4},{3,5},{4,14},{5,15},{6,12},{7,13},{8,2},{9,3},{1... | collective-permute-start | bytes 147464 | tf_op jit(solution)/shard_map/ppermute | solution.py:202
  16.4 5.2 %collective-permute-start.9 = (bf16[16,1536]{1,0:T(8,128)(2,1)S(1)}, bf16[16,1536]{1,0:T(8,128)(2,1)S(1)}, u32[]{:S(2)}, u32[]{:S(2)}) collective-permute-start(bf16[16,1536]{1,0:T(8,128)(2,1)S(1)} %step.4.previous), channel_id=1, source_target_pairs={{0,4},{1,5},{2,6},{3,7},{4,12},{5,13},{6,14},{7,15},{8,0},{9,1},{1... | collective-permute-start | bytes 147464 | tf_op jit(solution)/shard_map/ppermute | solution.py:202
  21.7 5.0 %collective-permute-start.10 = (bf16[16,1536]{1,0:T(8,128)(2,1)S(1)}, bf16[16,1536]{1,0:T(8,128)(2,1)S(1)}, u32[]{:S(2)}, u32[]{:S(2)}) collective-permute-start(bf16[16,1536]{1,0:T(8,128)(2,1)S(1)} %step.5.previous), channel_id=1, source_target_pairs={{0,1},{1,0},{2,3},{3,2},{4,10},{5,11},{6,8},{7,9},{8,14},{9,15},{1... | collective-permute-start | bytes 147464 | tf_op jit(solution)/shard_map/ppermute | solution.py:202
  25.5 3.7 %collective-permute-start.11 = (bf16[16,1536]{1,0:T(8,128)(2,1)S(1)}, bf16[16,1536]{1,0:T(8,128)(2,1)S(1)}, u32[]{:S(2)}, u32[]{:S(2)}) collective-permute-start(bf16[16,1536]{1,0:T(8,128)(2,1)S(1)} %step.5.previous), channel_id=1, source_target_pairs={{0,1},{1,0},{2,3},{3,2},{4,8},{5,9},{6,10},{7,11},{8,12},{9,13},{1... | collective-permute-start | bytes 147464 | tf_op jit(solution)/shard_map/ppermute | solution.py:202
  29.3 4.2 %collective-permute-start.12 = (bf16[16,1536]{1,0:T(8,128)(2,1)S(1)}, bf16[16,1536]{1,0:T(8,128)(2,1)S(1)}, u32[]{:S(2)}, u32[]{:S(2)}) collective-permute-start(bf16[16,1536]{1,0:T(8,128)(2,1)S(1)} %step.6.previous), channel_id=1, source_target_pairs={{0,1},{1,0},{2,3},{3,2},{4,10},{5,11},{6,8},{7,9},{8,14},{9,15},{1... | collective-permute-start | bytes 147464 | tf_op jit(solution)/shard_map/ppermute | solution.py:202
  30.4 3.9 %collective-permute-start.13 = (bf16[16,1536]{1,0:T(8,128)(2,1)S(1)}, bf16[16,1536]{1,0:T(8,128)(2,1)S(1)}, u32[]{:S(2)}, u32[]{:S(2)}) collective-permute-start(bf16[16,1536]{1,0:T(8,128)(2,1)S(1)} %step.6.previous), channel_id=1, source_target_pairs={{0,1},{1,0},{2,3},{3,2},{4,8},{5,9},{6,10},{7,11},{8,12},{9,13},{1... | collective-permute-start | bytes 147464 | tf_op jit(solution)/shard_map/ppermute | solution.py:202
  37.4 5.5 %collective-permute-start.14 = (bf16[16,768]{1,0:T(8,128)(2,1)S(1)}, bf16[16,768]{1,0:T(8,128)(2,1)S(1)}, u32[]{:S(2)}, u32[]{:S(2)}) collective-permute-start(bf16[16,768]{1,0:T(8,128)(2,1)S(1)} %slice.4), channel_id=1, source_target_pairs={{0,1},{1,0},{2,3},{3,2},{4,5},{5,4},{6,7},{7,6},{8,9},{9,8},{10,11... | collective-permute-start | bytes 73736 | tf_op jit(solution)/shard_map/ppermute | solution.py:185

commit v8 on v7

--- a/solution.py
+++ b/solution.py
@@ -117,7 +117,7 @@
 
 
 def step_kernel(
-    step, far, near, previous, load,
+    step, chosen, far, near, previous, load,
     transfer_own, transfer_got, inverse, cols_own, cols_got, out, state, ids, sems,
 ):
     part, nonzero, freqs, block, _ = transfer_own.shape
@@ -139,8 +139,9 @@
                 state[home] = source[:, r * block:(r + 1) * block]
         for copy in copies:
             copy.wait()
-        for r in range(rows):
+        for r in chosen:
             cols = slice(r * block, (r + 1) * block)
+            goal = slice((r - chosen[0]) * block, (r - chosen[0] + 1) * block)
             transfer = transfer_own if r < part else transfer_got
             picked = jnp.concatenate([state[ids[r // part, r % part, 0, k]] for k in range(nonzero)], axis=1)
             matrix = jnp.concatenate(
@@ -149,25 +150,25 @@
             )
             summed = (load[:, cols] + diagonal(nn_dot(picked, matrix), freqs)).astype(jnp.bfloat16)
             solved = nn_dot(summed, jnp.concatenate([inverse[r, f] for f in range(freqs)], axis=1))
-            out[:, cols] = diagonal(solved, freqs).astype(jnp.bfloat16)
+            out[:, goal] = diagonal(solved, freqs).astype(jnp.bfloat16)
 
     @pl.when(bay != step)
     def _():
-        out[...] = previous[...]
-
-
-def finish_kernel(state, got, out):
+        out[...] = previous[:, chosen[0] * block:(chosen[-1] + 1) * block]
+
+
+def finish_kernel(kept, got, out):
     lines, width = got.shape
     odd = (lax.axis_index("sec") & 1) == 1
 
     @pl.when(odd)
     def _():
         out[:lines] = got[...]
-        out[lines:] = state[:, :width]
+        out[lines:] = kept[...]
 
     @pl.when(jnp.logical_not(odd))
     def _():
-        out[:lines] = state[:, :width]
+        out[:lines] = kept[...]
         out[lines:] = got[...]
 
 
@@ -265,13 +266,10 @@
     )(own, got1, got2, got3, inverse_own, inverse_got, transfer_out)
     transfer_got = moved(transfer_out, 0, 1)
 
-    for step in range(bays):
-        source = (step - 1) % bays
-        far = hop(state, source, 2)
-        near = hop(state, source, 0)
-        state = pl.pallas_call(
-            functools.partial(step_kernel, step),
-            out_shape=jax.ShapeDtypeStruct(wide, bf16),
+    def advance(step, chosen, far, near, state):
+        return pl.pallas_call(
+            functools.partial(step_kernel, step, chosen),
+            out_shape=jax.ShapeDtypeStruct((lines, len(chosen) * block), bf16),
             in_specs=[VMEM] * 9,
             out_specs=VMEM,
             scratch_shapes=[
@@ -283,7 +281,14 @@
             name="step",
         )(far, near, state, load, transfer_own, transfer_got, turned, cols_own, cols_got)
 
-    got = moved(state[:, width:], 0, 1)
+    for step in range(bays):
+        source = (step - 1) % bays
+        far = hop(state, source, 2)
+        near = hop(state, source, 0)
+        if step + 1 < bays:
+            state = advance(step, range(2 * rows), far, near, state)
+    got = moved(advance(bays - 1, range(rows, 2 * rows), far, near, state), 0, 1)
+    kept = advance(bays - 1, range(rows), far, near, state)
     result = pl.pallas_call(
         finish_kernel,
         out_shape=jax.ShapeDtypeStruct((2 * lines, width), bf16),
@@ -291,7 +296,7 @@
         out_specs=VMEM,
         compiler_params=params,
         name="finish",
-    )(state, got)
+    )(kept, got)
     return result.reshape(1, freqs, cases, width)
 
 

time: 43.6 us -> 43.6 us (level)
  waiting for transfers between devices: 9.39 us -> 8.54 us
  Pallas kernels: 10.3 us -> 11.1 us
    ppermute x7, waiting for transfers between devices: 3.3 us -> 2.45 us  [moved(): return lax.ppermute(value, ('bay', 'sec'), route)]
    pallas_call x4 -> x5, Pallas kernels: 3.09 us -> 3.85 us  [advance(): pl.pallas_call(functools.partial(step_kernel, step, chosen), out_shape=ja...]
  transfers between devices with their start and end apart: 15 -> 15, of which waited for: 7 -> 6; matrix products, arithmetic and copies ran while one was open for 0% -> 0% of each run, Pallas kernels for 8% -> 12%
where the time goes in v8:
time: 43.6 us; the launch traced here: 43.4 us
  starting transfers between devices  23.7 us (54%)
  Pallas kernels  11.1 us (25%)
  waiting for transfers between devices  8.54 us (20%)
    ppermute x8, starting transfers between devices, hop(): return lax.ppermute(value, ('bay', 'sec'), route)  14.7 us
    ppermute x7, starting transfers between devices, moved(): return lax.ppermute(value, ('bay', 'sec'), route)  8.95 us
    ppermute x8, waiting for transfers between devices, hop(): return lax.ppermute(value, ('bay', 'sec'), route)  6.09 us
    pallas_call x5, Pallas kernels, advance(): pl.pallas_call(functools.partial(step_kernel, step, chosen), out_shape=ja...  3.85 us
    pallas_call x1, Pallas kernels, per_device(): pl.pallas_call(transfer_kernel, out_shape=[pltpu.VMEM(matrices, bf16)] *...  3.44 us
    pallas_call x1, Pallas kernels, per_device(): pl.pallas_call(force_kernel, out_shape=[jax.ShapeDtypeStruct(wide, bf16)]...  2.82 us
    ppermute x7, waiting for transfers between devices, moved(): return lax.ppermute(value, ('bay', 'sec'), route)  2.45 us
  transfers between devices with their start and end apart: 15, of which 6 were waited for; matrix products, arithmetic and copies ran while one was open for 0% of the time, Pallas kernels for 12%

profile of v8, /device:TPU:29, one launch (start us, length us, event | category | flops | bytes accessed | tf_op | source)
XLA Modules:
  0.0 43.4 jit_solution(17208025233734717967)
XLA Ops:
  0.0 2.8 %force.1 = (bf16[16,1536]{1,0:T(8,128)(2,1)S(1)}, bf16[16,1536]{1,0:T(8,128)(2,1)S(1)}, bf16[16,1536]{1,0:T(8,128)(2,1)S(1)}, f32[16,1536]{1,0:T(8,128)S(1)}, bf...) custom-call(bf16[32,768]{1,0:T(8,128)(2,1)} %bitcast.16, bf16[32,768]{1,0:T(8,128)(2,1)} %bitcast.17, ...), custom_call_target="tpu_custom_call" | custom-call | tf_op jit(solution)/shard_map/force/pallas_call | solution.py:222
  2.8 0.7 %collective-permute-start.3 = (bf16[6,2,128,128]{3,2,1,0:T(8,128)(2,1)S(1)}, bf16[6,2,128,128]{3,2,1,0:T(8,128)(2,1)S(1)}, u32[]{:S(2)}, u32[]{:S(2)}) collective-permute-start(bf16[6,2,128,128]{3,2,1,0:T(8,128)(2,1)S(1)} %get-tuple-element.22), channel_id=1, source_target_pairs={{0,1},{1,0},{2,3},{3,2},{4,5},{5,4},{6,7},{7,6},{8,9},{9,8},{10,11... | collective-permute-start | bytes 1179656 | tf_op jit(solution)/shard_map/ppermute | solution.py:186
  3.6 0.1 collective-permute-start
  3.6 1.2 %collective-permute-start.1 = (bf16[16,1536]{1,0:T(8,128)(2,1)S(1)}, bf16[16,1536]{1,0:T(8,128)(2,1)S(1)}, u32[]{:S(2)}, u32[]{:S(2)}) collective-permute-start(bf16[16,1536]{1,0:T(8,128)(2,1)S(1)} %get-tuple-element.19), channel_id=1, source_target_pairs={{0,2},{1,3},{2,0},{3,1},{4,6},{5,7},{6,4},{7,5},{8,10},{9,11},{10,... | collective-permute-start | bytes 147464 | tf_op jit(solution)/shard_map/ppermute | solution.py:186
  4.9 0.9 %collective-permute-start.2 = (bf16[16,1536]{1,0:T(8,128)(2,1)S(1)}, bf16[16,1536]{1,0:T(8,128)(2,1)S(1)}, u32[]{:S(2)}, u32[]{:S(2)}) collective-permute-start(bf16[16,1536]{1,0:T(8,128)(2,1)S(1)} %get-tuple-element.20), channel_id=1, source_target_pairs={{0,3},{1,2},{2,1},{3,0},{4,7},{5,6},{6,5},{7,4},{8,11},{9,10},{10,... | collective-permute-start | bytes 147464 | tf_op jit(solution)/shard_map/ppermute | solution.py:186
  5.7 0.0 collective-permute-done.after.got1
  5.7 0.0 collective-permute-done.3.inverse_got
  5.7 3.4 %transfer.1 = (bf16[6,8,2,128,128]{4,3,2,1,0:T(8,128)(2,1)S(1)}, bf16[6,8,2,128,128]{4,3,2,1,0:T(8,128)(2,1)S(1)}, bf16[12,2,128,128]{3,2,1,0:T(8,128)(2,1)S(1)}) custom-call(bf16[6,8,4,128,128]{4,3,2,1,0:T(8,128)(2,1)} %bitcast.13, bf16[6,2,128,128]{3,2,1,0:T(8,128)(2,1)S(1)} %get-tuple-element.21.inverse_own, ...), custom_call_target="tpu_custom_call" | custom-call | tf_op jit(solution)/shard_map/transfer/pallas_call | solution.py:241
  9.2 0.0 copy-start
  9.2 0.0 collective-permute-done.1.got2
  9.2 0.0 collective-permute-done.2.got3
  9.2 0.3 initial.1
  9.5 0.4 collective-permute-start.6
  9.9 0.6 %collective-permute-start.4 = (bf16[16,1536]{1,0:T(8,128)(2,1)S(1)}, bf16[16,1536]{1,0:T(8,128)(2,1)S(1)}, u32[]{:S(2)}, u32[]{:S(2)}) collective-permute-start(bf16[16,1536]{1,0:T(8,128)(2,1)S(1)} %get-tuple-element.24.previous), channel_id=1, source_target_pairs={{0,6},{1,7},{2,4},{3,5},{4,10},{5,11},{6,8},{7,9},{8,14},{9,15},{1... | collective-permute-start | bytes 147464 | tf_op jit(solution)/shard_map/ppermute | solution.py:203
  10.5 1.3 %collective-permute-start.5 = (bf16[16,1536]{1,0:T(8,128)(2,1)S(1)}, bf16[16,1536]{1,0:T(8,128)(2,1)S(1)}, u32[]{:S(2)}, u32[]{:S(2)}) collective-permute-start(bf16[16,1536]{1,0:T(8,128)(2,1)S(1)} %get-tuple-element.24.previous), channel_id=1, source_target_pairs={{0,4},{1,5},{2,6},{3,7},{4,8},{5,9},{6,10},{7,11},{8,12},{9,13},{1... | collective-permute-start | bytes 147464 | tf_op jit(solution)/shard_map/ppermute | solution.py:203
  11.8 0.0 copy-done
  11.8 1.0 %collective-permute-start.7 = (s32[6,1,8]{2,1,0:T(1,128)S(1)}, s32[6,1,8]{2,1,0:T(1,128)S(1)}, u32[]{:S(2)}, u32[]{:S(2)}) collective-permute-start(s32[6,1,8]{2,1,0:T(1,128)S(1)} %bitcast.7), channel_id=1, source_target_pairs={{0,1},{1,0},{2,3},{3,2},{4,5},{5,4},{6,7},{7,6},{8,9},{9,8},{10,11... | collective-permute-start | bytes 584 | tf_op jit(solution)/shard_map/ppermute | solution.py:186
  12.8 2.4 %collective-permute-done.7.cols_got = s32[6,1,8]{2,1,0:T(1,128)S(1)} collective-permute-done((s32[6,1,8]{2,1,0:T(1,128)S(1)}, s32[6,1,8]{2,1,0:T(1,128)S(1)}, u32[]{:S(2)}, u32[]{:S(2)}) %collective-permute-start.7) | collective-permute-done | bytes 224 | tf_op jit(solution)/shard_map/ppermute | solution.py:186
  15.2 0.0 collective-permute-done.4.far
  15.2 0.0 collective-permute-done.5.near
  15.2 0.0 collective-permute-done.6.transfer_got
  15.3 1.1 %collective-permute-start.8 = (bf16[16,1536]{1,0:T(8,128)(2,1)S(1)}, bf16[16,1536]{1,0:T(8,128)(2,1)S(1)}, u32[]{:S(2)}, u32[]{:S(2)}) collective-permute-start(bf16[16,1536]{1,0:T(8,128)(2,1)S(1)} %step.5.previous), channel_id=1, source_target_pairs={{0,6},{1,7},{2,4},{3,5},{4,14},{5,15},{6,12},{7,13},{8,2},{9,3},{1... | collective-permute-start | bytes 147464 | tf_op jit(solution)/shard_map/ppermute | solution.py:203
  16.4 4.0 %collective-permute-start.9 = (bf16[16,1536]{1,0:T(8,128)(2,1)S(1)}, bf16[16,1536]{1,0:T(8,128)(2,1)S(1)}, u32[]{:S(2)}, u32[]{:S(2)}) collective-permute-start(bf16[16,1536]{1,0:T(8,128)(2,1)S(1)} %step.5.previous), channel_id=1, source_target_pairs={{0,4},{1,5},{2,6},{3,7},{4,12},{5,13},{6,14},{7,15},{8,0},{9,1},{1... | collective-permute-start | bytes 147464 | tf_op jit(solution)/shard_map/ppermute | solution.py:203
  20.5 0.0 collective-permute-done.8.far
  20.5 1.2 %collective-permute-done.9.near = bf16[16,1536]{1,0:T(8,128)(2,1)S(1)} collective-permute-done((bf16[16,1536]{1,0:T(8,128)(2,1)S(1)}, bf16[16,1536]{1,0:T(8,128)(2,1)S(1)}, u32[]{:S(2)}, u32[]{:S(2)}) %collective-permute-start.9) | collective-permute-done | bytes 49184 | tf_op jit(solution)/shard_map/ppermute | solution.py:203
  21.7 3.9 %collective-permute-start.10 = (bf16[16,1536]{1,0:T(8,128)(2,1)S(1)}, bf16[16,1536]{1,0:T(8,128)(2,1)S(1)}, u32[]{:S(2)}, u32[]{:S(2)}) collective-permute-start(bf16[16,1536]{1,0:T(8,128)(2,1)S(1)} %step.6.previous), channel_id=1, source_target_pairs={{0,1},{1,0},{2,3},{3,2},{4,10},{5,11},{6,8},{7,9},{8,14},{9,15},{1... | collective-permute-start | bytes 147464 | tf_op jit(solution)/shard_map/ppermute | solution.py:203
  25.5 0.0 collective-permute-start.11
  25.5 1.2 %collective-permute-done.10.far = bf16[16,1536]{1,0:T(8,128)(2,1)S(1)} collective-permute-done((bf16[16,1536]{1,0:T(8,128)(2,1)S(1)}, bf16[16,1536]{1,0:T(8,128)(2,1)S(1)}, u32[]{:S(2)}, u32[]{:S(2)}) %collective-permute-start.10) | collective-permute-done | bytes 49184 | tf_op jit(solution)/shard_map/ppermute | solution.py:203
  26.7 2.6 %collective-permute-done.11.near = bf16[16,1536]{1,0:T(8,128)(2,1)S(1)} collective-permute-done((bf16[16,1536]{1,0:T(8,128)(2,1)S(1)}, bf16[16,1536]{1,0:T(8,128)(2,1)S(1)}, u32[]{:S(2)}, u32[]{:S(2)}) %collective-permute-start.11) | collective-permute-done | bytes 49184 | tf_op jit(solution)/shard_map/ppermute | solution.py:203
  29.3 1.1 %collective-permute-start.12 = (bf16[16,1536]{1,0:T(8,128)(2,1)S(1)}, bf16[16,1536]{1,0:T(8,128)(2,1)S(1)}, u32[]{:S(2)}, u32[]{:S(2)}) collective-permute-start(bf16[16,1536]{1,0:T(8,128)(2,1)S(1)} %step.7.previous), channel_id=1, source_target_pairs={{0,1},{1,0},{2,3},{3,2},{4,10},{5,11},{6,8},{7,9},{8,14},{9,15},{1... | collective-permute-start | bytes 147464 | tf_op jit(solution)/shard_map/ppermute | solution.py:203
  30.4 2.7 %collective-permute-start.13 = (bf16[16,1536]{1,0:T(8,128)(2,1)S(1)}, bf16[16,1536]{1,0:T(8,128)(2,1)S(1)}, u32[]{:S(2)}, u32[]{:S(2)}) collective-permute-start(bf16[16,1536]{1,0:T(8,128)(2,1)S(1)} %step.7.previous), channel_id=1, source_target_pairs={{0,1},{1,0},{2,3},{3,2},{4,8},{5,9},{6,10},{7,11},{8,12},{9,13},{1... | collective-permute-start | bytes 147464 | tf_op jit(solution)/shard_map/ppermute | solution.py:203
  33.2 0.3 collective-permute-done.12.far
  33.5 0.9 %collective-permute-done.13.near = bf16[16,1536]{1,0:T(8,128)(2,1)S(1)} collective-permute-done((bf16[16,1536]{1,0:T(8,128)(2,1)S(1)}, bf16[16,1536]{1,0:T(8,128)(2,1)S(1)}, u32[]{:S(2)}, u32[]{:S(2)}) %collective-permute-start.13) | collective-permute-done | bytes 49184 | tf_op jit(solution)/shard_map/ppermute | solution.py:203
  34.3 1.9 %step.9 = bf16[16,768]{1,0:T(8,128)(2,1)S(1)} custom-call(bf16[16,1536]{1,0:T(8,128)(2,1)S(1)} %collective-permute-done.12.far, bf16[16,1536]{1,0:T(8,128)(2,1)S(1)} %collective-permute-done.13.near, bf16[16,1536]{1,0:T(8,128)(2,1)S(1)} %step.7.previous, f32[16,1536]{1,0:T(8,128)S(1)} %get-tuple-element.25.load, ...), custom_call_target="tpu_custom_call" | custom-call | tf_op jit(solution)/shard_map/step/pallas_call | solution.py:270
  36.2 4.6 %collective-permute-start.14 = (bf16[16,768]{1,0:T(8,128)(2,1)S(1)}, bf16[16,768]{1,0:T(8,128)(2,1)S(1)}, u32[]{:S(2)}, u32[]{:S(2)}) collective-permute-start(bf16[16,768]{1,0:T(8,128)(2,1)S(1)} %step.9), channel_id=1, source_target_pairs={{0,1},{1,0},{2,3},{3,2},{4,5},{5,4},{6,7},{7,6},{8,9},{9,8},{10,11... | collective-permute-start | bytes 73736 | tf_op jit(solution)/shard_map/ppermute | solution.py:186
  40.9 1.9 %step.8.kept = bf16[16,768]{1,0:T(8,128)(2,1)S(1)} custom-call(bf16[16,1536]{1,0:T(8,128)(2,1)S(1)} %collective-permute-done.12.far, bf16[16,1536]{1,0:T(8,128)(2,1)S(1)} %collective-permute-done.13.near, bf16[16,1536]{1,0:T(8,128)(2,1)S(1)} %step.7.previous, f32[16,1536]{1,0:T(8,128)S(1)} %get-tuple-element.25.load, ...), custom_call_target="tpu_custom_call" | custom-call | tf_op jit(solution)/shard_map/step/pallas_call | solution.py:270
  42.8 0.0 collective-permute-done.14.got
  42.8 0.6 %finish.1 = bf16[32,768]{1,0:T(8,128)(2,1)} custom-call(bf16[16,768]{1,0:T(8,128)(2,1)S(1)} %step.8.kept, bf16[16,768]{1,0:T(8,128)(2,1)S(1)} %collective-permute-done.14.got), custom_call_target="tpu_custom_call" | custom-call | tf_op jit(solution)/shard_map/finish/pallas_call | solution.py:292
  (3 shorter events, 0.1 us)
Async XLA Ops:
  2.8 2.9 %collective-permute-start.3 = (bf16[6,2,128,128]{3,2,1,0:T(8,128)(2,1)S(1)}, bf16[6,2,128,128]{3,2,1,0:T(8,128)(2,1)S(1)}, u32[]{:S(2)}, u32[]{:S(2)}) collective-permute-start(bf16[6,2,128,128]{3,2,1,0:T(8,128)(2,1)S(1)} %get-tuple-element.22), channel_id=1, source_target_pairs={{0,1},{1,0},{2,3},{3,2},{4,5},{5,4},{6,7},{7,6},{8,9},{9,8},{10,11... | collective-permute-start | bytes 1179656 | tf_op jit(solution)/shard_map/ppermute | solution.py:186
  3.6 2.1 %collective-permute-start = (bf16[16,1536]{1,0:T(8,128)(2,1)S(1)}, bf16[16,1536]{1,0:T(8,128)(2,1)S(1)}, u32[]{:S(2)}, u32[]{:S(2)}) collective-permute-start(bf16[16,1536]{1,0:T(8,128)(2,1)S(1)} %get-tuple-element.18), channel_id=1, source_target_pairs={{0,1},{1,0},{2,3},{3,2},{4,5},{5,4},{6,7},{7,6},{8,9},{9,8},{10,11... | collective-permute-start | bytes 147464 | tf_op jit(solution)/shard_map/ppermute | solution.py:186
  3.6 5.5 %collective-permute-start.1 = (bf16[16,1536]{1,0:T(8,128)(2,1)S(1)}, bf16[16,1536]{1,0:T(8,128)(2,1)S(1)}, u32[]{:S(2)}, u32[]{:S(2)}) collective-permute-start(bf16[16,1536]{1,0:T(8,128)(2,1)S(1)} %get-tuple-element.19), channel_id=1, source_target_pairs={{0,2},{1,3},{2,0},{3,1},{4,6},{5,7},{6,4},{7,5},{8,10},{9,11},{10,... | collective-permute-start | bytes 147464 | tf_op jit(solution)/shard_map/ppermute | solution.py:186
  4.9 4.3 %collective-permute-start.2 = (bf16[16,1536]{1,0:T(8,128)(2,1)S(1)}, bf16[16,1536]{1,0:T(8,128)(2,1)S(1)}, u32[]{:S(2)}, u32[]{:S(2)}) collective-permute-start(bf16[16,1536]{1,0:T(8,128)(2,1)S(1)} %get-tuple-element.20), channel_id=1, source_target_pairs={{0,3},{1,2},{2,1},{3,0},{4,7},{5,6},{6,5},{7,4},{8,11},{9,10},{10,... | collective-permute-start | bytes 147464 | tf_op jit(solution)/shard_map/ppermute | solution.py:186
  9.2 2.6 %copy-start = (s32[1,6,8]{2,0,1:T(1,128)S(1)}, s32[1,6,8]{2,0,1:T(1,128)}, u32[]{:S(2)}) copy-start(s32[1,6,8]{2,0,1:T(1,128)} %param.9) | copy-start | bytes 580
  9.5 5.7 %collective-permute-start.6 = (bf16[6,8,2,128,128]{4,3,2,1,0:T(8,128)(2,1)S(1)}, bf16[6,8,2,128,128]{4,3,2,1,0:T(8,128)(2,1)S(1)}, u32[]{:S(2)}, u32[]{:S(2)}) collective-permute-start(bf16[6,8,2,128,128]{4,3,2,1,0:T(8,128)(2,1)S(1)} %get-tuple-element.27), channel_id=1, source_target_pairs={{0,1},{1,0},{2,3},{3,2},{4,5},{5,4},{6,7},{7,6},{8,9},{9,8},{10,11... | collective-permute-start | bytes 9437192 | tf_op jit(solution)/shard_map/ppermute | solution.py:186
  9.9 5.3 %collective-permute-start.4 = (bf16[16,1536]{1,0:T(8,128)(2,1)S(1)}, bf16[16,1536]{1,0:T(8,128)(2,1)S(1)}, u32[]{:S(2)}, u32[]{:S(2)}) collective-permute-start(bf16[16,1536]{1,0:T(8,128)(2,1)S(1)} %get-tuple-element.24.previous), channel_id=1, source_target_pairs={{0,6},{1,7},{2,4},{3,5},{4,10},{5,11},{6,8},{7,9},{8,14},{9,15},{1... | collective-permute-start | bytes 147464 | tf_op jit(solution)/shard_map/ppermute | solution.py:203
  10.5 4.7 %collective-permute-start.5 = (bf16[16,1536]{1,0:T(8,128)(2,1)S(1)}, bf16[16,1536]{1,0:T(8,128)(2,1)S(1)}, u32[]{:S(2)}, u32[]{:S(2)}) collective-permute-start(bf16[16,1536]{1,0:T(8,128)(2,1)S(1)} %get-tuple-element.24.previous), channel_id=1, source_target_pairs={{0,4},{1,5},{2,6},{3,7},{4,8},{5,9},{6,10},{7,11},{8,12},{9,13},{1... | collective-permute-start | bytes 147464 | tf_op jit(solution)/shard_map/ppermute | solution.py:203
  11.8 3.4 %collective-permute-start.7 = (s32[6,1,8]{2,1,0:T(1,128)S(1)}, s32[6,1,8]{2,1,0:T(1,128)S(1)}, u32[]{:S(2)}, u32[]{:S(2)}) collective-permute-start(s32[6,1,8]{2,1,0:T(1,128)S(1)} %bitcast.7), channel_id=1, source_target_pairs={{0,1},{1,0},{2,3},{3,2},{4,5},{5,4},{6,7},{7,6},{8,9},{9,8},{10,11... | collective-permute-start | bytes 584 | tf_op jit(solution)/shard_map/ppermute | solution.py:186
  15.3 5.2 %collective-permute-start.8 = (bf16[16,1536]{1,0:T(8,128)(2,1)S(1)}, bf16[16,1536]{1,0:T(8,128)(2,1)S(1)}, u32[]{:S(2)}, u32[]{:S(2)}) collective-permute-start(bf16[16,1536]{1,0:T(8,128)(2,1)S(1)} %step.5.previous), channel_id=1, source_target_pairs={{0,6},{1,7},{2,4},{3,5},{4,14},{5,15},{6,12},{7,13},{8,2},{9,3},{1... | collective-permute-start | bytes 147464 | tf_op jit(solution)/shard_map/ppermute | solution.py:203
  16.4 5.2 %collective-permute-start.9 = (bf16[16,1536]{1,0:T(8,128)(2,1)S(1)}, bf16[16,1536]{1,0:T(8,128)(2,1)S(1)}, u32[]{:S(2)}, u32[]{:S(2)}) collective-permute-start(bf16[16,1536]{1,0:T(8,128)(2,1)S(1)} %step.5.previous), channel_id=1, source_target_pairs={{0,4},{1,5},{2,6},{3,7},{4,12},{5,13},{6,14},{7,15},{8,0},{9,1},{1... | collective-permute-start | bytes 147464 | tf_op jit(solution)/shard_map/ppermute | solution.py:203
  21.7 5.0 %collective-permute-start.10 = (bf16[16,1536]{1,0:T(8,128)(2,1)S(1)}, bf16[16,1536]{1,0:T(8,128)(2,1)S(1)}, u32[]{:S(2)}, u32[]{:S(2)}) collective-permute-start(bf16[16,1536]{1,0:T(8,128)(2,1)S(1)} %step.6.previous), channel_id=1, source_target_pairs={{0,1},{1,0},{2,3},{3,2},{4,10},{5,11},{6,8},{7,9},{8,14},{9,15},{1... | collective-permute-start | bytes 147464 | tf_op jit(solution)/shard_map/ppermute | solution.py:203
  25.5 3.7 %collective-permute-start.11 = (bf16[16,1536]{1,0:T(8,128)(2,1)S(1)}, bf16[16,1536]{1,0:T(8,128)(2,1)S(1)}, u32[]{:S(2)}, u32[]{:S(2)}) collective-permute-start(bf16[16,1536]{1,0:T(8,128)(2,1)S(1)} %step.6.previous), channel_id=1, source_target_pairs={{0,1},{1,0},{2,3},{3,2},{4,8},{5,9},{6,10},{7,11},{8,12},{9,13},{1... | collective-permute-start | bytes 147464 | tf_op jit(solution)/shard_map/ppermute | solution.py:203
  29.3 4.2 %collective-permute-start.12 = (bf16[16,1536]{1,0:T(8,128)(2,1)S(1)}, bf16[16,1536]{1,0:T(8,128)(2,1)S(1)}, u32[]{:S(2)}, u32[]{:S(2)}) collective-permute-start(bf16[16,1536]{1,0:T(8,128)(2,1)S(1)} %step.7.previous), channel_id=1, source_target_pairs={{0,1},{1,0},{2,3},{3,2},{4,10},{5,11},{6,8},{7,9},{8,14},{9,15},{1... | collective-permute-start | bytes 147464 | tf_op jit(solution)/shard_map/ppermute | solution.py:203
  30.4 3.9 %collective-permute-start.13 = (bf16[16,1536]{1,0:T(8,128)(2,1)S(1)}, bf16[16,1536]{1,0:T(8,128)(2,1)S(1)}, u32[]{:S(2)}, u32[]{:S(2)}) collective-permute-start(bf16[16,1536]{1,0:T(8,128)(2,1)S(1)} %step.7.previous), channel_id=1, source_target_pairs={{0,1},{1,0},{2,3},{3,2},{4,8},{5,9},{6,10},{7,11},{8,12},{9,13},{1... | collective-permute-start | bytes 147464 | tf_op jit(solution)/shard_map/ppermute | solution.py:203
  36.2 6.5 %collective-permute-start.14 = (bf16[16,768]{1,0:T(8,128)(2,1)S(1)}, bf16[16,768]{1,0:T(8,128)(2,1)S(1)}, u32[]{:S(2)}, u32[]{:S(2)}) collective-permute-start(bf16[16,768]{1,0:T(8,128)(2,1)S(1)} %step.9), channel_id=1, source_target_pairs={{0,1},{1,0},{2,3},{3,2},{4,5},{5,4},{6,7},{7,6},{8,9},{9,8},{10,11... | collective-permute-start | bytes 73736 | tf_op jit(solution)/shard_map/ppermute | solution.py:186

commit v9 on v8

--- a/solution.py
+++ b/solution.py
@@ -118,7 +118,7 @@
 
 def step_kernel(
     step, chosen, far, near, previous, load,
-    transfer_own, transfer_got, inverse, cols_own, cols_got, out, state, ids, sems,
+    transfer_own, transfer_got, inverse, cols_own, cols_got, out, state, sums, ids, sems,
 ):
     part, nonzero, freqs, block, _ = transfer_own.shape
     rows = 2 * part
@@ -132,6 +132,11 @@
         ]
         for copy in copies:
             copy.start()
+        for r in chosen:
+            cols = slice(r * block, (r + 1) * block)
+            transfer = transfer_own if r < part else transfer_got
+            first = jnp.concatenate([transfer[r % part, 0, f] for f in range(freqs)], axis=1)
+            sums[:, cols] = load[:, cols] + diagonal(nn_dot(near[:, cols], first), freqs)
         for n in range(2):
             source = (near, far)[n]
             for r in range(rows):
@@ -143,12 +148,12 @@
             cols = slice(r * block, (r + 1) * block)
             goal = slice((r - chosen[0]) * block, (r - chosen[0] + 1) * block)
             transfer = transfer_own if r < part else transfer_got
-            picked = jnp.concatenate([state[ids[r // part, r % part, 0, k]] for k in range(nonzero)], axis=1)
+            picked = jnp.concatenate([state[ids[r // part, r % part, 0, k]] for k in range(1, nonzero)], axis=1)
             matrix = jnp.concatenate(
-                [jnp.concatenate([transfer[r % part, k, f] for f in range(freqs)], axis=1) for k in range(nonzero)],
+                [jnp.concatenate([transfer[r % part, k, f] for f in range(freqs)], axis=1) for k in range(1, nonzero)],
                 axis=0,
             )
-            summed = (load[:, cols] + diagonal(nn_dot(picked, matrix), freqs)).astype(jnp.bfloat16)
+            summed = (sums[:, cols] + diagonal(nn_dot(picked, matrix), freqs)).astype(jnp.bfloat16)
             solved = nn_dot(summed, jnp.concatenate([inverse[r, f] for f in range(freqs)], axis=1))
             out[:, goal] = diagonal(solved, freqs).astype(jnp.bfloat16)
 
@@ -193,7 +198,8 @@
     if bays > 3 and target == 1:
         cycle = [0, 1, 3, 2]
     elif bays > 3 and target > 1:
-        cycle = [source, target, target + 1 if target + 1 < bays else source - 1]
+        after = target + 1 if target + 1 < bays else 0 if offset else source - 1
+        cycle = [source, target, after]
     goes = {b: cycle[(n + 1) % len(cycle)] for n, b in enumerate(cycle)}
     route = [
         (b * secs + s, goes[b] * secs + (s ^ offset) if b in goes else b * secs + (s ^ 1))
@@ -274,6 +280,7 @@
             out_specs=VMEM,
             scratch_shapes=[
                 pltpu.VMEM((4 * rows, lines, block), bf16),
+                pltpu.VMEM(wide, f32),
                 pltpu.SMEM((2,) + cols_own.shape, jnp.int32),
                 pltpu.SemaphoreType.DMA((2,)),
             ],

time: 43.6 us -> 44.8 us (1.028)
  starting transfers between devices: 23.7 us -> 25.1 us
  waiting for transfers between devices: 8.54 us -> 7.75 us
  Pallas kernels: 11.1 us -> 11.6 us
    ppermute x8, starting transfers between devices: 14.7 us -> 17.7 us  [hop(): return lax.ppermute(value, ('bay', 'sec'), route)]
    ppermute x7, starting transfers between devices: 8.95 us -> 7.38 us  [moved(): return lax.ppermute(value, ('bay', 'sec'), route)]
    ppermute x8, waiting for transfers between devices: 6.09 us -> 5.3 us  [hop(): return lax.ppermute(value, ('bay', 'sec'), route)]
    pallas_call x5, Pallas kernels: 3.85 us -> 4.44 us  [advance(): pl.pallas_call(functools.partial(step_kernel, step, chosen), out_shape=ja...]
  transfers between devices with their start and end apart: 15 -> 15, of which waited for: 6 -> 5; matrix products, arithmetic and copies ran while one was open for 0% -> 0% of each run, Pallas kernels for 12% -> 13%
where the time goes in v9:
time: 44.8 us; the launch traced here: 44.6 us
  starting transfers between devices  25.1 us (56%)
  Pallas kernels  11.6 us (26%)
  waiting for transfers between devices  7.75 us (17%)
    ppermute x8, starting transfers between devices, hop(): return lax.ppermute(value, ('bay', 'sec'), route)  17.7 us
    ppermute x7, starting transfers between devices, moved(): return lax.ppermute(value, ('bay', 'sec'), route)  7.38 us
    ppermute x8, waiting for transfers between devices, hop(): return lax.ppermute(value, ('bay', 'sec'), route)  5.3 us
    pallas_call x5, Pallas kernels, advance(): pl.pallas_call(functools.partial(step_kernel, step, chosen), out_shape=ja...  4.44 us
    pallas_call x1, Pallas kernels, per_device(): pl.pallas_call(transfer_kernel, out_shape=[pltpu.VMEM(matrices, bf16)] *...  3.44 us
    pallas_call x1, Pallas kernels, per_device(): pl.pallas_call(force_kernel, out_shape=[jax.ShapeDtypeStruct(wide, bf16)]...  2.82 us
    ppermute x7, waiting for transfers between devices, moved(): return lax.ppermute(value, ('bay', 'sec'), route)  2.45 us
  transfers between devices with their start and end apart: 15, of which 5 were waited for; matrix products, arithmetic and copies ran while one was open for 0% of the time, Pallas kernels for 13%

profile of v9, /device:TPU:29, one launch (start us, length us, event | category | flops | bytes accessed | tf_op | source)
XLA Modules:
  0.0 44.6 jit_solution(12014024937841848067)
XLA Ops:
  0.0 2.8 %force.1 = (bf16[16,1536]{1,0:T(8,128)(2,1)S(1)}, bf16[16,1536]{1,0:T(8,128)(2,1)S(1)}, bf16[16,1536]{1,0:T(8,128)(2,1)S(1)}, f32[16,1536]{1,0:T(8,128)S(1)}, bf...) custom-call(bf16[32,768]{1,0:T(8,128)(2,1)} %bitcast.16, bf16[32,768]{1,0:T(8,128)(2,1)} %bitcast.17, ...), custom_call_target="tpu_custom_call" | custom-call | tf_op jit(solution)/shard_map/force/pallas_call | solution.py:228
  2.8 0.7 %collective-permute-start.3 = (bf16[6,2,128,128]{3,2,1,0:T(8,128)(2,1)S(1)}, bf16[6,2,128,128]{3,2,1,0:T(8,128)(2,1)S(1)}, u32[]{:S(2)}, u32[]{:S(2)}) collective-permute-start(bf16[6,2,128,128]{3,2,1,0:T(8,128)(2,1)S(1)} %get-tuple-element.22), channel_id=1, source_target_pairs={{0,1},{1,0},{2,3},{3,2},{4,5},{5,4},{6,7},{7,6},{8,9},{9,8},{10,11... | collective-permute-start | bytes 1179656 | tf_op jit(solution)/shard_map/ppermute | solution.py:191
  3.6 0.1 collective-permute-start
  3.6 1.2 %collective-permute-start.1 = (bf16[16,1536]{1,0:T(8,128)(2,1)S(1)}, bf16[16,1536]{1,0:T(8,128)(2,1)S(1)}, u32[]{:S(2)}, u32[]{:S(2)}) collective-permute-start(bf16[16,1536]{1,0:T(8,128)(2,1)S(1)} %get-tuple-element.19), channel_id=1, source_target_pairs={{0,2},{1,3},{2,0},{3,1},{4,6},{5,7},{6,4},{7,5},{8,10},{9,11},{10,... | collective-permute-start | bytes 147464 | tf_op jit(solution)/shard_map/ppermute | solution.py:191
  4.9 0.9 %collective-permute-start.2 = (bf16[16,1536]{1,0:T(8,128)(2,1)S(1)}, bf16[16,1536]{1,0:T(8,128)(2,1)S(1)}, u32[]{:S(2)}, u32[]{:S(2)}) collective-permute-start(bf16[16,1536]{1,0:T(8,128)(2,1)S(1)} %get-tuple-element.20), channel_id=1, source_target_pairs={{0,3},{1,2},{2,1},{3,0},{4,7},{5,6},{6,5},{7,4},{8,11},{9,10},{10,... | collective-permute-start | bytes 147464 | tf_op jit(solution)/shard_map/ppermute | solution.py:191
  5.7 0.0 collective-permute-done.after.got1
  5.7 0.0 collective-permute-done.3.inverse_got
  5.7 3.4 %transfer.1 = (bf16[6,8,2,128,128]{4,3,2,1,0:T(8,128)(2,1)S(1)}, bf16[6,8,2,128,128]{4,3,2,1,0:T(8,128)(2,1)S(1)}, bf16[12,2,128,128]{3,2,1,0:T(8,128)(2,1)S(1)}) custom-call(bf16[6,8,4,128,128]{4,3,2,1,0:T(8,128)(2,1)} %bitcast.13, bf16[6,2,128,128]{3,2,1,0:T(8,128)(2,1)S(1)} %get-tuple-element.21.inverse_own, ...), custom_call_target="tpu_custom_call" | custom-call | tf_op jit(solution)/shard_map/transfer/pallas_call | solution.py:247
  9.2 0.0 copy-start
  9.2 0.0 collective-permute-done.1.got2
  9.2 0.0 collective-permute-done.2.got3
  9.2 0.3 initial.1
  9.5 0.4 collective-permute-start.6
  9.9 0.6 %collective-permute-start.4 = (bf16[16,1536]{1,0:T(8,128)(2,1)S(1)}, bf16[16,1536]{1,0:T(8,128)(2,1)S(1)}, u32[]{:S(2)}, u32[]{:S(2)}) collective-permute-start(bf16[16,1536]{1,0:T(8,128)(2,1)S(1)} %get-tuple-element.24.previous), channel_id=1, source_target_pairs={{0,6},{1,7},{2,4},{3,5},{4,10},{5,11},{6,8},{7,9},{8,14},{9,15},{1... | collective-permute-start | bytes 147464 | tf_op jit(solution)/shard_map/ppermute | solution.py:209
  10.5 1.3 %collective-permute-start.5 = (bf16[16,1536]{1,0:T(8,128)(2,1)S(1)}, bf16[16,1536]{1,0:T(8,128)(2,1)S(1)}, u32[]{:S(2)}, u32[]{:S(2)}) collective-permute-start(bf16[16,1536]{1,0:T(8,128)(2,1)S(1)} %get-tuple-element.24.previous), channel_id=1, source_target_pairs={{0,4},{1,5},{2,6},{3,7},{4,8},{5,9},{6,10},{7,11},{8,12},{9,13},{1... | collective-permute-start | bytes 147464 | tf_op jit(solution)/shard_map/ppermute | solution.py:209
  11.8 0.0 copy-done
  11.8 1.0 %collective-permute-start.7 = (s32[6,1,8]{2,1,0:T(1,128)S(1)}, s32[6,1,8]{2,1,0:T(1,128)S(1)}, u32[]{:S(2)}, u32[]{:S(2)}) collective-permute-start(s32[6,1,8]{2,1,0:T(1,128)S(1)} %bitcast.7), channel_id=1, source_target_pairs={{0,1},{1,0},{2,3},{3,2},{4,5},{5,4},{6,7},{7,6},{8,9},{9,8},{10,11... | collective-permute-start | bytes 584 | tf_op jit(solution)/shard_map/ppermute | solution.py:191
  12.8 2.4 %collective-permute-done.7.cols_got = s32[6,1,8]{2,1,0:T(1,128)S(1)} collective-permute-done((s32[6,1,8]{2,1,0:T(1,128)S(1)}, s32[6,1,8]{2,1,0:T(1,128)S(1)}, u32[]{:S(2)}, u32[]{:S(2)}) %collective-permute-start.7) | collective-permute-done | bytes 224 | tf_op jit(solution)/shard_map/ppermute | solution.py:191
  15.2 0.0 collective-permute-done.4.far
  15.2 0.0 collective-permute-done.5.near
  15.2 0.0 collective-permute-done.6.transfer_got
  15.3 1.1 %collective-permute-start.8 = (bf16[16,1536]{1,0:T(8,128)(2,1)S(1)}, bf16[16,1536]{1,0:T(8,128)(2,1)S(1)}, u32[]{:S(2)}, u32[]{:S(2)}) collective-permute-start(bf16[16,1536]{1,0:T(8,128)(2,1)S(1)} %step.5.previous), channel_id=1, source_target_pairs={{0,6},{1,7},{2,4},{3,5},{4,14},{5,15},{6,12},{7,13},{8,2},{9,3},{1... | collective-permute-start | bytes 147464 | tf_op jit(solution)/shard_map/ppermute | solution.py:209
  16.4 4.6 %collective-permute-start.9 = (bf16[16,1536]{1,0:T(8,128)(2,1)S(1)}, bf16[16,1536]{1,0:T(8,128)(2,1)S(1)}, u32[]{:S(2)}, u32[]{:S(2)}) collective-permute-start(bf16[16,1536]{1,0:T(8,128)(2,1)S(1)} %step.5.previous), channel_id=1, source_target_pairs={{0,4},{1,5},{2,6},{3,7},{4,12},{5,13},{6,14},{7,15},{8,0},{9,1},{1... | collective-permute-start | bytes 147464 | tf_op jit(solution)/shard_map/ppermute | solution.py:209
  21.0 0.0 collective-permute-done.8.far
  21.0 1.2 %collective-permute-done.9.near = bf16[16,1536]{1,0:T(8,128)(2,1)S(1)} collective-permute-done((bf16[16,1536]{1,0:T(8,128)(2,1)S(1)}, bf16[16,1536]{1,0:T(8,128)(2,1)S(1)}, u32[]{:S(2)}, u32[]{:S(2)}) %collective-permute-start.9) | collective-permute-done | bytes 49184 | tf_op jit(solution)/shard_map/ppermute | solution.py:209
  22.3 4.4 %collective-permute-start.10 = (bf16[16,1536]{1,0:T(8,128)(2,1)S(1)}, bf16[16,1536]{1,0:T(8,128)(2,1)S(1)}, u32[]{:S(2)}, u32[]{:S(2)}) collective-permute-start(bf16[16,1536]{1,0:T(8,128)(2,1)S(1)} %step.6.previous), channel_id=1, source_target_pairs={{0,1},{1,0},{2,3},{3,2},{4,10},{5,11},{6,8},{7,9},{8,14},{9,15},{1... | collective-permute-start | bytes 147464 | tf_op jit(solution)/shard_map/ppermute | solution.py:209
  26.7 0.0 collective-permute-start.11
  26.7 1.2 %collective-permute-done.10.far = bf16[16,1536]{1,0:T(8,128)(2,1)S(1)} collective-permute-done((bf16[16,1536]{1,0:T(8,128)(2,1)S(1)}, bf16[16,1536]{1,0:T(8,128)(2,1)S(1)}, u32[]{:S(2)}, u32[]{:S(2)}) %collective-permute-start.10) | collective-permute-done | bytes 49184 | tf_op jit(solution)/shard_map/ppermute | solution.py:209
  27.9 1.8 %collective-permute-done.11.near = bf16[16,1536]{1,0:T(8,128)(2,1)S(1)} collective-permute-done((bf16[16,1536]{1,0:T(8,128)(2,1)S(1)}, bf16[16,1536]{1,0:T(8,128)(2,1)S(1)}, u32[]{:S(2)}, u32[]{:S(2)}) %collective-permute-start.11) | collective-permute-done | bytes 49184 | tf_op jit(solution)/shard_map/ppermute | solution.py:209
  29.7 0.2 collective-permute-start.12
  29.9 5.5 %collective-permute-start.13 = (bf16[16,1536]{1,0:T(8,128)(2,1)S(1)}, bf16[16,1536]{1,0:T(8,128)(2,1)S(1)}, u32[]{:S(2)}, u32[]{:S(2)}) collective-permute-start(bf16[16,1536]{1,0:T(8,128)(2,1)S(1)} %step.7.previous), channel_id=1, source_target_pairs={{0,1},{1,0},{2,3},{3,2},{4,8},{5,9},{6,10},{7,11},{8,12},{9,13},{1... | collective-permute-start | bytes 147464 | tf_op jit(solution)/shard_map/ppermute | solution.py:209
  35.4 0.0 collective-permute-done.12.far
  35.4 1.2 %collective-permute-done.13.near = bf16[16,1536]{1,0:T(8,128)(2,1)S(1)} collective-permute-done((bf16[16,1536]{1,0:T(8,128)(2,1)S(1)}, bf16[16,1536]{1,0:T(8,128)(2,1)S(1)}, u32[]{:S(2)}, u32[]{:S(2)}) %collective-permute-start.13) | collective-permute-done | bytes 49184 | tf_op jit(solution)/shard_map/ppermute | solution.py:209
  36.5 2.2 %step.9 = bf16[16,768]{1,0:T(8,128)(2,1)S(1)} custom-call(bf16[16,1536]{1,0:T(8,128)(2,1)S(1)} %collective-permute-done.12.far, bf16[16,1536]{1,0:T(8,128)(2,1)S(1)} %collective-permute-done.13.near, bf16[16,1536]{1,0:T(8,128)(2,1)S(1)} %step.7.previous, f32[16,1536]{1,0:T(8,128)S(1)} %get-tuple-element.25.load, ...), custom_call_target="tpu_custom_call" | custom-call | tf_op jit(solution)/shard_map/step/pallas_call | solution.py:276
  38.7 3.1 %collective-permute-start.14 = (bf16[16,768]{1,0:T(8,128)(2,1)S(1)}, bf16[16,768]{1,0:T(8,128)(2,1)S(1)}, u32[]{:S(2)}, u32[]{:S(2)}) collective-permute-start(bf16[16,768]{1,0:T(8,128)(2,1)S(1)} %step.9), channel_id=1, source_target_pairs={{0,1},{1,0},{2,3},{3,2},{4,5},{5,4},{6,7},{7,6},{8,9},{9,8},{10,11... | collective-permute-start | bytes 73736 | tf_op jit(solution)/shard_map/ppermute | solution.py:191
  41.8 2.2 %step.8.kept = bf16[16,768]{1,0:T(8,128)(2,1)S(1)} custom-call(bf16[16,1536]{1,0:T(8,128)(2,1)S(1)} %collective-permute-done.12.far, bf16[16,1536]{1,0:T(8,128)(2,1)S(1)} %collective-permute-done.13.near, bf16[16,1536]{1,0:T(8,128)(2,1)S(1)} %step.7.previous, f32[16,1536]{1,0:T(8,128)S(1)} %get-tuple-element.25.load, ...), custom_call_target="tpu_custom_call" | custom-call | tf_op jit(solution)/shard_map/step/pallas_call | solution.py:276
  44.0 0.0 collective-permute-done.14.got
  44.0 0.6 %finish.1 = bf16[32,768]{1,0:T(8,128)(2,1)} custom-call(bf16[16,768]{1,0:T(8,128)(2,1)S(1)} %step.8.kept, bf16[16,768]{1,0:T(8,128)(2,1)S(1)} %collective-permute-done.14.got), custom_call_target="tpu_custom_call" | custom-call | tf_op jit(solution)/shard_map/finish/pallas_call | solution.py:299
  (3 shorter events, 0.1 us)
Async XLA Ops:
  2.8 2.9 %collective-permute-start.3 = (bf16[6,2,128,128]{3,2,1,0:T(8,128)(2,1)S(1)}, bf16[6,2,128,128]{3,2,1,0:T(8,128)(2,1)S(1)}, u32[]{:S(2)}, u32[]{:S(2)}) collective-permute-start(bf16[6,2,128,128]{3,2,1,0:T(8,128)(2,1)S(1)} %get-tuple-element.22), channel_id=1, source_target_pairs={{0,1},{1,0},{2,3},{3,2},{4,5},{5,4},{6,7},{7,6},{8,9},{9,8},{10,11... | collective-permute-start | bytes 1179656 | tf_op jit(solution)/shard_map/ppermute | solution.py:191
  3.6 2.1 %collective-permute-start = (bf16[16,1536]{1,0:T(8,128)(2,1)S(1)}, bf16[16,1536]{1,0:T(8,128)(2,1)S(1)}, u32[]{:S(2)}, u32[]{:S(2)}) collective-permute-start(bf16[16,1536]{1,0:T(8,128)(2,1)S(1)} %get-tuple-element.18), channel_id=1, source_target_pairs={{0,1},{1,0},{2,3},{3,2},{4,5},{5,4},{6,7},{7,6},{8,9},{9,8},{10,11... | collective-permute-start | bytes 147464 | tf_op jit(solution)/shard_map/ppermute | solution.py:191
  3.6 5.5 %collective-permute-start.1 = (bf16[16,1536]{1,0:T(8,128)(2,1)S(1)}, bf16[16,1536]{1,0:T(8,128)(2,1)S(1)}, u32[]{:S(2)}, u32[]{:S(2)}) collective-permute-start(bf16[16,1536]{1,0:T(8,128)(2,1)S(1)} %get-tuple-element.19), channel_id=1, source_target_pairs={{0,2},{1,3},{2,0},{3,1},{4,6},{5,7},{6,4},{7,5},{8,10},{9,11},{10,... | collective-permute-start | bytes 147464 | tf_op jit(solution)/shard_map/ppermute | solution.py:191
  4.9 4.3 %collective-permute-start.2 = (bf16[16,1536]{1,0:T(8,128)(2,1)S(1)}, bf16[16,1536]{1,0:T(8,128)(2,1)S(1)}, u32[]{:S(2)}, u32[]{:S(2)}) collective-permute-start(bf16[16,1536]{1,0:T(8,128)(2,1)S(1)} %get-tuple-element.20), channel_id=1, source_target_pairs={{0,3},{1,2},{2,1},{3,0},{4,7},{5,6},{6,5},{7,4},{8,11},{9,10},{10,... | collective-permute-start | bytes 147464 | tf_op jit(solution)/shard_map/ppermute | solution.py:191
  9.2 2.6 %copy-start = (s32[1,6,8]{2,0,1:T(1,128)S(1)}, s32[1,6,8]{2,0,1:T(1,128)}, u32[]{:S(2)}) copy-start(s32[1,6,8]{2,0,1:T(1,128)} %param.9) | copy-start | bytes 580
  9.5 5.7 %collective-permute-start.6 = (bf16[6,8,2,128,128]{4,3,2,1,0:T(8,128)(2,1)S(1)}, bf16[6,8,2,128,128]{4,3,2,1,0:T(8,128)(2,1)S(1)}, u32[]{:S(2)}, u32[]{:S(2)}) collective-permute-start(bf16[6,8,2,128,128]{4,3,2,1,0:T(8,128)(2,1)S(1)} %get-tuple-element.27), channel_id=1, source_target_pairs={{0,1},{1,0},{2,3},{3,2},{4,5},{5,4},{6,7},{7,6},{8,9},{9,8},{10,11... | collective-permute-start | bytes 9437192 | tf_op jit(solution)/shard_map/ppermute | solution.py:191
  9.9 5.3 %collective-permute-start.4 = (bf16[16,1536]{1,0:T(8,128)(2,1)S(1)}, bf16[16,1536]{1,0:T(8,128)(2,1)S(1)}, u32[]{:S(2)}, u32[]{:S(2)}) collective-permute-start(bf16[16,1536]{1,0:T(8,128)(2,1)S(1)} %get-tuple-element.24.previous), channel_id=1, source_target_pairs={{0,6},{1,7},{2,4},{3,5},{4,10},{5,11},{6,8},{7,9},{8,14},{9,15},{1... | collective-permute-start | bytes 147464 | tf_op jit(solution)/shard_map/ppermute | solution.py:209
  10.5 4.7 %collective-permute-start.5 = (bf16[16,1536]{1,0:T(8,128)(2,1)S(1)}, bf16[16,1536]{1,0:T(8,128)(2,1)S(1)}, u32[]{:S(2)}, u32[]{:S(2)}) collective-permute-start(bf16[16,1536]{1,0:T(8,128)(2,1)S(1)} %get-tuple-element.24.previous), channel_id=1, source_target_pairs={{0,4},{1,5},{2,6},{3,7},{4,8},{5,9},{6,10},{7,11},{8,12},{9,13},{1... | collective-permute-start | bytes 147464 | tf_op jit(solution)/shard_map/ppermute | solution.py:209
  11.8 3.4 %collective-permute-start.7 = (s32[6,1,8]{2,1,0:T(1,128)S(1)}, s32[6,1,8]{2,1,0:T(1,128)S(1)}, u32[]{:S(2)}, u32[]{:S(2)}) collective-permute-start(s32[6,1,8]{2,1,0:T(1,128)S(1)} %bitcast.7), channel_id=1, source_target_pairs={{0,1},{1,0},{2,3},{3,2},{4,5},{5,4},{6,7},{7,6},{8,9},{9,8},{10,11... | collective-permute-start | bytes 584 | tf_op jit(solution)/shard_map/ppermute | solution.py:191
  15.3 5.8 %collective-permute-start.8 = (bf16[16,1536]{1,0:T(8,128)(2,1)S(1)}, bf16[16,1536]{1,0:T(8,128)(2,1)S(1)}, u32[]{:S(2)}, u32[]{:S(2)}) collective-permute-start(bf16[16,1536]{1,0:T(8,128)(2,1)S(1)} %step.5.previous), channel_id=1, source_target_pairs={{0,6},{1,7},{2,4},{3,5},{4,14},{5,15},{6,12},{7,13},{8,2},{9,3},{1... | collective-permute-start | bytes 147464 | tf_op jit(solution)/shard_map/ppermute | solution.py:209
  16.4 5.8 %collective-permute-start.9 = (bf16[16,1536]{1,0:T(8,128)(2,1)S(1)}, bf16[16,1536]{1,0:T(8,128)(2,1)S(1)}, u32[]{:S(2)}, u32[]{:S(2)}) collective-permute-start(bf16[16,1536]{1,0:T(8,128)(2,1)S(1)} %step.5.previous), channel_id=1, source_target_pairs={{0,4},{1,5},{2,6},{3,7},{4,12},{5,13},{6,14},{7,15},{8,0},{9,1},{1... | collective-permute-start | bytes 147464 | tf_op jit(solution)/shard_map/ppermute | solution.py:209
  22.3 5.6 %collective-permute-start.10 = (bf16[16,1536]{1,0:T(8,128)(2,1)S(1)}, bf16[16,1536]{1,0:T(8,128)(2,1)S(1)}, u32[]{:S(2)}, u32[]{:S(2)}) collective-permute-start(bf16[16,1536]{1,0:T(8,128)(2,1)S(1)} %step.6.previous), channel_id=1, source_target_pairs={{0,1},{1,0},{2,3},{3,2},{4,10},{5,11},{6,8},{7,9},{8,14},{9,15},{1... | collective-permute-start | bytes 147464 | tf_op jit(solution)/shard_map/ppermute | solution.py:209
  26.7 2.9 %collective-permute-start.11 = (bf16[16,1536]{1,0:T(8,128)(2,1)S(1)}, bf16[16,1536]{1,0:T(8,128)(2,1)S(1)}, u32[]{:S(2)}, u32[]{:S(2)}) collective-permute-start(bf16[16,1536]{1,0:T(8,128)(2,1)S(1)} %step.6.previous), channel_id=1, source_target_pairs={{0,1},{1,0},{2,3},{3,2},{4,8},{5,9},{6,10},{7,11},{8,12},{9,13},{1... | collective-permute-start | bytes 147464 | tf_op jit(solution)/shard_map/ppermute | solution.py:209
  29.7 5.7 %collective-permute-start.12 = (bf16[16,1536]{1,0:T(8,128)(2,1)S(1)}, bf16[16,1536]{1,0:T(8,128)(2,1)S(1)}, u32[]{:S(2)}, u32[]{:S(2)}) collective-permute-start(bf16[16,1536]{1,0:T(8,128)(2,1)S(1)} %step.7.previous), channel_id=1, source_target_pairs={{0,10},{1,11},{2,8},{3,9},{4,5},{5,4},{6,7},{7,6},{8,14},{9,15},{1... | collective-permute-start | bytes 147464 | tf_op jit(solution)/shard_map/ppermute | solution.py:209
  29.9 6.7 %collective-permute-start.13 = (bf16[16,1536]{1,0:T(8,128)(2,1)S(1)}, bf16[16,1536]{1,0:T(8,128)(2,1)S(1)}, u32[]{:S(2)}, u32[]{:S(2)}) collective-permute-start(bf16[16,1536]{1,0:T(8,128)(2,1)S(1)} %step.7.previous), channel_id=1, source_target_pairs={{0,1},{1,0},{2,3},{3,2},{4,8},{5,9},{6,10},{7,11},{8,12},{9,13},{1... | collective-permute-start | bytes 147464 | tf_op jit(solution)/shard_map/ppermute | solution.py:209
  38.7 5.3 %collective-permute-start.14 = (bf16[16,768]{1,0:T(8,128)(2,1)S(1)}, bf16[16,768]{1,0:T(8,128)(2,1)S(1)}, u32[]{:S(2)}, u32[]{:S(2)}) collective-permute-start(bf16[16,768]{1,0:T(8,128)(2,1)S(1)} %step.9), channel_id=1, source_target_pairs={{0,1},{1,0},{2,3},{3,2},{4,5},{5,4},{6,7},{7,6},{8,9},{9,8},{10,11... | collective-permute-start | bytes 73736 | tf_op jit(solution)/shard_map/ppermute | solution.py:191

commit v10 on v8

--- a/solution.py
+++ b/solution.py
@@ -19,6 +19,16 @@
 
 def nn_dot(left, right):
     return jnp.dot(left, right, preferred_element_type=jnp.float32)
+
+
+def beside(first, second):
+    return jnp.concatenate(
+        [
+            jnp.concatenate([first, jnp.zeros_like(second)], axis=1),
+            jnp.concatenate([jnp.zeros_like(first), second], axis=1),
+        ],
+        axis=0,
+    )
 
 
 def diagonal(product, freqs):
@@ -125,6 +135,21 @@
     sec = lax.axis_index("sec")
     bay = lax.axis_index("bay")
 
+    height = out.shape[0]
+
+    def across(blocks, *place):
+        return jnp.concatenate([blocks[(*place, f)] for f in range(freqs)], axis=1)
+
+    def transfer_of(r):
+        return transfer_own if r < part else transfer_got
+
+    def solve(pair, summed):
+        matrix = jnp.concatenate([across(inverse, n) for n in pair], axis=0)
+        solved = nn_dot(beside(*summed), matrix)
+        for i, n in enumerate(pair):
+            goal = slice((n - chosen[0]) * block, (n - chosen[0] + 1) * block)
+            out[:, goal] = diagonal(solved[i * height:(i + 1) * height], freqs).astype(jnp.bfloat16)
+
     @pl.when(bay == step)
     def _():
         copies = [
@@ -139,18 +164,18 @@
                 state[home] = source[:, r * block:(r + 1) * block]
         for copy in copies:
             copy.wait()
-        for r in chosen:
-            cols = slice(r * block, (r + 1) * block)
-            goal = slice((r - chosen[0]) * block, (r - chosen[0] + 1) * block)
-            transfer = transfer_own if r < part else transfer_got
-            picked = jnp.concatenate([state[ids[r // part, r % part, 0, k]] for k in range(nonzero)], axis=1)
-            matrix = jnp.concatenate(
-                [jnp.concatenate([transfer[r % part, k, f] for f in range(freqs)], axis=1) for k in range(nonzero)],
-                axis=0,
-            )
-            summed = (load[:, cols] + diagonal(nn_dot(picked, matrix), freqs)).astype(jnp.bfloat16)
-            solved = nn_dot(summed, jnp.concatenate([inverse[r, f] for f in range(freqs)], axis=1))
-            out[:, goal] = diagonal(solved, freqs).astype(jnp.bfloat16)
+        for r in chosen[::2]:
+            pair = (r, r + 1)
+            spans = [slice(n * block, (n + 1) * block) for n in pair]
+            summed = []
+            for n, cols in zip(pair, spans):
+                transfer = transfer_own if n < part else transfer_got
+                picked = jnp.concatenate(
+                    [state[ids[n // part, n % part, 0, k]] for k in range(nonzero)], axis=1
+                )
+                matrix = jnp.concatenate([across(transfer, n % part, k) for k in range(nonzero)], axis=0)
+                summed.append((load[:, cols] + diagonal(nn_dot(picked, matrix), freqs)).astype(jnp.bfloat16))
+            solve(pair, summed)
 
     @pl.when(bay != step)
     def _():
@@ -193,7 +218,8 @@
     if bays > 3 and target == 1:
         cycle = [0, 1, 3, 2]
     elif bays > 3 and target > 1:
-        cycle = [source, target, target + 1 if target + 1 < bays else source - 1]
+        after = target + 1 if target + 1 < bays else 0 if offset else source - 1
+        cycle = [source, target, after]
     goes = {b: cycle[(n + 1) % len(cycle)] for n, b in enumerate(cycle)}
     route = [
         (b * secs + s, goes[b] * secs + (s ^ offset) if b in goes else b * secs + (s ^ 1))

time: 43.6 us -> 40.5 us (0.929); the launches traced: 43.4 us -> 39.7 us
  starting transfers between devices: 23.7 us -> 21.3 us
  Pallas kernels: 11.1 us -> 10.3 us
  waiting for transfers between devices: 8.54 us -> 7.93 us
    ppermute x7, starting transfers between devices: 8.95 us -> 6.09 us  [moved(): return lax.ppermute(value, ('bay', 'sec'), route)]
    pallas_call x5, Pallas kernels: 3.85 us -> 3.1 us  [advance(): pl.pallas_call(functools.partial(step_kernel, step, chosen), out_shape=ja...]
    ppermute x8, waiting for transfers between devices: 6.09 us -> 5.48 us  [hop(): return lax.ppermute(value, ('bay', 'sec'), route)]
    ppermute x8, starting transfers between devices: 14.7 us -> 15.3 us  [hop(): return lax.ppermute(value, ('bay', 'sec'), route)]
where the time goes in v10:
time: 40.5 us; the launch traced here: 39.7 us
  starting transfers between devices  21.3 us (53%)
  Pallas kernels  10.3 us (25%)
  waiting for transfers between devices  7.93 us (20%)
    ppermute x8, starting transfers between devices, hop(): return lax.ppermute(value, ('bay', 'sec'), route)  15.3 us
    ppermute x7, starting transfers between devices, moved(): return lax.ppermute(value, ('bay', 'sec'), route)  6.09 us
    ppermute x8, waiting for transfers between devices, hop(): return lax.ppermute(value, ('bay', 'sec'), route)  5.48 us
    pallas_call x1, Pallas kernels, per_device(): pl.pallas_call(transfer_kernel, out_shape=[pltpu.VMEM(matrices, bf16)] *...  3.44 us
    pallas_call x5, Pallas kernels, advance(): pl.pallas_call(functools.partial(step_kernel, step, chosen), out_shape=ja...  3.1 us
    pallas_call x1, Pallas kernels, per_device(): pl.pallas_call(force_kernel, out_shape=[jax.ShapeDtypeStruct(wide, bf16)]...  2.82 us
    ppermute x7, waiting for transfers between devices, moved(): return lax.ppermute(value, ('bay', 'sec'), route)  2.45 us
  transfers between devices with their start and end apart: 15, of which 6 were waited for; matrix products, arithmetic and copies ran while one was open for 0% of the time, Pallas kernels for 12%

profile of v10, /device:TPU:29, one launch (start us, length us, event | category | flops | bytes accessed | tf_op | source)
XLA Modules:
  0.0 39.7 jit_solution(9097649150866406244)
XLA Ops:
  0.0 2.8 %force.1 = (bf16[16,1536]{1,0:T(8,128)(2,1)S(1)}, bf16[16,1536]{1,0:T(8,128)(2,1)S(1)}, bf16[16,1536]{1,0:T(8,128)(2,1)S(1)}, f32[16,1536]{1,0:T(8,128)S(1)}, bf...) custom-call(bf16[32,768]{1,0:T(8,128)(2,1)} %bitcast.16, bf16[32,768]{1,0:T(8,128)(2,1)} %bitcast.17, ...), custom_call_target="tpu_custom_call" | custom-call | tf_op jit(solution)/shard_map/force/pallas_call | solution.py:248
  2.8 0.7 %collective-permute-start.3 = (bf16[6,2,128,128]{3,2,1,0:T(8,128)(2,1)S(1)}, bf16[6,2,128,128]{3,2,1,0:T(8,128)(2,1)S(1)}, u32[]{:S(2)}, u32[]{:S(2)}) collective-permute-start(bf16[6,2,128,128]{3,2,1,0:T(8,128)(2,1)S(1)} %get-tuple-element.22), channel_id=1, source_target_pairs={{0,1},{1,0},{2,3},{3,2},{4,5},{5,4},{6,7},{7,6},{8,9},{9,8},{10,11... | collective-permute-start | bytes 1179656 | tf_op jit(solution)/shard_map/ppermute | solution.py:211
  3.6 0.1 collective-permute-start
  3.6 1.2 %collective-permute-start.1 = (bf16[16,1536]{1,0:T(8,128)(2,1)S(1)}, bf16[16,1536]{1,0:T(8,128)(2,1)S(1)}, u32[]{:S(2)}, u32[]{:S(2)}) collective-permute-start(bf16[16,1536]{1,0:T(8,128)(2,1)S(1)} %get-tuple-element.19), channel_id=1, source_target_pairs={{0,2},{1,3},{2,0},{3,1},{4,6},{5,7},{6,4},{7,5},{8,10},{9,11},{10,... | collective-permute-start | bytes 147464 | tf_op jit(solution)/shard_map/ppermute | solution.py:211
  4.9 0.9 %collective-permute-start.2 = (bf16[16,1536]{1,0:T(8,128)(2,1)S(1)}, bf16[16,1536]{1,0:T(8,128)(2,1)S(1)}, u32[]{:S(2)}, u32[]{:S(2)}) collective-permute-start(bf16[16,1536]{1,0:T(8,128)(2,1)S(1)} %get-tuple-element.20), channel_id=1, source_target_pairs={{0,3},{1,2},{2,1},{3,0},{4,7},{5,6},{6,5},{7,4},{8,11},{9,10},{10,... | collective-permute-start | bytes 147464 | tf_op jit(solution)/shard_map/ppermute | solution.py:211
  5.7 0.0 collective-permute-done.after.got1
  5.7 0.0 collective-permute-done.3.inverse_got
  5.7 3.4 %transfer.1 = (bf16[6,8,2,128,128]{4,3,2,1,0:T(8,128)(2,1)S(1)}, bf16[6,8,2,128,128]{4,3,2,1,0:T(8,128)(2,1)S(1)}, bf16[12,2,128,128]{3,2,1,0:T(8,128)(2,1)S(1)}) custom-call(bf16[6,8,4,128,128]{4,3,2,1,0:T(8,128)(2,1)} %bitcast.13, bf16[6,2,128,128]{3,2,1,0:T(8,128)(2,1)S(1)} %get-tuple-element.21.inverse_own, ...), custom_call_target="tpu_custom_call" | custom-call | tf_op jit(solution)/shard_map/transfer/pallas_call | solution.py:267
  9.2 0.0 copy-start
  9.2 0.0 collective-permute-done.1.got2
  9.2 0.0 collective-permute-done.2.got3
  9.2 0.3 initial.1
  9.5 0.4 %collective-permute-start.6 = (bf16[6,8,2,128,128]{4,3,2,1,0:T(8,128)(2,1)S(1)}, bf16[6,8,2,128,128]{4,3,2,1,0:T(8,128)(2,1)S(1)}, u32[]{:S(2)}, u32[]{:S(2)}) collective-permute-start(bf16[6,8,2,128,128]{4,3,2,1,0:T(8,128)(2,1)S(1)} %get-tuple-element.27), channel_id=1, source_target_pairs={{0,1},{1,0},{2,3},{3,2},{4,5},{5,4},{6,7},{7,6},{8,9},{9,8},{10,11... | collective-permute-start | bytes 9437192 | tf_op jit(solution)/shard_map/ppermute | solution.py:211
  9.9 0.6 %collective-permute-start.4 = (bf16[16,1536]{1,0:T(8,128)(2,1)S(1)}, bf16[16,1536]{1,0:T(8,128)(2,1)S(1)}, u32[]{:S(2)}, u32[]{:S(2)}) collective-permute-start(bf16[16,1536]{1,0:T(8,128)(2,1)S(1)} %get-tuple-element.24.previous), channel_id=1, source_target_pairs={{0,6},{1,7},{2,4},{3,5},{4,10},{5,11},{6,8},{7,9},{8,14},{9,15},{1... | collective-permute-start | bytes 147464 | tf_op jit(solution)/shard_map/ppermute | solution.py:229
  10.5 1.3 %collective-permute-start.5 = (bf16[16,1536]{1,0:T(8,128)(2,1)S(1)}, bf16[16,1536]{1,0:T(8,128)(2,1)S(1)}, u32[]{:S(2)}, u32[]{:S(2)}) collective-permute-start(bf16[16,1536]{1,0:T(8,128)(2,1)S(1)} %get-tuple-element.24.previous), channel_id=1, source_target_pairs={{0,4},{1,5},{2,6},{3,7},{4,8},{5,9},{6,10},{7,11},{8,12},{9,13},{1... | collective-permute-start | bytes 147464 | tf_op jit(solution)/shard_map/ppermute | solution.py:229
  11.8 0.0 copy-done
  11.8 1.0 %collective-permute-start.7 = (s32[6,1,8]{2,1,0:T(1,128)S(1)}, s32[6,1,8]{2,1,0:T(1,128)S(1)}, u32[]{:S(2)}, u32[]{:S(2)}) collective-permute-start(s32[6,1,8]{2,1,0:T(1,128)S(1)} %bitcast.7), channel_id=1, source_target_pairs={{0,1},{1,0},{2,3},{3,2},{4,5},{5,4},{6,7},{7,6},{8,9},{9,8},{10,11... | collective-permute-start | bytes 584 | tf_op jit(solution)/shard_map/ppermute | solution.py:211
  12.8 2.4 %collective-permute-done.7.cols_got = s32[6,1,8]{2,1,0:T(1,128)S(1)} collective-permute-done((s32[6,1,8]{2,1,0:T(1,128)S(1)}, s32[6,1,8]{2,1,0:T(1,128)S(1)}, u32[]{:S(2)}, u32[]{:S(2)}) %collective-permute-start.7) | collective-permute-done | bytes 224 | tf_op jit(solution)/shard_map/ppermute | solution.py:211
  15.2 0.0 collective-permute-done.4.far
  15.2 0.0 collective-permute-done.5.near
  15.2 0.0 collective-permute-done.6.transfer_got
  15.3 1.1 %collective-permute-start.8 = (bf16[16,1536]{1,0:T(8,128)(2,1)S(1)}, bf16[16,1536]{1,0:T(8,128)(2,1)S(1)}, u32[]{:S(2)}, u32[]{:S(2)}) collective-permute-start(bf16[16,1536]{1,0:T(8,128)(2,1)S(1)} %step.5.previous), channel_id=1, source_target_pairs={{0,6},{1,7},{2,4},{3,5},{4,14},{5,15},{6,12},{7,13},{8,2},{9,3},{1... | collective-permute-start | bytes 147464 | tf_op jit(solution)/shard_map/ppermute | solution.py:229
  16.4 3.2 %collective-permute-start.9 = (bf16[16,1536]{1,0:T(8,128)(2,1)S(1)}, bf16[16,1536]{1,0:T(8,128)(2,1)S(1)}, u32[]{:S(2)}, u32[]{:S(2)}) collective-permute-start(bf16[16,1536]{1,0:T(8,128)(2,1)S(1)} %step.5.previous), channel_id=1, source_target_pairs={{0,4},{1,5},{2,6},{3,7},{4,12},{5,13},{6,14},{7,15},{8,0},{9,1},{1... | collective-permute-start | bytes 147464 | tf_op jit(solution)/shard_map/ppermute | solution.py:229
  19.6 0.5 %collective-permute-done.8.far = bf16[16,1536]{1,0:T(8,128)(2,1)S(1)} collective-permute-done((bf16[16,1536]{1,0:T(8,128)(2,1)S(1)}, bf16[16,1536]{1,0:T(8,128)(2,1)S(1)}, u32[]{:S(2)}, u32[]{:S(2)}) %collective-permute-start.8) | collective-permute-done | bytes 49184 | tf_op jit(solution)/shard_map/ppermute | solution.py:229
  20.1 1.3 %collective-permute-done.9.near = bf16[16,1536]{1,0:T(8,128)(2,1)S(1)} collective-permute-done((bf16[16,1536]{1,0:T(8,128)(2,1)S(1)}, bf16[16,1536]{1,0:T(8,128)(2,1)S(1)}, u32[]{:S(2)}, u32[]{:S(2)}) %collective-permute-start.9) | collective-permute-done | bytes 49184 | tf_op jit(solution)/shard_map/ppermute | solution.py:229
  21.4 2.4 %collective-permute-start.10 = (bf16[16,1536]{1,0:T(8,128)(2,1)S(1)}, bf16[16,1536]{1,0:T(8,128)(2,1)S(1)}, u32[]{:S(2)}, u32[]{:S(2)}) collective-permute-start(bf16[16,1536]{1,0:T(8,128)(2,1)S(1)} %step.6.previous), channel_id=1, source_target_pairs={{0,1},{1,0},{2,3},{3,2},{4,10},{5,11},{6,8},{7,9},{8,14},{9,15},{1... | collective-permute-start | bytes 147464 | tf_op jit(solution)/shard_map/ppermute | solution.py:229
  23.8 0.4 %collective-permute-start.11 = (bf16[16,1536]{1,0:T(8,128)(2,1)S(1)}, bf16[16,1536]{1,0:T(8,128)(2,1)S(1)}, u32[]{:S(2)}, u32[]{:S(2)}) collective-permute-start(bf16[16,1536]{1,0:T(8,128)(2,1)S(1)} %step.6.previous), channel_id=1, source_target_pairs={{0,1},{1,0},{2,3},{3,2},{4,8},{5,9},{6,10},{7,11},{8,12},{9,13},{1... | collective-permute-start | bytes 147464 | tf_op jit(solution)/shard_map/ppermute | solution.py:229
  24.3 1.1 %collective-permute-done.10.far = bf16[16,1536]{1,0:T(8,128)(2,1)S(1)} collective-permute-done((bf16[16,1536]{1,0:T(8,128)(2,1)S(1)}, bf16[16,1536]{1,0:T(8,128)(2,1)S(1)}, u32[]{:S(2)}, u32[]{:S(2)}) %collective-permute-start.10) | collective-permute-done | bytes 49184 | tf_op jit(solution)/shard_map/ppermute | solution.py:229
  25.3 1.4 %collective-permute-done.11.near = bf16[16,1536]{1,0:T(8,128)(2,1)S(1)} collective-permute-done((bf16[16,1536]{1,0:T(8,128)(2,1)S(1)}, bf16[16,1536]{1,0:T(8,128)(2,1)S(1)}, u32[]{:S(2)}, u32[]{:S(2)}) %collective-permute-start.11) | collective-permute-done | bytes 49184 | tf_op jit(solution)/shard_map/ppermute | solution.py:229
  26.8 1.6 %collective-permute-start.12 = (bf16[16,1536]{1,0:T(8,128)(2,1)S(1)}, bf16[16,1536]{1,0:T(8,128)(2,1)S(1)}, u32[]{:S(2)}, u32[]{:S(2)}) collective-permute-start(bf16[16,1536]{1,0:T(8,128)(2,1)S(1)} %step.7.previous), channel_id=1, source_target_pairs={{0,10},{1,11},{2,8},{3,9},{4,5},{5,4},{6,7},{7,6},{8,14},{9,15},{1... | collective-permute-start | bytes 147464 | tf_op jit(solution)/shard_map/ppermute | solution.py:229
  28.4 4.6 %collective-permute-start.13 = (bf16[16,1536]{1,0:T(8,128)(2,1)S(1)}, bf16[16,1536]{1,0:T(8,128)(2,1)S(1)}, u32[]{:S(2)}, u32[]{:S(2)}) collective-permute-start(bf16[16,1536]{1,0:T(8,128)(2,1)S(1)} %step.7.previous), channel_id=1, source_target_pairs={{0,1},{1,0},{2,3},{3,2},{4,8},{5,9},{6,10},{7,11},{8,12},{9,13},{1... | collective-permute-start | bytes 147464 | tf_op jit(solution)/shard_map/ppermute | solution.py:229
  33.1 0.0 collective-permute-done.12.far
  33.1 1.2 %collective-permute-done.13.near = bf16[16,1536]{1,0:T(8,128)(2,1)S(1)} collective-permute-done((bf16[16,1536]{1,0:T(8,128)(2,1)S(1)}, bf16[16,1536]{1,0:T(8,128)(2,1)S(1)}, u32[]{:S(2)}, u32[]{:S(2)}) %collective-permute-start.13) | collective-permute-done | bytes 49184 | tf_op jit(solution)/shard_map/ppermute | solution.py:229
  34.2 1.5 %step.9 = bf16[16,768]{1,0:T(8,128)(2,1)S(1)} custom-call(bf16[16,1536]{1,0:T(8,128)(2,1)S(1)} %collective-permute-done.12.far, bf16[16,1536]{1,0:T(8,128)(2,1)S(1)} %collective-permute-done.13.near, bf16[16,1536]{1,0:T(8,128)(2,1)S(1)} %step.7.previous, f32[16,1536]{1,0:T(8,128)S(1)} %get-tuple-element.25.load, ...), custom_call_target="tpu_custom_call" | custom-call | tf_op jit(solution)/shard_map/step/pallas_call | solution.py:296
  35.7 1.8 %collective-permute-start.14 = (bf16[16,768]{1,0:T(8,128)(2,1)S(1)}, bf16[16,768]{1,0:T(8,128)(2,1)S(1)}, u32[]{:S(2)}, u32[]{:S(2)}) collective-permute-start(bf16[16,768]{1,0:T(8,128)(2,1)S(1)} %step.9), channel_id=1, source_target_pairs={{0,1},{1,0},{2,3},{3,2},{4,5},{5,4},{6,7},{7,6},{8,9},{9,8},{10,11... | collective-permute-start | bytes 73736 | tf_op jit(solution)/shard_map/ppermute | solution.py:211
  37.5 1.5 %step.8.kept = bf16[16,768]{1,0:T(8,128)(2,1)S(1)} custom-call(bf16[16,1536]{1,0:T(8,128)(2,1)S(1)} %collective-permute-done.12.far, bf16[16,1536]{1,0:T(8,128)(2,1)S(1)} %collective-permute-done.13.near, bf16[16,1536]{1,0:T(8,128)(2,1)S(1)} %step.7.previous, f32[16,1536]{1,0:T(8,128)S(1)} %get-tuple-element.25.load, ...), custom_call_target="tpu_custom_call" | custom-call | tf_op jit(solution)/shard_map/step/pallas_call | solution.py:296
  39.0 0.0 collective-permute-done.14.got
  39.1 0.6 %finish.1 = bf16[32,768]{1,0:T(8,128)(2,1)} custom-call(bf16[16,768]{1,0:T(8,128)(2,1)S(1)} %step.8.kept, bf16[16,768]{1,0:T(8,128)(2,1)S(1)} %collective-permute-done.14.got), custom_call_target="tpu_custom_call" | custom-call | tf_op jit(solution)/shard_map/finish/pallas_call | solution.py:318
  (3 shorter events, 0.1 us)
Async XLA Ops:
  2.8 2.9 %collective-permute-start.3 = (bf16[6,2,128,128]{3,2,1,0:T(8,128)(2,1)S(1)}, bf16[6,2,128,128]{3,2,1,0:T(8,128)(2,1)S(1)}, u32[]{:S(2)}, u32[]{:S(2)}) collective-permute-start(bf16[6,2,128,128]{3,2,1,0:T(8,128)(2,1)S(1)} %get-tuple-element.22), channel_id=1, source_target_pairs={{0,1},{1,0},{2,3},{3,2},{4,5},{5,4},{6,7},{7,6},{8,9},{9,8},{10,11... | collective-permute-start | bytes 1179656 | tf_op jit(solution)/shard_map/ppermute | solution.py:211
  3.6 2.1 %collective-permute-start = (bf16[16,1536]{1,0:T(8,128)(2,1)S(1)}, bf16[16,1536]{1,0:T(8,128)(2,1)S(1)}, u32[]{:S(2)}, u32[]{:S(2)}) collective-permute-start(bf16[16,1536]{1,0:T(8,128)(2,1)S(1)} %get-tuple-element.18), channel_id=1, source_target_pairs={{0,1},{1,0},{2,3},{3,2},{4,5},{5,4},{6,7},{7,6},{8,9},{9,8},{10,11... | collective-permute-start | bytes 147464 | tf_op jit(solution)/shard_map/ppermute | solution.py:211
  3.6 5.5 %collective-permute-start.1 = (bf16[16,1536]{1,0:T(8,128)(2,1)S(1)}, bf16[16,1536]{1,0:T(8,128)(2,1)S(1)}, u32[]{:S(2)}, u32[]{:S(2)}) collective-permute-start(bf16[16,1536]{1,0:T(8,128)(2,1)S(1)} %get-tuple-element.19), channel_id=1, source_target_pairs={{0,2},{1,3},{2,0},{3,1},{4,6},{5,7},{6,4},{7,5},{8,10},{9,11},{10,... | collective-permute-start | bytes 147464 | tf_op jit(solution)/shard_map/ppermute | solution.py:211
  4.9 4.3 %collective-permute-start.2 = (bf16[16,1536]{1,0:T(8,128)(2,1)S(1)}, bf16[16,1536]{1,0:T(8,128)(2,1)S(1)}, u32[]{:S(2)}, u32[]{:S(2)}) collective-permute-start(bf16[16,1536]{1,0:T(8,128)(2,1)S(1)} %get-tuple-element.20), channel_id=1, source_target_pairs={{0,3},{1,2},{2,1},{3,0},{4,7},{5,6},{6,5},{7,4},{8,11},{9,10},{10,... | collective-permute-start | bytes 147464 | tf_op jit(solution)/shard_map/ppermute | solution.py:211
  9.2 2.6 %copy-start = (s32[1,6,8]{2,0,1:T(1,128)S(1)}, s32[1,6,8]{2,0,1:T(1,128)}, u32[]{:S(2)}) copy-start(s32[1,6,8]{2,0,1:T(1,128)} %param.9) | copy-start | bytes 580
  9.5 5.7 %collective-permute-start.6 = (bf16[6,8,2,128,128]{4,3,2,1,0:T(8,128)(2,1)S(1)}, bf16[6,8,2,128,128]{4,3,2,1,0:T(8,128)(2,1)S(1)}, u32[]{:S(2)}, u32[]{:S(2)}) collective-permute-start(bf16[6,8,2,128,128]{4,3,2,1,0:T(8,128)(2,1)S(1)} %get-tuple-element.27), channel_id=1, source_target_pairs={{0,1},{1,0},{2,3},{3,2},{4,5},{5,4},{6,7},{7,6},{8,9},{9,8},{10,11... | collective-permute-start | bytes 9437192 | tf_op jit(solution)/shard_map/ppermute | solution.py:211
  9.9 5.3 %collective-permute-start.4 = (bf16[16,1536]{1,0:T(8,128)(2,1)S(1)}, bf16[16,1536]{1,0:T(8,128)(2,1)S(1)}, u32[]{:S(2)}, u32[]{:S(2)}) collective-permute-start(bf16[16,1536]{1,0:T(8,128)(2,1)S(1)} %get-tuple-element.24.previous), channel_id=1, source_target_pairs={{0,6},{1,7},{2,4},{3,5},{4,10},{5,11},{6,8},{7,9},{8,14},{9,15},{1... | collective-permute-start | bytes 147464 | tf_op jit(solution)/shard_map/ppermute | solution.py:229
  10.5 4.7 %collective-permute-start.5 = (bf16[16,1536]{1,0:T(8,128)(2,1)S(1)}, bf16[16,1536]{1,0:T(8,128)(2,1)S(1)}, u32[]{:S(2)}, u32[]{:S(2)}) collective-permute-start(bf16[16,1536]{1,0:T(8,128)(2,1)S(1)} %get-tuple-element.24.previous), channel_id=1, source_target_pairs={{0,4},{1,5},{2,6},{3,7},{4,8},{5,9},{6,10},{7,11},{8,12},{9,13},{1... | collective-permute-start | bytes 147464 | tf_op jit(solution)/shard_map/ppermute | solution.py:229
  11.8 3.4 %collective-permute-start.7 = (s32[6,1,8]{2,1,0:T(1,128)S(1)}, s32[6,1,8]{2,1,0:T(1,128)S(1)}, u32[]{:S(2)}, u32[]{:S(2)}) collective-permute-start(s32[6,1,8]{2,1,0:T(1,128)S(1)} %bitcast.7), channel_id=1, source_target_pairs={{0,1},{1,0},{2,3},{3,2},{4,5},{5,4},{6,7},{7,6},{8,9},{9,8},{10,11... | collective-permute-start | bytes 584 | tf_op jit(solution)/shard_map/ppermute | solution.py:211
  15.3 4.8 %collective-permute-start.8 = (bf16[16,1536]{1,0:T(8,128)(2,1)S(1)}, bf16[16,1536]{1,0:T(8,128)(2,1)S(1)}, u32[]{:S(2)}, u32[]{:S(2)}) collective-permute-start(bf16[16,1536]{1,0:T(8,128)(2,1)S(1)} %step.5.previous), channel_id=1, source_target_pairs={{0,6},{1,7},{2,4},{3,5},{4,14},{5,15},{6,12},{7,13},{8,2},{9,3},{1... | collective-permute-start | bytes 147464 | tf_op jit(solution)/shard_map/ppermute | solution.py:229
  16.4 5.0 %collective-permute-start.9 = (bf16[16,1536]{1,0:T(8,128)(2,1)S(1)}, bf16[16,1536]{1,0:T(8,128)(2,1)S(1)}, u32[]{:S(2)}, u32[]{:S(2)}) collective-permute-start(bf16[16,1536]{1,0:T(8,128)(2,1)S(1)} %step.5.previous), channel_id=1, source_target_pairs={{0,4},{1,5},{2,6},{3,7},{4,12},{5,13},{6,14},{7,15},{8,0},{9,1},{1... | collective-permute-start | bytes 147464 | tf_op jit(solution)/shard_map/ppermute | solution.py:229
  21.4 3.9 %collective-permute-start.10 = (bf16[16,1536]{1,0:T(8,128)(2,1)S(1)}, bf16[16,1536]{1,0:T(8,128)(2,1)S(1)}, u32[]{:S(2)}, u32[]{:S(2)}) collective-permute-start(bf16[16,1536]{1,0:T(8,128)(2,1)S(1)} %step.6.previous), channel_id=1, source_target_pairs={{0,1},{1,0},{2,3},{3,2},{4,10},{5,11},{6,8},{7,9},{8,14},{9,15},{1... | collective-permute-start | bytes 147464 | tf_op jit(solution)/shard_map/ppermute | solution.py:229
  23.8 2.9 %collective-permute-start.11 = (bf16[16,1536]{1,0:T(8,128)(2,1)S(1)}, bf16[16,1536]{1,0:T(8,128)(2,1)S(1)}, u32[]{:S(2)}, u32[]{:S(2)}) collective-permute-start(bf16[16,1536]{1,0:T(8,128)(2,1)S(1)} %step.6.previous), channel_id=1, source_target_pairs={{0,1},{1,0},{2,3},{3,2},{4,8},{5,9},{6,10},{7,11},{8,12},{9,13},{1... | collective-permute-start | bytes 147464 | tf_op jit(solution)/shard_map/ppermute | solution.py:229
  26.8 6.3 %collective-permute-start.12 = (bf16[16,1536]{1,0:T(8,128)(2,1)S(1)}, bf16[16,1536]{1,0:T(8,128)(2,1)S(1)}, u32[]{:S(2)}, u32[]{:S(2)}) collective-permute-start(bf16[16,1536]{1,0:T(8,128)(2,1)S(1)} %step.7.previous), channel_id=1, source_target_pairs={{0,10},{1,11},{2,8},{3,9},{4,5},{5,4},{6,7},{7,6},{8,14},{9,15},{1... | collective-permute-start | bytes 147464 | tf_op jit(solution)/shard_map/ppermute | solution.py:229
  28.4 5.8 %collective-permute-start.13 = (bf16[16,1536]{1,0:T(8,128)(2,1)S(1)}, bf16[16,1536]{1,0:T(8,128)(2,1)S(1)}, u32[]{:S(2)}, u32[]{:S(2)}) collective-permute-start(bf16[16,1536]{1,0:T(8,128)(2,1)S(1)} %step.7.previous), channel_id=1, source_target_pairs={{0,1},{1,0},{2,3},{3,2},{4,8},{5,9},{6,10},{7,11},{8,12},{9,13},{1... | collective-permute-start | bytes 147464 | tf_op jit(solution)/shard_map/ppermute | solution.py:229
  35.7 3.3 %collective-permute-start.14 = (bf16[16,768]{1,0:T(8,128)(2,1)S(1)}, bf16[16,768]{1,0:T(8,128)(2,1)S(1)}, u32[]{:S(2)}, u32[]{:S(2)}) collective-permute-start(bf16[16,768]{1,0:T(8,128)(2,1)S(1)} %step.9), channel_id=1, source_target_pairs={{0,1},{1,0},{2,3},{3,2},{4,5},{5,4},{6,7},{7,6},{8,9},{9,8},{10,11... | collective-permute-start | bytes 73736 | tf_op jit(solution)/shard_map/ppermute | solution.py:211

commit v11 on v10

--- a/solution.py
+++ b/solution.py
@@ -140,9 +140,6 @@
     def across(blocks, *place):
         return jnp.concatenate([blocks[(*place, f)] for f in range(freqs)], axis=1)
 
-    def transfer_of(r):
-        return transfer_own if r < part else transfer_got
-
     def solve(pair, summed):
         matrix = jnp.concatenate([across(inverse, n) for n in pair], axis=0)
         solved = nn_dot(beside(*summed), matrix)
@@ -164,17 +161,22 @@
                 state[home] = source[:, r * block:(r + 1) * block]
         for copy in copies:
             copy.wait()
+        waiting = []
         for r in chosen[::2]:
             pair = (r, r + 1)
-            spans = [slice(n * block, (n + 1) * block) for n in pair]
             summed = []
-            for n, cols in zip(pair, spans):
+            for n in pair:
+                cols = slice(n * block, (n + 1) * block)
                 transfer = transfer_own if n < part else transfer_got
                 picked = jnp.concatenate(
                     [state[ids[n // part, n % part, 0, k]] for k in range(nonzero)], axis=1
                 )
                 matrix = jnp.concatenate([across(transfer, n % part, k) for k in range(nonzero)], axis=0)
                 summed.append((load[:, cols] + diagonal(nn_dot(picked, matrix), freqs)).astype(jnp.bfloat16))
+            waiting.append((pair, summed))
+            if len(waiting) > len(chosen):
+                solve(*waiting.pop(0))
+        for pair, summed in waiting:
             solve(pair, summed)
 
     @pl.when(bay != step)

time: 40.5 us -> 39.7 us (0.980)
  the two profiles are of different devices: /device:TPU:29 before, /device:TPU:17 now
where the time goes in v11:
time: 39.7 us; the launch traced here: 39.5 us
  starting transfers between devices  17.9 us (45%)
  waiting for transfers between devices  12.5 us (31%)
  Pallas kernels  9.03 us (23%)
    ppermute x8, starting transfers between devices, hop(): return lax.ppermute(value, ('bay', 'sec'), route)  9.87 us
    ppermute x8, waiting for transfers between devices, hop(): return lax.ppermute(value, ('bay', 'sec'), route)  9.21 us
    ppermute x7, starting transfers between devices, moved(): return lax.ppermute(value, ('bay', 'sec'), route)  8.05 us
    pallas_call x1, Pallas kernels, per_device(): pl.pallas_call(transfer_kernel, out_shape=[pltpu.VMEM(matrices, bf16)] *...  3.44 us
    ppermute x7, waiting for transfers between devices, moved(): return lax.ppermute(value, ('bay', 'sec'), route)  3.27 us
    pallas_call x1, Pallas kernels, per_device(): pl.pallas_call(force_kernel, out_shape=[jax.ShapeDtypeStruct(wide, bf16)]...  2.82 us
    pallas_call x5, Pallas kernels, advance(): pl.pallas_call(functools.partial(step_kernel, step, chosen), out_shape=ja...  1.84 us
  transfers between devices with their start and end apart: 15, of which 8 were waited for; matrix products, arithmetic and copies ran while one was open for 0% of the time, Pallas kernels for 9%

profile of v11, /device:TPU:17, one launch (start us, length us, event | category | flops | bytes accessed | tf_op | source)
XLA Modules:
  0.0 39.5 jit_solution(14383237100248047006)
XLA Ops:
  0.0 2.8 %force.1 = (bf16[16,1536]{1,0:T(8,128)(2,1)S(1)}, bf16[16,1536]{1,0:T(8,128)(2,1)S(1)}, bf16[16,1536]{1,0:T(8,128)(2,1)S(1)}, f32[16,1536]{1,0:T(8,128)S(1)}, bf...) custom-call(bf16[32,768]{1,0:T(8,128)(2,1)} %bitcast.16, bf16[32,768]{1,0:T(8,128)(2,1)} %bitcast.17, ...), custom_call_target="tpu_custom_call" | custom-call | tf_op jit(solution)/shard_map/force/pallas_call | solution.py:250
  2.8 0.7 %collective-permute-start.3 = (bf16[6,2,128,128]{3,2,1,0:T(8,128)(2,1)S(1)}, bf16[6,2,128,128]{3,2,1,0:T(8,128)(2,1)S(1)}, u32[]{:S(2)}, u32[]{:S(2)}) collective-permute-start(bf16[6,2,128,128]{3,2,1,0:T(8,128)(2,1)S(1)} %get-tuple-element.22), channel_id=1, source_target_pairs={{0,1},{1,0},{2,3},{3,2},{4,5},{5,4},{6,7},{7,6},{8,9},{9,8},{10,11... | collective-permute-start | bytes 1179656 | tf_op jit(solution)/shard_map/ppermute | solution.py:213
  3.6 0.1 collective-permute-start
  3.6 1.2 %collective-permute-start.1 = (bf16[16,1536]{1,0:T(8,128)(2,1)S(1)}, bf16[16,1536]{1,0:T(8,128)(2,1)S(1)}, u32[]{:S(2)}, u32[]{:S(2)}) collective-permute-start(bf16[16,1536]{1,0:T(8,128)(2,1)S(1)} %get-tuple-element.19), channel_id=1, source_target_pairs={{0,2},{1,3},{2,0},{3,1},{4,6},{5,7},{6,4},{7,5},{8,10},{9,11},{10,... | collective-permute-start | bytes 147464 | tf_op jit(solution)/shard_map/ppermute | solution.py:213
  4.9 0.9 %collective-permute-start.2 = (bf16[16,1536]{1,0:T(8,128)(2,1)S(1)}, bf16[16,1536]{1,0:T(8,128)(2,1)S(1)}, u32[]{:S(2)}, u32[]{:S(2)}) collective-permute-start(bf16[16,1536]{1,0:T(8,128)(2,1)S(1)} %get-tuple-element.20), channel_id=1, source_target_pairs={{0,3},{1,2},{2,1},{3,0},{4,7},{5,6},{6,5},{7,4},{8,11},{9,10},{10,... | collective-permute-start | bytes 147464 | tf_op jit(solution)/shard_map/ppermute | solution.py:213
  5.7 0.0 collective-permute-done.after.got1
  5.7 0.0 collective-permute-done.3.inverse_got
  5.7 3.4 %transfer.1 = (bf16[6,8,2,128,128]{4,3,2,1,0:T(8,128)(2,1)S(1)}, bf16[6,8,2,128,128]{4,3,2,1,0:T(8,128)(2,1)S(1)}, bf16[12,2,128,128]{3,2,1,0:T(8,128)(2,1)S(1)}) custom-call(bf16[6,8,4,128,128]{4,3,2,1,0:T(8,128)(2,1)} %bitcast.13, bf16[6,2,128,128]{3,2,1,0:T(8,128)(2,1)S(1)} %get-tuple-element.21.inverse_own, ...), custom_call_target="tpu_custom_call" | custom-call | tf_op jit(solution)/shard_map/transfer/pallas_call | solution.py:269
  9.2 0.0 copy-start
  9.2 0.0 collective-permute-done.1.got2
  9.2 0.0 collective-permute-done.2.got3
  9.2 0.3 initial.1
  9.5 0.4 %collective-permute-start.6 = (bf16[6,8,2,128,128]{4,3,2,1,0:T(8,128)(2,1)S(1)}, bf16[6,8,2,128,128]{4,3,2,1,0:T(8,128)(2,1)S(1)}, u32[]{:S(2)}, u32[]{:S(2)}) collective-permute-start(bf16[6,8,2,128,128]{4,3,2,1,0:T(8,128)(2,1)S(1)} %get-tuple-element.27), channel_id=1, source_target_pairs={{0,1},{1,0},{2,3},{3,2},{4,5},{5,4},{6,7},{7,6},{8,9},{9,8},{10,11... | collective-permute-start | bytes 9437192 | tf_op jit(solution)/shard_map/ppermute | solution.py:213
  9.9 1.9 %collective-permute-start.4 = (bf16[16,1536]{1,0:T(8,128)(2,1)S(1)}, bf16[16,1536]{1,0:T(8,128)(2,1)S(1)}, u32[]{:S(2)}, u32[]{:S(2)}) collective-permute-start(bf16[16,1536]{1,0:T(8,128)(2,1)S(1)} %get-tuple-element.24.previous), channel_id=1, source_target_pairs={{0,6},{1,7},{2,4},{3,5},{4,10},{5,11},{6,8},{7,9},{8,14},{9,15},{1... | collective-permute-start | bytes 147464 | tf_op jit(solution)/shard_map/ppermute | solution.py:231
  11.8 0.0 collective-permute-start.5
  11.8 0.0 copy-done
  11.8 0.9 %collective-permute-start.7 = (s32[6,1,8]{2,1,0:T(1,128)S(1)}, s32[6,1,8]{2,1,0:T(1,128)S(1)}, u32[]{:S(2)}, u32[]{:S(2)}) collective-permute-start(s32[6,1,8]{2,1,0:T(1,128)S(1)} %bitcast.7), channel_id=1, source_target_pairs={{0,1},{1,0},{2,3},{3,2},{4,5},{5,4},{6,7},{7,6},{8,9},{9,8},{10,11... | collective-permute-start | bytes 584 | tf_op jit(solution)/shard_map/ppermute | solution.py:213
  12.8 2.4 %collective-permute-done.7.cols_got = s32[6,1,8]{2,1,0:T(1,128)S(1)} collective-permute-done((s32[6,1,8]{2,1,0:T(1,128)S(1)}, s32[6,1,8]{2,1,0:T(1,128)S(1)}, u32[]{:S(2)}, u32[]{:S(2)}) %collective-permute-start.7) | collective-permute-done | bytes 224 | tf_op jit(solution)/shard_map/ppermute | solution.py:213
  15.2 0.0 collective-permute-done.4.far
  15.2 0.0 collective-permute-done.5.near
  15.2 0.0 collective-permute-done.6.transfer_got
  15.3 3.7 %collective-permute-start.8 = (bf16[16,1536]{1,0:T(8,128)(2,1)S(1)}, bf16[16,1536]{1,0:T(8,128)(2,1)S(1)}, u32[]{:S(2)}, u32[]{:S(2)}) collective-permute-start(bf16[16,1536]{1,0:T(8,128)(2,1)S(1)} %step.5.previous), channel_id=1, source_target_pairs={{0,6},{1,7},{2,4},{3,5},{4,14},{5,15},{6,12},{7,13},{8,2},{9,3},{1... | collective-permute-start | bytes 147464 | tf_op jit(solution)/shard_map/ppermute | solution.py:231
  19.0 0.0 collective-permute-start.9
  19.0 1.2 %collective-permute-done.8.far = bf16[16,1536]{1,0:T(8,128)(2,1)S(1)} collective-permute-done((bf16[16,1536]{1,0:T(8,128)(2,1)S(1)}, bf16[16,1536]{1,0:T(8,128)(2,1)S(1)}, u32[]{:S(2)}, u32[]{:S(2)}) %collective-permute-start.8) | collective-permute-done | bytes 49184 | tf_op jit(solution)/shard_map/ppermute | solution.py:231
  20.2 1.8 %collective-permute-done.9.near = bf16[16,1536]{1,0:T(8,128)(2,1)S(1)} collective-permute-done((bf16[16,1536]{1,0:T(8,128)(2,1)S(1)}, bf16[16,1536]{1,0:T(8,128)(2,1)S(1)}, u32[]{:S(2)}, u32[]{:S(2)}) %collective-permute-start.9) | collective-permute-done | bytes 49184 | tf_op jit(solution)/shard_map/ppermute | solution.py:231
  22.0 0.4 collective-permute-start.10
  22.4 2.3 %collective-permute-start.11 = (bf16[16,1536]{1,0:T(8,128)(2,1)S(1)}, bf16[16,1536]{1,0:T(8,128)(2,1)S(1)}, u32[]{:S(2)}, u32[]{:S(2)}) collective-permute-start(bf16[16,1536]{1,0:T(8,128)(2,1)S(1)} %step.6.previous), channel_id=1, source_target_pairs={{0,1},{1,0},{2,3},{3,2},{4,8},{5,9},{6,10},{7,11},{8,12},{9,13},{1... | collective-permute-start | bytes 147464 | tf_op jit(solution)/shard_map/ppermute | solution.py:231
  24.6 1.3 %collective-permute-done.10.far = bf16[16,1536]{1,0:T(8,128)(2,1)S(1)} collective-permute-done((bf16[16,1536]{1,0:T(8,128)(2,1)S(1)}, bf16[16,1536]{1,0:T(8,128)(2,1)S(1)}, u32[]{:S(2)}, u32[]{:S(2)}) %collective-permute-start.10) | collective-permute-done | bytes 49184 | tf_op jit(solution)/shard_map/ppermute | solution.py:231
  25.9 0.1 collective-permute-done.11.near
  26.0 1.7 %step.7.previous = bf16[16,1536]{1,0:T(8,128)(2,1)S(1)} custom-call(bf16[16,1536]{1,0:T(8,128)(2,1)S(1)} %collective-permute-done.10.far, bf16[16,1536]{1,0:T(8,128)(2,1)S(1)} %collective-permute-done.11.near, bf16[16,1536]{1,0:T(8,128)(2,1)S(1)} %step.6.previous, f32[16,1536]{1,0:T(8,128)S(1)} %get-tuple-element.25.load, ...), custom_call_target="tpu_custom_call" | custom-call | tf_op jit(solution)/shard_map/step/pallas_call | solution.py:298
  27.7 1.1 %collective-permute-start.12 = (bf16[16,1536]{1,0:T(8,128)(2,1)S(1)}, bf16[16,1536]{1,0:T(8,128)(2,1)S(1)}, u32[]{:S(2)}, u32[]{:S(2)}) collective-permute-start(bf16[16,1536]{1,0:T(8,128)(2,1)S(1)} %step.7.previous), channel_id=1, source_target_pairs={{0,10},{1,11},{2,8},{3,9},{4,5},{5,4},{6,7},{7,6},{8,14},{9,15},{1... | collective-permute-start | bytes 147464 | tf_op jit(solution)/shard_map/ppermute | solution.py:231
  28.8 0.5 %collective-permute-start.13 = (bf16[16,1536]{1,0:T(8,128)(2,1)S(1)}, bf16[16,1536]{1,0:T(8,128)(2,1)S(1)}, u32[]{:S(2)}, u32[]{:S(2)}) collective-permute-start(bf16[16,1536]{1,0:T(8,128)(2,1)S(1)} %step.7.previous), channel_id=1, source_target_pairs={{0,1},{1,0},{2,3},{3,2},{4,8},{5,9},{6,10},{7,11},{8,12},{9,13},{1... | collective-permute-start | bytes 147464 | tf_op jit(solution)/shard_map/ppermute | solution.py:231
  29.3 3.2 %collective-permute-done.12.far = bf16[16,1536]{1,0:T(8,128)(2,1)S(1)} collective-permute-done((bf16[16,1536]{1,0:T(8,128)(2,1)S(1)}, bf16[16,1536]{1,0:T(8,128)(2,1)S(1)}, u32[]{:S(2)}, u32[]{:S(2)}) %collective-permute-start.12) | collective-permute-done | bytes 49184 | tf_op jit(solution)/shard_map/ppermute | solution.py:231
  32.5 1.7 %collective-permute-done.13.near = bf16[16,1536]{1,0:T(8,128)(2,1)S(1)} collective-permute-done((bf16[16,1536]{1,0:T(8,128)(2,1)S(1)}, bf16[16,1536]{1,0:T(8,128)(2,1)S(1)}, u32[]{:S(2)}, u32[]{:S(2)}) %collective-permute-start.13) | collective-permute-done | bytes 49184 | tf_op jit(solution)/shard_map/ppermute | solution.py:231
  34.3 3.8 %collective-permute-start.14 = (bf16[16,768]{1,0:T(8,128)(2,1)S(1)}, bf16[16,768]{1,0:T(8,128)(2,1)S(1)}, u32[]{:S(2)}, u32[]{:S(2)}) collective-permute-start(bf16[16,768]{1,0:T(8,128)(2,1)S(1)} %step.9), channel_id=1, source_target_pairs={{0,1},{1,0},{2,3},{3,2},{4,5},{5,4},{6,7},{7,6},{8,9},{9,8},{10,11... | collective-permute-start | bytes 73736 | tf_op jit(solution)/shard_map/ppermute | solution.py:213
  38.1 0.8 %collective-permute-done.14.got = bf16[16,768]{1,0:T(8,128)(2,1)S(1)} collective-permute-done((bf16[16,768]{1,0:T(8,128)(2,1)S(1)}, bf16[16,768]{1,0:T(8,128)(2,1)S(1)}, u32[]{:S(2)}, u32[]{:S(2)}) %collective-permute-start.14) | collective-permute-done | bytes 24608 | tf_op jit(solution)/shard_map/ppermute | solution.py:213
  38.9 0.6 %finish.1 = bf16[32,768]{1,0:T(8,128)(2,1)} custom-call(bf16[16,768]{1,0:T(8,128)(2,1)S(1)} %step.8.kept, bf16[16,768]{1,0:T(8,128)(2,1)S(1)} %collective-permute-done.14.got), custom_call_target="tpu_custom_call" | custom-call | tf_op jit(solution)/shard_map/finish/pallas_call | solution.py:320
  (4 shorter events, 0.1 us)
Async XLA Ops:
  2.8 2.9 %collective-permute-start.3 = (bf16[6,2,128,128]{3,2,1,0:T(8,128)(2,1)S(1)}, bf16[6,2,128,128]{3,2,1,0:T(8,128)(2,1)S(1)}, u32[]{:S(2)}, u32[]{:S(2)}) collective-permute-start(bf16[6,2,128,128]{3,2,1,0:T(8,128)(2,1)S(1)} %get-tuple-element.22), channel_id=1, source_target_pairs={{0,1},{1,0},{2,3},{3,2},{4,5},{5,4},{6,7},{7,6},{8,9},{9,8},{10,11... | collective-permute-start | bytes 1179656 | tf_op jit(solution)/shard_map/ppermute | solution.py:213
  3.6 2.1 %collective-permute-start = (bf16[16,1536]{1,0:T(8,128)(2,1)S(1)}, bf16[16,1536]{1,0:T(8,128)(2,1)S(1)}, u32[]{:S(2)}, u32[]{:S(2)}) collective-permute-start(bf16[16,1536]{1,0:T(8,128)(2,1)S(1)} %get-tuple-element.18), channel_id=1, source_target_pairs={{0,1},{1,0},{2,3},{3,2},{4,5},{5,4},{6,7},{7,6},{8,9},{9,8},{10,11... | collective-permute-start | bytes 147464 | tf_op jit(solution)/shard_map/ppermute | solution.py:213
  3.6 5.5 %collective-permute-start.1 = (bf16[16,1536]{1,0:T(8,128)(2,1)S(1)}, bf16[16,1536]{1,0:T(8,128)(2,1)S(1)}, u32[]{:S(2)}, u32[]{:S(2)}) collective-permute-start(bf16[16,1536]{1,0:T(8,128)(2,1)S(1)} %get-tuple-element.19), channel_id=1, source_target_pairs={{0,2},{1,3},{2,0},{3,1},{4,6},{5,7},{6,4},{7,5},{8,10},{9,11},{10,... | collective-permute-start | bytes 147464 | tf_op jit(solution)/shard_map/ppermute | solution.py:213
  4.9 4.3 %collective-permute-start.2 = (bf16[16,1536]{1,0:T(8,128)(2,1)S(1)}, bf16[16,1536]{1,0:T(8,128)(2,1)S(1)}, u32[]{:S(2)}, u32[]{:S(2)}) collective-permute-start(bf16[16,1536]{1,0:T(8,128)(2,1)S(1)} %get-tuple-element.20), channel_id=1, source_target_pairs={{0,3},{1,2},{2,1},{3,0},{4,7},{5,6},{6,5},{7,4},{8,11},{9,10},{10,... | collective-permute-start | bytes 147464 | tf_op jit(solution)/shard_map/ppermute | solution.py:213
  9.2 2.7 %copy-start = (s32[1,6,8]{2,0,1:T(1,128)S(1)}, s32[1,6,8]{2,0,1:T(1,128)}, u32[]{:S(2)}) copy-start(s32[1,6,8]{2,0,1:T(1,128)} %param.9) | copy-start | bytes 580
  9.5 5.7 %collective-permute-start.6 = (bf16[6,8,2,128,128]{4,3,2,1,0:T(8,128)(2,1)S(1)}, bf16[6,8,2,128,128]{4,3,2,1,0:T(8,128)(2,1)S(1)}, u32[]{:S(2)}, u32[]{:S(2)}) collective-permute-start(bf16[6,8,2,128,128]{4,3,2,1,0:T(8,128)(2,1)S(1)} %get-tuple-element.27), channel_id=1, source_target_pairs={{0,1},{1,0},{2,3},{3,2},{4,5},{5,4},{6,7},{7,6},{8,9},{9,8},{10,11... | collective-permute-start | bytes 9437192 | tf_op jit(solution)/shard_map/ppermute | solution.py:213
  9.9 5.3 %collective-permute-start.4 = (bf16[16,1536]{1,0:T(8,128)(2,1)S(1)}, bf16[16,1536]{1,0:T(8,128)(2,1)S(1)}, u32[]{:S(2)}, u32[]{:S(2)}) collective-permute-start(bf16[16,1536]{1,0:T(8,128)(2,1)S(1)} %get-tuple-element.24.previous), channel_id=1, source_target_pairs={{0,6},{1,7},{2,4},{3,5},{4,10},{5,11},{6,8},{7,9},{8,14},{9,15},{1... | collective-permute-start | bytes 147464 | tf_op jit(solution)/shard_map/ppermute | solution.py:231
  11.8 3.4 %collective-permute-start.5 = (bf16[16,1536]{1,0:T(8,128)(2,1)S(1)}, bf16[16,1536]{1,0:T(8,128)(2,1)S(1)}, u32[]{:S(2)}, u32[]{:S(2)}) collective-permute-start(bf16[16,1536]{1,0:T(8,128)(2,1)S(1)} %get-tuple-element.24.previous), channel_id=1, source_target_pairs={{0,4},{1,5},{2,6},{3,7},{4,8},{5,9},{6,10},{7,11},{8,12},{9,13},{1... | collective-permute-start | bytes 147464 | tf_op jit(solution)/shard_map/ppermute | solution.py:231
  11.8 3.4 %collective-permute-start.7 = (s32[6,1,8]{2,1,0:T(1,128)S(1)}, s32[6,1,8]{2,1,0:T(1,128)S(1)}, u32[]{:S(2)}, u32[]{:S(2)}) collective-permute-start(s32[6,1,8]{2,1,0:T(1,128)S(1)} %bitcast.7), channel_id=1, source_target_pairs={{0,1},{1,0},{2,3},{3,2},{4,5},{5,4},{6,7},{7,6},{8,9},{9,8},{10,11... | collective-permute-start | bytes 584 | tf_op jit(solution)/shard_map/ppermute | solution.py:213
  15.3 4.9 %collective-permute-start.8 = (bf16[16,1536]{1,0:T(8,128)(2,1)S(1)}, bf16[16,1536]{1,0:T(8,128)(2,1)S(1)}, u32[]{:S(2)}, u32[]{:S(2)}) collective-permute-start(bf16[16,1536]{1,0:T(8,128)(2,1)S(1)} %step.5.previous), channel_id=1, source_target_pairs={{0,6},{1,7},{2,4},{3,5},{4,14},{5,15},{6,12},{7,13},{8,2},{9,3},{1... | collective-permute-start | bytes 147464 | tf_op jit(solution)/shard_map/ppermute | solution.py:231
  19.0 2.9 %collective-permute-start.9 = (bf16[16,1536]{1,0:T(8,128)(2,1)S(1)}, bf16[16,1536]{1,0:T(8,128)(2,1)S(1)}, u32[]{:S(2)}, u32[]{:S(2)}) collective-permute-start(bf16[16,1536]{1,0:T(8,128)(2,1)S(1)} %step.5.previous), channel_id=1, source_target_pairs={{0,4},{1,5},{2,6},{3,7},{4,12},{5,13},{6,14},{7,15},{8,0},{9,1},{1... | collective-permute-start | bytes 147464 | tf_op jit(solution)/shard_map/ppermute | solution.py:231
  22.0 3.9 %collective-permute-start.10 = (bf16[16,1536]{1,0:T(8,128)(2,1)S(1)}, bf16[16,1536]{1,0:T(8,128)(2,1)S(1)}, u32[]{:S(2)}, u32[]{:S(2)}) collective-permute-start(bf16[16,1536]{1,0:T(8,128)(2,1)S(1)} %step.6.previous), channel_id=1, source_target_pairs={{0,1},{1,0},{2,3},{3,2},{4,10},{5,11},{6,8},{7,9},{8,14},{9,15},{1... | collective-permute-start | bytes 147464 | tf_op jit(solution)/shard_map/ppermute | solution.py:231
  22.4 3.6 %collective-permute-start.11 = (bf16[16,1536]{1,0:T(8,128)(2,1)S(1)}, bf16[16,1536]{1,0:T(8,128)(2,1)S(1)}, u32[]{:S(2)}, u32[]{:S(2)}) collective-permute-start(bf16[16,1536]{1,0:T(8,128)(2,1)S(1)} %step.6.previous), channel_id=1, source_target_pairs={{0,1},{1,0},{2,3},{3,2},{4,8},{5,9},{6,10},{7,11},{8,12},{9,13},{1... | collective-permute-start | bytes 147464 | tf_op jit(solution)/shard_map/ppermute | solution.py:231
  27.7 4.8 %collective-permute-start.12 = (bf16[16,1536]{1,0:T(8,128)(2,1)S(1)}, bf16[16,1536]{1,0:T(8,128)(2,1)S(1)}, u32[]{:S(2)}, u32[]{:S(2)}) collective-permute-start(bf16[16,1536]{1,0:T(8,128)(2,1)S(1)} %step.7.previous), channel_id=1, source_target_pairs={{0,10},{1,11},{2,8},{3,9},{4,5},{5,4},{6,7},{7,6},{8,14},{9,15},{1... | collective-permute-start | bytes 147464 | tf_op jit(solution)/shard_map/ppermute | solution.py:231
  28.8 5.4 %collective-permute-start.13 = (bf16[16,1536]{1,0:T(8,128)(2,1)S(1)}, bf16[16,1536]{1,0:T(8,128)(2,1)S(1)}, u32[]{:S(2)}, u32[]{:S(2)}) collective-permute-start(bf16[16,1536]{1,0:T(8,128)(2,1)S(1)} %step.7.previous), channel_id=1, source_target_pairs={{0,1},{1,0},{2,3},{3,2},{4,8},{5,9},{6,10},{7,11},{8,12},{9,13},{1... | collective-permute-start | bytes 147464 | tf_op jit(solution)/shard_map/ppermute | solution.py:231
  34.3 4.7 %collective-permute-start.14 = (bf16[16,768]{1,0:T(8,128)(2,1)S(1)}, bf16[16,768]{1,0:T(8,128)(2,1)S(1)}, u32[]{:S(2)}, u32[]{:S(2)}) collective-permute-start(bf16[16,768]{1,0:T(8,128)(2,1)S(1)} %step.9), channel_id=1, source_target_pairs={{0,1},{1,0},{2,3},{3,2},{4,5},{5,4},{6,7},{7,6},{8,9},{9,8},{10,11... | collective-permute-start | bytes 73736 | tf_op jit(solution)/shard_map/ppermute | solution.py:213

commit v12 on v11

--- a/solution.py
+++ b/solution.py
@@ -217,10 +217,12 @@
     bays, secs = lax.axis_size("bay"), lax.axis_size("sec")
     target = (source + 1) % bays
     cycle = list(range(bays))
-    if bays > 3 and target == 1:
-        cycle = [0, 1, 3, 2]
-    elif bays > 3 and target > 1:
-        after = target + 1 if target + 1 < bays else 0 if offset else source - 1
+    if bays > 3 and target > 0:
+        after = target + 1
+        if target == 1:
+            after = 2 if offset else 3
+        elif after == bays:
+            after = 0 if offset else source - 1
         cycle = [source, target, after]
     goes = {b: cycle[(n + 1) % len(cycle)] for n, b in enumerate(cycle)}
     route = [

time: 39.7 us -> 39 us (0.982)
  the two profiles are of different devices: /device:TPU:17 before, /device:TPU:29 now
where the time goes in v12:
time: 39 us; the launch traced here: 38.5 us
  starting transfers between devices  20.7 us (53%)
  Pallas kernels  9.91 us (25%)
  waiting for transfers between devices  7.75 us (20%)
    ppermute x8, starting transfers between devices, hop(): return lax.ppermute(value, ('bay', 'sec'), route)  13.5 us
    ppermute x7, starting transfers between devices, moved(): return lax.ppermute(value, ('bay', 'sec'), route)  7.19 us
    ppermute x8, waiting for transfers between devices, hop(): return lax.ppermute(value, ('bay', 'sec'), route)  5.3 us
    pallas_call x1, Pallas kernels, per_device(): pl.pallas_call(transfer_kernel, out_shape=[pltpu.VMEM(matrices, bf16)] *...  3.44 us
    pallas_call x1, Pallas kernels, per_device(): pl.pallas_call(force_kernel, out_shape=[jax.ShapeDtypeStruct(wide, bf16)]...  2.82 us
    pallas_call x5, Pallas kernels, advance(): pl.pallas_call(functools.partial(step_kernel, step, chosen), out_shape=ja...  2.7 us
    ppermute x7, waiting for transfers between devices, moved(): return lax.ppermute(value, ('bay', 'sec'), route)  2.45 us
  transfers between devices with their start and end apart: 15, of which 5 were waited for; matrix products, arithmetic and copies ran while one was open for 0% of the time, Pallas kernels for 12%

profile of v12, /device:TPU:29, one launch (start us, length us, event | category | flops | bytes accessed | tf_op | source)
XLA Modules:
  0.0 38.5 jit_solution(14874530315736693034)
XLA Ops:
  0.0 2.8 %force.1 = (bf16[16,1536]{1,0:T(8,128)(2,1)S(1)}, bf16[16,1536]{1,0:T(8,128)(2,1)S(1)}, bf16[16,1536]{1,0:T(8,128)(2,1)S(1)}, f32[16,1536]{1,0:T(8,128)S(1)}, bf...) custom-call(bf16[32,768]{1,0:T(8,128)(2,1)} %bitcast.16, bf16[32,768]{1,0:T(8,128)(2,1)} %bitcast.17, ...), custom_call_target="tpu_custom_call" | custom-call | tf_op jit(solution)/shard_map/force/pallas_call | solution.py:252
  2.8 0.7 %collective-permute-start.3 = (bf16[6,2,128,128]{3,2,1,0:T(8,128)(2,1)S(1)}, bf16[6,2,128,128]{3,2,1,0:T(8,128)(2,1)S(1)}, u32[]{:S(2)}, u32[]{:S(2)}) collective-permute-start(bf16[6,2,128,128]{3,2,1,0:T(8,128)(2,1)S(1)} %get-tuple-element.22), channel_id=1, source_target_pairs={{0,1},{1,0},{2,3},{3,2},{4,5},{5,4},{6,7},{7,6},{8,9},{9,8},{10,11... | collective-permute-start | bytes 1179656 | tf_op jit(solution)/shard_map/ppermute | solution.py:213
  3.6 0.1 collective-permute-start
  3.6 1.2 %collective-permute-start.1 = (bf16[16,1536]{1,0:T(8,128)(2,1)S(1)}, bf16[16,1536]{1,0:T(8,128)(2,1)S(1)}, u32[]{:S(2)}, u32[]{:S(2)}) collective-permute-start(bf16[16,1536]{1,0:T(8,128)(2,1)S(1)} %get-tuple-element.19), channel_id=1, source_target_pairs={{0,2},{1,3},{2,0},{3,1},{4,6},{5,7},{6,4},{7,5},{8,10},{9,11},{10,... | collective-permute-start | bytes 147464 | tf_op jit(solution)/shard_map/ppermute | solution.py:213
  4.9 0.9 %collective-permute-start.2 = (bf16[16,1536]{1,0:T(8,128)(2,1)S(1)}, bf16[16,1536]{1,0:T(8,128)(2,1)S(1)}, u32[]{:S(2)}, u32[]{:S(2)}) collective-permute-start(bf16[16,1536]{1,0:T(8,128)(2,1)S(1)} %get-tuple-element.20), channel_id=1, source_target_pairs={{0,3},{1,2},{2,1},{3,0},{4,7},{5,6},{6,5},{7,4},{8,11},{9,10},{10,... | collective-permute-start | bytes 147464 | tf_op jit(solution)/shard_map/ppermute | solution.py:213
  5.7 0.0 collective-permute-done.after.got1
  5.7 0.0 collective-permute-done.3.inverse_got
  5.7 3.4 %transfer.1 = (bf16[6,8,2,128,128]{4,3,2,1,0:T(8,128)(2,1)S(1)}, bf16[6,8,2,128,128]{4,3,2,1,0:T(8,128)(2,1)S(1)}, bf16[12,2,128,128]{3,2,1,0:T(8,128)(2,1)S(1)}) custom-call(bf16[6,8,4,128,128]{4,3,2,1,0:T(8,128)(2,1)} %bitcast.13, bf16[6,2,128,128]{3,2,1,0:T(8,128)(2,1)S(1)} %get-tuple-element.21.inverse_own, ...), custom_call_target="tpu_custom_call" | custom-call | tf_op jit(solution)/shard_map/transfer/pallas_call | solution.py:271
  9.2 0.0 copy-start
  9.2 0.0 collective-permute-done.1.got2
  9.2 0.0 collective-permute-done.2.got3
  9.2 0.3 initial.1
  9.5 0.4 %collective-permute-start.6 = (bf16[6,8,2,128,128]{4,3,2,1,0:T(8,128)(2,1)S(1)}, bf16[6,8,2,128,128]{4,3,2,1,0:T(8,128)(2,1)S(1)}, u32[]{:S(2)}, u32[]{:S(2)}) collective-permute-start(bf16[6,8,2,128,128]{4,3,2,1,0:T(8,128)(2,1)S(1)} %get-tuple-element.27), channel_id=1, source_target_pairs={{0,1},{1,0},{2,3},{3,2},{4,5},{5,4},{6,7},{7,6},{8,9},{9,8},{10,11... | collective-permute-start | bytes 9437192 | tf_op jit(solution)/shard_map/ppermute | solution.py:213
  9.9 0.6 %collective-permute-start.4 = (bf16[16,1536]{1,0:T(8,128)(2,1)S(1)}, bf16[16,1536]{1,0:T(8,128)(2,1)S(1)}, u32[]{:S(2)}, u32[]{:S(2)}) collective-permute-start(bf16[16,1536]{1,0:T(8,128)(2,1)S(1)} %get-tuple-element.24.previous), channel_id=1, source_target_pairs={{0,6},{1,7},{2,4},{3,5},{4,10},{5,11},{6,8},{7,9},{8,14},{9,15},{1... | collective-permute-start | bytes 147464 | tf_op jit(solution)/shard_map/ppermute | solution.py:233
  10.5 1.3 %collective-permute-start.5 = (bf16[16,1536]{1,0:T(8,128)(2,1)S(1)}, bf16[16,1536]{1,0:T(8,128)(2,1)S(1)}, u32[]{:S(2)}, u32[]{:S(2)}) collective-permute-start(bf16[16,1536]{1,0:T(8,128)(2,1)S(1)} %get-tuple-element.24.previous), channel_id=1, source_target_pairs={{0,4},{1,5},{2,6},{3,7},{4,8},{5,9},{6,10},{7,11},{8,12},{9,13},{1... | collective-permute-start | bytes 147464 | tf_op jit(solution)/shard_map/ppermute | solution.py:233
  11.8 0.0 copy-done
  11.8 1.0 %collective-permute-start.7 = (s32[6,1,8]{2,1,0:T(1,128)S(1)}, s32[6,1,8]{2,1,0:T(1,128)S(1)}, u32[]{:S(2)}, u32[]{:S(2)}) collective-permute-start(s32[6,1,8]{2,1,0:T(1,128)S(1)} %bitcast.7), channel_id=1, source_target_pairs={{0,1},{1,0},{2,3},{3,2},{4,5},{5,4},{6,7},{7,6},{8,9},{9,8},{10,11... | collective-permute-start | bytes 584 | tf_op jit(solution)/shard_map/ppermute | solution.py:213
  12.8 2.4 %collective-permute-done.7.cols_got = s32[6,1,8]{2,1,0:T(1,128)S(1)} collective-permute-done((s32[6,1,8]{2,1,0:T(1,128)S(1)}, s32[6,1,8]{2,1,0:T(1,128)S(1)}, u32[]{:S(2)}, u32[]{:S(2)}) %collective-permute-start.7) | collective-permute-done | bytes 224 | tf_op jit(solution)/shard_map/ppermute | solution.py:213
  15.2 0.0 collective-permute-done.4.far
  15.2 0.0 collective-permute-done.5.near
  15.2 0.0 collective-permute-done.6.transfer_got
  15.3 0.6 %collective-permute-start.8 = (bf16[16,1536]{1,0:T(8,128)(2,1)S(1)}, bf16[16,1536]{1,0:T(8,128)(2,1)S(1)}, u32[]{:S(2)}, u32[]{:S(2)}) collective-permute-start(bf16[16,1536]{1,0:T(8,128)(2,1)S(1)} %step.5.previous), channel_id=1, source_target_pairs={{0,6},{1,7},{2,4},{3,5},{4,10},{5,11},{6,8},{7,9},{8,2},{9,3},{10,... | collective-permute-start | bytes 147464 | tf_op jit(solution)/shard_map/ppermute | solution.py:233
  15.8 2.7 %collective-permute-start.9 = (bf16[16,1536]{1,0:T(8,128)(2,1)S(1)}, bf16[16,1536]{1,0:T(8,128)(2,1)S(1)}, u32[]{:S(2)}, u32[]{:S(2)}) collective-permute-start(bf16[16,1536]{1,0:T(8,128)(2,1)S(1)} %step.5.previous), channel_id=1, source_target_pairs={{0,4},{1,5},{2,6},{3,7},{4,12},{5,13},{6,14},{7,15},{8,9},{9,8},{1... | collective-permute-start | bytes 147464 | tf_op jit(solution)/shard_map/ppermute | solution.py:233
  18.5 0.0 collective-permute-done.8.far
  18.5 1.3 %collective-permute-done.9.near = bf16[16,1536]{1,0:T(8,128)(2,1)S(1)} collective-permute-done((bf16[16,1536]{1,0:T(8,128)(2,1)S(1)}, bf16[16,1536]{1,0:T(8,128)(2,1)S(1)}, u32[]{:S(2)}, u32[]{:S(2)}) %collective-permute-start.9) | collective-permute-done | bytes 49184 | tf_op jit(solution)/shard_map/ppermute | solution.py:233
  19.9 3.1 %collective-permute-start.10 = (bf16[16,1536]{1,0:T(8,128)(2,1)S(1)}, bf16[16,1536]{1,0:T(8,128)(2,1)S(1)}, u32[]{:S(2)}, u32[]{:S(2)}) collective-permute-start(bf16[16,1536]{1,0:T(8,128)(2,1)S(1)} %step.6.previous), channel_id=1, source_target_pairs={{0,1},{1,0},{2,3},{3,2},{4,10},{5,11},{6,8},{7,9},{8,14},{9,15},{1... | collective-permute-start | bytes 147464 | tf_op jit(solution)/shard_map/ppermute | solution.py:233
  23.0 0.8 %collective-permute-start.11 = (bf16[16,1536]{1,0:T(8,128)(2,1)S(1)}, bf16[16,1536]{1,0:T(8,128)(2,1)S(1)}, u32[]{:S(2)}, u32[]{:S(2)}) collective-permute-start(bf16[16,1536]{1,0:T(8,128)(2,1)S(1)} %step.6.previous), channel_id=1, source_target_pairs={{0,1},{1,0},{2,3},{3,2},{4,8},{5,9},{6,10},{7,11},{8,12},{9,13},{1... | collective-permute-start | bytes 147464 | tf_op jit(solution)/shard_map/ppermute | solution.py:233
  23.8 0.4 collective-permute-done.10.far
  24.2 2.4 %collective-permute-done.11.near = bf16[16,1536]{1,0:T(8,128)(2,1)S(1)} collective-permute-done((bf16[16,1536]{1,0:T(8,128)(2,1)S(1)}, bf16[16,1536]{1,0:T(8,128)(2,1)S(1)}, u32[]{:S(2)}, u32[]{:S(2)}) %collective-permute-start.11) | collective-permute-done | bytes 49184 | tf_op jit(solution)/shard_map/ppermute | solution.py:233
  26.6 1.0 %collective-permute-start.12 = (bf16[16,1536]{1,0:T(8,128)(2,1)S(1)}, bf16[16,1536]{1,0:T(8,128)(2,1)S(1)}, u32[]{:S(2)}, u32[]{:S(2)}) collective-permute-start(bf16[16,1536]{1,0:T(8,128)(2,1)S(1)} %step.7.previous), channel_id=1, source_target_pairs={{0,10},{1,11},{2,8},{3,9},{4,5},{5,4},{6,7},{7,6},{8,14},{9,15},{1... | collective-permute-start | bytes 147464 | tf_op jit(solution)/shard_map/ppermute | solution.py:233
  27.6 3.5 %collective-permute-start.13 = (bf16[16,1536]{1,0:T(8,128)(2,1)S(1)}, bf16[16,1536]{1,0:T(8,128)(2,1)S(1)}, u32[]{:S(2)}, u32[]{:S(2)}) collective-permute-start(bf16[16,1536]{1,0:T(8,128)(2,1)S(1)} %step.7.previous), channel_id=1, source_target_pairs={{0,1},{1,0},{2,3},{3,2},{4,8},{5,9},{6,10},{7,11},{8,12},{9,13},{1... | collective-permute-start | bytes 147464 | tf_op jit(solution)/shard_map/ppermute | solution.py:233
  31.1 0.0 collective-permute-done.12.far
  31.1 1.2 %collective-permute-done.13.near = bf16[16,1536]{1,0:T(8,128)(2,1)S(1)} collective-permute-done((bf16[16,1536]{1,0:T(8,128)(2,1)S(1)}, bf16[16,1536]{1,0:T(8,128)(2,1)S(1)}, u32[]{:S(2)}, u32[]{:S(2)}) %collective-permute-start.13) | collective-permute-done | bytes 49184 | tf_op jit(solution)/shard_map/ppermute | solution.py:233
  32.3 1.3 %step.9 = bf16[16,768]{1,0:T(8,128)(2,1)S(1)} custom-call(bf16[16,1536]{1,0:T(8,128)(2,1)S(1)} %collective-permute-done.12.far, bf16[16,1536]{1,0:T(8,128)(2,1)S(1)} %collective-permute-done.13.near, bf16[16,1536]{1,0:T(8,128)(2,1)S(1)} %step.7.previous, f32[16,1536]{1,0:T(8,128)S(1)} %get-tuple-element.25.load, ...), custom_call_target="tpu_custom_call" | custom-call | tf_op jit(solution)/shard_map/step/pallas_call | solution.py:300
  33.6 2.9 %collective-permute-start.14 = (bf16[16,768]{1,0:T(8,128)(2,1)S(1)}, bf16[16,768]{1,0:T(8,128)(2,1)S(1)}, u32[]{:S(2)}, u32[]{:S(2)}) collective-permute-start(bf16[16,768]{1,0:T(8,128)(2,1)S(1)} %step.9), channel_id=1, source_target_pairs={{0,1},{1,0},{2,3},{3,2},{4,5},{5,4},{6,7},{7,6},{8,9},{9,8},{10,11... | collective-permute-start | bytes 73736 | tf_op jit(solution)/shard_map/ppermute | solution.py:213
  36.5 1.3 %step.8.kept = bf16[16,768]{1,0:T(8,128)(2,1)S(1)} custom-call(bf16[16,1536]{1,0:T(8,128)(2,1)S(1)} %collective-permute-done.12.far, bf16[16,1536]{1,0:T(8,128)(2,1)S(1)} %collective-permute-done.13.near, bf16[16,1536]{1,0:T(8,128)(2,1)S(1)} %step.7.previous, f32[16,1536]{1,0:T(8,128)S(1)} %get-tuple-element.25.load, ...), custom_call_target="tpu_custom_call" | custom-call | tf_op jit(solution)/shard_map/step/pallas_call | solution.py:300
  37.8 0.0 collective-permute-done.14.got
  37.8 0.6 %finish.1 = bf16[32,768]{1,0:T(8,128)(2,1)} custom-call(bf16[16,768]{1,0:T(8,128)(2,1)S(1)} %step.8.kept, bf16[16,768]{1,0:T(8,128)(2,1)S(1)} %collective-permute-done.14.got), custom_call_target="tpu_custom_call" | custom-call | tf_op jit(solution)/shard_map/finish/pallas_call | solution.py:322
  (3 shorter events, 0.1 us)
Async XLA Ops:
  2.8 2.9 %collective-permute-start.3 = (bf16[6,2,128,128]{3,2,1,0:T(8,128)(2,1)S(1)}, bf16[6,2,128,128]{3,2,1,0:T(8,128)(2,1)S(1)}, u32[]{:S(2)}, u32[]{:S(2)}) collective-permute-start(bf16[6,2,128,128]{3,2,1,0:T(8,128)(2,1)S(1)} %get-tuple-element.22), channel_id=1, source_target_pairs={{0,1},{1,0},{2,3},{3,2},{4,5},{5,4},{6,7},{7,6},{8,9},{9,8},{10,11... | collective-permute-start | bytes 1179656 | tf_op jit(solution)/shard_map/ppermute | solution.py:213
  3.6 2.1 %collective-permute-start = (bf16[16,1536]{1,0:T(8,128)(2,1)S(1)}, bf16[16,1536]{1,0:T(8,128)(2,1)S(1)}, u32[]{:S(2)}, u32[]{:S(2)}) collective-permute-start(bf16[16,1536]{1,0:T(8,128)(2,1)S(1)} %get-tuple-element.18), channel_id=1, source_target_pairs={{0,1},{1,0},{2,3},{3,2},{4,5},{5,4},{6,7},{7,6},{8,9},{9,8},{10,11... | collective-permute-start | bytes 147464 | tf_op jit(solution)/shard_map/ppermute | solution.py:213
  3.6 5.5 %collective-permute-start.1 = (bf16[16,1536]{1,0:T(8,128)(2,1)S(1)}, bf16[16,1536]{1,0:T(8,128)(2,1)S(1)}, u32[]{:S(2)}, u32[]{:S(2)}) collective-permute-start(bf16[16,1536]{1,0:T(8,128)(2,1)S(1)} %get-tuple-element.19), channel_id=1, source_target_pairs={{0,2},{1,3},{2,0},{3,1},{4,6},{5,7},{6,4},{7,5},{8,10},{9,11},{10,... | collective-permute-start | bytes 147464 | tf_op jit(solution)/shard_map/ppermute | solution.py:213
  4.9 4.3 %collective-permute-start.2 = (bf16[16,1536]{1,0:T(8,128)(2,1)S(1)}, bf16[16,1536]{1,0:T(8,128)(2,1)S(1)}, u32[]{:S(2)}, u32[]{:S(2)}) collective-permute-start(bf16[16,1536]{1,0:T(8,128)(2,1)S(1)} %get-tuple-element.20), channel_id=1, source_target_pairs={{0,3},{1,2},{2,1},{3,0},{4,7},{5,6},{6,5},{7,4},{8,11},{9,10},{10,... | collective-permute-start | bytes 147464 | tf_op jit(solution)/shard_map/ppermute | solution.py:213
  9.2 2.6 %copy-start = (s32[1,6,8]{2,0,1:T(1,128)S(1)}, s32[1,6,8]{2,0,1:T(1,128)}, u32[]{:S(2)}) copy-start(s32[1,6,8]{2,0,1:T(1,128)} %param.9) | copy-start | bytes 580
  9.5 5.7 %collective-permute-start.6 = (bf16[6,8,2,128,128]{4,3,2,1,0:T(8,128)(2,1)S(1)}, bf16[6,8,2,128,128]{4,3,2,1,0:T(8,128)(2,1)S(1)}, u32[]{:S(2)}, u32[]{:S(2)}) collective-permute-start(bf16[6,8,2,128,128]{4,3,2,1,0:T(8,128)(2,1)S(1)} %get-tuple-element.27), channel_id=1, source_target_pairs={{0,1},{1,0},{2,3},{3,2},{4,5},{5,4},{6,7},{7,6},{8,9},{9,8},{10,11... | collective-permute-start | bytes 9437192 | tf_op jit(solution)/shard_map/ppermute | solution.py:213
  9.9 5.3 %collective-permute-start.4 = (bf16[16,1536]{1,0:T(8,128)(2,1)S(1)}, bf16[16,1536]{1,0:T(8,128)(2,1)S(1)}, u32[]{:S(2)}, u32[]{:S(2)}) collective-permute-start(bf16[16,1536]{1,0:T(8,128)(2,1)S(1)} %get-tuple-element.24.previous), channel_id=1, source_target_pairs={{0,6},{1,7},{2,4},{3,5},{4,10},{5,11},{6,8},{7,9},{8,14},{9,15},{1... | collective-permute-start | bytes 147464 | tf_op jit(solution)/shard_map/ppermute | solution.py:233
  10.5 4.7 %collective-permute-start.5 = (bf16[16,1536]{1,0:T(8,128)(2,1)S(1)}, bf16[16,1536]{1,0:T(8,128)(2,1)S(1)}, u32[]{:S(2)}, u32[]{:S(2)}) collective-permute-start(bf16[16,1536]{1,0:T(8,128)(2,1)S(1)} %get-tuple-element.24.previous), channel_id=1, source_target_pairs={{0,4},{1,5},{2,6},{3,7},{4,8},{5,9},{6,10},{7,11},{8,12},{9,13},{1... | collective-permute-start | bytes 147464 | tf_op jit(solution)/shard_map/ppermute | solution.py:233
  11.8 3.4 %collective-permute-start.7 = (s32[6,1,8]{2,1,0:T(1,128)S(1)}, s32[6,1,8]{2,1,0:T(1,128)S(1)}, u32[]{:S(2)}, u32[]{:S(2)}) collective-permute-start(s32[6,1,8]{2,1,0:T(1,128)S(1)} %bitcast.7), channel_id=1, source_target_pairs={{0,1},{1,0},{2,3},{3,2},{4,5},{5,4},{6,7},{7,6},{8,9},{9,8},{10,11... | collective-permute-start | bytes 584 | tf_op jit(solution)/shard_map/ppermute | solution.py:213
  15.3 3.2 %collective-permute-start.8 = (bf16[16,1536]{1,0:T(8,128)(2,1)S(1)}, bf16[16,1536]{1,0:T(8,128)(2,1)S(1)}, u32[]{:S(2)}, u32[]{:S(2)}) collective-permute-start(bf16[16,1536]{1,0:T(8,128)(2,1)S(1)} %step.5.previous), channel_id=1, source_target_pairs={{0,6},{1,7},{2,4},{3,5},{4,10},{5,11},{6,8},{7,9},{8,2},{9,3},{10,... | collective-permute-start | bytes 147464 | tf_op jit(solution)/shard_map/ppermute | solution.py:233
  15.8 4.0 %collective-permute-start.9 = (bf16[16,1536]{1,0:T(8,128)(2,1)S(1)}, bf16[16,1536]{1,0:T(8,128)(2,1)S(1)}, u32[]{:S(2)}, u32[]{:S(2)}) collective-permute-start(bf16[16,1536]{1,0:T(8,128)(2,1)S(1)} %step.5.previous), channel_id=1, source_target_pairs={{0,4},{1,5},{2,6},{3,7},{4,12},{5,13},{6,14},{7,15},{8,9},{9,8},{1... | collective-permute-start | bytes 147464 | tf_op jit(solution)/shard_map/ppermute | solution.py:233
  19.9 4.3 %collective-permute-start.10 = (bf16[16,1536]{1,0:T(8,128)(2,1)S(1)}, bf16[16,1536]{1,0:T(8,128)(2,1)S(1)}, u32[]{:S(2)}, u32[]{:S(2)}) collective-permute-start(bf16[16,1536]{1,0:T(8,128)(2,1)S(1)} %step.6.previous), channel_id=1, source_target_pairs={{0,1},{1,0},{2,3},{3,2},{4,10},{5,11},{6,8},{7,9},{8,14},{9,15},{1... | collective-permute-start | bytes 147464 | tf_op jit(solution)/shard_map/ppermute | solution.py:233
  23.0 3.6 %collective-permute-start.11 = (bf16[16,1536]{1,0:T(8,128)(2,1)S(1)}, bf16[16,1536]{1,0:T(8,128)(2,1)S(1)}, u32[]{:S(2)}, u32[]{:S(2)}) collective-permute-start(bf16[16,1536]{1,0:T(8,128)(2,1)S(1)} %step.6.previous), channel_id=1, source_target_pairs={{0,1},{1,0},{2,3},{3,2},{4,8},{5,9},{6,10},{7,11},{8,12},{9,13},{1... | collective-permute-start | bytes 147464 | tf_op jit(solution)/shard_map/ppermute | solution.py:233
  26.6 4.5 %collective-permute-start.12 = (bf16[16,1536]{1,0:T(8,128)(2,1)S(1)}, bf16[16,1536]{1,0:T(8,128)(2,1)S(1)}, u32[]{:S(2)}, u32[]{:S(2)}) collective-permute-start(bf16[16,1536]{1,0:T(8,128)(2,1)S(1)} %step.7.previous), channel_id=1, source_target_pairs={{0,10},{1,11},{2,8},{3,9},{4,5},{5,4},{6,7},{7,6},{8,14},{9,15},{1... | collective-permute-start | bytes 147464 | tf_op jit(solution)/shard_map/ppermute | solution.py:233
  27.6 4.7 %collective-permute-start.13 = (bf16[16,1536]{1,0:T(8,128)(2,1)S(1)}, bf16[16,1536]{1,0:T(8,128)(2,1)S(1)}, u32[]{:S(2)}, u32[]{:S(2)}) collective-permute-start(bf16[16,1536]{1,0:T(8,128)(2,1)S(1)} %step.7.previous), channel_id=1, source_target_pairs={{0,1},{1,0},{2,3},{3,2},{4,8},{5,9},{6,10},{7,11},{8,12},{9,13},{1... | collective-permute-start | bytes 147464 | tf_op jit(solution)/shard_map/ppermute | solution.py:233
  33.6 4.2 %collective-permute-start.14 = (bf16[16,768]{1,0:T(8,128)(2,1)S(1)}, bf16[16,768]{1,0:T(8,128)(2,1)S(1)}, u32[]{:S(2)}, u32[]{:S(2)}) collective-permute-start(bf16[16,768]{1,0:T(8,128)(2,1)S(1)} %step.9), channel_id=1, source_target_pairs={{0,1},{1,0},{2,3},{3,2},{4,5},{5,4},{6,7},{7,6},{8,9},{9,8},{10,11... | collective-permute-start | bytes 73736 | tf_op jit(solution)/shard_map/ppermute | solution.py:213
